TPU v7x, 512 devices: a whole 4x4x16 slice. The times are simulated.
512 devices in a mesh: dp: 16 (over y, x), expert: 16 (over z), tensor: 2 (over core).
Axes of the slice: x: 4, y: 4, z: 16, core: 2. Of those that a mesh axis runs over, the one named last changes fastest.
Arguments:
- tokens: bfloat16 [4096, 3072], P(('expert', 'tensor')), may hold values from -6 to 6
- expert_ids: int32 [4096, 4], P('expert'), may hold values from 0 to 15, all different within a row; in each aligned block of 128 rows (0 to 127, 128 to 255, ...) at most 34 rows name the same one
- gate_values: float32 [4096, 4], P('expert'), may hold values from 0.1 to 1
- w_gate: bfloat16 [16, 5376, 3072], P('expert', ('dp', 'tensor')), may hold values from -0.109375 to 0.109375
- w_up: bfloat16 [16, 5376, 3072], P('expert', ('dp', 'tensor')), may hold values from -0.109375 to 0.109375
- w_down: bfloat16 [16, 5376, 3072], P('expert', ('dp', 'tensor')), may hold values from -0.15625 to 0.15625
Outputs:
- mixed: bfloat16 [4096, 3072], P(('expert', 'tensor'), 'dp')
Inputs may be any that keep to these rules, and one draw needn't show every extreme that they name: `expert_ids`: each row names 4 different experts; in each aligned block of 128 rows (the rows of one device) no expert is named by more than 34 entries.
All inputs are finite; a program needn't handle non-finite values.
Results may differ from a plain program's by a relative error of at most 0.012.
Values may be sent and summed in bfloat16 or wider, within the bound.
No kernel may reach another device: no remote copies, remote signals or barrier semaphores. Data moves between devices by JAX's collectives and lax.ppermute only.
A program may use at most 128 MiB of HBM per device.

v0:
```python
import jax
import jax.numpy as jnp
from jax import lax
from jax.sharding import PartitionSpec as P

EXPERTS = 16
TOP = 4
CAP = 34


def block_slots(id_block):
    flat_ids = id_block.reshape(-1)
    onehot = (flat_ids[:, None] == jnp.arange(EXPERTS, dtype=jnp.int32)[None, :]).astype(jnp.int32)
    ranked = jnp.cumsum(onehot, axis=0) - onehot
    return jnp.sum(ranked * onehot, axis=1).reshape(id_block.shape)


def block_table(id_block, slot_ids):
    row_count = id_block.shape[0]
    position = (id_block * CAP + slot_ids).reshape(-1)
    owners = jnp.repeat(jnp.arange(row_count, dtype=jnp.int32), id_block.shape[1])
    empty_slots = jnp.full((EXPERTS * CAP,), row_count, jnp.int32)
    return empty_slots.at[position].set(owners)


def fill_slots(token_rows, table):
    padded = jnp.concatenate(
        [token_rows, jnp.zeros((1, token_rows.shape[1]), token_rows.dtype)], axis=0
    )
    return padded[table]


def pick_rows(returned_rows, positions):
    return returned_rows[positions]


def expert_work(received, w_gate, w_up, w_down):
    hidden_width = w_gate.shape[1]
    stacked = jnp.concatenate([w_gate, w_up], axis=1)
    both_act = jnp.einsum("pslcd,lfd->pslcf", received, stacked, preferred_element_type=jnp.float32)
    gate_act = both_act[..., :hidden_width]
    up_act = both_act[..., hidden_width:]
    hidden = (jax.nn.silu(gate_act) * up_act).astype(jnp.bfloat16)
    partial_out = jnp.einsum("pslcf,lfd->pslcd", hidden, w_down, preferred_element_type=jnp.float32)
    return partial_out.astype(jnp.bfloat16)


def shards(tokens, expert_ids, gate_values, w_gate, w_up, w_down):
    tok_dev, model_width = tokens.shape
    pair_size = lax.axis_size("tensor")
    expert_devs = lax.axis_size("expert")
    local_experts = w_gate.shape[0]
    id_planes = expert_ids.reshape(pair_size, tok_dev, TOP)
    slot_planes = jax.vmap(block_slots)(id_planes)
    tables = jax.vmap(block_table)(id_planes, slot_planes)
    both_planes = lax.all_gather(tokens[None], "tensor", axis=0, tiled=True)
    outgoing = jax.vmap(fill_slots)(both_planes, tables)
    outgoing = outgoing.reshape(pair_size, expert_devs, local_experts, CAP, model_width)
    arrived = lax.all_to_all(outgoing, "expert", split_axis=1, concat_axis=1, tiled=True)
    partials = expert_work(arrived, w_gate, w_up, w_down)
    positions = id_planes * CAP + slot_planes
    weights = gate_values.reshape(pair_size, tok_dev, TOP)
    returned = lax.all_to_all(partials, "expert", split_axis=1, concat_axis=1, tiled=True)
    returned = returned.reshape(pair_size, EXPERTS * CAP, model_width)
    combined = jnp.zeros((pair_size, tok_dev, model_width), jnp.float32)
    for choice_k in range(TOP):
        picked = jax.vmap(pick_rows)(returned, positions[:, :, choice_k])
        combined = combined + weights[:, :, choice_k, None] * picked.astype(jnp.float32)
    own_plane = lax.psum_scatter(combined, "tensor", scatter_dimension=0, tiled=True)
    mixed_out = lax.psum_scatter(own_plane[0], "dp", scatter_dimension=1, tiled=True)
    return mixed_out.astype(jnp.bfloat16)


def solution(mesh):
    placed = (
        P(("expert", "tensor"), None),
        P("expert", None),
        P("expert", None),
        P("expert", ("dp", "tensor"), None),
        P("expert", ("dp", "tensor"), None),
        P("expert", ("dp", "tensor"), None),
    )
    return jax.shard_map(
        shards, mesh=mesh, in_specs=placed, out_specs=P(("expert", "tensor"), "dp"), check_vma=False
    )
```

profile of v0, /device:TPU:6, one launch (start us, length us, event | category | flops | bytes accessed | tf_op | source)
XLA Modules:
  0.0 874.7 jit_solution(361281822496444285)
XLA Ops:
  6.5 0.7 all-gather.3.cloned.1.call-update
  7.3 0.8 copy.43
  8.1 0.1 eq.29
  8.2 0.1 eq.25
  8.3 0.1 reshape.78
  8.5 0.7 broadcast_multiply_fusion
  9.2 0.1 copy.42
  9.3 0.1 mul.71
  9.5 2.3 reduce-window.6
  11.7 0.3 slice_reduce_fusion
  12.1 0.1 fusion.30
  12.2 0.7 multiply_reduce_fusion
  13.0 0.7 and_reduce_fusion
  13.7 4.3 scatter_custom_fusion
  18.1 0.1 reshape.88
  18.2 0.1 reshape.89
  18.2 15.9 %all-gather.3.cloned.1.call-done = bf16[256,3072]{1,0:T(8,128)(2,1)} async-done(((bf16[128,3072]{1,0:T(8,128)(2,1)}), bf16[256,3072]{1,0:T(8,128)(2,1)}) %all-gather.3.cloned.1.call-update) | async-done | bytes 1572880 | tf_op jit(solution)/shard_map/all_gather | solution.py:56
  34.1 3.0 copy.41
  37.2 1.2 concatenate.7
  38.4 25.7 %gather_fusion = bf16[1088,3072]{1,0:T(8,128)(2,1)} fusion(bf16[2,129,3072]{2,0,1:T(2,128)(2,1)S(1)} %concatenate.7, s32[1088]{0:T(1024)S(1)} %reshape.89), kind=kCustom, calls=%fused_computation | custom fusion | bytes 13378048 | tf_op jit(solution)/shard_map/vmap()/gather | solution.py:30
  64.1 8.8 %reshape.79 = bf16[2,16,1,34,3072]{4,3,1,0,2:T(8,128)(2,1)} reshape(bf16[1088,3072]{1,0:T(8,128)(2,1)} %gather_fusion) | data formatting | bytes 13369344 | tf_op jit(solution)/shard_map/reshape | solution.py:58
  72.9 12.7 %copy.46 = bf16[2,16,1,34,3072]{4,0,3,2,1:T(2,128)(2,1)S(1)} copy(bf16[2,16,1,34,3072]{4,3,1,0,2:T(8,128)(2,1)} %reshape.79) | data formatting | bytes 13369344 | tf_op jit(solution)/shard_map/reshape | solution.py:58
  85.6 0.0 copy-start.3
  85.6 306.7 %all_to_all.10 = bf16[2,16,1,34,3072]{4,0,3,2,1:T(2,128)(2,1)S(1)} all-to-all(bf16[2,16,1,34,3072]{4,0,3,2,1:T(2,128)(2,1)S(1)} %copy.46), channel_id=1, replica_groups=mesh['dp'=16,'expert'=16,'tensor'=2] {'expert'}, dimensions={1} | all-to-all | bytes 13369344 | tf_op jit(solution)/shard_map/all_to_all | solution.py:59
  392.2 4.3 fusion.5
  396.6 2.4 convert_bitcast_fusion
  399.0 6.5 copy.48
  405.5 5.8 all-to-all-start.1
  411.3 0.3 reduce-scatter.3.cloned.1.call-start
  411.6 0.1 reshape.84
  411.8 0.3 fusion.15
  412.1 288.4 %all-to-all-done.1 = bf16[2,16,1,34,3072]{4,0,3,2,1:T(2,128)(2,1)} async-done(((bf16[2,16,1,34,3072]{4,0,3,2,1:T(2,128)(2,1)}), bf16[2,16,1,34,3072]{4,0,3,2,1:T(2,128)(2,1)}, u32[]{:S(2)}, u32[]{:S(2)}) %all-to-all-start.1) | async-done | bytes 6684704 | tf_op jit(solution)/shard_map/all_to_all | solution.py:63
  700.5 7.6 copy.50
  708.2 5.0 gather_fusion.4
  713.2 6.2 gather_fusion.3
  719.4 6.4 gather_fusion.2
  725.7 6.1 gather_fusion.1
  731.9 3.1 copy.53
  735.0 3.1 copy.51
  738.1 3.1 copy.55
  741.2 2.0 copy.57
  743.2 7.1 multiply_add_fusion
  750.3 0.0 reduce-scatter.3.cloned.1.call-update
  750.3 0.0 reduce-scatter.5.cloned.1.call-start
  750.4 21.1 %reduce-scatter.3.cloned.1.call-done = f32[1,128,3072]{1,2,0:T(8,128)} async-done(((f32[2,128,3072]{1,2,0:T(8,128)}), f32[1,128,3072]{1,2,0:T(8,128)}) %reduce-scatter.3.cloned.1.call-update) | async-done | bytes 1572880 | tf_op jit(solution)/shard_map/reduce_scatter | solution.py:69
  771.5 0.0 reduce-scatter.5.cloned.1.call-update
  771.5 94.7 %reduce-scatter.5.cloned.1.call-done = f32[128,192]{0,1:T(8,128)} async-done(((f32[128,3072]{0,1:T(8,128)}), f32[128,192]{0,1:T(8,128)}) %reduce-scatter.5.cloned.1.call-update) | async-done | bytes 98320 | tf_op jit(solution)/shard_map/reduce_scatter | solution.py:70
  866.2 1.5 convert_element_type.48
  (24 shorter events, 0.2 us)
Async XLA Ops:
  6.5 390.1 %copy-start = (bf16[1,168,3072]{2,1,0:T(8,128)(2,1)S(1)}, bf16[1,168,3072]{2,1,0:T(8,128)(2,1)}, u32[]{:S(2)}) copy-start(bf16[1,168,3072]{2,1,0:T(8,128)(2,1)} %param.11) | copy-start | bytes 3096580
  6.5 27.6 %all-gather.3.cloned.1.call-start = ((), (), s32[]{:S(2)}) async-start(), calls=%async_computation.6 | async-start | bytes 2359296 | tf_op jit(solution)/shard_map/all_gather | solution.py:56
  85.6 306.7 %copy-start.3 = (bf16[1,168,3072]{2,1,0:T(8,128)(2,1)S(1)}, bf16[1,168,3072]{2,1,0:T(8,128)(2,1)}, u32[]{:S(2)}) copy-start(bf16[1,168,3072]{2,1,0:T(8,128)(2,1)} %param.10) | copy-start | bytes 3096580
  85.6 306.7 %copy-start.4 = (bf16[1,168,3072]{2,1,0:T(8,128)(2,1)S(1)}, bf16[1,168,3072]{2,1,0:T(8,128)(2,1)}, u32[]{:S(2)}) copy-start(bf16[1,168,3072]{2,1,0:T(8,128)(2,1)} %param.9) | copy-start | bytes 3096580
  405.5 6.2 copy-start.2
  405.5 295.0 %all-to-all-start.1 = ((bf16[2,16,1,34,3072]{4,0,3,2,1:T(2,128)(2,1)}), bf16[2,16,1,34,3072]{4,0,3,2,1:T(2,128)(2,1)}, u32[]{:S(2)}, u32[]{:S(2)}) async-start(bf16[2,16,1,34,3072]{4,0,3,2,1:T(2,128)(2,1)} %copy.48), calls=%async_computation.1 | async-start | bytes 13369344 | tf_op jit(solution)/shard_map/all_to_all | solution.py:63
  411.3 360.2 %reduce-scatter.3.cloned.1.call-start = ((), (), s32[]{:S(2)}) async-start(), calls=%async_computation.4 | async-start | bytes 4718592 | tf_op jit(solution)/shard_map/reduce_scatter | solution.py:69
  743.2 124.5 %copy-start.1 = (bf16[1,168,3072]{2,1,0:T(8,128)(2,1)S(1)}, bf16[1,168,3072]{2,1,0:T(8,128)(2,1)}, u32[]{:S(2)}) copy-start(bf16[1,168,3072]{2,1,0:T(8,128)(2,1)} %param.11) | copy-start | bytes 3096580
  750.3 115.8 %reduce-scatter.5.cloned.1.call-start = ((), (), s32[]{:S(2)}) async-start(), calls=%async_computation.5 | async-start | bytes 1671168 | tf_op jit(solution)/shard_map/reduce_scatter | solution.py:70
Sparse Core Ops, SparseCore 0:
  9.4 24.6 all-gather.2
  750.4 20.9 reduce-scatter.2
  776.1 89.9 reduce-scatter.4
where the time goes:
time: 883 us; the launch traced here: 875 us
  waiting for transfers between devices  421 us (48%)
  blocking collectives  307 us (35%)
  local copies, waits for them, and re-layouts  107 us (12%)
  between operations  13.7 us (2%)
  other arithmetic  13.6 us (2%)
    all_to_all x1, blocking collectives, shards(): lax.all_to_all(outgoing, 'expert', split_axis=1, concat_axis=1, tiled=True)  307 us
    all_to_all x1, waiting for transfers between devices, shards(): lax.all_to_all(partials, 'expert', split_axis=1, concat_axis=1, tiled=True)  288 us
    reduce_scatter x1, waiting for transfers between devices, shards(): lax.psum_scatter(own_plane[0], 'dp', scatter_dimension=1, tiled=True)  94.7 us
    gather x2, local copies, waits for them, and re-layouts, fill_slots(): return padded[table]  25.8 us
    gather x4, local copies, waits for them, and re-layouts, pick_rows(): return returned_rows[positions]  23.7 us
    reshape x2, local copies, waits for them, and re-layouts, shards(): outgoing.reshape(pair_size, expert_devs, local_experts, CAP, model_width)  21.4 us
    reduce_scatter x1, waiting for transfers between devices, shards(): lax.psum_scatter(combined, 'tensor', scatter_dimension=0, tiled=True)  21.1 us
  transfers between devices with their start and end apart: 4, of which 4 were waited for; matrix products, arithmetic and copies ran while one was open for 1% of the time, Pallas kernels for 0%

commit v1 on v0

v1 whole, which is shorter than its diff:
```python
import jax
import jax.numpy as jnp
from jax import lax
from jax.experimental import pallas as pl
from jax.experimental.pallas import tpu as pltpu
from jax.sharding import PartitionSpec as P

EXPERTS = 16
TOP = 4
CAP = 34
HALF = CAP // 2
DP = 16
VMEM = 60 * 1024 * 1024
F32 = jnp.float32
BF16 = jnp.bfloat16


def dot(a, b):
    return jnp.dot(a, b, preferred_element_type=F32)


def dot_t(a, b):
    return lax.dot_general(a, b, (((1,), (1,)), ((), ())), preferred_element_type=F32)


def row_places(shape, dim):
    row = lax.broadcasted_iota(jnp.int32, shape, dim).astype(F32)
    expert = jnp.floor((row + 0.5) * (1.0 / HALF))
    return expert, row - HALF * expert


def dispatch_kernel(ids_ref, rows_ref, out_ref):
    n = ids_ref.shape[1]
    experts = lax.broadcasted_iota(jnp.int32, (EXPERTS, n), 0)
    named = jnp.zeros((EXPERTS, n), F32)
    for k in range(TOP):
        named += (ids_ref[k : k + 1, :] == experts).astype(F32)
    earlier = lax.broadcasted_iota(jnp.int32, (n, n), 0) < lax.broadcasted_iota(jnp.int32, (n, n), 1)
    rank = dot(named.astype(BF16), earlier.astype(BF16))
    key = jnp.where(named > 0.0, rank, -1.0)
    expert, _ = row_places((EXPERTS * HALF, EXPERTS), 0)
    spread = (expert == lax.broadcasted_iota(jnp.int32, (EXPERTS * HALF, EXPERTS), 1).astype(F32)).astype(BF16)
    wide = dot(spread, key.astype(BF16))
    _, s = row_places((EXPERTS * HALF, n), 0)
    first = dot((wide == s).astype(BF16), rows_ref[...])
    second = dot((wide == s + HALF).astype(BF16), rows_ref[...])
    out_ref[...] = jnp.concatenate([first, second], axis=1).astype(BF16)


def expert_kernel(x_ref, gate0, up0, down0, gate1, up1, down1, out_ref, rows):
    parts, half_rows, two = x_ref.shape
    width = two // 2
    for side in range(2):
        for d in range(parts):
            rows[side * half_rows : (side + 1) * half_rows, d * width : (d + 1) * width] = x_ref[
                d, :, side * width : (side + 1) * width
            ]
    for side in range(2):
        x = rows[side * half_rows : (side + 1) * half_rows, :]
        total = None
        for gate, up, down in ((gate0, up0, down0), (gate1, up1, down1)):
            g = dot_t(x, gate[...])
            u = dot_t(x, up[...])
            hidden = (g / (1.0 + jnp.exp(-g)) * u).astype(BF16)
            part = dot(hidden, down[...])
            total = part if total is None else total + part
        y = total.astype(BF16)
        for d in range(parts):
            out_ref[d, :, side * width : (side + 1) * width] = y[:, d * width : (d + 1) * width]


def combine_kernel(ids_ref, gates_ref, rows_ref, out_ref):
    n = ids_ref.shape[0]
    width = out_ref.shape[1]
    experts = lax.broadcasted_iota(jnp.int32, (n, EXPERTS), 1)
    named = jnp.zeros((n, EXPERTS), F32)
    gates = jnp.zeros((n, EXPERTS), F32)
    for k in range(TOP):
        hit = (ids_ref[:, k : k + 1] == experts).astype(F32)
        named += hit
        gates += hit * gates_ref[:, k : k + 1]
    earlier = lax.broadcasted_iota(jnp.int32, (n, n), 1) < lax.broadcasted_iota(jnp.int32, (n, n), 0)
    rank = dot(earlier.astype(BF16), named.astype(BF16))
    key = jnp.where(named > 0.0, rank, -1.0)
    expert, _ = row_places((EXPERTS, EXPERTS * HALF), 1)
    spread = (expert == lax.broadcasted_iota(jnp.int32, (EXPERTS, EXPERTS * HALF), 0).astype(F32)).astype(BF16)
    wide = dot(key.astype(BF16), spread)
    _, s = row_places((n, EXPERTS * HALF), 1)
    first, second = wide == s, wide == s + HALF
    total = jnp.zeros((n, width), F32)
    for _ in range(3):
        piece = gates.astype(BF16)
        gates = gates - piece.astype(F32)
        weight = dot(piece, spread)
        total += dot(jnp.where(first, weight, 0.0).astype(BF16), rows_ref[:, :width])
        total += dot(jnp.where(second, weight, 0.0).astype(BF16), rows_ref[:, width:])
    out_ref[...] = total.astype(BF16)


def call(kernel, out, *args, scratch=()):
    return pl.pallas_call(
        kernel,
        out_shape=out,
        scratch_shapes=scratch,
        compiler_params=pltpu.CompilerParams(vmem_limit_bytes=VMEM),
    )(*args)


def swap(value):
    return lax.ppermute(value, "tensor", [(0, 1), (1, 0)])


def exchange(value, axis):
    return lax.all_to_all(value, axis, split_axis=0, concat_axis=0, tiled=True)


def shards(tokens, expert_ids, gate_values, w_gate, w_up, w_down):
    n, width = tokens.shape
    part = width // DP
    slots = EXPERTS * HALF
    core, place = lax.axis_index("tensor"), lax.axis_index("dp")
    weights = [w_gate[0], w_up[0], w_down[0]]
    others = [swap(w) for w in weights]
    ids = lax.dynamic_slice_in_dim(expert_ids, core * n, n, 0)
    gates = lax.dynamic_slice_in_dim(gate_values, core * n, n, 0)
    own = lax.dynamic_slice_in_dim(tokens, place * part, part, 1)
    sent = call(dispatch_kernel, jax.ShapeDtypeStruct((slots, 2 * part), BF16), ids.T, own)
    arrived = exchange(sent.reshape(EXPERTS, HALF, 2 * part), "expert").reshape(1, slots, 2 * part)
    rows = exchange(jnp.broadcast_to(arrived, (DP, slots, 2 * part)), "dp")
    partial = call(
        expert_kernel,
        jax.ShapeDtypeStruct((DP, slots, 2 * part), BF16),
        rows,
        *weights,
        *others,
        scratch=[pltpu.VMEM((2 * slots, width), BF16)],
    )
    partial = exchange(partial, "dp")
    summed = jnp.sum(partial.astype(F32), axis=0).astype(BF16)
    back = exchange(summed.reshape(EXPERTS, HALF, 2 * part), "expert").reshape(slots, 2 * part)
    return call(combine_kernel, jax.ShapeDtypeStruct((n, part), BF16), ids, gates, back)


def solution(mesh):
    placed = (
        P(("expert", "tensor"), None),
        P("expert", None),
        P("expert", None),
        P("expert", ("dp", "tensor"), None),
        P("expert", ("dp", "tensor"), None),
        P("expert", ("dp", "tensor"), None),
    )
    return jax.shard_map(
        shards, mesh=mesh, in_specs=placed, out_specs=P(("expert", "tensor"), "dp"), check_vma=False
    )
```

time: 883 us -> 190 us (0.22)
  waiting for transfers between devices: 421 us -> 42.4 us
  blocking collectives: 307 us -> 79 us
  local copies, waits for them, and re-layouts: 107 us -> 11 us
  starting transfers between devices: 6.11 us -> 34.9 us
  Pallas kernels: 0 us -> 15.9 us
  between operations: 13.7 us -> 0.1 us
  other arithmetic: 13.6 us -> 2.5 us
    all_to_all x1 -> x2, waiting for transfers between devices: 288 us -> 41.2 us  [exchange(): return lax.all_to_all(value, axis, split_axis=0, concat_axis=0, tiled=True)]
    all_to_all x1 -> x2, blocking collectives: 307 us -> 79 us  [exchange(): return lax.all_to_all(value, axis, split_axis=0, concat_axis=0, tiled=True)]
    reduce_scatter x2 -> x0, waiting for transfers between devices: 116 us -> none  [the longest x1 94.7 us: shards(): lax.psum_scatter(own_plane[0], 'dp', scatter_dimension=1, tiled=True)]
    gather x6 -> x0, local copies, waits for them, and re-layouts: 49.5 us -> none  [the longest x2 25.8 us: fill_slots(): return padded[table]]
    reshape x6 -> x3, local copies, waits for them, and re-layouts: 29.3 us -> 2.57 us  [the longest x1 1.01 us: shards(): sent.reshape(EXPERTS, HALF, 2 * part)]
    all_to_all x1 -> x2, starting transfers between devices: 5.81 us -> 28.7 us  [exchange(): return lax.all_to_all(value, axis, split_axis=0, concat_axis=0, tiled=True)]
    convert_element_type x5 -> x0, local copies, waits for them, and re-layouts: 17.8 us -> none  [the longest x4 11.3 us: shards(): picked.astype(jnp.float32)]
    all_gather x1 -> x0, waiting for transfers between devices: 15.9 us -> none  [shards(): both_planes = lax.all_gather(tokens[None], 'tensor', axis=0, tiled=True)]
  transfers between devices with their start and end apart: 4 -> 5, of which waited for: 4 -> 4; matrix products, arithmetic and copies ran while one was open for 1% -> 0% of each run, Pallas kernels for 0% -> 0%
where the time goes in v1:
time: 190 us; the launch traced here: 186 us
  blocking collectives  79 us (42%)
  waiting for transfers between devices  42.4 us (22%)
  starting transfers between devices  34.9 us (18%)
  Pallas kernels  15.9 us (8%)
  local copies, waits for them, and re-layouts  11 us (6%)
  other arithmetic  2.5 us (1%)
    all_to_all x2, blocking collectives, exchange(): return lax.all_to_all(value, axis, split_axis=0, concat_axis=0, tiled=True)  79 us
    all_to_all x2, waiting for transfers between devices, exchange(): return lax.all_to_all(value, axis, split_axis=0, concat_axis=0, tiled=True)  41.2 us
    all_to_all x2, starting transfers between devices, exchange(): return lax.all_to_all(value, axis, split_axis=0, concat_axis=0, tiled=True)  28.7 us
    pallas_call x3, Pallas kernels, call(): pl.pallas_call(kernel, out_shape=out, scratch_shapes=scratch, compiler_pa...  15.9 us
    ppermute x3, starting transfers between devices, swap(): return lax.ppermute(value, 'tensor', [(0, 1), (1, 0)])  6.25 us
  transfers between devices with their start and end apart: 5, of which 4 were waited for; matrix products, arithmetic and copies ran while one was open for 0% of the time, Pallas kernels for 0%

profile of v1, /device:TPU:6, one launch (start us, length us, event | category | flops | bytes accessed | tf_op | source)
XLA Modules:
  0.0 185.7 jit_solution(6725191354662712776)
XLA Ops:
  0.0 0.0 copy-start
  0.0 0.8 constant_dynamic-slice_fusion.2
  0.8 0.1 copy.15.ids_ref
  0.9 0.0 copy-start.5
  0.9 0.7 copy.13.ids_ref
  1.5 0.0 copy-done
  1.5 0.7 constant_dynamic-slice_fusion.rows_ref
  2.2 2.1 %shard_map.64 = bf16[272,384]{1,0:T(8,128)(2,1)} custom-call(s32[4,128]{1,0:T(4,128)} %copy.13.ids_ref, bf16[128,192]{1,0:T(8,128)(2,1)} %constant_dynamic-slice_fusion.rows_ref), custom_call_target="tpu_custom_call" | custom-call | tf_op jit(solution)/shard_map/pallas_call | solution.py:101
  4.3 1.0 reshape.11
  5.3 34.3 %all_to_all.20 = bf16[16,17,384]{2,1,0:T(8,128)(2,1)S(1)} all-to-all(bf16[16,17,384]{2,1,0:T(8,128)(2,1)S(1)} %reshape.11), channel_id=1, replica_groups=mesh['dp'=16,'expert'=16,'tensor'=2] {'expert'}, dimensions={0} | all-to-all | bytes 417792 | tf_op jit(solution)/shard_map/all_to_all | solution.py:114
  39.6 0.1 broadcast_in_dim.7
  39.7 2.0 %broadcast_in_dim.8 = bf16[16,272,384]{2,1,0:T(8,128)(2,1)} broadcast(bf16[272,384]{1,0:T(8,128)(2,1)S(1)} %broadcast_in_dim.7), dimensions={1,2} | broadcast | bytes 3551232 | tf_op jit(solution)/shard_map/broadcast_in_dim | solution.py:129
  41.7 0.0 copy-start.1
  41.7 0.0 copy-start.2
  41.7 0.0 copy-done.5
  41.7 7.6 %all-to-all-start.1 = ((bf16[16,272,384]{2,1,0:T(8,128)(2,1)}), bf16[16,272,384]{2,1,0:T(8,128)(2,1)}, u32[]{:S(2)}, u32[]{:S(2)}) async-start(bf16[16,272,384]{2,1,0:T(8,128)(2,1)} %broadcast_in_dim.8), calls=%async_computation.1 | async-start | bytes 6684672 | tf_op jit(solution)/shard_map/all_to_all | solution.py:114
  49.3 0.0 copy-done.1
  49.3 1.9 %collective-permute-start = (bf16[168,3072]{1,0:T(8,128)(2,1)S(1)}, bf16[168,3072]{1,0:T(8,128)(2,1)S(1)}, u32[]{:S(2)}, u32[]{:S(2)}) collective-permute-start(bf16[168,3072]{1,0:T(8,128)(2,1)S(1)} %bitcast.5), channel_id=1, source_target_pairs={{0,1},{1,0},{2,3},{3,2},{4,5},{5,4},{6,7},{7,6},{8,9},{9,8},{10,11... | collective-permute-start | bytes 3096584 | tf_op jit(solution)/shard_map/ppermute | solution.py:110
  51.2 0.0 copy-done.2
  51.2 2.4 %collective-permute-start.1 = (bf16[168,3072]{1,0:T(8,128)(2,1)S(1)}, bf16[168,3072]{1,0:T(8,128)(2,1)S(1)}, u32[]{:S(2)}, u32[]{:S(2)}) collective-permute-start(bf16[168,3072]{1,0:T(8,128)(2,1)S(1)} %bitcast.7), channel_id=1, source_target_pairs={{0,1},{1,0},{2,3},{3,2},{4,5},{5,4},{6,7},{7,6},{8,9},{9,8},{10,11... | collective-permute-start | bytes 3096584 | tf_op jit(solution)/shard_map/ppermute | solution.py:110
  53.6 1.9 %collective-permute-start.2 = (bf16[168,3072]{1,0:T(8,128)(2,1)}, bf16[168,3072]{1,0:T(8,128)(2,1)}, u32[]{:S(2)}, u32[]{:S(2)}) collective-permute-start(bf16[168,3072]{1,0:T(8,128)(2,1)} %bitcast.8), channel_id=1, source_target_pairs={{0,1},{1,0},{2,3},{3,2},{4,5},{5,4},{6,7},{7,6},{8,9},{9,8},{10,11... | collective-permute-start | bytes 3096584 | tf_op jit(solution)/shard_map/ppermute | solution.py:110
  55.6 0.0 collective-permute-done.gate1
  55.6 0.0 copy-start.3
  55.6 0.3 collective-permute-done.1.up1
  55.9 0.6 copy-done.3
  56.5 0.0 copy-start.4
  56.5 1.1 copy-done.4
  57.6 0.9 collective-permute-done.2.down1
  58.5 24.8 %all-to-all-done.1.x_ref = bf16[16,272,384]{2,1,0:T(8,128)(2,1)} async-done(((bf16[16,272,384]{2,1,0:T(8,128)(2,1)}), bf16[16,272,384]{2,1,0:T(8,128)(2,1)}, u32[]{:S(2)}, u32[]{:S(2)}) %all-to-all-start.1) | async-done | bytes 3342368 | tf_op jit(solution)/shard_map/all_to_all | solution.py:114
  83.3 11.2 %shard_map.65 = bf16[16,272,384]{2,1,0:T(8,128)(2,1)} custom-call(bf16[16,272,384]{2,1,0:T(8,128)(2,1)} %all-to-all-done.1.x_ref, bf16[168,3072]{1,0:T(8,128)(2,1)} %bitcast.4, bf16[168,3072]{1,0:T(8,128)(2,1)} %bitcast.6, bf16[168,3072]{1,0:T(8,128)(2,1)} %bitcast.9, bf16[168,3072]{1,0:T(8,128)(2,1)} %copy-done.3, bf16[168,3072]{1,0:T(8,128)(2,1)} %copy-done.4, ...), custom_call_target="tpu_custom_call" | custom-call | tf_op jit(solution)/shard_map/pallas_call | solution.py:101
  94.5 44.7 %all_to_all.21 = bf16[16,272,384]{2,1,0:T(8,128)(2,1)} all-to-all(bf16[16,272,384]{2,1,0:T(8,128)(2,1)} %shard_map.65), channel_id=1, replica_groups=mesh['dp'=16,'expert'=16,'tensor'=2] {'dp'}, dimensions={0} | all-to-all | bytes 6684672 | tf_op jit(solution)/shard_map/all_to_all | solution.py:114
  139.2 0.0 copy-start.6
  139.2 2.5 %reduce_sum.12 = bf16[272,384]{1,0:T(8,128)(2,1)S(1)} reduce(bf16[16,272,384]{2,1,0:T(8,128)(2,1)} %all_to_all.21, bf16[]{:T(256)} %constant.22.clone.1), dimensions={0}, to_apply=%region_0.0 | reduce | flops 1566720 | bytes 3551234 | tf_op jit(solution)/shard_map/reduce_sum | solution.py:139
  141.7 0.8 reshape.12
  142.5 21.1 %all-to-all-start.3 = ((bf16[16,17,384]{2,1,0:T(8,128)(2,1)}), bf16[16,17,384]{2,1,0:T(8,128)(2,1)S(1)}, u32[]{:S(2)}, u32[]{:S(2)}) async-start(bf16[16,17,384]{2,1,0:T(8,128)(2,1)} %reshape.12), calls=%async_computation.3 | async-start | bytes 589824 | tf_op jit(solution)/shard_map/all_to_all | solution.py:114
  163.7 0.0 copy-done.6
  163.7 0.7 copy.16.gates_ref
  164.4 16.3 %all-to-all-done.3 = bf16[16,17,384]{2,1,0:T(8,128)(2,1)S(1)} async-done(((bf16[16,17,384]{2,1,0:T(8,128)(2,1)}), bf16[16,17,384]{2,1,0:T(8,128)(2,1)S(1)}, u32[]{:S(2)}, u32[]{:S(2)}) %all-to-all-start.3) | async-done | bytes 208928 | tf_op jit(solution)/shard_map/all_to_all | solution.py:114
  180.7 0.8 reshape.13.rows_ref
  181.5 2.7 %shard_map.66 = bf16[128,192]{1,0:T(8,128)(2,1)} custom-call(s32[128,4]{1,0:T(8,128)} %copy-done.5, f32[128,4]{1,0:T(8,128)} %copy.16.gates_ref, bf16[272,384]{1,0:T(8,128)(2,1)} %reshape.13.rows_ref), custom_call_target="tpu_custom_call" | custom-call | tf_op jit(solution)/shard_map/pallas_call | solution.py:101
  184.2 1.6 copy.14
  (1 shorter events, 0.0 us)
Async XLA Ops:
  0.0 1.5 copy-start
  0.9 40.9 %copy-start.5 = (s32[128,4]{1,0:T(8,128)}, s32[128,4]{1,0:T(8,128)S(1)}, u32[]{:S(2)}) copy-start(s32[128,4]{1,0:T(8,128)S(1)} %copy.15.ids_ref) | copy-start | bytes 6148
  41.7 7.6 %copy-start.1 = (bf16[1,168,3072]{2,1,0:T(8,128)(2,1)S(1)}, bf16[1,168,3072]{2,1,0:T(8,128)(2,1)}, u32[]{:S(2)}) copy-start(bf16[1,168,3072]{2,1,0:T(8,128)(2,1)} %param.9) | copy-start | bytes 3096580
  41.7 9.5 %copy-start.2 = (bf16[1,168,3072]{2,1,0:T(8,128)(2,1)S(1)}, bf16[1,168,3072]{2,1,0:T(8,128)(2,1)}, u32[]{:S(2)}) copy-start(bf16[1,168,3072]{2,1,0:T(8,128)(2,1)} %param.10) | copy-start | bytes 3096580
  41.7 41.6 %all-to-all-start.1 = ((bf16[16,272,384]{2,1,0:T(8,128)(2,1)}), bf16[16,272,384]{2,1,0:T(8,128)(2,1)}, u32[]{:S(2)}, u32[]{:S(2)}) async-start(bf16[16,272,384]{2,1,0:T(8,128)(2,1)} %broadcast_in_dim.8), calls=%async_computation.1 | async-start | bytes 6684672 | tf_op jit(solution)/shard_map/all_to_all | solution.py:114
  49.3 6.3 %collective-permute-start = (bf16[168,3072]{1,0:T(8,128)(2,1)S(1)}, bf16[168,3072]{1,0:T(8,128)(2,1)S(1)}, u32[]{:S(2)}, u32[]{:S(2)}) collective-permute-start(bf16[168,3072]{1,0:T(8,128)(2,1)S(1)} %bitcast.5), channel_id=1, source_target_pairs={{0,1},{1,0},{2,3},{3,2},{4,5},{5,4},{6,7},{7,6},{8,9},{9,8},{10,11... | collective-permute-start | bytes 3096584 | tf_op jit(solution)/shard_map/ppermute | solution.py:110
  51.2 4.7 %collective-permute-start.1 = (bf16[168,3072]{1,0:T(8,128)(2,1)S(1)}, bf16[168,3072]{1,0:T(8,128)(2,1)S(1)}, u32[]{:S(2)}, u32[]{:S(2)}) collective-permute-start(bf16[168,3072]{1,0:T(8,128)(2,1)S(1)} %bitcast.7), channel_id=1, source_target_pairs={{0,1},{1,0},{2,3},{3,2},{4,5},{5,4},{6,7},{7,6},{8,9},{9,8},{10,11... | collective-permute-start | bytes 3096584 | tf_op jit(solution)/shard_map/ppermute | solution.py:110
  53.6 4.9 %collective-permute-start.2 = (bf16[168,3072]{1,0:T(8,128)(2,1)}, bf16[168,3072]{1,0:T(8,128)(2,1)}, u32[]{:S(2)}, u32[]{:S(2)}) collective-permute-start(bf16[168,3072]{1,0:T(8,128)(2,1)} %bitcast.8), channel_id=1, source_target_pairs={{0,1},{1,0},{2,3},{3,2},{4,5},{5,4},{6,7},{7,6},{8,9},{9,8},{10,11... | collective-permute-start | bytes 3096584 | tf_op jit(solution)/shard_map/ppermute | solution.py:110
  55.6 0.9 copy-start.3
  56.5 1.1 copy-start.4
  139.2 24.4 %copy-start.6 = (f32[256,4]{0,1:T(4,128)S(1)}, f32[256,4]{0,1:T(4,128)}, u32[]{:S(2)}) copy-start(f32[256,4]{0,1:T(4,128)} %param.8) | copy-start | bytes 12292
  142.5 38.2 %all-to-all-start.3 = ((bf16[16,17,384]{2,1,0:T(8,128)(2,1)}), bf16[16,17,384]{2,1,0:T(8,128)(2,1)S(1)}, u32[]{:S(2)}, u32[]{:S(2)}) async-start(bf16[16,17,384]{2,1,0:T(8,128)(2,1)} %reshape.12), calls=%async_computation.3 | async-start | bytes 589824 | tf_op jit(solution)/shard_map/all_to_all | solution.py:114

commit v2 on v0

v2 whole, which is shorter than its diff:
```python
import jax
import jax.numpy as jnp
from jax import lax
from jax.experimental import pallas as pl
from jax.experimental.pallas import tpu as pltpu
from jax.sharding import PartitionSpec as P

EXPERTS = 16
TOP = 4
CAP = 34
HALF = CAP // 2
SIZE = 4
DP = SIZE * SIZE
LANES = 128
HLANES = 64
BLOCK = 56
SIDE = EXPERTS * HALF
PART = 3 * SIDE
F32 = jnp.float32
BF16 = jnp.bfloat16


def quarter(y, x, core):
    a, b = (y + core) % SIZE, (x + core) % SIZE
    return a // 2 * 2 + b // 2, a % 2 * 2 + b % 2


def device(y, x, core):
    return (y % SIZE * SIZE + x % SIZE) * 2 + core


def quarter_groups():
    groups = {}
    for core in range(2):
        for y in range(SIZE):
            for x in range(SIZE):
                q, at = quarter(y, x, core)
                groups.setdefault((core, q), [0] * 4)[at] = device(y, x, core)
    return [groups[key] for key in sorted(groups)]


def across(mask):
    pairs = []
    for core in range(2):
        for y in range(SIZE):
            for x in range(SIZE):
                up = y + 1 if (y + core) % 2 else y - 1
                right = x + 1 if (x + core) % 2 else x - 1
                pairs.append((device(y, x, core), device(up if mask & 2 else y, right if mask & 1 else x, core)))
    return pairs


def dot(a, b):
    return jnp.dot(a, b, preferred_element_type=F32)


def dot_t(a, b):
    return lax.dot_general(a, b, (((1,), (1,)), ((), ())), preferred_element_type=F32)


def t_dot(a, b):
    return lax.dot_general(a, b, (((0,), (0,)), ((), ())), preferred_element_type=F32)


def iota(shape, dim):
    return lax.broadcasted_iota(jnp.int32, shape, dim)


def slot_picks(ids):
    n = ids.shape[1]
    named = jnp.zeros((EXPERTS, n), F32)
    for k in range(TOP):
        named += (ids[k : k + 1, :] == iota((EXPERTS, n), 0)).astype(F32)
    earlier = (iota((n, n), 0) < iota((n, n), 1)).astype(BF16)
    slot = jnp.where(named > 0.0, dot(named.astype(BF16), earlier), -1.0)
    rows = EXPERTS * BLOCK

    def expert_of(shape):
        return jnp.floor((iota(shape, 0).astype(F32) + 0.5) * (1.0 / BLOCK))

    spread = (expert_of((rows, EXPERTS)) == iota((rows, EXPERTS), 1).astype(F32)).astype(BF16)
    wide = dot(spread, slot.astype(BF16))
    at = iota((rows, n), 0).astype(F32) - BLOCK * expert_of((rows, n))
    main, half = at < CAP, (at >= CAP) & (at < CAP + HALF)
    return [main & (wide == at), half & (wide == at - CAP), half & (wide == at - HALF)], spread


def dispatch_kernel(ids_ref, tokens_ref, out_ref):
    n = tokens_ref.shape[0]
    core, dp = lax.axis_index("tensor"), lax.axis_index("dp")
    q, at = quarter(dp // SIZE, dp % SIZE, core)
    part = 4 * q + at
    picks, _ = slot_picks(ids_ref[:, pl.ds(pl.multiple_of(core * n, n), n)])
    picks = jnp.concatenate([p.astype(BF16) for p in picks], axis=1)
    first = tokens_ref[:, pl.ds(pl.multiple_of(part * LANES, LANES), LANES)]
    rest = tokens_ref[:, pl.ds(pl.multiple_of((DP + part // 2) * LANES, LANES), LANES)].astype(F32)
    low = iota((n, LANES), 1) < HLANES
    turned = pltpu.roll(rest, HLANES, 1)
    odd = part % 2 == 1
    here = jnp.where(odd, turned, rest)
    there = jnp.where(odd, rest, turned)
    rows = jnp.concatenate(
        [first, jnp.where(low, here, 0.0).astype(BF16), jnp.where(low, 0.0, there).astype(BF16)], axis=0
    )
    out_ref[...] = dot(picks, rows).astype(BF16)


def pack_kernel(blocks_ref, out_ref, source, packed):
    source[...] = blocks_ref[...].astype(F32)
    for e in range(EXPERTS):
        for third in range(3):
            packed[third * SIDE + e * HALF : third * SIDE + (e + 1) * HALF, :] = source[
                e * BLOCK + third * HALF : e * BLOCK + (third + 1) * HALF, :
            ]
    value = packed[...].astype(BF16)
    for copy in range(out_ref.shape[0]):
        out_ref[copy] = value


def expert_kernel(x0, x1, x2, x3, weights_ref, down_ref, out0, out1, out2, out3, rows):
    core, own = lax.axis_index("tensor"), lax.axis_index("dp")
    q, _ = quarter(own // SIZE, own % SIZE, core)
    hidden_width = down_ref.shape[0]
    low = iota((SIDE, LANES), 1) < HLANES
    for mask, x_ref in enumerate((x0, x1, x2, x3)):
        part = 4 * (q ^ mask)
        for at in range(4):
            rows[:, pl.ds(pl.multiple_of((part + at) * LANES, LANES), LANES)] = x_ref[at, : 2 * SIDE, :]
        for pair in range(2):
            even = x_ref[2 * pair, 2 * SIDE :, :].astype(F32)
            odd = x_ref[2 * pair + 1, 2 * SIDE :, :].astype(F32)
            lanes = pl.ds(pl.multiple_of((DP + part // 2 + pair) * LANES, LANES), LANES)
            rows[:SIDE, lanes] = jnp.where(low, even, pltpu.roll(odd, HLANES, 1)).astype(BF16)
            rows[SIDE:, lanes] = jnp.where(low, pltpu.roll(even, HLANES, 1), odd).astype(BF16)
    x = rows[...]
    g = dot_t(x, weights_ref[:hidden_width, :])
    u = dot_t(x, weights_ref[hidden_width:, :])
    hidden = (g / (1.0 + jnp.exp(-g)) * u).astype(BF16)
    for mask, out_ref in ((3, out3), (1, out1), (2, out2), (0, out0)):
        to = q ^ mask
        for at in range(4):
            dp = (to // 2 * 2 + at // 2 - core) % SIZE * SIZE + (to % 2 * 2 + at % 2 - core) % SIZE
            odd = dp % 2 == 1
            y = dot(hidden, down_ref[:, pl.ds(pl.multiple_of((dp * 3 - dp % 2) // 2 * LANES, LANES), 2 * LANES)])
            first, second = y[:, :LANES], y[:, LANES:]
            out_ref[at, : 2 * SIDE, :] = jnp.where(odd, second, first).astype(BF16)
            half = jnp.where(odd, first, second)
            turned = pltpu.roll(half, HLANES, 1)
            left, right = jnp.where(odd, turned, half), jnp.where(odd, half, turned)
            out_ref[at, 2 * SIDE :, :] = jnp.where(low, left[:SIDE], right[SIDE:]).astype(BF16)


def add_kernel(a, b, c, d, out_ref):
    out_ref[...] = (a[...].astype(F32) + b[...].astype(F32) + c[...].astype(F32) + d[...].astype(F32)).astype(BF16)


def add_blocks_kernel(parts_ref, out_ref, packed, blocks):
    total = parts_ref[0].astype(F32)
    for i in range(1, parts_ref.shape[0]):
        total += parts_ref[i].astype(F32)
    packed[...] = total
    for e in range(EXPERTS):
        for third in range(3):
            blocks[e * BLOCK + third * HALF : e * BLOCK + (third + 1) * HALF, :] = packed[
                third * SIDE + e * HALF : third * SIDE + (e + 1) * HALF, :
            ]
        blocks[e * BLOCK + 3 * HALF : (e + 1) * BLOCK, :] = jnp.zeros((BLOCK - 3 * HALF, LANES), F32)
    out_ref[...] = blocks[...].astype(BF16)


def combine_kernel(ids_ref, gates_ref, blocks_ref, out_ref):
    n = out_ref.shape[1]
    core, dp = lax.axis_index("tensor"), lax.axis_index("dp")
    own = pl.ds(pl.multiple_of(core * n, n), n)
    ids, given = ids_ref[:, own], gates_ref[:, own]
    picks, spread = slot_picks(ids)
    picks = jnp.concatenate(picks, axis=1)
    gates = jnp.zeros((EXPERTS, n), F32)
    for k in range(TOP):
        gates += jnp.where(ids[k : k + 1, :] == iota((EXPERTS, n), 0), given[k : k + 1, :], 0.0)
    total = jnp.zeros((LANES, 3 * n), F32)
    for _ in range(3):
        piece = gates.astype(BF16)
        gates = gates - piece.astype(F32)
        weight = dot(spread, piece)
        weight = jnp.concatenate([weight, weight, weight], axis=1)
        total += t_dot(blocks_ref[...], jnp.where(picks, weight, 0.0).astype(BF16))
    first = total[:, :n]
    rest = total[:HLANES, n : 2 * n] + total[HLANES:, 2 * n :]
    odd = dp % 2 == 1
    out_ref[:HLANES, :] = jnp.where(odd, rest, first[:HLANES]).astype(BF16)
    out_ref[HLANES:LANES, :] = jnp.where(odd, first[:HLANES], first[HLANES:]).astype(BF16)
    out_ref[LANES:, :] = jnp.where(odd, first[HLANES:], rest).astype(BF16)


def call(kernel, shape, *args, scratch=(), limit=16, outs=0):
    one = jax.ShapeDtypeStruct(shape, BF16)
    return pl.pallas_call(
        kernel,
        out_shape=[one] * outs if outs else one,
        scratch_shapes=scratch,
        compiler_params=pltpu.CompilerParams(vmem_limit_bytes=limit * 1024 * 1024),
    )(*args)


def swap(value):
    return lax.ppermute(value, "tensor", [(0, 1), (1, 0)])


def exchange(value, axis, groups=None):
    return lax.all_to_all(value, axis, split_axis=0, concat_axis=0, tiled=True, axis_index_groups=groups)


def shards(tokens, expert_ids, gate_values, w_gate, w_up, w_down):
    n, width = tokens.shape
    hidden = w_gate.shape[1]
    plane, inside = ("dp", "tensor"), quarter_groups()
    ids, gates = expert_ids.T, gate_values.T
    gap = jnp.zeros((-2 * hidden % LANES, width), BF16)
    gate, up, down = w_gate[0], w_up[0], w_down[0]
    weights = jnp.concatenate([gate, swap(gate), gap, up, swap(up), gap], axis=0)
    downs = jnp.concatenate([down, swap(down), gap], axis=0)
    part_scratch = pltpu.VMEM((PART, LANES), F32)
    block_scratch = pltpu.VMEM((EXPERTS * BLOCK, LANES), F32)

    sent = call(dispatch_kernel, (EXPERTS * BLOCK, LANES), ids, tokens)
    arrived = exchange(sent.reshape(EXPERTS, BLOCK, LANES), "expert").reshape(EXPERTS * BLOCK, LANES)
    rows = call(pack_kernel, (4, PART, LANES), arrived, scratch=[block_scratch, part_scratch])
    rows = exchange(rows, plane, inside)
    others = {mask: lax.ppermute(rows, plane, across(mask)) for mask in (3, 1, 2)}
    partial = call(
        expert_kernel,
        (4, PART, LANES),
        *(rows, others[1], others[2], others[3]),
        *(weights, downs),
        scratch=[pltpu.VMEM((2 * SIDE, width), BF16)],
        limit=48,
        outs=4,
    )
    others = {mask: lax.ppermute(partial[mask], plane, across(mask)) for mask in (3, 1, 2)}
    partial = call(add_kernel, (4, PART, LANES), partial[0], others[1], others[2], others[3], limit=24)
    partial = exchange(partial, plane, inside)
    summed = call(add_blocks_kernel, (EXPERTS * BLOCK, LANES), partial, scratch=[part_scratch, block_scratch])
    back = exchange(summed.reshape(EXPERTS, BLOCK, LANES), "expert").reshape(EXPERTS * BLOCK, LANES)
    return call(combine_kernel, (width // DP, n), ids, gates, back).T


def solution(mesh):
    placed = (
        P(("expert", "tensor"), None),
        P("expert", None),
        P("expert", None),
        P("expert", ("dp", "tensor"), None),
        P("expert", ("dp", "tensor"), None),
        P("expert", ("dp", "tensor"), None),
    )
    return jax.shard_map(
        shards, mesh=mesh, in_specs=placed, out_specs=P(("expert", "tensor"), "dp"), check_vma=False
    )
```

time: 883 us -> 155 us (0.18)
  waiting for transfers between devices: 421 us -> 43.9 us
  blocking collectives: 307 us -> 31.7 us
  local copies, waits for them, and re-layouts: 107 us -> 10.9 us
  starting transfers between devices: 6.11 us -> 49 us
  Pallas kernels: 0 us -> 15.5 us
  between operations: 13.7 us -> 0.14 us
  other arithmetic: 13.6 us -> 3.13 us
    all_to_all x1 -> x2, blocking collectives: 307 us -> 31.7 us  [exchange(): lax.all_to_all(value, axis, split_axis=0, concat_axis=0, tiled=True, axis...]
    all_to_all x1 -> x2, waiting for transfers between devices: 288 us -> 14.3 us  [exchange(): lax.all_to_all(value, axis, split_axis=0, concat_axis=0, tiled=True, axis...]
    reduce_scatter x2 -> x0, waiting for transfers between devices: 116 us -> none  [the longest x1 94.7 us: shards(): lax.psum_scatter(own_plane[0], 'dp', scatter_dimension=1, tiled=True)]
    gather x6 -> x0, local copies, waits for them, and re-layouts: 49.5 us -> none  [the longest x2 25.8 us: fill_slots(): return padded[table]]
    ppermute x0 -> x9, waiting for transfers between devices: none -> 29.5 us  [the longest x3 19.1 us: shards(): lax.ppermute(partial[mask], plane, across(mask))]
    ppermute x0 -> x9, starting transfers between devices: none -> 29.5 us  [the longest x3 11.6 us: shards(): lax.ppermute(partial[mask], plane, across(mask))]
    reshape x6 -> x0, local copies, waits for them, and re-layouts: 29.3 us -> none  [the longest x2 21.4 us: shards(): outgoing.reshape(pair_size, expert_devs, local_experts, CAP, model_width)]
    convert_element_type x5 -> x0, local copies, waits for them, and re-layouts: 17.8 us -> none  [the longest x4 11.3 us: shards(): picked.astype(jnp.float32)]
  transfers between devices with their start and end apart: 4 -> 11, of which waited for: 4 -> 5; matrix products, arithmetic and copies ran while one was open for 1% -> 7% of each run, Pallas kernels for 0% -> 2%
where the time goes in v2:
time: 155 us; the launch traced here: 154 us
  starting transfers between devices  49 us (32%)
  waiting for transfers between devices  43.9 us (28%)
  blocking collectives  31.7 us (20%)
  Pallas kernels  15.5 us (10%)
  local copies, waits for them, and re-layouts  10.9 us (7%)
  other arithmetic  3.13 us (2%)
    all_to_all x2, blocking collectives, exchange(): lax.all_to_all(value, axis, split_axis=0, concat_axis=0, tiled=True, axis...  31.7 us
    all_to_all x2, starting transfers between devices, exchange(): lax.all_to_all(value, axis, split_axis=0, concat_axis=0, tiled=True, axis...  19.5 us
    ppermute x3, waiting for transfers between devices, shards(): lax.ppermute(partial[mask], plane, across(mask))  19.1 us
    pallas_call x6, Pallas kernels, call(): pl.pallas_call(kernel, out_shape=[one] * outs if outs else one, scratch_s...  15.5 us
    all_to_all x2, waiting for transfers between devices, exchange(): lax.all_to_all(value, axis, split_axis=0, concat_axis=0, tiled=True, axis...  14.3 us
    ppermute x3, starting transfers between devices, shards(): lax.ppermute(partial[mask], plane, across(mask))  11.6 us
    ppermute x3, starting transfers between devices, shards(): lax.ppermute(rows, plane, across(mask))  11.6 us
    ppermute x3, waiting for transfers between devices, shards(): lax.ppermute(rows, plane, across(mask))  10.4 us
  transfers between devices with their start and end apart: 11, of which 5 were waited for; matrix products, arithmetic and copies ran while one was open for 7% of the time, Pallas kernels for 2%

profile of v2, /device:TPU:6, one launch (start us, length us, event | category | flops | bytes accessed | tf_op | source)
XLA Modules:
  0.0 154.2 jit_solution(5012690805380415864)
XLA Ops:
  0.0 1.9 %collective-permute-start.3 = (bf16[168,3072]{1,0:T(8,128)(2,1)}, bf16[168,3072]{1,0:T(8,128)(2,1)}, u32[]{:S(2)}, u32[]{:S(2)}) collective-permute-start(bf16[168,3072]{1,0:T(8,128)(2,1)} %bitcast.18), channel_id=1, source_target_pairs={{0,1},{1,0},{2,3},{3,2},{4,5},{5,4},{6,7},{7,6},{8,9},{9,8},{10,11... | collective-permute-start | bytes 3096584 | tf_op jit(solution)/shard_map/ppermute | solution.py:207
  1.9 0.0 copy-start
  1.9 1.1 copy-done
  3.1 0.0 copy-start.1
  3.1 0.7 copy-done.1
  3.7 0.0 copy-start.4
  3.7 1.4 shard_map.64
  5.1 15.2 %all-to-all-start = ((bf16[16,56,128]{2,1,0:T(8,128)(2,1)}), bf16[16,56,128]{2,1,0:T(8,128)(2,1)S(1)}, u32[]{:S(2)}, u32[]{:S(2)}) async-start(bf16[16,56,128]{2,1,0:T(8,128)(2,1)} %bitcast.2), calls=%async_computation | async-start | bytes 458752 | tf_op jit(solution)/shard_map/all_to_all | solution.py:211
  20.3 2.1 %collective-permute-start.4 = (bf16[168,3072]{1,0:T(8,128)(2,1)}, bf16[168,3072]{1,0:T(8,128)(2,1)S(1)}, u32[]{:S(2)}, u32[]{:S(2)}) collective-permute-start(bf16[168,3072]{1,0:T(8,128)(2,1)} %bitcast.19), channel_id=1, source_target_pairs={{0,1},{1,0},{2,3},{3,2},{4,5},{5,4},{6,7},{7,6},{8,9},{9,8},{10,11... | collective-permute-start | bytes 3096584 | tf_op jit(solution)/shard_map/ppermute | solution.py:207
  22.5 2.2 %collective-permute-start.5 = (bf16[168,3072]{1,0:T(8,128)(2,1)}, bf16[168,3072]{1,0:T(8,128)(2,1)}, u32[]{:S(2)}, u32[]{:S(2)}) collective-permute-start(bf16[168,3072]{1,0:T(8,128)(2,1)} %bitcast.20), channel_id=1, source_target_pairs={{0,1},{1,0},{2,3},{3,2},{4,5},{5,4},{6,7},{7,6},{8,9},{9,8},{10,11... | collective-permute-start | bytes 3096584 | tf_op jit(solution)/shard_map/ppermute | solution.py:207
  24.7 2.3 %constant_dynamic-update-slice_fusion.3 = bf16[768,3072]{1,0:T(8,128)(2,1)} fusion(bf16[1,168,3072]{2,1,0:T(8,128)(2,1)} %param.9), kind=kLoop, calls=%fused_computation.6 | loop fusion | bytes 2064384
  26.9 10.7 %all-to-all-done = bf16[16,56,128]{2,1,0:T(8,128)(2,1)S(1)} async-done(((bf16[16,56,128]{2,1,0:T(8,128)(2,1)}), bf16[16,56,128]{2,1,0:T(8,128)(2,1)S(1)}, u32[]{:S(2)}, u32[]{:S(2)}) %all-to-all-start) | async-done | bytes 229408 | tf_op jit(solution)/shard_map/all_to_all | solution.py:211
  37.7 1.0 shard_map.65
  38.7 4.3 %all-to-all-start.1 = ((bf16[4,816,128]{2,1,0:T(8,128)(2,1)}), bf16[4,816,128]{2,1,0:T(8,128)(2,1)S(1)}, u32[]{:S(2)}, u32[]{:S(2)}) async-start(bf16[4,816,128]{2,1,0:T(8,128)(2,1)} %shard_map.65), calls=%async_computation.1 | async-start | bytes 1671168 | tf_op jit(solution)/shard_map/all_to_all | solution.py:211
  43.0 0.0 collective-permute-done.3
  43.0 2.3 %constant_dynamic-update-slice_fusion.2 = bf16[768,3072]{1,0:T(8,128)(2,1)} fusion(bf16[768,3072]{1,0:T(8,128)(2,1)} %constant_dynamic-update-slice_fusion.3, bf16[168,3072]{1,0:T(8,128)(2,1)} %collective-permute-done.3), kind=kLoop, calls=%fused_computation.5 | loop fusion | bytes 2064384
  45.3 0.7 broadcast_dynamic-update-slice_fusion
  46.1 0.0 copy-done.4
  46.1 1.1 constant_dynamic-update-slice_fusion.1
  47.1 3.6 %all-to-all-done.1.x0 = bf16[4,816,128]{2,1,0:T(8,128)(2,1)S(1)} async-done(((bf16[4,816,128]{2,1,0:T(8,128)(2,1)}), bf16[4,816,128]{2,1,0:T(8,128)(2,1)S(1)}, u32[]{:S(2)}, u32[]{:S(2)}) %all-to-all-start.1) | async-done | bytes 835616 | tf_op jit(solution)/shard_map/all_to_all | solution.py:211
  50.7 2.4 %collective-permute-start = (bf16[4,816,128]{2,1,0:T(8,128)(2,1)S(1)}, bf16[4,816,128]{2,1,0:T(8,128)(2,1)S(1)}, u32[]{:S(2)}, u32[]{:S(2)}) collective-permute-start(bf16[4,816,128]{2,1,0:T(8,128)(2,1)S(1)} %all-to-all-done.1.x0), channel_id=1, source_target_pairs={{0,96},{32,64},{64,32},{96,0},{128,224},{160,192},{192,160},{224,1... | collective-permute-start | bytes 2506760 | tf_op jit(solution)/shard_map/ppermute | solution.py:230
  53.2 4.8 %collective-permute-start.1 = (bf16[4,816,128]{2,1,0:T(8,128)(2,1)S(1)}, bf16[4,816,128]{2,1,0:T(8,128)(2,1)S(1)}, u32[]{:S(2)}, u32[]{:S(2)}) collective-permute-start(bf16[4,816,128]{2,1,0:T(8,128)(2,1)S(1)} %all-to-all-done.1.x0), channel_id=1, source_target_pairs={{0,384},{32,416},{64,448},{96,480},{128,256},{160,288},{192,320},{... | collective-permute-start | bytes 2506760 | tf_op jit(solution)/shard_map/ppermute | solution.py:230
  58.0 4.4 %collective-permute-start.2 = (bf16[4,816,128]{2,1,0:T(8,128)(2,1)S(1)}, bf16[4,816,128]{2,1,0:T(8,128)(2,1)S(1)}, u32[]{:S(2)}, u32[]{:S(2)}) collective-permute-start(bf16[4,816,128]{2,1,0:T(8,128)(2,1)S(1)} %all-to-all-done.1.x0), channel_id=1, source_target_pairs={{0,480},{32,448},{64,416},{96,384},{128,352},{160,320},{192,288},{... | collective-permute-start | bytes 2506760 | tf_op jit(solution)/shard_map/ppermute | solution.py:230
  62.4 0.0 collective-permute-done.4
  62.4 1.0 constant_dynamic-update-slice_fusion
  63.4 0.7 broadcast_dynamic-update-slice_fusion.1.weights_ref
  64.2 0.0 collective-permute-done.5
  64.2 3.1 %pad_maximum_fusion.down_ref = bf16[384,3072]{1,0:T(8,128)(2,1)} fusion(bf16[48,3072]{1,0:T(8,128)(2,1)S(1)} %broadcast_in_dim.3, bf16[168,3072]{1,0:T(8,128)(2,1)} %collective-permute-done.5, bf16[168,3072]{1,0:T(8,128)(2,1)} %bitcast.21), kind=kLoop, calls=%fused_computation | loop fusion | flops 7077888 | bytes 4718592 | tf_op jit(solution)/shard_map/concatenate | solution.py:222
  67.3 0.0 collective-permute-done.x1
  67.3 10.4 %collective-permute-done.1.x2 = bf16[4,816,128]{2,1,0:T(8,128)(2,1)S(1)} collective-permute-done((bf16[4,816,128]{2,1,0:T(8,128)(2,1)S(1)}, bf16[4,816,128]{2,1,0:T(8,128)(2,1)S(1)}, u32[]{:S(2)}, u32[]{:S(2)}) %collective-permute-start.1) | collective-permute-done | bytes 835616 | tf_op jit(solution)/shard_map/ppermute | solution.py:230
  77.8 0.0 collective-permute-done.2.x3
  77.8 0.9 copy-done.5
  78.7 10.6 %shard_map.66 = (bf16[4,816,128]{2,1,0:T(8,128)(2,1)S(1)}, bf16[4,816,128]{2,1,0:T(8,128)(2,1)S(1)}, bf16[4,816,128]{2,1,0:T(8,128)(2,1)S(1)}, bf16[4,816,128]{2,1,0:T(8,128)(2,1)S(1)}) custom-call(bf16[4,816,128]{2,1,0:T(8,128)(2,1)S(1)} %all-to-all-done.1.x0, bf16[4,816,128]{2,1,0:T(8,128)(2,1)S(1)} %collective-permute-done.x1, ...), custom_call_target="tpu_custom_call" | custom-call | tf_op jit(solution)/shard_map/pallas_call | solution.py:198
  89.3 0.0 copy-start.2
  89.3 0.0 copy-start.3
  89.3 4.6 %collective-permute-start.6 = (bf16[4,816,128]{2,1,0:T(8,128)(2,1)S(1)}, bf16[4,816,128]{2,1,0:T(8,128)(2,1)S(1)}, u32[]{:S(2)}, u32[]{:S(2)}) collective-permute-start(bf16[4,816,128]{2,1,0:T(8,128)(2,1)S(1)} %get-tuple-element.10), channel_id=1, source_target_pairs={{0,96},{32,64},{64,32},{96,0},{128,224},{160,192},{192,160},{224,1... | collective-permute-start | bytes 2506760 | tf_op jit(solution)/shard_map/ppermute | solution.py:240
  93.9 4.2 %collective-permute-start.7 = (bf16[4,816,128]{2,1,0:T(8,128)(2,1)S(1)}, bf16[4,816,128]{2,1,0:T(8,128)(2,1)S(1)}, u32[]{:S(2)}, u32[]{:S(2)}) collective-permute-start(bf16[4,816,128]{2,1,0:T(8,128)(2,1)S(1)} %get-tuple-element.11), channel_id=1, source_target_pairs={{0,384},{32,416},{64,448},{96,480},{128,256},{160,288},{192,320},{... | collective-permute-start | bytes 2506760 | tf_op jit(solution)/shard_map/ppermute | solution.py:240
  98.1 2.9 %collective-permute-start.8 = (bf16[4,816,128]{2,1,0:T(8,128)(2,1)S(1)}, bf16[4,816,128]{2,1,0:T(8,128)(2,1)S(1)}, u32[]{:S(2)}, u32[]{:S(2)}) collective-permute-start(bf16[4,816,128]{2,1,0:T(8,128)(2,1)S(1)} %get-tuple-element.12), channel_id=1, source_target_pairs={{0,480},{32,448},{64,416},{96,384},{128,352},{160,320},{192,288},{... | collective-permute-start | bytes 2506760 | tf_op jit(solution)/shard_map/ppermute | solution.py:240
  100.9 4.0 %collective-permute-done.6.b = bf16[4,816,128]{2,1,0:T(8,128)(2,1)S(1)} collective-permute-done((bf16[4,816,128]{2,1,0:T(8,128)(2,1)S(1)}, bf16[4,816,128]{2,1,0:T(8,128)(2,1)S(1)}, u32[]{:S(2)}, u32[]{:S(2)}) %collective-permute-start.6) | collective-permute-done | bytes 835616 | tf_op jit(solution)/shard_map/ppermute | solution.py:240
  104.9 15.1 %collective-permute-done.7.c = bf16[4,816,128]{2,1,0:T(8,128)(2,1)S(1)} collective-permute-done((bf16[4,816,128]{2,1,0:T(8,128)(2,1)S(1)}, bf16[4,816,128]{2,1,0:T(8,128)(2,1)S(1)}, u32[]{:S(2)}, u32[]{:S(2)}) %collective-permute-start.7) | collective-permute-done | bytes 835616 | tf_op jit(solution)/shard_map/ppermute | solution.py:240
  120.0 0.0 collective-permute-done.8.d
  120.0 0.4 shard_map.67
  120.4 10.8 %all_to_all.20.parts_ref = bf16[4,816,128]{2,1,0:T(8,128)(2,1)S(1)} all-to-all(bf16[4,816,128]{2,1,0:T(8,128)(2,1)S(1)} %shard_map.67), channel_id=1, replica_groups={{0,32,128,160},{64,96,192,224},{256,288,384,416},{320,352,448,480},{481..., dimensions={0} | all-to-all | bytes 1671168 | tf_op jit(solution)/shard_map/all_to_all | solution.py:211
  131.2 0.2 shard_map.68
  131.4 20.9 %all_to_all.21 = bf16[16,56,128]{2,1,0:T(8,128)(2,1)S(1)} all-to-all(bf16[16,56,128]{2,1,0:T(8,128)(2,1)S(1)} %bitcast.14), channel_id=1, replica_groups=mesh['dp'=16,'expert'=16,'tensor'=2] {'expert'}, dimensions={0} | all-to-all | bytes 458752 | tf_op jit(solution)/shard_map/all_to_all | solution.py:211
  152.3 0.0 copy-done.2
  152.3 0.0 copy-done.3
  152.3 1.9 %shard_map.69 = bf16[192,128]{1,0:T(8,128)(2,1)} custom-call(s32[4,256]{1,0:T(4,128)S(1)} %bitcast.16, f32[4,256]{1,0:T(4,128)S(1)} %bitcast.17, bf16[896,128]{1,0:T(8,128)(2,1)S(1)} %bitcast.12), custom_call_target="tpu_custom_call" | custom-call | tf_op jit(solution)/shard_map/pallas_call | solution.py:198
  (2 shorter events, 0.0 us)
Async XLA Ops:
  0.0 43.0 %collective-permute-start.3 = (bf16[168,3072]{1,0:T(8,128)(2,1)}, bf16[168,3072]{1,0:T(8,128)(2,1)}, u32[]{:S(2)}, u32[]{:S(2)}) collective-permute-start(bf16[168,3072]{1,0:T(8,128)(2,1)} %bitcast.18), channel_id=1, source_target_pairs={{0,1},{1,0},{2,3},{3,2},{4,5},{5,4},{6,7},{7,6},{8,9},{9,8},{10,11... | collective-permute-start | bytes 3096584 | tf_op jit(solution)/shard_map/ppermute | solution.py:207
  1.9 1.1 copy-start
  3.1 0.7 copy-start.1
  3.7 42.3 %copy-start.4 = (bf16[1,168,3072]{2,1,0:T(8,128)(2,1)S(1)}, bf16[1,168,3072]{2,1,0:T(8,128)(2,1)}, u32[]{:S(2)}) copy-start(bf16[1,168,3072]{2,1,0:T(8,128)(2,1)} %param.10) | copy-start | bytes 3096580
  5.1 32.5 %all-to-all-start = ((bf16[16,56,128]{2,1,0:T(8,128)(2,1)}), bf16[16,56,128]{2,1,0:T(8,128)(2,1)S(1)}, u32[]{:S(2)}, u32[]{:S(2)}) async-start(bf16[16,56,128]{2,1,0:T(8,128)(2,1)} %bitcast.2), calls=%async_computation | async-start | bytes 458752 | tf_op jit(solution)/shard_map/all_to_all | solution.py:211
  20.3 42.0 %collective-permute-start.4 = (bf16[168,3072]{1,0:T(8,128)(2,1)}, bf16[168,3072]{1,0:T(8,128)(2,1)S(1)}, u32[]{:S(2)}, u32[]{:S(2)}) collective-permute-start(bf16[168,3072]{1,0:T(8,128)(2,1)} %bitcast.19), channel_id=1, source_target_pairs={{0,1},{1,0},{2,3},{3,2},{4,5},{5,4},{6,7},{7,6},{8,9},{9,8},{10,11... | collective-permute-start | bytes 3096584 | tf_op jit(solution)/shard_map/ppermute | solution.py:207
  22.5 41.7 %collective-permute-start.5 = (bf16[168,3072]{1,0:T(8,128)(2,1)}, bf16[168,3072]{1,0:T(8,128)(2,1)}, u32[]{:S(2)}, u32[]{:S(2)}) collective-permute-start(bf16[168,3072]{1,0:T(8,128)(2,1)} %bitcast.20), channel_id=1, source_target_pairs={{0,1},{1,0},{2,3},{3,2},{4,5},{5,4},{6,7},{7,6},{8,9},{9,8},{10,11... | collective-permute-start | bytes 3096584 | tf_op jit(solution)/shard_map/ppermute | solution.py:207
  38.7 12.0 %all-to-all-start.1 = ((bf16[4,816,128]{2,1,0:T(8,128)(2,1)}), bf16[4,816,128]{2,1,0:T(8,128)(2,1)S(1)}, u32[]{:S(2)}, u32[]{:S(2)}) async-start(bf16[4,816,128]{2,1,0:T(8,128)(2,1)} %shard_map.65), calls=%async_computation.1 | async-start | bytes 1671168 | tf_op jit(solution)/shard_map/all_to_all | solution.py:211
  50.7 16.6 %collective-permute-start = (bf16[4,816,128]{2,1,0:T(8,128)(2,1)S(1)}, bf16[4,816,128]{2,1,0:T(8,128)(2,1)S(1)}, u32[]{:S(2)}, u32[]{:S(2)}) collective-permute-start(bf16[4,816,128]{2,1,0:T(8,128)(2,1)S(1)} %all-to-all-done.1.x0), channel_id=1, source_target_pairs={{0,96},{32,64},{64,32},{96,0},{128,224},{160,192},{192,160},{224,1... | collective-permute-start | bytes 2506760 | tf_op jit(solution)/shard_map/ppermute | solution.py:230
  53.2 24.6 %collective-permute-start.1 = (bf16[4,816,128]{2,1,0:T(8,128)(2,1)S(1)}, bf16[4,816,128]{2,1,0:T(8,128)(2,1)S(1)}, u32[]{:S(2)}, u32[]{:S(2)}) collective-permute-start(bf16[4,816,128]{2,1,0:T(8,128)(2,1)S(1)} %all-to-all-done.1.x0), channel_id=1, source_target_pairs={{0,384},{32,416},{64,448},{96,480},{128,256},{160,288},{192,320},{... | collective-permute-start | bytes 2506760 | tf_op jit(solution)/shard_map/ppermute | solution.py:230
  58.0 19.8 %collective-permute-start.2 = (bf16[4,816,128]{2,1,0:T(8,128)(2,1)S(1)}, bf16[4,816,128]{2,1,0:T(8,128)(2,1)S(1)}, u32[]{:S(2)}, u32[]{:S(2)}) collective-permute-start(bf16[4,816,128]{2,1,0:T(8,128)(2,1)S(1)} %all-to-all-done.1.x0), channel_id=1, source_target_pairs={{0,480},{32,448},{64,416},{96,384},{128,352},{160,320},{192,288},{... | collective-permute-start | bytes 2506760 | tf_op jit(solution)/shard_map/ppermute | solution.py:230
  77.8 0.9 copy-start.5
  89.3 63.0 %copy-start.2 = (s32[256,4]{0,1:T(4,128)S(1)}, s32[256,4]{0,1:T(4,128)}, u32[]{:S(2)}) copy-start(s32[256,4]{0,1:T(4,128)} %param.7) | copy-start | bytes 12292
  89.3 63.0 %copy-start.3 = (f32[256,4]{0,1:T(4,128)S(1)}, f32[256,4]{0,1:T(4,128)}, u32[]{:S(2)}) copy-start(f32[256,4]{0,1:T(4,128)} %param.8) | copy-start | bytes 12292
  89.3 15.6 %collective-permute-start.6 = (bf16[4,816,128]{2,1,0:T(8,128)(2,1)S(1)}, bf16[4,816,128]{2,1,0:T(8,128)(2,1)S(1)}, u32[]{:S(2)}, u32[]{:S(2)}) collective-permute-start(bf16[4,816,128]{2,1,0:T(8,128)(2,1)S(1)} %get-tuple-element.10), channel_id=1, source_target_pairs={{0,96},{32,64},{64,32},{96,0},{128,224},{160,192},{192,160},{224,1... | collective-permute-start | bytes 2506760 | tf_op jit(solution)/shard_map/ppermute | solution.py:240
  93.9 26.1 %collective-permute-start.7 = (bf16[4,816,128]{2,1,0:T(8,128)(2,1)S(1)}, bf16[4,816,128]{2,1,0:T(8,128)(2,1)S(1)}, u32[]{:S(2)}, u32[]{:S(2)}) collective-permute-start(bf16[4,816,128]{2,1,0:T(8,128)(2,1)S(1)} %get-tuple-element.11), channel_id=1, source_target_pairs={{0,384},{32,416},{64,448},{96,480},{128,256},{160,288},{192,320},{... | collective-permute-start | bytes 2506760 | tf_op jit(solution)/shard_map/ppermute | solution.py:240
  98.1 22.0 %collective-permute-start.8 = (bf16[4,816,128]{2,1,0:T(8,128)(2,1)S(1)}, bf16[4,816,128]{2,1,0:T(8,128)(2,1)S(1)}, u32[]{:S(2)}, u32[]{:S(2)}) collective-permute-start(bf16[4,816,128]{2,1,0:T(8,128)(2,1)S(1)} %get-tuple-element.12), channel_id=1, source_target_pairs={{0,480},{32,448},{64,416},{96,384},{128,352},{160,320},{192,288},{... | collective-permute-start | bytes 2506760 | tf_op jit(solution)/shard_map/ppermute | solution.py:240

commit v3 on v2

--- a/solution.py
+++ b/solution.py
@@ -1,3 +1,5 @@
+import functools
+
 import jax
 import jax.numpy as jnp
 from jax import lax
@@ -16,6 +18,8 @@
 BLOCK = 56
 SIDE = EXPERTS * HALF
 PART = 3 * SIDE
+WIDE = 384
+MASKS = (3, 1, 2)
 F32 = jnp.float32
 BF16 = jnp.bfloat16
 
@@ -117,37 +121,72 @@
         out_ref[copy] = value
 
 
-def expert_kernel(x0, x1, x2, x3, weights_ref, down_ref, out0, out1, out2, out3, rows):
-    core, own = lax.axis_index("tensor"), lax.axis_index("dp")
-    q, _ = quarter(own // SIZE, own % SIZE, core)
-    hidden_width = down_ref.shape[0]
+def weights_kernel(gate0, up0, down0, gate1, up1, down1, weights_ref, down_ref):
+    hidden, width = gate0.shape
+    second = -(-hidden // 16) * 16
+    for out_ref, at, pair in ((weights_ref, 0, (gate0, gate1)), (weights_ref, WIDE, (up0, up1)), (down_ref, 0, (down0, down1))):
+        for start, ref, end in ((0, pair[0], second), (second, pair[1], WIDE)):
+            out_ref[at + start : at + start + hidden, :] = ref[...]
+            out_ref[at + start + hidden : at + end, :] = jnp.zeros((end - start - hidden, width), BF16)
+
+
+def place_of():
+    core, dp = lax.axis_index("tensor"), lax.axis_index("dp")
+    return core, quarter(dp // SIZE, dp % SIZE, core)[0]
+
+
+def products(mask, x_ref, weights_ref):
+    _, q = place_of()
+    q = q ^ mask
     low = iota((SIDE, LANES), 1) < HLANES
-    for mask, x_ref in enumerate((x0, x1, x2, x3)):
-        part = 4 * (q ^ mask)
-        for at in range(4):
-            rows[:, pl.ds(pl.multiple_of((part + at) * LANES, LANES), LANES)] = x_ref[at, : 2 * SIDE, :]
-        for pair in range(2):
-            even = x_ref[2 * pair, 2 * SIDE :, :].astype(F32)
-            odd = x_ref[2 * pair + 1, 2 * SIDE :, :].astype(F32)
-            lanes = pl.ds(pl.multiple_of((DP + part // 2 + pair) * LANES, LANES), LANES)
-            rows[:SIDE, lanes] = jnp.where(low, even, pltpu.roll(odd, HLANES, 1)).astype(BF16)
-            rows[SIDE:, lanes] = jnp.where(low, pltpu.roll(even, HLANES, 1), odd).astype(BF16)
-    x = rows[...]
-    g = dot_t(x, weights_ref[:hidden_width, :])
-    u = dot_t(x, weights_ref[hidden_width:, :])
+    main = jnp.concatenate([x_ref[at, : 2 * SIDE, :] for at in range(4)], axis=1)
+    halves = []
+    for pair in range(2):
+        even = x_ref[2 * pair, 2 * SIDE :, :].astype(F32)
+        odd = x_ref[2 * pair + 1, 2 * SIDE :, :].astype(F32)
+        upper = jnp.where(low, even, pltpu.roll(odd, HLANES, 1)).astype(BF16)
+        lower = jnp.where(low, pltpu.roll(even, HLANES, 1), odd).astype(BF16)
+        halves.append(jnp.concatenate([upper, lower], axis=0))
+    rest = jnp.concatenate(halves, axis=1)
+    main_lanes = pl.ds(pl.multiple_of(q * 4 * LANES, LANES), 4 * LANES)
+    rest_lanes = pl.ds(pl.multiple_of((DP + q * 2) * LANES, LANES), 2 * LANES)
+    return dot_t(main, weights_ref[:, main_lanes]) + dot_t(rest, weights_ref[:, rest_lanes])
+
+
+def down_products(mask, hidden, down_ref, out_ref):
+    core, q = place_of()
+    to = q ^ mask
+    low = iota((SIDE, LANES), 1) < HLANES
+    for at in range(4):
+        dp = (to // 2 * 2 + at // 2 - core) % SIZE * SIZE + (to % 2 * 2 + at % 2 - core) % SIZE
+        odd = dp % 2 == 1
+        y = dot(hidden, down_ref[:, pl.ds(pl.multiple_of((dp * 3 - dp % 2) // 2 * LANES, LANES), 2 * LANES)])
+        first, second = y[:, :LANES], y[:, LANES:]
+        out_ref[at, : 2 * SIDE, :] = jnp.where(odd, second, first).astype(BF16)
+        half = jnp.where(odd, first, second)
+        turned = pltpu.roll(half, HLANES, 1)
+        left, right = jnp.where(odd, turned, half), jnp.where(odd, half, turned)
+        out_ref[at, 2 * SIDE :, :] = jnp.where(low, left[:SIDE], right[SIDE:]).astype(BF16)
+
+
+def first_kernel(mask, x_ref, weights_ref, total_ref):
+    total_ref[...] = products(mask, x_ref, weights_ref)
+
+
+def next_kernel(mask, x_ref, weights_ref, sofar_ref, total_ref):
+    total_ref[...] = sofar_ref[...] + products(mask, x_ref, weights_ref)
+
+
+def last_kernel(mask, out_mask, x_ref, weights_ref, sofar_ref, down_ref, hidden_ref, out_ref):
+    total = sofar_ref[...] + products(mask, x_ref, weights_ref)
+    g, u = total[:, :WIDE], total[:, WIDE:]
     hidden = (g / (1.0 + jnp.exp(-g)) * u).astype(BF16)
-    for mask, out_ref in ((3, out3), (1, out1), (2, out2), (0, out0)):
-        to = q ^ mask
-        for at in range(4):
-            dp = (to // 2 * 2 + at // 2 - core) % SIZE * SIZE + (to % 2 * 2 + at % 2 - core) % SIZE
-            odd = dp % 2 == 1
-            y = dot(hidden, down_ref[:, pl.ds(pl.multiple_of((dp * 3 - dp % 2) // 2 * LANES, LANES), 2 * LANES)])
-            first, second = y[:, :LANES], y[:, LANES:]
-            out_ref[at, : 2 * SIDE, :] = jnp.where(odd, second, first).astype(BF16)
-            half = jnp.where(odd, first, second)
-            turned = pltpu.roll(half, HLANES, 1)
-            left, right = jnp.where(odd, turned, half), jnp.where(odd, half, turned)
-            out_ref[at, 2 * SIDE :, :] = jnp.where(low, left[:SIDE], right[SIDE:]).astype(BF16)
+    hidden_ref[...] = hidden
+    down_products(out_mask, hidden, down_ref, out_ref)
+
+
+def down_kernel(mask, hidden_ref, down_ref, out_ref):
+    down_products(mask, hidden_ref[...], down_ref, out_ref)
 
 
 def add_kernel(a, b, c, d, out_ref):
@@ -193,16 +232,20 @@
     out_ref[LANES:, :] = jnp.where(odd, first[HLANES:], rest).astype(BF16)
 
 
-def call(kernel, shape, *args, scratch=(), limit=16, outs=0):
-    one = jax.ShapeDtypeStruct(shape, BF16)
+def call(kernel, shape, *args, scratch=(), limit=16, dtype=BF16):
+    out = jax.ShapeDtypeStruct(shape, dtype) if isinstance(shape, tuple) else [pltpu.VMEM(s, d) for s, d in shape]
     return pl.pallas_call(
         kernel,
-        out_shape=[one] * outs if outs else one,
+        out_shape=out,
         scratch_shapes=scratch,
         compiler_params=pltpu.CompilerParams(vmem_limit_bytes=limit * 1024 * 1024),
     )(*args)
 
 
+def held(value):
+    return pltpu.with_memory_space_constraint(value, pltpu.VMEM)
+
+
 def swap(value):
     return lax.ppermute(value, "tensor", [(0, 1), (1, 0)])
 
@@ -213,13 +256,13 @@
 
 def shards(tokens, expert_ids, gate_values, w_gate, w_up, w_down):
     n, width = tokens.shape
-    hidden = w_gate.shape[1]
     plane, inside = ("dp", "tensor"), quarter_groups()
     ids, gates = expert_ids.T, gate_values.T
-    gap = jnp.zeros((-2 * hidden % LANES, width), BF16)
-    gate, up, down = w_gate[0], w_up[0], w_down[0]
-    weights = jnp.concatenate([gate, swap(gate), gap, up, swap(up), gap], axis=0)
-    downs = jnp.concatenate([down, swap(down), gap], axis=0)
+    own = [w_gate[0], w_up[0], w_down[0]]
+    weights, down = call(
+        weights_kernel, [((2 * WIDE, width), BF16), ((WIDE, width), BF16)], *own, *map(swap, own), limit=24
+    )
+    weights, down = held(weights), held(down)
     part_scratch = pltpu.VMEM((PART, LANES), F32)
     block_scratch = pltpu.VMEM((EXPERTS * BLOCK, LANES), F32)
 
@@ -227,18 +270,23 @@
     arrived = exchange(sent.reshape(EXPERTS, BLOCK, LANES), "expert").reshape(EXPERTS * BLOCK, LANES)
     rows = call(pack_kernel, (4, PART, LANES), arrived, scratch=[block_scratch, part_scratch])
     rows = exchange(rows, plane, inside)
-    others = {mask: lax.ppermute(rows, plane, across(mask)) for mask in (3, 1, 2)}
-    partial = call(
-        expert_kernel,
-        (4, PART, LANES),
-        *(rows, others[1], others[2], others[3]),
-        *(weights, downs),
-        scratch=[pltpu.VMEM((2 * SIDE, width), BF16)],
-        limit=48,
-        outs=4,
-    )
-    others = {mask: lax.ppermute(partial[mask], plane, across(mask)) for mask in (3, 1, 2)}
-    partial = call(add_kernel, (4, PART, LANES), partial[0], others[1], others[2], others[3], limit=24)
+    others = [lax.ppermute(rows, plane, across(mask)) for mask in MASKS]
+    total_shape, out_shape = ((2 * SIDE, 2 * WIDE), F32), ((4, PART, LANES), BF16)
+    (total,) = call(functools.partial(first_kernel, 0), [total_shape], rows, weights, limit=32)
+    for mask, other in zip(MASKS[:2], others[:2]):
+        (total,) = call(functools.partial(next_kernel, mask), [total_shape], other, weights, held(total), limit=32)
+    hidden, first = call(
+        functools.partial(last_kernel, MASKS[2], MASKS[0]),
+        [((2 * SIDE, WIDE), BF16), out_shape],
+        *(others[2], weights, held(total), down),
+        limit=32,
+    )
+    hidden = held(hidden)
+    outs = [first]
+    for mask in (*MASKS[1:], 0):
+        outs += call(functools.partial(down_kernel, mask), [out_shape], hidden, down, limit=32)
+    others = [lax.ppermute(out, plane, across(mask)) for mask, out in zip(MASKS, outs[:3])]
+    partial = call(add_kernel, (4, PART, LANES), *others, outs[3], limit=24)
     partial = exchange(partial, plane, inside)
     summed = call(add_blocks_kernel, (EXPERTS * BLOCK, LANES), partial, scratch=[part_scratch, block_scratch])
     back = exchange(summed.reshape(EXPERTS, BLOCK, LANES), "expert").reshape(EXPERTS * BLOCK, LANES)

time: 155 us -> 145 us (0.935)
  the two profiles are of different devices: /device:TPU:6 before, /device:TPU:32 now
where the time goes in v3:
time: 145 us; the launch traced here: 144 us
  starting transfers between devices  52.1 us (36%)
  waiting for transfers between devices  42 us (29%)
  blocking collectives  32.3 us (22%)
  Pallas kernels  14.7 us (10%)
  local copies, waits for them, and re-layouts  3.05 us (2%)
    all_to_all x2, blocking collectives, exchange(): lax.all_to_all(value, axis, split_axis=0, concat_axis=0, tiled=True, axis...  32.3 us
    all_to_all x2, starting transfers between devices, exchange(): lax.all_to_all(value, axis, split_axis=0, concat_axis=0, tiled=True, axis...  19.1 us
    ppermute x3, waiting for transfers between devices, shards(): lax.ppermute(out, plane, across(mask))  16.6 us
    all_to_all x2, waiting for transfers between devices, exchange(): lax.all_to_all(value, axis, split_axis=0, concat_axis=0, tiled=True, axis...  15.5 us
    pallas_call x13, Pallas kernels, call(): pl.pallas_call(kernel, out_shape=out, scratch_shapes=scratch, compiler_pa...  14.7 us
    ppermute x3, starting transfers between devices, shards(): lax.ppermute(out, plane, across(mask))  11.6 us
    ppermute x3, starting transfers between devices, shards(): others = [lax.ppermute(rows, plane, across(mask)) for mask in MASKS]  11.6 us
    ppermute x3, waiting for transfers between devices, shards(): others = [lax.ppermute(rows, plane, across(mask)) for mask in MASKS]  9.91 us
  transfers between devices with their start and end apart: 11, of which 7 were waited for; matrix products, arithmetic and copies ran while one was open for 0% of the time, Pallas kernels for 5%

profile of v3, /device:TPU:32, one launch (start us, length us, event | category | flops | bytes accessed | tf_op | source)
XLA Modules:
  0.0 144.4 jit_solution(12905488185378344597)
XLA Ops:
  0.0 1.1 copy-done.3
  1.1 0.0 copy-start.4
  1.1 0.7 copy-done.4
  1.8 1.4 shard_map.64
  3.2 15.3 %all-to-all-start = ((bf16[16,56,128]{2,1,0:T(8,128)(2,1)}), bf16[16,56,128]{2,1,0:T(8,128)(2,1)S(1)}, u32[]{:S(2)}, u32[]{:S(2)}) async-start(bf16[16,56,128]{2,1,0:T(8,128)(2,1)} %bitcast.2), calls=%async_computation | async-start | bytes 458752 | tf_op jit(solution)/shard_map/all_to_all | solution.py:254
  18.5 1.9 %collective-permute-start.1 = (bf16[168,3072]{1,0:T(8,128)(2,1)}, bf16[168,3072]{1,0:T(8,128)(2,1)}, u32[]{:S(2)}, u32[]{:S(2)}) collective-permute-start(bf16[168,3072]{1,0:T(8,128)(2,1)} %bitcast.10), channel_id=1, source_target_pairs={{0,1},{1,0},{2,3},{3,2},{4,5},{5,4},{6,7},{7,6},{8,9},{9,8},{10,11... | collective-permute-start | bytes 3096584 | tf_op jit(solution)/shard_map/ppermute | solution.py:250
  20.5 15.0 %all-to-all-done = bf16[16,56,128]{2,1,0:T(8,128)(2,1)S(1)} async-done(((bf16[16,56,128]{2,1,0:T(8,128)(2,1)}), bf16[16,56,128]{2,1,0:T(8,128)(2,1)S(1)}, u32[]{:S(2)}, u32[]{:S(2)}) %all-to-all-start) | async-done | bytes 229408 | tf_op jit(solution)/shard_map/all_to_all | solution.py:254
  35.5 1.0 shard_map.65
  36.5 3.8 %all-to-all-start.1 = ((bf16[4,816,128]{2,1,0:T(8,128)(2,1)}), bf16[4,816,128]{2,1,0:T(8,128)(2,1)S(1)}, u32[]{:S(2)}, u32[]{:S(2)}) async-start(bf16[4,816,128]{2,1,0:T(8,128)(2,1)} %shard_map.65), calls=%async_computation.1 | async-start | bytes 1671168 | tf_op jit(solution)/shard_map/all_to_all | solution.py:254
  40.3 0.0 copy-done.1
  40.3 5.9 %collective-permute-start.2 = (bf16[168,3072]{1,0:T(8,128)(2,1)S(1)}, bf16[168,3072]{1,0:T(8,128)(2,1)}, u32[]{:S(2)}, u32[]{:S(2)}) collective-permute-start(bf16[168,3072]{1,0:T(8,128)(2,1)S(1)} %bitcast.12), channel_id=1, source_target_pairs={{0,1},{1,0},{2,3},{3,2},{4,5},{5,4},{6,7},{7,6},{8,9},{9,8},{10,11... | collective-permute-start | bytes 3096584 | tf_op jit(solution)/shard_map/ppermute | solution.py:250
  46.1 1.9 %collective-permute-start.3 = (bf16[168,3072]{1,0:T(8,128)(2,1)}, bf16[168,3072]{1,0:T(8,128)(2,1)}, u32[]{:S(2)}, u32[]{:S(2)}) collective-permute-start(bf16[168,3072]{1,0:T(8,128)(2,1)} %bitcast.14), channel_id=1, source_target_pairs={{0,1},{1,0},{2,3},{3,2},{4,5},{5,4},{6,7},{7,6},{8,9},{9,8},{10,11... | collective-permute-start | bytes 3096584 | tf_op jit(solution)/shard_map/ppermute | solution.py:250
  48.1 0.5 all-to-all-done.1.x_ref
  48.6 6.3 %collective-permute-start.5 = (bf16[4,816,128]{2,1,0:T(8,128)(2,1)S(1)}, bf16[4,816,128]{2,1,0:T(8,128)(2,1)S(1)}, u32[]{:S(2)}, u32[]{:S(2)}) collective-permute-start(bf16[4,816,128]{2,1,0:T(8,128)(2,1)S(1)} %all-to-all-done.1.x_ref), channel_id=1, source_target_pairs={{0,480},{32,448},{64,416},{96,384},{128,352},{160,320},{192,288},{... | collective-permute-start | bytes 2506760 | tf_op jit(solution)/shard_map/ppermute | solution.py:273
  54.9 3.1 %collective-permute-start.4 = (bf16[4,816,128]{2,1,0:T(8,128)(2,1)S(1)}, bf16[4,816,128]{2,1,0:T(8,128)(2,1)S(1)}, u32[]{:S(2)}, u32[]{:S(2)}) collective-permute-start(bf16[4,816,128]{2,1,0:T(8,128)(2,1)S(1)} %all-to-all-done.1.x_ref), channel_id=1, source_target_pairs={{0,96},{32,64},{64,32},{96,0},{128,224},{160,192},{192,160},{224,1... | collective-permute-start | bytes 2506760 | tf_op jit(solution)/shard_map/ppermute | solution.py:273
  58.0 0.0 collective-permute-done.1.gate1
  58.0 2.2 %collective-permute-start = (bf16[4,816,128]{2,1,0:T(8,128)(2,1)S(1)}, bf16[4,816,128]{2,1,0:T(8,128)(2,1)S(1)}, u32[]{:S(2)}, u32[]{:S(2)}) collective-permute-start(bf16[4,816,128]{2,1,0:T(8,128)(2,1)S(1)} %all-to-all-done.1.x_ref), channel_id=1, source_target_pairs={{0,384},{32,416},{64,448},{96,480},{128,256},{160,288},{192,320},{... | collective-permute-start | bytes 2506760 | tf_op jit(solution)/shard_map/ppermute | solution.py:273
  60.2 0.0 collective-permute-done.2.up1
  60.2 0.0 collective-permute-done.3.down1
  60.2 0.0 copy-done
  60.3 0.0 copy-start.2
  60.3 1.2 copy-done.2
  61.5 2.3 %shard_map.66 = (bf16[768,3072]{1,0:T(8,128)(2,1)S(1)}, bf16[384,3072]{1,0:T(8,128)(2,1)S(1)}) custom-call(bf16[168,3072]{1,0:T(8,128)(2,1)S(1)} %bitcast.11, bf16[168,3072]{1,0:T(8,128)(2,1)S(1)} %bitcast.13, bf16[168,3072]{1,0:T(8,128)(2,1)S(1)} %bitcast.15, bf16[168,3072]{1,0:T(8,128)(2,1)} %collective-permute-done.1.gate1, ...), custom_call_target="tpu_custom_call" | custom-call | tf_op jit(solution)/shard_map/pallas_call | solution.py:237
  63.8 0.9 shard_map.67.sofar_ref
  64.7 1.7 %collective-permute-done.5.x_ref = bf16[4,816,128]{2,1,0:T(8,128)(2,1)S(1)} collective-permute-done((bf16[4,816,128]{2,1,0:T(8,128)(2,1)S(1)}, bf16[4,816,128]{2,1,0:T(8,128)(2,1)S(1)}, u32[]{:S(2)}, u32[]{:S(2)}) %collective-permute-start.5) | collective-permute-done | bytes 835616 | tf_op jit(solution)/shard_map/ppermute | solution.py:273
  66.4 0.9 shard_map.68.sofar_ref
  67.3 8.2 %collective-permute-done.4.x_ref = bf16[4,816,128]{2,1,0:T(8,128)(2,1)S(1)} collective-permute-done((bf16[4,816,128]{2,1,0:T(8,128)(2,1)S(1)}, bf16[4,816,128]{2,1,0:T(8,128)(2,1)S(1)}, u32[]{:S(2)}, u32[]{:S(2)}) %collective-permute-start.4) | collective-permute-done | bytes 835616 | tf_op jit(solution)/shard_map/ppermute | solution.py:273
  75.5 0.9 shard_map.69.sofar_ref
  76.4 0.0 collective-permute-done.x_ref
  76.5 2.2 %shard_map.70 = (bf16[544,384]{1,0:T(8,128)(2,1)S(1)}, bf16[4,816,128]{2,1,0:T(8,128)(2,1)S(1)}) custom-call(bf16[4,816,128]{2,1,0:T(8,128)(2,1)S(1)} %collective-permute-done.x_ref, bf16[768,3072]{1,0:T(8,128)(2,1)S(1)} %get-tuple-element.9.weights_ref, f32[544,768]{1,0:T(8,128)S(1)} %shard_map.69.sofar_ref, bf16[384,3072]{1,0:T(8,128)(2,1)S(1)} %get-tuple-element.10.down_ref), custom_call_target="tpu_custom_call" | custom-call | tf_op jit(solution)/shard_map/pallas_call | solution.py:237
  78.6 0.9 shard_map.72
  79.5 0.9 shard_map.71
  80.4 3.6 %collective-permute-start.8 = (bf16[4,816,128]{2,1,0:T(8,128)(2,1)S(1)}, bf16[4,816,128]{2,1,0:T(8,128)(2,1)S(1)}, u32[]{:S(2)}, u32[]{:S(2)}) collective-permute-start(bf16[4,816,128]{2,1,0:T(8,128)(2,1)S(1)} %shard_map.72), channel_id=1, source_target_pairs={{0,384},{32,416},{64,448},{96,480},{128,256},{160,288},{192,320},{... | collective-permute-start | bytes 2506760 | tf_op jit(solution)/shard_map/ppermute | solution.py:288
  84.0 4.0 %collective-permute-start.7 = (bf16[4,816,128]{2,1,0:T(8,128)(2,1)S(1)}, bf16[4,816,128]{2,1,0:T(8,128)(2,1)S(1)}, u32[]{:S(2)}, u32[]{:S(2)}) collective-permute-start(bf16[4,816,128]{2,1,0:T(8,128)(2,1)S(1)} %shard_map.71), channel_id=1, source_target_pairs={{0,96},{32,64},{64,32},{96,0},{128,224},{160,192},{192,160},{224,1... | collective-permute-start | bytes 2506760 | tf_op jit(solution)/shard_map/ppermute | solution.py:288
  88.0 4.1 %collective-permute-start.6 = (bf16[4,816,128]{2,1,0:T(8,128)(2,1)S(1)}, bf16[4,816,128]{2,1,0:T(8,128)(2,1)S(1)}, u32[]{:S(2)}, u32[]{:S(2)}) collective-permute-start(bf16[4,816,128]{2,1,0:T(8,128)(2,1)S(1)} %get-tuple-element.11), channel_id=1, source_target_pairs={{0,480},{32,448},{64,416},{96,384},{128,352},{160,320},{192,288},{... | collective-permute-start | bytes 2506760 | tf_op jit(solution)/shard_map/ppermute | solution.py:288
  92.1 0.9 shard_map.73.d
  92.9 3.1 %collective-permute-done.8.c = bf16[4,816,128]{2,1,0:T(8,128)(2,1)S(1)} collective-permute-done((bf16[4,816,128]{2,1,0:T(8,128)(2,1)S(1)}, bf16[4,816,128]{2,1,0:T(8,128)(2,1)S(1)}, u32[]{:S(2)}, u32[]{:S(2)}) %collective-permute-start.8) | collective-permute-done | bytes 835616 | tf_op jit(solution)/shard_map/ppermute | solution.py:288
  96.0 3.6 %collective-permute-done.7.b = bf16[4,816,128]{2,1,0:T(8,128)(2,1)S(1)} collective-permute-done((bf16[4,816,128]{2,1,0:T(8,128)(2,1)S(1)}, bf16[4,816,128]{2,1,0:T(8,128)(2,1)S(1)}, u32[]{:S(2)}, u32[]{:S(2)}) %collective-permute-start.7) | collective-permute-done | bytes 835616 | tf_op jit(solution)/shard_map/ppermute | solution.py:288
  99.6 9.9 %collective-permute-done.6.a = bf16[4,816,128]{2,1,0:T(8,128)(2,1)S(1)} collective-permute-done((bf16[4,816,128]{2,1,0:T(8,128)(2,1)S(1)}, bf16[4,816,128]{2,1,0:T(8,128)(2,1)S(1)}, u32[]{:S(2)}, u32[]{:S(2)}) %collective-permute-start.6) | collective-permute-done | bytes 835616 | tf_op jit(solution)/shard_map/ppermute | solution.py:288
  109.6 0.4 shard_map.74
  110.0 0.0 copy-start.5
  110.0 0.0 copy-start.6
  110.0 11.4 %all_to_all.20.parts_ref = bf16[4,816,128]{2,1,0:T(8,128)(2,1)S(1)} all-to-all(bf16[4,816,128]{2,1,0:T(8,128)(2,1)S(1)} %shard_map.74), channel_id=1, replica_groups={{0,32,128,160},{64,96,192,224},{256,288,384,416},{320,352,448,480},{481..., dimensions={0} | all-to-all | bytes 1671168 | tf_op jit(solution)/shard_map/all_to_all | solution.py:254
  121.4 0.2 shard_map.75
  121.6 20.9 %all_to_all.21 = bf16[16,56,128]{2,1,0:T(8,128)(2,1)S(1)} all-to-all(bf16[16,56,128]{2,1,0:T(8,128)(2,1)S(1)} %bitcast.18), channel_id=1, replica_groups=mesh['dp'=16,'expert'=16,'tensor'=2] {'expert'}, dimensions={0} | all-to-all | bytes 458752 | tf_op jit(solution)/shard_map/all_to_all | solution.py:254
  142.5 0.0 copy-done.5
  142.5 0.0 copy-done.6
  142.5 1.9 %shard_map.76 = bf16[192,128]{1,0:T(8,128)(2,1)} custom-call(s32[4,256]{1,0:T(4,128)S(1)} %bitcast.20, f32[4,256]{1,0:T(4,128)S(1)} %bitcast.21, bf16[896,128]{1,0:T(8,128)(2,1)S(1)} %bitcast.16), custom_call_target="tpu_custom_call" | custom-call | tf_op jit(solution)/shard_map/pallas_call | solution.py:237
  (3 shorter events, 0.0 us)
Async XLA Ops:
  0.0 1.1 copy-start.3
  1.1 0.7 copy-start.4
  3.2 37.1 %copy-start.1 = (bf16[1,168,3072]{2,1,0:T(8,128)(2,1)S(1)}, bf16[1,168,3072]{2,1,0:T(8,128)(2,1)}, u32[]{:S(2)}) copy-start(bf16[1,168,3072]{2,1,0:T(8,128)(2,1)} %param.10) | copy-start | bytes 3096580
  3.2 57.0 %copy-start = (bf16[1,168,3072]{2,1,0:T(8,128)(2,1)S(1)}, bf16[1,168,3072]{2,1,0:T(8,128)(2,1)}, u32[]{:S(2)}) copy-start(bf16[1,168,3072]{2,1,0:T(8,128)(2,1)} %param.9) | copy-start | bytes 3096580
  3.2 32.3 %all-to-all-start = ((bf16[16,56,128]{2,1,0:T(8,128)(2,1)}), bf16[16,56,128]{2,1,0:T(8,128)(2,1)S(1)}, u32[]{:S(2)}, u32[]{:S(2)}) async-start(bf16[16,56,128]{2,1,0:T(8,128)(2,1)} %bitcast.2), calls=%async_computation | async-start | bytes 458752 | tf_op jit(solution)/shard_map/all_to_all | solution.py:254
  18.5 39.4 %collective-permute-start.1 = (bf16[168,3072]{1,0:T(8,128)(2,1)}, bf16[168,3072]{1,0:T(8,128)(2,1)}, u32[]{:S(2)}, u32[]{:S(2)}) collective-permute-start(bf16[168,3072]{1,0:T(8,128)(2,1)} %bitcast.10), channel_id=1, source_target_pairs={{0,1},{1,0},{2,3},{3,2},{4,5},{5,4},{6,7},{7,6},{8,9},{9,8},{10,11... | collective-permute-start | bytes 3096584 | tf_op jit(solution)/shard_map/ppermute | solution.py:250
  36.5 12.1 %all-to-all-start.1 = ((bf16[4,816,128]{2,1,0:T(8,128)(2,1)}), bf16[4,816,128]{2,1,0:T(8,128)(2,1)S(1)}, u32[]{:S(2)}, u32[]{:S(2)}) async-start(bf16[4,816,128]{2,1,0:T(8,128)(2,1)} %shard_map.65), calls=%async_computation.1 | async-start | bytes 1671168 | tf_op jit(solution)/shard_map/all_to_all | solution.py:254
  40.3 19.9 %collective-permute-start.2 = (bf16[168,3072]{1,0:T(8,128)(2,1)S(1)}, bf16[168,3072]{1,0:T(8,128)(2,1)}, u32[]{:S(2)}, u32[]{:S(2)}) collective-permute-start(bf16[168,3072]{1,0:T(8,128)(2,1)S(1)} %bitcast.12), channel_id=1, source_target_pairs={{0,1},{1,0},{2,3},{3,2},{4,5},{5,4},{6,7},{7,6},{8,9},{9,8},{10,11... | collective-permute-start | bytes 3096584 | tf_op jit(solution)/shard_map/ppermute | solution.py:250
  46.1 14.1 %collective-permute-start.3 = (bf16[168,3072]{1,0:T(8,128)(2,1)}, bf16[168,3072]{1,0:T(8,128)(2,1)}, u32[]{:S(2)}, u32[]{:S(2)}) collective-permute-start(bf16[168,3072]{1,0:T(8,128)(2,1)} %bitcast.14), channel_id=1, source_target_pairs={{0,1},{1,0},{2,3},{3,2},{4,5},{5,4},{6,7},{7,6},{8,9},{9,8},{10,11... | collective-permute-start | bytes 3096584 | tf_op jit(solution)/shard_map/ppermute | solution.py:250
  48.6 17.8 %collective-permute-start.5 = (bf16[4,816,128]{2,1,0:T(8,128)(2,1)S(1)}, bf16[4,816,128]{2,1,0:T(8,128)(2,1)S(1)}, u32[]{:S(2)}, u32[]{:S(2)}) collective-permute-start(bf16[4,816,128]{2,1,0:T(8,128)(2,1)S(1)} %all-to-all-done.1.x_ref), channel_id=1, source_target_pairs={{0,480},{32,448},{64,416},{96,384},{128,352},{160,320},{192,288},{... | collective-permute-start | bytes 2506760 | tf_op jit(solution)/shard_map/ppermute | solution.py:273
  54.9 20.6 %collective-permute-start.4 = (bf16[4,816,128]{2,1,0:T(8,128)(2,1)S(1)}, bf16[4,816,128]{2,1,0:T(8,128)(2,1)S(1)}, u32[]{:S(2)}, u32[]{:S(2)}) collective-permute-start(bf16[4,816,128]{2,1,0:T(8,128)(2,1)S(1)} %all-to-all-done.1.x_ref), channel_id=1, source_target_pairs={{0,96},{32,64},{64,32},{96,0},{128,224},{160,192},{192,160},{224,1... | collective-permute-start | bytes 2506760 | tf_op jit(solution)/shard_map/ppermute | solution.py:273
  58.0 18.5 %collective-permute-start = (bf16[4,816,128]{2,1,0:T(8,128)(2,1)S(1)}, bf16[4,816,128]{2,1,0:T(8,128)(2,1)S(1)}, u32[]{:S(2)}, u32[]{:S(2)}) collective-permute-start(bf16[4,816,128]{2,1,0:T(8,128)(2,1)S(1)} %all-to-all-done.1.x_ref), channel_id=1, source_target_pairs={{0,384},{32,416},{64,448},{96,480},{128,256},{160,288},{192,320},{... | collective-permute-start | bytes 2506760 | tf_op jit(solution)/shard_map/ppermute | solution.py:273
  60.3 1.2 copy-start.2
  80.4 15.6 %collective-permute-start.8 = (bf16[4,816,128]{2,1,0:T(8,128)(2,1)S(1)}, bf16[4,816,128]{2,1,0:T(8,128)(2,1)S(1)}, u32[]{:S(2)}, u32[]{:S(2)}) collective-permute-start(bf16[4,816,128]{2,1,0:T(8,128)(2,1)S(1)} %shard_map.72), channel_id=1, source_target_pairs={{0,384},{32,416},{64,448},{96,480},{128,256},{160,288},{192,320},{... | collective-permute-start | bytes 2506760 | tf_op jit(solution)/shard_map/ppermute | solution.py:288
  84.0 15.6 %collective-permute-start.7 = (bf16[4,816,128]{2,1,0:T(8,128)(2,1)S(1)}, bf16[4,816,128]{2,1,0:T(8,128)(2,1)S(1)}, u32[]{:S(2)}, u32[]{:S(2)}) collective-permute-start(bf16[4,816,128]{2,1,0:T(8,128)(2,1)S(1)} %shard_map.71), channel_id=1, source_target_pairs={{0,96},{32,64},{64,32},{96,0},{128,224},{160,192},{192,160},{224,1... | collective-permute-start | bytes 2506760 | tf_op jit(solution)/shard_map/ppermute | solution.py:288
  88.0 21.6 %collective-permute-start.6 = (bf16[4,816,128]{2,1,0:T(8,128)(2,1)S(1)}, bf16[4,816,128]{2,1,0:T(8,128)(2,1)S(1)}, u32[]{:S(2)}, u32[]{:S(2)}) collective-permute-start(bf16[4,816,128]{2,1,0:T(8,128)(2,1)S(1)} %get-tuple-element.11), channel_id=1, source_target_pairs={{0,480},{32,448},{64,416},{96,384},{128,352},{160,320},{192,288},{... | collective-permute-start | bytes 2506760 | tf_op jit(solution)/shard_map/ppermute | solution.py:288
  110.0 32.6 %copy-start.5 = (s32[256,4]{0,1:T(4,128)S(1)}, s32[256,4]{0,1:T(4,128)}, u32[]{:S(2)}) copy-start(s32[256,4]{0,1:T(4,128)} %param.7) | copy-start | bytes 12292
  110.0 32.5 %copy-start.6 = (f32[256,4]{0,1:T(4,128)S(1)}, f32[256,4]{0,1:T(4,128)}, u32[]{:S(2)}) copy-start(f32[256,4]{0,1:T(4,128)} %param.8) | copy-start | bytes 12292

commit v4 on v3

--- a/solution.py
+++ b/solution.py
@@ -15,9 +15,11 @@
 DP = SIZE * SIZE
 LANES = 128
 HLANES = 64
+RISE = 40
 BLOCK = 56
 SIDE = EXPERTS * HALF
 PART = 3 * SIDE
+AWAY = ((8, 4, -4, 0), (7, -7, 1, -1), (6, -6, 2, -2), (5, -5, 3, -3))
 WIDE = 384
 MASKS = (3, 1, 2)
 F32 = jnp.float32
@@ -41,6 +43,18 @@
                 q, at = quarter(y, x, core)
                 groups.setdefault((core, q), [0] * 4)[at] = device(y, x, core)
     return [groups[key] for key in sorted(groups)]
+
+
+def rising(k):
+    pairs = []
+    for y in range(SIZE):
+        for x in range(SIZE):
+            for z in range(EXPERTS):
+                for core in range(2):
+                    to = (z + AWAY[quarter(y, x, core)[1]][k]) % EXPERTS
+                    at = (y * SIZE + x) * EXPERTS
+                    pairs.append(((at + z) * 2 + core, (at + to) * 2 + core))
+    return pairs
 
 
 def across(mask):
@@ -70,52 +84,44 @@
     return lax.broadcasted_iota(jnp.int32, shape, dim)
 
 
-def slot_picks(ids):
+def slots_of(ids):
     n = ids.shape[1]
     named = jnp.zeros((EXPERTS, n), F32)
     for k in range(TOP):
         named += (ids[k : k + 1, :] == iota((EXPERTS, n), 0)).astype(F32)
     earlier = (iota((n, n), 0) < iota((n, n), 1)).astype(BF16)
-    slot = jnp.where(named > 0.0, dot(named.astype(BF16), earlier), -1.0)
-    rows = EXPERTS * BLOCK
-
-    def expert_of(shape):
-        return jnp.floor((iota(shape, 0).astype(F32) + 0.5) * (1.0 / BLOCK))
-
-    spread = (expert_of((rows, EXPERTS)) == iota((rows, EXPERTS), 1).astype(F32)).astype(BF16)
-    wide = dot(spread, slot.astype(BF16))
-    at = iota((rows, n), 0).astype(F32) - BLOCK * expert_of((rows, n))
-    main, half = at < CAP, (at >= CAP) & (at < CAP + HALF)
-    return [main & (wide == at), half & (wide == at - CAP), half & (wide == at - HALF)], spread
-
-
-def dispatch_kernel(ids_ref, tokens_ref, out_ref):
-    n = tokens_ref.shape[0]
+    return jnp.where(named > 0.0, dot(named.astype(BF16), earlier), -1.0).astype(BF16)
+
+
+def place_of():
     core, dp = lax.axis_index("tensor"), lax.axis_index("dp")
-    q, at = quarter(dp // SIZE, dp % SIZE, core)
-    part = 4 * q + at
-    picks, _ = slot_picks(ids_ref[:, pl.ds(pl.multiple_of(core * n, n), n)])
-    picks = jnp.concatenate([p.astype(BF16) for p in picks], axis=1)
-    first = tokens_ref[:, pl.ds(pl.multiple_of(part * LANES, LANES), LANES)]
-    rest = tokens_ref[:, pl.ds(pl.multiple_of((DP + part // 2) * LANES, LANES), LANES)].astype(F32)
-    low = iota((n, LANES), 1) < HLANES
-    turned = pltpu.roll(rest, HLANES, 1)
-    odd = part % 2 == 1
-    here = jnp.where(odd, turned, rest)
-    there = jnp.where(odd, rest, turned)
-    rows = jnp.concatenate(
-        [first, jnp.where(low, here, 0.0).astype(BF16), jnp.where(low, 0.0, there).astype(BF16)], axis=0
-    )
-    out_ref[...] = dot(picks, rows).astype(BF16)
-
-
-def pack_kernel(blocks_ref, out_ref, source, packed):
-    source[...] = blocks_ref[...].astype(F32)
-    for e in range(EXPERTS):
-        for third in range(3):
-            packed[third * SIDE + e * HALF : third * SIDE + (e + 1) * HALF, :] = source[
-                e * BLOCK + third * HALF : e * BLOCK + (third + 1) * HALF, :
-            ]
+    return core, *quarter(dp // SIZE, dp % SIZE, core)
+
+
+def away_of(at, k):
+    away = AWAY[0][k]
+    for j in range(1, 4):
+        away = jnp.where(at == j, AWAY[j][k], away)
+    return away
+
+
+def dispatch_kernel(ids_ref, tokens_ref, *out_refs):
+    n, width = tokens_ref.shape
+    core, q, at = place_of()
+    slots = slots_of(ids_ref[:, pl.ds(pl.multiple_of(core * n, n), n)])
+    part = width // 4
+    rows = tokens_ref[:, pl.ds(pl.multiple_of(q * part, part), part)]
+    for k, out_ref in enumerate(out_refs):
+        expert = lax.rem(lax.axis_index("expert") + away_of(at, k) + EXPERTS, EXPERTS)
+        spread = (iota((RISE, EXPERTS), 1) == expert).astype(BF16)
+        picks = dot(spread, slots) == iota((RISE, n), 0).astype(F32)
+        out_ref[...] = dot(picks.astype(BF16), rows).astype(BF16)
+
+
+def pack_kernel(*refs):
+    blocks, out_ref, packed = refs[:4], refs[4], refs[5]
+    for k, ref in enumerate(blocks):
+        packed[k * CAP : (k + 1) * CAP, :] = ref[...].astype(F32)[:CAP]
     value = packed[...].astype(BF16)
     for copy in range(out_ref.shape[0]):
         out_ref[copy] = value
@@ -130,31 +136,15 @@
             out_ref[at + start + hidden : at + end, :] = jnp.zeros((end - start - hidden, width), BF16)
 
 
-def place_of():
-    core, dp = lax.axis_index("tensor"), lax.axis_index("dp")
-    return core, quarter(dp // SIZE, dp % SIZE, core)[0]
-
-
 def products(mask, x_ref, weights_ref):
-    _, q = place_of()
-    q = q ^ mask
-    low = iota((SIDE, LANES), 1) < HLANES
-    main = jnp.concatenate([x_ref[at, : 2 * SIDE, :] for at in range(4)], axis=1)
-    halves = []
-    for pair in range(2):
-        even = x_ref[2 * pair, 2 * SIDE :, :].astype(F32)
-        odd = x_ref[2 * pair + 1, 2 * SIDE :, :].astype(F32)
-        upper = jnp.where(low, even, pltpu.roll(odd, HLANES, 1)).astype(BF16)
-        lower = jnp.where(low, pltpu.roll(even, HLANES, 1), odd).astype(BF16)
-        halves.append(jnp.concatenate([upper, lower], axis=0))
-    rest = jnp.concatenate(halves, axis=1)
-    main_lanes = pl.ds(pl.multiple_of(q * 4 * LANES, LANES), 4 * LANES)
-    rest_lanes = pl.ds(pl.multiple_of((DP + q * 2) * LANES, LANES), 2 * LANES)
-    return dot_t(main, weights_ref[:, main_lanes]) + dot_t(rest, weights_ref[:, rest_lanes])
+    _, q, _ = place_of()
+    part = x_ref.shape[1]
+    lanes = pl.ds(pl.multiple_of((q ^ mask) * part, part), part)
+    return dot_t(x_ref[...], weights_ref[:, lanes])
 
 
 def down_products(mask, hidden, down_ref, out_ref):
-    core, q = place_of()
+    core, q, _ = place_of()
     to = q ^ mask
     low = iota((SIDE, LANES), 1) < HLANES
     for at in range(4):
@@ -198,13 +188,22 @@
     for i in range(1, parts_ref.shape[0]):
         total += parts_ref[i].astype(F32)
     packed[...] = total
+    low = iota((HALF, LANES), 1) < HLANES
+
+    def put(b, at, value):
+        home = lax.rem(lax.axis_index("expert") - AWAY[b // 4][b % 4] + EXPERTS, EXPERTS)
+        blocks[home, at : at + value.shape[0], :] = value
+
+    for b in range(EXPERTS):
+        put(b, 0, packed[b * CAP : (b + 1) * CAP, :])
+        put(b, CAP + HALF, jnp.zeros((BLOCK - CAP - HALF, LANES), F32))
+    for b in range(EXPERTS // 2):
+        at = 2 * SIDE + b * CAP
+        upper, lower = packed[at : at + HALF, :], packed[at + HALF : at + CAP, :]
+        put(b, CAP, jnp.where(low, upper, pltpu.roll(lower, HLANES, 1)))
+        put(b + EXPERTS // 2, CAP, jnp.where(low, pltpu.roll(upper, HLANES, 1), lower))
     for e in range(EXPERTS):
-        for third in range(3):
-            blocks[e * BLOCK + third * HALF : e * BLOCK + (third + 1) * HALF, :] = packed[
-                third * SIDE + e * HALF : third * SIDE + (e + 1) * HALF, :
-            ]
-        blocks[e * BLOCK + 3 * HALF : (e + 1) * BLOCK, :] = jnp.zeros((BLOCK - 3 * HALF, LANES), F32)
-    out_ref[...] = blocks[...].astype(BF16)
+        out_ref[e] = blocks[e].astype(BF16)
 
 
 def combine_kernel(ids_ref, gates_ref, blocks_ref, out_ref):
@@ -212,8 +211,18 @@
     core, dp = lax.axis_index("tensor"), lax.axis_index("dp")
     own = pl.ds(pl.multiple_of(core * n, n), n)
     ids, given = ids_ref[:, own], gates_ref[:, own]
-    picks, spread = slot_picks(ids)
-    picks = jnp.concatenate(picks, axis=1)
+    rows = EXPERTS * BLOCK
+
+    def expert_of(shape):
+        return jnp.floor((iota(shape, 0).astype(F32) + 0.5) * (1.0 / BLOCK))
+
+    spread = (expert_of((rows, EXPERTS)) == iota((rows, EXPERTS), 1).astype(F32)).astype(BF16)
+    wide = dot(spread, slots_of(ids))
+    at = iota((rows, n), 0).astype(F32) - BLOCK * expert_of((rows, n))
+    half = (at >= CAP) & (at < CAP + HALF)
+    picks = jnp.concatenate(
+        [(at < CAP) & (wide == at), half & (wide == at - CAP), half & (wide == at - HALF)], axis=1
+    )
     gates = jnp.zeros((EXPERTS, n), F32)
     for k in range(TOP):
         gates += jnp.where(ids[k : k + 1, :] == iota((EXPERTS, n), 0), given[k : k + 1, :], 0.0)
@@ -263,13 +272,11 @@
         weights_kernel, [((2 * WIDE, width), BF16), ((WIDE, width), BF16)], *own, *map(swap, own), limit=24
     )
     weights, down = held(weights), held(down)
-    part_scratch = pltpu.VMEM((PART, LANES), F32)
-    block_scratch = pltpu.VMEM((EXPERTS * BLOCK, LANES), F32)
-
-    sent = call(dispatch_kernel, (EXPERTS * BLOCK, LANES), ids, tokens)
-    arrived = exchange(sent.reshape(EXPERTS, BLOCK, LANES), "expert").reshape(EXPERTS * BLOCK, LANES)
-    rows = call(pack_kernel, (4, PART, LANES), arrived, scratch=[block_scratch, part_scratch])
-    rows = exchange(rows, plane, inside)
+    part = width // 4
+    sent = call(dispatch_kernel, [((RISE, part), BF16)] * 4, ids, tokens)
+    arrived = [lax.ppermute(v, ("dp", "expert", "tensor"), rising(k)) for k, v in enumerate(sent)]
+    rows = call(pack_kernel, (4, 4 * CAP, part), *arrived, scratch=[pltpu.VMEM((4 * CAP, part), F32)])
+    rows = exchange(rows, plane, inside).reshape(2 * SIDE, part)
     others = [lax.ppermute(rows, plane, across(mask)) for mask in MASKS]
     total_shape, out_shape = ((2 * SIDE, 2 * WIDE), F32), ((4, PART, LANES), BF16)
     (total,) = call(functools.partial(first_kernel, 0), [total_shape], rows, weights, limit=32)
@@ -288,8 +295,13 @@
     others = [lax.ppermute(out, plane, across(mask)) for mask, out in zip(MASKS, outs[:3])]
     partial = call(add_kernel, (4, PART, LANES), *others, outs[3], limit=24)
     partial = exchange(partial, plane, inside)
-    summed = call(add_blocks_kernel, (EXPERTS * BLOCK, LANES), partial, scratch=[part_scratch, block_scratch])
-    back = exchange(summed.reshape(EXPERTS, BLOCK, LANES), "expert").reshape(EXPERTS * BLOCK, LANES)
+    summed = call(
+        add_blocks_kernel,
+        (EXPERTS, BLOCK, LANES),
+        partial,
+        scratch=[pltpu.VMEM((PART, LANES), F32), pltpu.VMEM((EXPERTS, BLOCK, LANES), F32)],
+    )
+    back = exchange(summed, "expert").reshape(EXPERTS * BLOCK, LANES)
     return call(combine_kernel, (width // DP, n), ids, gates, back).T
 
 

time: 145 us -> 148 us (1.021)
  starting transfers between devices: 52.1 us -> 61.6 us
  waiting for transfers between devices: 42 us -> 34.7 us
    ppermute x0 -> x4, starting transfers between devices: none -> 25.2 us  [shards(): lax.ppermute(v, ('dp', 'expert', 'tensor'), rising(k))]
    all_to_all x2 -> x1, starting transfers between devices: 19.1 us -> 3.5 us  [exchange(): lax.all_to_all(value, axis, split_axis=0, concat_axis=0, tiled=True, axis...]
    all_to_all x2 -> x1, waiting for transfers between devices: 15.5 us -> 0.52 us  [exchange(): lax.all_to_all(value, axis, split_axis=0, concat_axis=0, tiled=True, axis...]
    ppermute x0 -> x4, waiting for transfers between devices: none -> 7.7 us  [shards(): lax.ppermute(v, ('dp', 'expert', 'tensor'), rising(k))]
  transfers between devices with their start and end apart: 11 -> 14, of which waited for: 7 -> 8; matrix products, arithmetic and copies ran while one was open for 0% -> 0% of each run, Pallas kernels for 5% -> 5%
where the time goes in v4:
time: 148 us; the launch traced here: 147 us
  starting transfers between devices  61.6 us (42%)
  waiting for transfers between devices  34.7 us (23%)
  blocking collectives  33.6 us (23%)
  Pallas kernels  14 us (9%)
  local copies, waits for them, and re-layouts  3.05 us (2%)
    all_to_all x2, blocking collectives, exchange(): lax.all_to_all(value, axis, split_axis=0, concat_axis=0, tiled=True, axis...  33.6 us
    ppermute x4, starting transfers between devices, shards(): lax.ppermute(v, ('dp', 'expert', 'tensor'), rising(k))  25.2 us
    ppermute x3, waiting for transfers between devices, shards(): lax.ppermute(out, plane, across(mask))  16.6 us
    pallas_call x13, Pallas kernels, call(): pl.pallas_call(kernel, out_shape=out, scratch_shapes=scratch, compiler_pa...  14 us
    ppermute x3, starting transfers between devices, shards(): lax.ppermute(out, plane, across(mask))  11.6 us
    ppermute x3, starting transfers between devices, shards(): others = [lax.ppermute(rows, plane, across(mask)) for mask in MASKS]  11.6 us
    ppermute x3, waiting for transfers between devices, shards(): others = [lax.ppermute(rows, plane, across(mask)) for mask in MASKS]  9.87 us
    ppermute x3, starting transfers between devices, swap(): return lax.ppermute(value, 'tensor', [(0, 1), (1, 0)])  9.62 us
  transfers between devices with their start and end apart: 14, of which 8 were waited for; matrix products, arithmetic and copies ran while one was open for 0% of the time, Pallas kernels for 5%

profile of v4, /device:TPU:32, one launch (start us, length us, event | category | flops | bytes accessed | tf_op | source)
XLA Modules:
  0.0 147.2 jit_solution(58449176927636671)
XLA Ops:
  0.0 1.9 %collective-permute-start.5 = (bf16[168,3072]{1,0:T(8,128)(2,1)}, bf16[168,3072]{1,0:T(8,128)(2,1)}, u32[]{:S(2)}, u32[]{:S(2)}) collective-permute-start(bf16[168,3072]{1,0:T(8,128)(2,1)} %bitcast.12), channel_id=1, source_target_pairs={{0,1},{1,0},{2,3},{3,2},{4,5},{5,4},{6,7},{7,6},{8,9},{9,8},{10,11... | collective-permute-start | bytes 3096584 | tf_op jit(solution)/shard_map/ppermute | solution.py:259
  1.9 1.1 copy-done.3
  3.1 0.7 copy-done.4
  3.7 0.8 shard_map.64
  4.5 14.8 %collective-permute-start = (bf16[40,768]{1,0:T(8,128)(2,1)S(1)}, bf16[40,768]{1,0:T(8,128)(2,1)S(1)}, u32[]{:S(2)}, u32[]{:S(2)}) collective-permute-start(bf16[40,768]{1,0:T(8,128)(2,1)S(1)} %get-tuple-element.13), channel_id=1, source_target_pairs={{0,16},{1,11},{2,18},{3,13},{4,20},{5,15},{6,22},{7,17},{8,24},{9,... | collective-permute-start | bytes 184328 | tf_op jit(solution)/shard_map/ppermute | solution.py:277
  19.4 4.3 %collective-permute-start.1 = (bf16[40,768]{1,0:T(8,128)(2,1)S(1)}, bf16[40,768]{1,0:T(8,128)(2,1)S(1)}, u32[]{:S(2)}, u32[]{:S(2)}) collective-permute-start(bf16[40,768]{1,0:T(8,128)(2,1)S(1)} %get-tuple-element.14), channel_id=1, source_target_pairs={{0,8},{1,23},{2,10},{3,25},{4,12},{5,27},{6,14},{7,29},{8,16},{9,3... | collective-permute-start | bytes 184328 | tf_op jit(solution)/shard_map/ppermute | solution.py:277
  23.7 5.5 %collective-permute-start.2 = (bf16[40,768]{1,0:T(8,128)(2,1)S(1)}, bf16[40,768]{1,0:T(8,128)(2,1)S(1)}, u32[]{:S(2)}, u32[]{:S(2)}) collective-permute-start(bf16[40,768]{1,0:T(8,128)(2,1)S(1)} %get-tuple-element.15), channel_id=1, source_target_pairs={{0,24},{1,7},{2,26},{3,9},{4,28},{5,11},{6,30},{7,13},{8,0},{9,15}... | collective-permute-start | bytes 184328 | tf_op jit(solution)/shard_map/ppermute | solution.py:277
  29.1 0.7 collective-permute-start.3
  29.8 0.0 collective-permute-done.refs_0_
  29.8 2.8 %collective-permute-done.1.refs_1_ = bf16[40,768]{1,0:T(8,128)(2,1)S(1)} collective-permute-done((bf16[40,768]{1,0:T(8,128)(2,1)S(1)}, bf16[40,768]{1,0:T(8,128)(2,1)S(1)}, u32[]{:S(2)}, u32[]{:S(2)}) %collective-permute-start.1) | collective-permute-done | bytes 61472 | tf_op jit(solution)/shard_map/ppermute | solution.py:277
  32.6 4.9 %collective-permute-done.2.refs_2_ = bf16[40,768]{1,0:T(8,128)(2,1)S(1)} collective-permute-done((bf16[40,768]{1,0:T(8,128)(2,1)S(1)}, bf16[40,768]{1,0:T(8,128)(2,1)S(1)}, u32[]{:S(2)}, u32[]{:S(2)}) %collective-permute-start.2) | collective-permute-done | bytes 61472 | tf_op jit(solution)/shard_map/ppermute | solution.py:277
  37.5 0.0 collective-permute-done.3.refs_3_
  37.5 1.0 shard_map.65
  38.5 3.5 %all-to-all-start = ((bf16[4,136,768]{2,1,0:T(8,128)(2,1)}), bf16[4,136,768]{2,1,0:T(8,128)(2,1)S(1)}, u32[]{:S(2)}, u32[]{:S(2)}) async-start(bf16[4,136,768]{2,1,0:T(8,128)(2,1)} %shard_map.65), calls=%async_computation | async-start | bytes 1671168 | tf_op jit(solution)/shard_map/all_to_all | solution.py:263
  42.0 5.8 %collective-permute-start.6 = (bf16[168,3072]{1,0:T(8,128)(2,1)S(1)}, bf16[168,3072]{1,0:T(8,128)(2,1)}, u32[]{:S(2)}, u32[]{:S(2)}) collective-permute-start(bf16[168,3072]{1,0:T(8,128)(2,1)S(1)} %bitcast.14), channel_id=1, source_target_pairs={{0,1},{1,0},{2,3},{3,2},{4,5},{5,4},{6,7},{7,6},{8,9},{9,8},{10,11... | collective-permute-start | bytes 3096584 | tf_op jit(solution)/shard_map/ppermute | solution.py:259
  47.8 1.9 %collective-permute-start.7 = (bf16[168,3072]{1,0:T(8,128)(2,1)}, bf16[168,3072]{1,0:T(8,128)(2,1)}, u32[]{:S(2)}, u32[]{:S(2)}) collective-permute-start(bf16[168,3072]{1,0:T(8,128)(2,1)} %bitcast.16), channel_id=1, source_target_pairs={{0,1},{1,0},{2,3},{3,2},{4,5},{5,4},{6,7},{7,6},{8,9},{9,8},{10,11... | collective-permute-start | bytes 3096584 | tf_op jit(solution)/shard_map/ppermute | solution.py:259
  49.8 0.5 all-to-all-done
  50.3 6.2 %collective-permute-start.9 = (bf16[544,768]{1,0:T(8,128)(2,1)S(1)}, bf16[544,768]{1,0:T(8,128)(2,1)S(1)}, u32[]{:S(2)}, u32[]{:S(2)}) collective-permute-start(bf16[544,768]{1,0:T(8,128)(2,1)S(1)} %bitcast.8), channel_id=1, source_target_pairs={{0,480},{32,448},{64,416},{96,384},{128,352},{160,320},{192,288},{... | collective-permute-start | bytes 2506760 | tf_op jit(solution)/shard_map/ppermute | solution.py:280
  56.5 3.1 %collective-permute-start.8 = (bf16[544,768]{1,0:T(8,128)(2,1)S(1)}, bf16[544,768]{1,0:T(8,128)(2,1)S(1)}, u32[]{:S(2)}, u32[]{:S(2)}) collective-permute-start(bf16[544,768]{1,0:T(8,128)(2,1)S(1)} %bitcast.9), channel_id=1, source_target_pairs={{0,96},{32,64},{64,32},{96,0},{128,224},{160,192},{192,160},{224,1... | collective-permute-start | bytes 2506760 | tf_op jit(solution)/shard_map/ppermute | solution.py:280
  59.6 0.0 collective-permute-done.5.gate1
  59.6 2.3 %collective-permute-start.4 = (bf16[544,768]{1,0:T(8,128)(2,1)S(1)}, bf16[544,768]{1,0:T(8,128)(2,1)S(1)}, u32[]{:S(2)}, u32[]{:S(2)}) collective-permute-start(bf16[544,768]{1,0:T(8,128)(2,1)S(1)} %bitcast.10), channel_id=1, source_target_pairs={{0,384},{32,416},{64,448},{96,480},{128,256},{160,288},{192,320},{... | collective-permute-start | bytes 2506760 | tf_op jit(solution)/shard_map/ppermute | solution.py:280
  61.9 0.0 collective-permute-done.6.up1
  62.0 0.0 copy-start.2
  62.0 1.2 copy-done.2
  63.2 2.3 %shard_map.66 = (bf16[768,3072]{1,0:T(8,128)(2,1)S(1)}, bf16[384,3072]{1,0:T(8,128)(2,1)S(1)}) custom-call(bf16[168,3072]{1,0:T(8,128)(2,1)S(1)} %bitcast.13, bf16[168,3072]{1,0:T(8,128)(2,1)S(1)} %bitcast.15, bf16[168,3072]{1,0:T(8,128)(2,1)S(1)} %bitcast.17, bf16[168,3072]{1,0:T(8,128)(2,1)} %collective-permute-done.5.gate1, ...), custom_call_target="tpu_custom_call" | custom-call | tf_op jit(solution)/shard_map/pallas_call | solution.py:246
  65.5 0.9 shard_map.67.sofar_ref
  66.4 1.7 %collective-permute-done.9.x_ref = bf16[544,768]{1,0:T(8,128)(2,1)S(1)} collective-permute-done((bf16[544,768]{1,0:T(8,128)(2,1)S(1)}, bf16[544,768]{1,0:T(8,128)(2,1)S(1)}, u32[]{:S(2)}, u32[]{:S(2)}) %collective-permute-start.9) | collective-permute-done | bytes 835616 | tf_op jit(solution)/shard_map/ppermute | solution.py:280
  68.1 0.9 shard_map.68.sofar_ref
  69.0 8.1 %collective-permute-done.8.x_ref = bf16[544,768]{1,0:T(8,128)(2,1)S(1)} collective-permute-done((bf16[544,768]{1,0:T(8,128)(2,1)S(1)}, bf16[544,768]{1,0:T(8,128)(2,1)S(1)}, u32[]{:S(2)}, u32[]{:S(2)}) %collective-permute-start.8) | collective-permute-done | bytes 835616 | tf_op jit(solution)/shard_map/ppermute | solution.py:280
  77.1 0.9 shard_map.69.sofar_ref
  78.0 0.0 collective-permute-done.4.x_ref
  78.0 2.2 %shard_map.70 = (bf16[544,384]{1,0:T(8,128)(2,1)S(1)}, bf16[4,816,128]{2,1,0:T(8,128)(2,1)S(1)}) custom-call(bf16[544,768]{1,0:T(8,128)(2,1)S(1)} %collective-permute-done.4.x_ref, bf16[768,3072]{1,0:T(8,128)(2,1)S(1)} %get-tuple-element.17.weights_ref, f32[544,768]{1,0:T(8,128)S(1)} %shard_map.69.sofar_ref, bf16[384,3072]{1,0:T(8,128)(2,1)S(1)} %get-tuple-element.18.down_ref), custom_call_target="tpu_custom_call" | custom-call | tf_op jit(solution)/shard_map/pallas_call | solution.py:246
  80.2 0.9 shard_map.72
  81.1 0.9 shard_map.71
  81.9 3.6 %collective-permute-start.12 = (bf16[4,816,128]{2,1,0:T(8,128)(2,1)S(1)}, bf16[4,816,128]{2,1,0:T(8,128)(2,1)S(1)}, u32[]{:S(2)}, u32[]{:S(2)}) collective-permute-start(bf16[4,816,128]{2,1,0:T(8,128)(2,1)S(1)} %shard_map.72), channel_id=1, source_target_pairs={{0,384},{32,416},{64,448},{96,480},{128,256},{160,288},{192,320},{... | collective-permute-start | bytes 2506760 | tf_op jit(solution)/shard_map/ppermute | solution.py:295
  85.6 4.0 %collective-permute-start.11 = (bf16[4,816,128]{2,1,0:T(8,128)(2,1)S(1)}, bf16[4,816,128]{2,1,0:T(8,128)(2,1)S(1)}, u32[]{:S(2)}, u32[]{:S(2)}) collective-permute-start(bf16[4,816,128]{2,1,0:T(8,128)(2,1)S(1)} %shard_map.71), channel_id=1, source_target_pairs={{0,96},{32,64},{64,32},{96,0},{128,224},{160,192},{192,160},{224,1... | collective-permute-start | bytes 2506760 | tf_op jit(solution)/shard_map/ppermute | solution.py:295
  89.6 4.0 %collective-permute-start.10 = (bf16[4,816,128]{2,1,0:T(8,128)(2,1)S(1)}, bf16[4,816,128]{2,1,0:T(8,128)(2,1)S(1)}, u32[]{:S(2)}, u32[]{:S(2)}) collective-permute-start(bf16[4,816,128]{2,1,0:T(8,128)(2,1)S(1)} %get-tuple-element.19), channel_id=1, source_target_pairs={{0,480},{32,448},{64,416},{96,384},{128,352},{160,320},{192,288},{... | collective-permute-start | bytes 2506760 | tf_op jit(solution)/shard_map/ppermute | solution.py:295
  93.6 0.9 shard_map.73.d
  94.5 3.1 %collective-permute-done.12.c = bf16[4,816,128]{2,1,0:T(8,128)(2,1)S(1)} collective-permute-done((bf16[4,816,128]{2,1,0:T(8,128)(2,1)S(1)}, bf16[4,816,128]{2,1,0:T(8,128)(2,1)S(1)}, u32[]{:S(2)}, u32[]{:S(2)}) %collective-permute-start.12) | collective-permute-done | bytes 835616 | tf_op jit(solution)/shard_map/ppermute | solution.py:295
  97.6 3.6 %collective-permute-done.11.b = bf16[4,816,128]{2,1,0:T(8,128)(2,1)S(1)} collective-permute-done((bf16[4,816,128]{2,1,0:T(8,128)(2,1)S(1)}, bf16[4,816,128]{2,1,0:T(8,128)(2,1)S(1)}, u32[]{:S(2)}, u32[]{:S(2)}) %collective-permute-start.11) | collective-permute-done | bytes 835616 | tf_op jit(solution)/shard_map/ppermute | solution.py:295
  101.2 9.9 %collective-permute-done.10.a = bf16[4,816,128]{2,1,0:T(8,128)(2,1)S(1)} collective-permute-done((bf16[4,816,128]{2,1,0:T(8,128)(2,1)S(1)}, bf16[4,816,128]{2,1,0:T(8,128)(2,1)S(1)}, u32[]{:S(2)}, u32[]{:S(2)}) %collective-permute-start.10) | collective-permute-done | bytes 835616 | tf_op jit(solution)/shard_map/ppermute | solution.py:295
  111.1 0.4 shard_map.74
  111.5 0.0 copy-start.5
  111.5 0.0 copy-start.6
  111.5 11.4 %all_to_all.15.parts_ref = bf16[4,816,128]{2,1,0:T(8,128)(2,1)S(1)} all-to-all(bf16[4,816,128]{2,1,0:T(8,128)(2,1)S(1)} %shard_map.74), channel_id=1, replica_groups={{0,32,128,160},{64,96,192,224},{256,288,384,416},{320,352,448,480},{481..., dimensions={0} | all-to-all | bytes 1671168 | tf_op jit(solution)/shard_map/all_to_all | solution.py:263
  122.9 0.2 shard_map.75
  123.2 22.2 %all_to_all.16 = bf16[16,56,128]{2,1,0:T(8,128)(2,1)S(1)} all-to-all(bf16[16,56,128]{2,1,0:T(8,128)(2,1)S(1)} %shard_map.75), channel_id=1, replica_groups=mesh['dp'=16,'expert'=16,'tensor'=2] {'expert'}, dimensions={0} | all-to-all | bytes 458752 | tf_op jit(solution)/shard_map/all_to_all | solution.py:263
  145.3 1.9 %shard_map.76 = bf16[192,128]{1,0:T(8,128)(2,1)} custom-call(s32[4,256]{1,0:T(4,128)S(1)} %bitcast.20, f32[4,256]{1,0:T(4,128)S(1)} %bitcast.21, bf16[896,128]{1,0:T(8,128)(2,1)S(1)} %bitcast.18), custom_call_target="tpu_custom_call" | custom-call | tf_op jit(solution)/shard_map/pallas_call | solution.py:246
  (9 shorter events, 0.0 us)
Async XLA Ops:
  0.0 59.6 %collective-permute-start.5 = (bf16[168,3072]{1,0:T(8,128)(2,1)}, bf16[168,3072]{1,0:T(8,128)(2,1)}, u32[]{:S(2)}, u32[]{:S(2)}) collective-permute-start(bf16[168,3072]{1,0:T(8,128)(2,1)} %bitcast.12), channel_id=1, source_target_pairs={{0,1},{1,0},{2,3},{3,2},{4,5},{5,4},{6,7},{7,6},{8,9},{9,8},{10,11... | collective-permute-start | bytes 3096584 | tf_op jit(solution)/shard_map/ppermute | solution.py:259
  1.9 1.1 copy-start.3
  3.1 0.7 copy-start.4
  3.7 38.3 %copy-start.1 = (bf16[1,168,3072]{2,1,0:T(8,128)(2,1)S(1)}, bf16[1,168,3072]{2,1,0:T(8,128)(2,1)}, u32[]{:S(2)}) copy-start(bf16[1,168,3072]{2,1,0:T(8,128)(2,1)} %param.10) | copy-start | bytes 3096580
  3.7 58.2 %copy-start = (bf16[1,168,3072]{2,1,0:T(8,128)(2,1)S(1)}, bf16[1,168,3072]{2,1,0:T(8,128)(2,1)}, u32[]{:S(2)}) copy-start(bf16[1,168,3072]{2,1,0:T(8,128)(2,1)} %param.9) | copy-start | bytes 3096580
  4.5 25.3 %collective-permute-start = (bf16[40,768]{1,0:T(8,128)(2,1)S(1)}, bf16[40,768]{1,0:T(8,128)(2,1)S(1)}, u32[]{:S(2)}, u32[]{:S(2)}) collective-permute-start(bf16[40,768]{1,0:T(8,128)(2,1)S(1)} %get-tuple-element.13), channel_id=1, source_target_pairs={{0,16},{1,11},{2,18},{3,13},{4,20},{5,15},{6,22},{7,17},{8,24},{9,... | collective-permute-start | bytes 184328 | tf_op jit(solution)/shard_map/ppermute | solution.py:277
  19.4 13.2 %collective-permute-start.1 = (bf16[40,768]{1,0:T(8,128)(2,1)S(1)}, bf16[40,768]{1,0:T(8,128)(2,1)S(1)}, u32[]{:S(2)}, u32[]{:S(2)}) collective-permute-start(bf16[40,768]{1,0:T(8,128)(2,1)S(1)} %get-tuple-element.14), channel_id=1, source_target_pairs={{0,8},{1,23},{2,10},{3,25},{4,12},{5,27},{6,14},{7,29},{8,16},{9,3... | collective-permute-start | bytes 184328 | tf_op jit(solution)/shard_map/ppermute | solution.py:277
  23.7 13.8 %collective-permute-start.2 = (bf16[40,768]{1,0:T(8,128)(2,1)S(1)}, bf16[40,768]{1,0:T(8,128)(2,1)S(1)}, u32[]{:S(2)}, u32[]{:S(2)}) collective-permute-start(bf16[40,768]{1,0:T(8,128)(2,1)S(1)} %get-tuple-element.15), channel_id=1, source_target_pairs={{0,24},{1,7},{2,26},{3,9},{4,28},{5,11},{6,30},{7,13},{8,0},{9,15}... | collective-permute-start | bytes 184328 | tf_op jit(solution)/shard_map/ppermute | solution.py:277
  29.1 8.4 %collective-permute-start.3 = (bf16[40,768]{1,0:T(8,128)(2,1)S(1)}, bf16[40,768]{1,0:T(8,128)(2,1)S(1)}, u32[]{:S(2)}, u32[]{:S(2)}) collective-permute-start(bf16[40,768]{1,0:T(8,128)(2,1)S(1)} %get-tuple-element.16), channel_id=1, source_target_pairs={{0,0},{1,27},{2,2},{3,29},{4,4},{5,31},{6,6},{7,1},{8,8},{9,3},{10... | collective-permute-start | bytes 184328 | tf_op jit(solution)/shard_map/ppermute | solution.py:277
  38.5 11.8 %all-to-all-start = ((bf16[4,136,768]{2,1,0:T(8,128)(2,1)}), bf16[4,136,768]{2,1,0:T(8,128)(2,1)S(1)}, u32[]{:S(2)}, u32[]{:S(2)}) async-start(bf16[4,136,768]{2,1,0:T(8,128)(2,1)} %shard_map.65), calls=%async_computation | async-start | bytes 1671168 | tf_op jit(solution)/shard_map/all_to_all | solution.py:263
  42.0 19.9 %collective-permute-start.6 = (bf16[168,3072]{1,0:T(8,128)(2,1)S(1)}, bf16[168,3072]{1,0:T(8,128)(2,1)}, u32[]{:S(2)}, u32[]{:S(2)}) collective-permute-start(bf16[168,3072]{1,0:T(8,128)(2,1)S(1)} %bitcast.14), channel_id=1, source_target_pairs={{0,1},{1,0},{2,3},{3,2},{4,5},{5,4},{6,7},{7,6},{8,9},{9,8},{10,11... | collective-permute-start | bytes 3096584 | tf_op jit(solution)/shard_map/ppermute | solution.py:259
  47.8 14.1 %collective-permute-start.7 = (bf16[168,3072]{1,0:T(8,128)(2,1)}, bf16[168,3072]{1,0:T(8,128)(2,1)}, u32[]{:S(2)}, u32[]{:S(2)}) collective-permute-start(bf16[168,3072]{1,0:T(8,128)(2,1)} %bitcast.16), channel_id=1, source_target_pairs={{0,1},{1,0},{2,3},{3,2},{4,5},{5,4},{6,7},{7,6},{8,9},{9,8},{10,11... | collective-permute-start | bytes 3096584 | tf_op jit(solution)/shard_map/ppermute | solution.py:259
  50.3 17.8 %collective-permute-start.9 = (bf16[544,768]{1,0:T(8,128)(2,1)S(1)}, bf16[544,768]{1,0:T(8,128)(2,1)S(1)}, u32[]{:S(2)}, u32[]{:S(2)}) collective-permute-start(bf16[544,768]{1,0:T(8,128)(2,1)S(1)} %bitcast.8), channel_id=1, source_target_pairs={{0,480},{32,448},{64,416},{96,384},{128,352},{160,320},{192,288},{... | collective-permute-start | bytes 2506760 | tf_op jit(solution)/shard_map/ppermute | solution.py:280
  56.5 20.6 %collective-permute-start.8 = (bf16[544,768]{1,0:T(8,128)(2,1)S(1)}, bf16[544,768]{1,0:T(8,128)(2,1)S(1)}, u32[]{:S(2)}, u32[]{:S(2)}) collective-permute-start(bf16[544,768]{1,0:T(8,128)(2,1)S(1)} %bitcast.9), channel_id=1, source_target_pairs={{0,96},{32,64},{64,32},{96,0},{128,224},{160,192},{192,160},{224,1... | collective-permute-start | bytes 2506760 | tf_op jit(solution)/shard_map/ppermute | solution.py:280
  59.6 18.4 %collective-permute-start.4 = (bf16[544,768]{1,0:T(8,128)(2,1)S(1)}, bf16[544,768]{1,0:T(8,128)(2,1)S(1)}, u32[]{:S(2)}, u32[]{:S(2)}) collective-permute-start(bf16[544,768]{1,0:T(8,128)(2,1)S(1)} %bitcast.10), channel_id=1, source_target_pairs={{0,384},{32,416},{64,448},{96,480},{128,256},{160,288},{192,320},{... | collective-permute-start | bytes 2506760 | tf_op jit(solution)/shard_map/ppermute | solution.py:280
  62.0 1.2 copy-start.2
  81.9 15.6 %collective-permute-start.12 = (bf16[4,816,128]{2,1,0:T(8,128)(2,1)S(1)}, bf16[4,816,128]{2,1,0:T(8,128)(2,1)S(1)}, u32[]{:S(2)}, u32[]{:S(2)}) collective-permute-start(bf16[4,816,128]{2,1,0:T(8,128)(2,1)S(1)} %shard_map.72), channel_id=1, source_target_pairs={{0,384},{32,416},{64,448},{96,480},{128,256},{160,288},{192,320},{... | collective-permute-start | bytes 2506760 | tf_op jit(solution)/shard_map/ppermute | solution.py:295
  85.6 15.6 %collective-permute-start.11 = (bf16[4,816,128]{2,1,0:T(8,128)(2,1)S(1)}, bf16[4,816,128]{2,1,0:T(8,128)(2,1)S(1)}, u32[]{:S(2)}, u32[]{:S(2)}) collective-permute-start(bf16[4,816,128]{2,1,0:T(8,128)(2,1)S(1)} %shard_map.71), channel_id=1, source_target_pairs={{0,96},{32,64},{64,32},{96,0},{128,224},{160,192},{192,160},{224,1... | collective-permute-start | bytes 2506760 | tf_op jit(solution)/shard_map/ppermute | solution.py:295
  89.6 21.5 %collective-permute-start.10 = (bf16[4,816,128]{2,1,0:T(8,128)(2,1)S(1)}, bf16[4,816,128]{2,1,0:T(8,128)(2,1)S(1)}, u32[]{:S(2)}, u32[]{:S(2)}) collective-permute-start(bf16[4,816,128]{2,1,0:T(8,128)(2,1)S(1)} %get-tuple-element.19), channel_id=1, source_target_pairs={{0,480},{32,448},{64,416},{96,384},{128,352},{160,320},{192,288},{... | collective-permute-start | bytes 2506760 | tf_op jit(solution)/shard_map/ppermute | solution.py:295
  111.5 33.8 %copy-start.5 = (s32[256,4]{0,1:T(4,128)S(1)}, s32[256,4]{0,1:T(4,128)}, u32[]{:S(2)}) copy-start(s32[256,4]{0,1:T(4,128)} %param.7) | copy-start | bytes 12292
  111.5 33.8 %copy-start.6 = (f32[256,4]{0,1:T(4,128)S(1)}, f32[256,4]{0,1:T(4,128)}, u32[]{:S(2)}) copy-start(f32[256,4]{0,1:T(4,128)} %param.8) | copy-start | bytes 12292

commit v5 on v3

--- a/solution.py
+++ b/solution.py
@@ -189,8 +189,8 @@
     down_products(mask, hidden_ref[...], down_ref, out_ref)
 
 
-def add_kernel(a, b, c, d, out_ref):
-    out_ref[...] = (a[...].astype(F32) + b[...].astype(F32) + c[...].astype(F32) + d[...].astype(F32)).astype(BF16)
+def add_kernel(a, b, out_ref):
+    out_ref[...] = (a[...].astype(F32) + b[...].astype(F32)).astype(out_ref.dtype)
 
 
 def add_blocks_kernel(parts_ref, out_ref, packed, blocks):
@@ -207,37 +207,43 @@
     out_ref[...] = blocks[...].astype(BF16)
 
 
-def combine_kernel(ids_ref, gates_ref, blocks_ref, out_ref):
-    n = out_ref.shape[1]
-    core, dp = lax.axis_index("tensor"), lax.axis_index("dp")
-    own = pl.ds(pl.multiple_of(core * n, n), n)
+def gates_kernel(ids_ref, gates_ref, out_ref):
+    n = out_ref.shape[2] // 3
+    own = pl.ds(pl.multiple_of(lax.axis_index("tensor") * n, n), n)
     ids, given = ids_ref[:, own], gates_ref[:, own]
     picks, spread = slot_picks(ids)
     picks = jnp.concatenate(picks, axis=1)
     gates = jnp.zeros((EXPERTS, n), F32)
     for k in range(TOP):
         gates += jnp.where(ids[k : k + 1, :] == iota((EXPERTS, n), 0), given[k : k + 1, :], 0.0)
-    total = jnp.zeros((LANES, 3 * n), F32)
-    for _ in range(3):
+    for i in range(3):
         piece = gates.astype(BF16)
         gates = gates - piece.astype(F32)
         weight = dot(spread, piece)
         weight = jnp.concatenate([weight, weight, weight], axis=1)
-        total += t_dot(blocks_ref[...], jnp.where(picks, weight, 0.0).astype(BF16))
+        out_ref[i] = jnp.where(picks, weight, 0.0).astype(BF16)
+
+
+def combine_kernel(blocks_ref, gates_ref, out_ref):
+    n = out_ref.shape[1]
+    blocks = blocks_ref[...]
+    total = t_dot(blocks, gates_ref[0]) + t_dot(blocks, gates_ref[1]) + t_dot(blocks, gates_ref[2])
     first = total[:, :n]
     rest = total[:HLANES, n : 2 * n] + total[HLANES:, 2 * n :]
-    odd = dp % 2 == 1
+    odd = lax.axis_index("dp") % 2 == 1
     out_ref[:HLANES, :] = jnp.where(odd, rest, first[:HLANES]).astype(BF16)
     out_ref[HLANES:LANES, :] = jnp.where(odd, first[:HLANES], first[HLANES:]).astype(BF16)
     out_ref[LANES:, :] = jnp.where(odd, first[HLANES:], rest).astype(BF16)
 
 
-def call(kernel, shape, *args, scratch=(), limit=16, dtype=BF16):
-    out = jax.ShapeDtypeStruct(shape, dtype) if isinstance(shape, tuple) else [pltpu.VMEM(s, d) for s, d in shape]
+def call(kernel, shape, *args, scratch=(), limit=16, flops=0):
+    out = jax.ShapeDtypeStruct(shape, BF16) if isinstance(shape, tuple) else [pltpu.VMEM(s, d) for s, d in shape]
+    sizes = sum(v.size * v.dtype.itemsize for v in args)
     return pl.pallas_call(
         kernel,
         out_shape=out,
         scratch_shapes=scratch,
+        cost_estimate=pl.CostEstimate(flops=flops, transcendentals=0, bytes_accessed=sizes) if flops else None,
         compiler_params=pltpu.CompilerParams(vmem_limit_bytes=limit * 1024 * 1024),
     )(*args)
 
@@ -282,15 +288,18 @@
         limit=32,
     )
     hidden = held(hidden)
-    outs = [first]
+    outs, work = [first], 2 * hidden.size * 8 * LANES
     for mask in (*MASKS[1:], 0):
-        outs += call(functools.partial(down_kernel, mask), [out_shape], hidden, down, limit=32)
+        outs += call(functools.partial(down_kernel, mask), [out_shape], hidden, down, limit=32, flops=work)
     others = [lax.ppermute(out, plane, across(mask)) for mask, out in zip(MASKS, outs[:3])]
-    partial = call(add_kernel, (4, PART, LANES), *others, outs[3], limit=24)
+    partial = outs[3]
+    for other, kind in zip(others, (F32, F32, BF16)):
+        (partial,) = call(add_kernel, [((4, PART, LANES), kind)], held(partial), other, limit=24)
     partial = exchange(partial, plane, inside)
     summed = call(add_blocks_kernel, (EXPERTS * BLOCK, LANES), partial, scratch=[part_scratch, block_scratch])
     back = exchange(summed.reshape(EXPERTS, BLOCK, LANES), "expert").reshape(EXPERTS * BLOCK, LANES)
-    return call(combine_kernel, (width // DP, n), ids, gates, back).T
+    (factors,) = call(gates_kernel, [((3, EXPERTS * BLOCK, 3 * n), BF16)], ids, gates)
+    return call(combine_kernel, (width // DP, n), back, held(factors)).T
 
 
 def solution(mesh):

time: 145 us -> 151 us (1.041)
  the two profiles are of different devices: /device:TPU:32 before, /device:TPU:6 now
where the time goes in v5:
time: 151 us; the launch traced here: 149 us
  waiting for transfers between devices  65.3 us (43%)
  starting transfers between devices  54.5 us (36%)
  Pallas kernels  15.6 us (10%)
  blocking collectives  10.8 us (7%)
  local copies, waits for them, and re-layouts  3.05 us (2%)
    all_to_all x3, waiting for transfers between devices, exchange(): lax.all_to_all(value, axis, split_axis=0, concat_axis=0, tiled=True, axis...  31.7 us
    all_to_all x3, starting transfers between devices, exchange(): lax.all_to_all(value, axis, split_axis=0, concat_axis=0, tiled=True, axis...  25 us
    ppermute x3, waiting for transfers between devices, shards(): lax.ppermute(out, plane, across(mask))  24.3 us
    pallas_call x16, Pallas kernels, call(): pl.pallas_call(kernel, out_shape=out, scratch_shapes=scratch, cost_estima...  15.6 us
    ppermute x3, starting transfers between devices, shards(): lax.ppermute(out, plane, across(mask))  11.6 us
    ppermute x3, starting transfers between devices, shards(): others = [lax.ppermute(rows, plane, across(mask)) for mask in MASKS]  11.6 us
    all_to_all x1, blocking collectives, exchange(): lax.all_to_all(value, axis, split_axis=0, concat_axis=0, tiled=True, axis...  10.8 us
    ppermute x3, waiting for transfers between devices, shards(): others = [lax.ppermute(rows, plane, across(mask)) for mask in MASKS]  9.3 us
  transfers between devices with their start and end apart: 12, of which 7 were waited for; matrix products, arithmetic and copies ran while one was open for 0% of the time, Pallas kernels for 6%

profile of v5, /device:TPU:6, one launch (start us, length us, event | category | flops | bytes accessed | tf_op | source)
XLA Modules:
  0.0 149.5 jit_solution(1335372072685377591)
XLA Ops:
  0.0 1.1 copy-done.3
  1.1 0.7 copy-done.4
  1.8 1.4 shard_map.64
  3.2 15.3 %all-to-all-start = ((bf16[16,56,128]{2,1,0:T(8,128)(2,1)}), bf16[16,56,128]{2,1,0:T(8,128)(2,1)S(1)}, u32[]{:S(2)}, u32[]{:S(2)}) async-start(bf16[16,56,128]{2,1,0:T(8,128)(2,1)} %bitcast.1), calls=%async_computation | async-start | bytes 458752 | tf_op jit(solution)/shard_map/all_to_all | solution.py:260
  18.5 1.9 %collective-permute-start.1 = (bf16[168,3072]{1,0:T(8,128)(2,1)}, bf16[168,3072]{1,0:T(8,128)(2,1)}, u32[]{:S(2)}, u32[]{:S(2)}) collective-permute-start(bf16[168,3072]{1,0:T(8,128)(2,1)} %bitcast.10), channel_id=1, source_target_pairs={{0,1},{1,0},{2,3},{3,2},{4,5},{5,4},{6,7},{7,6},{8,9},{9,8},{10,11... | collective-permute-start | bytes 3096584 | tf_op jit(solution)/shard_map/ppermute | solution.py:256
  20.5 15.5 %all-to-all-done = bf16[16,56,128]{2,1,0:T(8,128)(2,1)S(1)} async-done(((bf16[16,56,128]{2,1,0:T(8,128)(2,1)}), bf16[16,56,128]{2,1,0:T(8,128)(2,1)S(1)}, u32[]{:S(2)}, u32[]{:S(2)}) %all-to-all-start) | async-done | bytes 229408 | tf_op jit(solution)/shard_map/all_to_all | solution.py:260
  35.9 1.0 shard_map.65
  37.0 4.3 %all-to-all-start.1 = ((bf16[4,816,128]{2,1,0:T(8,128)(2,1)}), bf16[4,816,128]{2,1,0:T(8,128)(2,1)S(1)}, u32[]{:S(2)}, u32[]{:S(2)}) async-start(bf16[4,816,128]{2,1,0:T(8,128)(2,1)} %shard_map.65), calls=%async_computation.1 | async-start | bytes 1671168 | tf_op jit(solution)/shard_map/all_to_all | solution.py:260
  41.3 1.9 %collective-permute-start.2 = (bf16[168,3072]{1,0:T(8,128)(2,1)S(1)}, bf16[168,3072]{1,0:T(8,128)(2,1)}, u32[]{:S(2)}, u32[]{:S(2)}) collective-permute-start(bf16[168,3072]{1,0:T(8,128)(2,1)S(1)} %bitcast.12), channel_id=1, source_target_pairs={{0,1},{1,0},{2,3},{3,2},{4,5},{5,4},{6,7},{7,6},{8,9},{9,8},{10,11... | collective-permute-start | bytes 3096584 | tf_op jit(solution)/shard_map/ppermute | solution.py:256
  43.2 2.4 %collective-permute-start.3 = (bf16[168,3072]{1,0:T(8,128)(2,1)}, bf16[168,3072]{1,0:T(8,128)(2,1)}, u32[]{:S(2)}, u32[]{:S(2)}) collective-permute-start(bf16[168,3072]{1,0:T(8,128)(2,1)} %bitcast.14), channel_id=1, source_target_pairs={{0,1},{1,0},{2,3},{3,2},{4,5},{5,4},{6,7},{7,6},{8,9},{9,8},{10,11... | collective-permute-start | bytes 3096584 | tf_op jit(solution)/shard_map/ppermute | solution.py:256
  45.6 3.4 %all-to-all-done.1.x_ref = bf16[4,816,128]{2,1,0:T(8,128)(2,1)S(1)} async-done(((bf16[4,816,128]{2,1,0:T(8,128)(2,1)}), bf16[4,816,128]{2,1,0:T(8,128)(2,1)S(1)}, u32[]{:S(2)}, u32[]{:S(2)}) %all-to-all-start.1) | async-done | bytes 835616 | tf_op jit(solution)/shard_map/all_to_all | solution.py:260
  48.9 4.8 %collective-permute-start.5 = (bf16[4,816,128]{2,1,0:T(8,128)(2,1)S(1)}, bf16[4,816,128]{2,1,0:T(8,128)(2,1)S(1)}, u32[]{:S(2)}, u32[]{:S(2)}) collective-permute-start(bf16[4,816,128]{2,1,0:T(8,128)(2,1)S(1)} %all-to-all-done.1.x_ref), channel_id=1, source_target_pairs={{0,480},{32,448},{64,416},{96,384},{128,352},{160,320},{192,288},{... | collective-permute-start | bytes 2506760 | tf_op jit(solution)/shard_map/ppermute | solution.py:279
  53.7 4.0 %collective-permute-start.4 = (bf16[4,816,128]{2,1,0:T(8,128)(2,1)S(1)}, bf16[4,816,128]{2,1,0:T(8,128)(2,1)S(1)}, u32[]{:S(2)}, u32[]{:S(2)}) collective-permute-start(bf16[4,816,128]{2,1,0:T(8,128)(2,1)S(1)} %all-to-all-done.1.x_ref), channel_id=1, source_target_pairs={{0,96},{32,64},{64,32},{96,0},{128,224},{160,192},{192,160},{224,1... | collective-permute-start | bytes 2506760 | tf_op jit(solution)/shard_map/ppermute | solution.py:279
  57.7 0.0 collective-permute-done.1.gate1
  57.7 2.9 %collective-permute-start = (bf16[4,816,128]{2,1,0:T(8,128)(2,1)S(1)}, bf16[4,816,128]{2,1,0:T(8,128)(2,1)S(1)}, u32[]{:S(2)}, u32[]{:S(2)}) collective-permute-start(bf16[4,816,128]{2,1,0:T(8,128)(2,1)S(1)} %all-to-all-done.1.x_ref), channel_id=1, source_target_pairs={{0,384},{32,416},{64,448},{96,480},{128,256},{160,288},{192,320},{... | collective-permute-start | bytes 2506760 | tf_op jit(solution)/shard_map/ppermute | solution.py:279
  60.6 0.0 collective-permute-done.2.up1
  60.6 0.0 collective-permute-done.3.down1
  60.6 0.0 copy-done
  60.6 0.0 copy-start.2
  60.6 1.2 copy-done.2
  61.9 2.3 %shard_map.66 = (bf16[768,3072]{1,0:T(8,128)(2,1)S(1)}, bf16[384,3072]{1,0:T(8,128)(2,1)S(1)}) custom-call(bf16[168,3072]{1,0:T(8,128)(2,1)S(1)} %bitcast.11, bf16[168,3072]{1,0:T(8,128)(2,1)S(1)} %bitcast.13, bf16[168,3072]{1,0:T(8,128)(2,1)S(1)} %bitcast.15, bf16[168,3072]{1,0:T(8,128)(2,1)} %collective-permute-done.1.gate1, ...), custom_call_target="tpu_custom_call" | custom-call | tf_op jit(solution)/shard_map/pallas_call | solution.py:242
  64.2 0.9 shard_map.67.sofar_ref
  65.1 1.7 %collective-permute-done.5.x_ref = bf16[4,816,128]{2,1,0:T(8,128)(2,1)S(1)} collective-permute-done((bf16[4,816,128]{2,1,0:T(8,128)(2,1)S(1)}, bf16[4,816,128]{2,1,0:T(8,128)(2,1)S(1)}, u32[]{:S(2)}, u32[]{:S(2)}) %collective-permute-start.5) | collective-permute-done | bytes 835616 | tf_op jit(solution)/shard_map/ppermute | solution.py:279
  66.8 0.9 shard_map.68.sofar_ref
  67.7 7.6 %collective-permute-done.4.x_ref = bf16[4,816,128]{2,1,0:T(8,128)(2,1)S(1)} collective-permute-done((bf16[4,816,128]{2,1,0:T(8,128)(2,1)S(1)}, bf16[4,816,128]{2,1,0:T(8,128)(2,1)S(1)}, u32[]{:S(2)}, u32[]{:S(2)}) %collective-permute-start.4) | collective-permute-done | bytes 835616 | tf_op jit(solution)/shard_map/ppermute | solution.py:279
  75.3 0.9 shard_map.69.sofar_ref
  76.2 0.0 collective-permute-done.x_ref
  76.2 2.2 %shard_map.70 = (bf16[544,384]{1,0:T(8,128)(2,1)S(1)}, bf16[4,816,128]{2,1,0:T(8,128)(2,1)S(1)}) custom-call(bf16[4,816,128]{2,1,0:T(8,128)(2,1)S(1)} %collective-permute-done.x_ref, bf16[768,3072]{1,0:T(8,128)(2,1)S(1)} %get-tuple-element.9.weights_ref, f32[544,768]{1,0:T(8,128)S(1)} %shard_map.69.sofar_ref, bf16[384,3072]{1,0:T(8,128)(2,1)S(1)} %get-tuple-element.10.down_ref), custom_call_target="tpu_custom_call" | custom-call | tf_op jit(solution)/shard_map/pallas_call | solution.py:242
  78.4 0.9 shard_map.73
  79.3 3.1 %collective-permute-start.7 = (bf16[4,816,128]{2,1,0:T(8,128)(2,1)S(1)}, bf16[4,816,128]{2,1,0:T(8,128)(2,1)S(1)}, u32[]{:S(2)}, u32[]{:S(2)}) collective-permute-start(bf16[4,816,128]{2,1,0:T(8,128)(2,1)S(1)} %shard_map.73), channel_id=1, source_target_pairs={{0,96},{32,64},{64,32},{96,0},{128,224},{160,192},{192,160},{224,1... | collective-permute-start | bytes 2506760 | tf_op jit(solution)/shard_map/ppermute | solution.py:294
  82.4 5.1 %collective-permute-start.6 = (bf16[4,816,128]{2,1,0:T(8,128)(2,1)S(1)}, bf16[4,816,128]{2,1,0:T(8,128)(2,1)S(1)}, u32[]{:S(2)}, u32[]{:S(2)}) collective-permute-start(bf16[4,816,128]{2,1,0:T(8,128)(2,1)S(1)} %get-tuple-element.12), channel_id=1, source_target_pairs={{0,480},{32,448},{64,416},{96,384},{128,352},{160,320},{192,288},{... | collective-permute-start | bytes 2506760 | tf_op jit(solution)/shard_map/ppermute | solution.py:294
  87.5 0.9 shard_map.75
  88.3 3.5 %collective-permute-start.8 = (bf16[4,816,128]{2,1,0:T(8,128)(2,1)S(1)}, bf16[4,816,128]{2,1,0:T(8,128)(2,1)S(1)}, u32[]{:S(2)}, u32[]{:S(2)}) collective-permute-start(bf16[4,816,128]{2,1,0:T(8,128)(2,1)S(1)} %shard_map.75), channel_id=1, source_target_pairs={{0,384},{32,416},{64,448},{96,480},{128,256},{160,288},{192,320},{... | collective-permute-start | bytes 2506760 | tf_op jit(solution)/shard_map/ppermute | solution.py:294
  91.8 0.9 shard_map.71.a
  92.7 12.4 %collective-permute-done.6.b = bf16[4,816,128]{2,1,0:T(8,128)(2,1)S(1)} collective-permute-done((bf16[4,816,128]{2,1,0:T(8,128)(2,1)S(1)}, bf16[4,816,128]{2,1,0:T(8,128)(2,1)S(1)}, u32[]{:S(2)}, u32[]{:S(2)}) %collective-permute-start.6) | collective-permute-done | bytes 835616 | tf_op jit(solution)/shard_map/ppermute | solution.py:294
  105.1 0.2 shard_map.72.a
  105.2 0.0 collective-permute-done.7.b
  105.2 0.2 shard_map.74.a
  105.5 11.9 %collective-permute-done.8.b = bf16[4,816,128]{2,1,0:T(8,128)(2,1)S(1)} collective-permute-done((bf16[4,816,128]{2,1,0:T(8,128)(2,1)S(1)}, bf16[4,816,128]{2,1,0:T(8,128)(2,1)S(1)}, u32[]{:S(2)}, u32[]{:S(2)}) %collective-permute-start.8) | collective-permute-done | bytes 835616 | tf_op jit(solution)/shard_map/ppermute | solution.py:294
  117.4 0.1 shard_map.76
  117.5 0.0 copy-start.5
  117.5 0.0 copy-start.6
  117.6 10.8 %all_to_all.20.parts_ref = bf16[4,816,128]{2,1,0:T(8,128)(2,1)S(1)} all-to-all(bf16[4,816,128]{2,1,0:T(8,128)(2,1)S(1)} %shard_map.76), channel_id=1, replica_groups={{0,32,128,160},{64,96,192,224},{256,288,384,416},{320,352,448,480},{481..., dimensions={0} | all-to-all | bytes 1671168 | tf_op jit(solution)/shard_map/all_to_all | solution.py:260
  128.3 0.9 shard_map.77
  129.2 5.4 %all-to-all-start.3 = ((bf16[16,56,128]{2,1,0:T(8,128)(2,1)}), bf16[16,56,128]{2,1,0:T(8,128)(2,1)S(1)}, u32[]{:S(2)}, u32[]{:S(2)}) async-start(bf16[16,56,128]{2,1,0:T(8,128)(2,1)} %bitcast.6), calls=%async_computation.3 | async-start | bytes 458752 | tf_op jit(solution)/shard_map/all_to_all | solution.py:260
  134.6 0.8 shard_map.78.gates_ref
  135.4 12.9 %all-to-all-done.3 = bf16[16,56,128]{2,1,0:T(8,128)(2,1)S(1)} async-done(((bf16[16,56,128]{2,1,0:T(8,128)(2,1)}), bf16[16,56,128]{2,1,0:T(8,128)(2,1)S(1)}, u32[]{:S(2)}, u32[]{:S(2)}) %all-to-all-start.3) | async-done | bytes 229408 | tf_op jit(solution)/shard_map/all_to_all | solution.py:260
  148.3 1.2 shard_map.79
  (7 shorter events, 0.0 us)
Async XLA Ops:
  0.0 1.1 copy-start.3
  1.1 0.7 copy-start.4
  3.2 38.1 %copy-start.1 = (bf16[1,168,3072]{2,1,0:T(8,128)(2,1)S(1)}, bf16[1,168,3072]{2,1,0:T(8,128)(2,1)}, u32[]{:S(2)}) copy-start(bf16[1,168,3072]{2,1,0:T(8,128)(2,1)} %param.10) | copy-start | bytes 3096580
  3.2 57.4 %copy-start = (bf16[1,168,3072]{2,1,0:T(8,128)(2,1)S(1)}, bf16[1,168,3072]{2,1,0:T(8,128)(2,1)}, u32[]{:S(2)}) copy-start(bf16[1,168,3072]{2,1,0:T(8,128)(2,1)} %param.9) | copy-start | bytes 3096580
  3.2 32.7 %all-to-all-start = ((bf16[16,56,128]{2,1,0:T(8,128)(2,1)}), bf16[16,56,128]{2,1,0:T(8,128)(2,1)S(1)}, u32[]{:S(2)}, u32[]{:S(2)}) async-start(bf16[16,56,128]{2,1,0:T(8,128)(2,1)} %bitcast.1), calls=%async_computation | async-start | bytes 458752 | tf_op jit(solution)/shard_map/all_to_all | solution.py:260
  18.5 39.2 %collective-permute-start.1 = (bf16[168,3072]{1,0:T(8,128)(2,1)}, bf16[168,3072]{1,0:T(8,128)(2,1)}, u32[]{:S(2)}, u32[]{:S(2)}) collective-permute-start(bf16[168,3072]{1,0:T(8,128)(2,1)} %bitcast.10), channel_id=1, source_target_pairs={{0,1},{1,0},{2,3},{3,2},{4,5},{5,4},{6,7},{7,6},{8,9},{9,8},{10,11... | collective-permute-start | bytes 3096584 | tf_op jit(solution)/shard_map/ppermute | solution.py:256
  37.0 12.0 %all-to-all-start.1 = ((bf16[4,816,128]{2,1,0:T(8,128)(2,1)}), bf16[4,816,128]{2,1,0:T(8,128)(2,1)S(1)}, u32[]{:S(2)}, u32[]{:S(2)}) async-start(bf16[4,816,128]{2,1,0:T(8,128)(2,1)} %shard_map.65), calls=%async_computation.1 | async-start | bytes 1671168 | tf_op jit(solution)/shard_map/all_to_all | solution.py:260
  41.3 19.3 %collective-permute-start.2 = (bf16[168,3072]{1,0:T(8,128)(2,1)S(1)}, bf16[168,3072]{1,0:T(8,128)(2,1)}, u32[]{:S(2)}, u32[]{:S(2)}) collective-permute-start(bf16[168,3072]{1,0:T(8,128)(2,1)S(1)} %bitcast.12), channel_id=1, source_target_pairs={{0,1},{1,0},{2,3},{3,2},{4,5},{5,4},{6,7},{7,6},{8,9},{9,8},{10,11... | collective-permute-start | bytes 3096584 | tf_op jit(solution)/shard_map/ppermute | solution.py:256
  43.2 17.4 %collective-permute-start.3 = (bf16[168,3072]{1,0:T(8,128)(2,1)}, bf16[168,3072]{1,0:T(8,128)(2,1)}, u32[]{:S(2)}, u32[]{:S(2)}) collective-permute-start(bf16[168,3072]{1,0:T(8,128)(2,1)} %bitcast.14), channel_id=1, source_target_pairs={{0,1},{1,0},{2,3},{3,2},{4,5},{5,4},{6,7},{7,6},{8,9},{9,8},{10,11... | collective-permute-start | bytes 3096584 | tf_op jit(solution)/shard_map/ppermute | solution.py:256
  48.9 17.8 %collective-permute-start.5 = (bf16[4,816,128]{2,1,0:T(8,128)(2,1)S(1)}, bf16[4,816,128]{2,1,0:T(8,128)(2,1)S(1)}, u32[]{:S(2)}, u32[]{:S(2)}) collective-permute-start(bf16[4,816,128]{2,1,0:T(8,128)(2,1)S(1)} %all-to-all-done.1.x_ref), channel_id=1, source_target_pairs={{0,480},{32,448},{64,416},{96,384},{128,352},{160,320},{192,288},{... | collective-permute-start | bytes 2506760 | tf_op jit(solution)/shard_map/ppermute | solution.py:279
  53.7 21.5 %collective-permute-start.4 = (bf16[4,816,128]{2,1,0:T(8,128)(2,1)S(1)}, bf16[4,816,128]{2,1,0:T(8,128)(2,1)S(1)}, u32[]{:S(2)}, u32[]{:S(2)}) collective-permute-start(bf16[4,816,128]{2,1,0:T(8,128)(2,1)S(1)} %all-to-all-done.1.x_ref), channel_id=1, source_target_pairs={{0,96},{32,64},{64,32},{96,0},{128,224},{160,192},{192,160},{224,1... | collective-permute-start | bytes 2506760 | tf_op jit(solution)/shard_map/ppermute | solution.py:279
  57.7 18.5 %collective-permute-start = (bf16[4,816,128]{2,1,0:T(8,128)(2,1)S(1)}, bf16[4,816,128]{2,1,0:T(8,128)(2,1)S(1)}, u32[]{:S(2)}, u32[]{:S(2)}) collective-permute-start(bf16[4,816,128]{2,1,0:T(8,128)(2,1)S(1)} %all-to-all-done.1.x_ref), channel_id=1, source_target_pairs={{0,384},{32,416},{64,448},{96,480},{128,256},{160,288},{192,320},{... | collective-permute-start | bytes 2506760 | tf_op jit(solution)/shard_map/ppermute | solution.py:279
  60.6 1.2 copy-start.2
  79.3 26.0 %collective-permute-start.7 = (bf16[4,816,128]{2,1,0:T(8,128)(2,1)S(1)}, bf16[4,816,128]{2,1,0:T(8,128)(2,1)S(1)}, u32[]{:S(2)}, u32[]{:S(2)}) collective-permute-start(bf16[4,816,128]{2,1,0:T(8,128)(2,1)S(1)} %shard_map.73), channel_id=1, source_target_pairs={{0,96},{32,64},{64,32},{96,0},{128,224},{160,192},{192,160},{224,1... | collective-permute-start | bytes 2506760 | tf_op jit(solution)/shard_map/ppermute | solution.py:294
  82.4 22.7 %collective-permute-start.6 = (bf16[4,816,128]{2,1,0:T(8,128)(2,1)S(1)}, bf16[4,816,128]{2,1,0:T(8,128)(2,1)S(1)}, u32[]{:S(2)}, u32[]{:S(2)}) collective-permute-start(bf16[4,816,128]{2,1,0:T(8,128)(2,1)S(1)} %get-tuple-element.12), channel_id=1, source_target_pairs={{0,480},{32,448},{64,416},{96,384},{128,352},{160,320},{192,288},{... | collective-permute-start | bytes 2506760 | tf_op jit(solution)/shard_map/ppermute | solution.py:294
  88.3 29.1 %collective-permute-start.8 = (bf16[4,816,128]{2,1,0:T(8,128)(2,1)S(1)}, bf16[4,816,128]{2,1,0:T(8,128)(2,1)S(1)}, u32[]{:S(2)}, u32[]{:S(2)}) collective-permute-start(bf16[4,816,128]{2,1,0:T(8,128)(2,1)S(1)} %shard_map.75), channel_id=1, source_target_pairs={{0,384},{32,416},{64,448},{96,480},{128,256},{160,288},{192,320},{... | collective-permute-start | bytes 2506760 | tf_op jit(solution)/shard_map/ppermute | solution.py:294
  117.5 17.1 %copy-start.5 = (s32[256,4]{0,1:T(4,128)S(1)}, s32[256,4]{0,1:T(4,128)}, u32[]{:S(2)}) copy-start(s32[256,4]{0,1:T(4,128)} %param.7) | copy-start | bytes 12292
  117.5 17.1 %copy-start.6 = (f32[256,4]{0,1:T(4,128)S(1)}, f32[256,4]{0,1:T(4,128)}, u32[]{:S(2)}) copy-start(f32[256,4]{0,1:T(4,128)} %param.8) | copy-start | bytes 12292
  129.2 19.0 %all-to-all-start.3 = ((bf16[16,56,128]{2,1,0:T(8,128)(2,1)}), bf16[16,56,128]{2,1,0:T(8,128)(2,1)S(1)}, u32[]{:S(2)}, u32[]{:S(2)}) async-start(bf16[16,56,128]{2,1,0:T(8,128)(2,1)} %bitcast.6), calls=%async_computation.3 | async-start | bytes 458752 | tf_op jit(solution)/shard_map/all_to_all | solution.py:260

commit v6 on v4

--- a/solution.py
+++ b/solution.py
@@ -21,6 +21,7 @@
 PART = 3 * SIDE
 AWAY = ((8, 4, -4, 0), (7, -7, 1, -1), (6, -6, 2, -2), (5, -5, 3, -3))
 WIDE = 384
+CHUNKS = (72, 64)
 MASKS = (3, 1, 2)
 F32 = jnp.float32
 BF16 = jnp.bfloat16
@@ -119,12 +120,15 @@
 
 
 def pack_kernel(*refs):
-    blocks, out_ref, packed = refs[:4], refs[4], refs[5]
+    blocks, out_refs, packed = refs[:4], refs[4:-1], refs[-1]
     for k, ref in enumerate(blocks):
         packed[k * CAP : (k + 1) * CAP, :] = ref[...].astype(F32)[:CAP]
-    value = packed[...].astype(BF16)
-    for copy in range(out_ref.shape[0]):
-        out_ref[copy] = value
+    at = 0
+    for out_ref in out_refs:
+        value = packed[at : at + out_ref.shape[1], :].astype(BF16)
+        at += out_ref.shape[1]
+        for copy in range(out_ref.shape[0]):
+            out_ref[copy] = value
 
 
 def weights_kernel(gate0, up0, down0, gate1, up1, down1, weights_ref, down_ref):
@@ -146,17 +150,19 @@
 def down_products(mask, hidden, down_ref, out_ref):
     core, q, _ = place_of()
     to = q ^ mask
-    low = iota((SIDE, LANES), 1) < HLANES
+    rows = hidden.shape[0]
+    side = rows // 2
+    low = iota((side, LANES), 1) < HLANES
     for at in range(4):
         dp = (to // 2 * 2 + at // 2 - core) % SIZE * SIZE + (to % 2 * 2 + at % 2 - core) % SIZE
         odd = dp % 2 == 1
         y = dot(hidden, down_ref[:, pl.ds(pl.multiple_of((dp * 3 - dp % 2) // 2 * LANES, LANES), 2 * LANES)])
         first, second = y[:, :LANES], y[:, LANES:]
-        out_ref[at, : 2 * SIDE, :] = jnp.where(odd, second, first).astype(BF16)
+        out_ref[at, :rows, :] = jnp.where(odd, second, first).astype(BF16)
         half = jnp.where(odd, first, second)
         turned = pltpu.roll(half, HLANES, 1)
         left, right = jnp.where(odd, turned, half), jnp.where(odd, half, turned)
-        out_ref[at, 2 * SIDE :, :] = jnp.where(low, left[:SIDE], right[SIDE:]).astype(BF16)
+        out_ref[at, rows:, :] = jnp.where(low, left[:side], right[side:]).astype(BF16)
 
 
 def first_kernel(mask, x_ref, weights_ref, total_ref):
@@ -167,49 +173,45 @@
     total_ref[...] = sofar_ref[...] + products(mask, x_ref, weights_ref)
 
 
-def last_kernel(mask, out_mask, x_ref, weights_ref, sofar_ref, down_ref, hidden_ref, out_ref):
+def last_kernel(mask, x_ref, weights_ref, sofar_ref, down_ref, *out_refs):
     total = sofar_ref[...] + products(mask, x_ref, weights_ref)
     g, u = total[:, :WIDE], total[:, WIDE:]
     hidden = (g / (1.0 + jnp.exp(-g)) * u).astype(BF16)
-    hidden_ref[...] = hidden
-    down_products(out_mask, hidden, down_ref, out_ref)
-
-
-def down_kernel(mask, hidden_ref, down_ref, out_ref):
-    down_products(mask, hidden_ref[...], down_ref, out_ref)
-
-
-def add_kernel(a, b, c, d, out_ref):
-    out_ref[...] = (a[...].astype(F32) + b[...].astype(F32) + c[...].astype(F32) + d[...].astype(F32)).astype(BF16)
-
-
-def add_blocks_kernel(parts_ref, out_ref, packed, blocks):
-    total = parts_ref[0].astype(F32)
-    for i in range(1, parts_ref.shape[0]):
-        total += parts_ref[i].astype(F32)
-    packed[...] = total
+    for to, out_ref in zip((*MASKS, 0), out_refs):
+        down_products(to, hidden, down_ref, out_ref)
+
+
+def add_kernel(a, b, out_ref):
+    out_ref[...] = (a[...].astype(F32) + b[...].astype(F32)).astype(out_ref.dtype)
+
+
+def add_blocks_kernel(*refs):
+    chunks, out_ref, mains, halves, blocks = refs[: len(CHUNKS)], *refs[len(CHUNKS) :]
+    start = 0
+    for parts_ref, count in zip(chunks, CHUNKS):
+        total = parts_ref[0].astype(F32)
+        for i in range(1, parts_ref.shape[0]):
+            total += parts_ref[i].astype(F32)
+        for j in range(4):
+            to = slice(j * 4 * CAP + start, j * 4 * CAP + start + count)
+            mains[to, :] = total[j * count : (j + 1) * count]
+            half = total[(4 + j % 2) * count : (5 + j % 2) * count]
+            halves[to, :] = half if j < 2 else pltpu.roll(half, HLANES, 1)
+        start += count
     low = iota((HALF, LANES), 1) < HLANES
-
-    def put(b, at, value):
+    for b in range(EXPERTS):
         home = lax.rem(lax.axis_index("expert") - AWAY[b // 4][b % 4] + EXPERTS, EXPERTS)
-        blocks[home, at : at + value.shape[0], :] = value
-
-    for b in range(EXPERTS):
-        put(b, 0, packed[b * CAP : (b + 1) * CAP, :])
-        put(b, CAP + HALF, jnp.zeros((BLOCK - CAP - HALF, LANES), F32))
-    for b in range(EXPERTS // 2):
-        at = 2 * SIDE + b * CAP
-        upper, lower = packed[at : at + HALF, :], packed[at + HALF : at + CAP, :]
-        put(b, CAP, jnp.where(low, upper, pltpu.roll(lower, HLANES, 1)))
-        put(b + EXPERTS // 2, CAP, jnp.where(low, pltpu.roll(upper, HLANES, 1), lower))
+        blocks[home, :CAP, :] = mains[b * CAP : (b + 1) * CAP, :]
+        upper, lower = halves[b * CAP : b * CAP + HALF, :], halves[b * CAP + HALF : (b + 1) * CAP, :]
+        blocks[home, CAP : CAP + HALF, :] = jnp.where(low, upper, pltpu.roll(lower, HLANES, 1))
+        blocks[home, CAP + HALF :, :] = jnp.zeros((BLOCK - CAP - HALF, LANES), F32)
     for e in range(EXPERTS):
         out_ref[e] = blocks[e].astype(BF16)
 
 
-def combine_kernel(ids_ref, gates_ref, blocks_ref, out_ref):
-    n = out_ref.shape[1]
-    core, dp = lax.axis_index("tensor"), lax.axis_index("dp")
-    own = pl.ds(pl.multiple_of(core * n, n), n)
+def gates_kernel(ids_ref, gates_ref, out_ref):
+    n = out_ref.shape[2] // 3
+    own = pl.ds(pl.multiple_of(lax.axis_index("tensor") * n, n), n)
     ids, given = ids_ref[:, own], gates_ref[:, own]
     rows = EXPERTS * BLOCK
 
@@ -226,23 +228,28 @@
     gates = jnp.zeros((EXPERTS, n), F32)
     for k in range(TOP):
         gates += jnp.where(ids[k : k + 1, :] == iota((EXPERTS, n), 0), given[k : k + 1, :], 0.0)
-    total = jnp.zeros((LANES, 3 * n), F32)
-    for _ in range(3):
+    for i in range(3):
         piece = gates.astype(BF16)
         gates = gates - piece.astype(F32)
         weight = dot(spread, piece)
         weight = jnp.concatenate([weight, weight, weight], axis=1)
-        total += t_dot(blocks_ref[...], jnp.where(picks, weight, 0.0).astype(BF16))
+        out_ref[i] = jnp.where(picks, weight, 0.0).astype(BF16)
+
+
+def combine_kernel(blocks_ref, gates_ref, out_ref):
+    n = out_ref.shape[1]
+    blocks = blocks_ref[...]
+    total = t_dot(blocks, gates_ref[0]) + t_dot(blocks, gates_ref[1]) + t_dot(blocks, gates_ref[2])
     first = total[:, :n]
     rest = total[:HLANES, n : 2 * n] + total[HLANES:, 2 * n :]
-    odd = dp % 2 == 1
+    odd = lax.axis_index("dp") % 2 == 1
     out_ref[:HLANES, :] = jnp.where(odd, rest, first[:HLANES]).astype(BF16)
     out_ref[HLANES:LANES, :] = jnp.where(odd, first[:HLANES], first[HLANES:]).astype(BF16)
     out_ref[LANES:, :] = jnp.where(odd, first[HLANES:], rest).astype(BF16)
 
 
-def call(kernel, shape, *args, scratch=(), limit=16, dtype=BF16):
-    out = jax.ShapeDtypeStruct(shape, dtype) if isinstance(shape, tuple) else [pltpu.VMEM(s, d) for s, d in shape]
+def call(kernel, shape, *args, scratch=(), limit=16):
+    out = jax.ShapeDtypeStruct(shape, BF16) if isinstance(shape, tuple) else [pltpu.VMEM(s, d) for s, d in shape]
     return pl.pallas_call(
         kernel,
         out_shape=out,
@@ -275,34 +282,40 @@
     part = width // 4
     sent = call(dispatch_kernel, [((RISE, part), BF16)] * 4, ids, tokens)
     arrived = [lax.ppermute(v, ("dp", "expert", "tensor"), rising(k)) for k, v in enumerate(sent)]
-    rows = call(pack_kernel, (4, 4 * CAP, part), *arrived, scratch=[pltpu.VMEM((4 * CAP, part), F32)])
-    rows = exchange(rows, plane, inside).reshape(2 * SIDE, part)
-    others = [lax.ppermute(rows, plane, across(mask)) for mask in MASKS]
-    total_shape, out_shape = ((2 * SIDE, 2 * WIDE), F32), ((4, PART, LANES), BF16)
-    (total,) = call(functools.partial(first_kernel, 0), [total_shape], rows, weights, limit=32)
-    for mask, other in zip(MASKS[:2], others[:2]):
-        (total,) = call(functools.partial(next_kernel, mask), [total_shape], other, weights, held(total), limit=32)
-    hidden, first = call(
-        functools.partial(last_kernel, MASKS[2], MASKS[0]),
-        [((2 * SIDE, WIDE), BF16), out_shape],
-        *(others[2], weights, held(total), down),
-        limit=32,
-    )
-    hidden = held(hidden)
-    outs = [first]
-    for mask in (*MASKS[1:], 0):
-        outs += call(functools.partial(down_kernel, mask), [out_shape], hidden, down, limit=32)
-    others = [lax.ppermute(out, plane, across(mask)) for mask, out in zip(MASKS, outs[:3])]
-    partial = call(add_kernel, (4, PART, LANES), *others, outs[3], limit=24)
-    partial = exchange(partial, plane, inside)
+    rows = call(
+        pack_kernel,
+        [((4, count, part), BF16) for count in CHUNKS],
+        *arrived,
+        scratch=[pltpu.VMEM((4 * CAP, part), F32)],
+    )
+    rows = [exchange(chunk, plane, inside).reshape(-1, part) for chunk in rows]
+    moved = [[lax.ppermute(chunk, plane, across(mask)) for mask in MASKS] for chunk in rows]
+    sums = []
+    for chunk, others, count in zip(rows, moved, CHUNKS):
+        total_shape = [((4 * count, 2 * WIDE), F32)]
+        out_shape = (4, 6 * count, LANES)
+        (total,) = call(functools.partial(first_kernel, 0), total_shape, chunk, weights, limit=24)
+        for mask, other in zip(MASKS[:2], others[:2]):
+            (total,) = call(functools.partial(next_kernel, mask), total_shape, other, weights, held(total), limit=24)
+        *outs, partial = call(
+            functools.partial(last_kernel, MASKS[2]),
+            [(out_shape, BF16)] * 4,
+            *(others[2], weights, held(total), down),
+            limit=24,
+        )
+        outs = [lax.ppermute(out, plane, across(mask)) for mask, out in zip(MASKS, outs)]
+        for other, kind in zip(outs, (F32, F32, BF16)):
+            (partial,) = call(add_kernel, [(out_shape, kind)], held(partial), other)
+        sums.append(exchange(partial, plane, inside))
     summed = call(
         add_blocks_kernel,
         (EXPERTS, BLOCK, LANES),
-        partial,
-        scratch=[pltpu.VMEM((PART, LANES), F32), pltpu.VMEM((EXPERTS, BLOCK, LANES), F32)],
+        *sums,
+        scratch=[pltpu.VMEM((2 * SIDE, LANES), F32)] * 2 + [pltpu.VMEM((EXPERTS, BLOCK, LANES), F32)],
     )
     back = exchange(summed, "expert").reshape(EXPERTS * BLOCK, LANES)
-    return call(combine_kernel, (width // DP, n), ids, gates, back).T
+    (factors,) = call(gates_kernel, [((3, EXPERTS * BLOCK, 3 * n), BF16)], ids, gates)
+    return call(combine_kernel, (width // DP, n), back, held(factors)).T
 
 
 def solution(mesh):

time: 148 us -> 160 us (1.081)
  the two profiles are of different devices: /device:TPU:32 before, /device:TPU:6 now
where the time goes in v6:
time: 160 us; the launch traced here: 158 us
  starting transfers between devices  96.2 us (60%)
  waiting for transfers between devices  21.1 us (13%)
  blocking collectives  18.5 us (12%)
  Pallas kernels  17.1 us (11%)
  local copies, waits for them, and re-layouts  4.24 us (3%)
    ppermute x4, starting transfers between devices, shards(): lax.ppermute(v, ('dp', 'expert', 'tensor'), rising(k))  25.8 us
    ppermute x6, starting transfers between devices, shards(): lax.ppermute(chunk, plane, across(mask))  24.2 us
    ppermute x6, starting transfers between devices, shards(): lax.ppermute(out, plane, across(mask))  23.3 us
    all_to_all x2, blocking collectives, exchange(): lax.all_to_all(value, axis, split_axis=0, concat_axis=0, tiled=True, axis...  18.5 us
    pallas_call x20, Pallas kernels, call(): pl.pallas_call(kernel, out_shape=out, scratch_shapes=scratch, compiler_pa...  17.1 us
    all_to_all x3, starting transfers between devices, exchange(): lax.all_to_all(value, axis, split_axis=0, concat_axis=0, tiled=True, axis...  16.6 us
    all_to_all x3, waiting for transfers between devices, exchange(): lax.all_to_all(value, axis, split_axis=0, concat_axis=0, tiled=True, axis...  15.9 us
    ppermute x3, starting transfers between devices, swap(): return lax.ppermute(value, 'tensor', [(0, 1), (1, 0)])  6.37 us
  transfers between devices with their start and end apart: 22, of which 5 were waited for; matrix products, arithmetic and copies ran while one was open for 0% of the time, Pallas kernels for 9%

profile of v6, /device:TPU:6, one launch (start us, length us, event | category | flops | bytes accessed | tf_op | source)
XLA Modules:
  0.0 157.6 jit_solution(12277005605554113403)
XLA Ops:
  0.0 2.0 %collective-permute-start.5 = (bf16[168,3072]{1,0:T(8,128)(2,1)}, bf16[168,3072]{1,0:T(8,128)(2,1)}, u32[]{:S(2)}, u32[]{:S(2)}) collective-permute-start(bf16[168,3072]{1,0:T(8,128)(2,1)} %bitcast.17), channel_id=1, source_target_pairs={{0,1},{1,0},{2,3},{3,2},{4,5},{5,4},{6,7},{7,6},{8,9},{9,8},{10,11... | collective-permute-start | bytes 3096584 | tf_op jit(solution)/shard_map/ppermute | solution.py:266
  2.1 1.1 copy-done.3
  3.2 0.7 copy-done.6
  3.9 0.8 shard_map.64
  4.7 13.2 %collective-permute-start = (bf16[40,768]{1,0:T(8,128)(2,1)S(1)}, bf16[40,768]{1,0:T(8,128)(2,1)S(1)}, u32[]{:S(2)}, u32[]{:S(2)}) collective-permute-start(bf16[40,768]{1,0:T(8,128)(2,1)S(1)} %get-tuple-element.21), channel_id=1, source_target_pairs={{0,16},{1,11},{2,18},{3,13},{4,20},{5,15},{6,22},{7,17},{8,24},{9,... | collective-permute-start | bytes 184328 | tf_op jit(solution)/shard_map/ppermute | solution.py:284
  17.9 4.0 %collective-permute-start.1 = (bf16[40,768]{1,0:T(8,128)(2,1)S(1)}, bf16[40,768]{1,0:T(8,128)(2,1)S(1)}, u32[]{:S(2)}, u32[]{:S(2)}) collective-permute-start(bf16[40,768]{1,0:T(8,128)(2,1)S(1)} %get-tuple-element.22), channel_id=1, source_target_pairs={{0,8},{1,23},{2,10},{3,25},{4,12},{5,27},{6,14},{7,29},{8,16},{9,3... | collective-permute-start | bytes 184328 | tf_op jit(solution)/shard_map/ppermute | solution.py:284
  21.9 2.9 %collective-permute-start.2 = (bf16[40,768]{1,0:T(8,128)(2,1)S(1)}, bf16[40,768]{1,0:T(8,128)(2,1)S(1)}, u32[]{:S(2)}, u32[]{:S(2)}) collective-permute-start(bf16[40,768]{1,0:T(8,128)(2,1)S(1)} %get-tuple-element.23), channel_id=1, source_target_pairs={{0,24},{1,7},{2,26},{3,9},{4,28},{5,11},{6,30},{7,13},{8,0},{9,15}... | collective-permute-start | bytes 184328 | tf_op jit(solution)/shard_map/ppermute | solution.py:284
  24.8 5.6 %collective-permute-start.3 = (bf16[40,768]{1,0:T(8,128)(2,1)S(1)}, bf16[40,768]{1,0:T(8,128)(2,1)S(1)}, u32[]{:S(2)}, u32[]{:S(2)}) collective-permute-start(bf16[40,768]{1,0:T(8,128)(2,1)S(1)} %get-tuple-element.24), channel_id=1, source_target_pairs={{0,0},{1,27},{2,2},{3,29},{4,4},{5,31},{6,6},{7,1},{8,8},{9,3},{10... | collective-permute-start | bytes 184328 | tf_op jit(solution)/shard_map/ppermute | solution.py:284
  30.5 1.9 %collective-permute-start.6 = (bf16[168,3072]{1,0:T(8,128)(2,1)}, bf16[168,3072]{1,0:T(8,128)(2,1)}, u32[]{:S(2)}, u32[]{:S(2)}) collective-permute-start(bf16[168,3072]{1,0:T(8,128)(2,1)} %bitcast.19), channel_id=1, source_target_pairs={{0,1},{1,0},{2,3},{3,2},{4,5},{5,4},{6,7},{7,6},{8,9},{9,8},{10,11... | collective-permute-start | bytes 3096584 | tf_op jit(solution)/shard_map/ppermute | solution.py:266
  32.4 2.4 %collective-permute-start.7 = (bf16[168,3072]{1,0:T(8,128)(2,1)}, bf16[168,3072]{1,0:T(8,128)(2,1)}, u32[]{:S(2)}, u32[]{:S(2)}) collective-permute-start(bf16[168,3072]{1,0:T(8,128)(2,1)} %bitcast.21), channel_id=1, source_target_pairs={{0,1},{1,0},{2,3},{3,2},{4,5},{5,4},{6,7},{7,6},{8,9},{9,8},{10,11... | collective-permute-start | bytes 3096584 | tf_op jit(solution)/shard_map/ppermute | solution.py:266
  34.9 0.8 shard_map.65
  35.7 9.7 %all_to_all.25 = bf16[4,64,768]{2,1,0:T(8,128)(2,1)S(1)} all-to-all(bf16[4,64,768]{2,1,0:T(8,128)(2,1)S(1)} %get-tuple-element.32), channel_id=1, replica_groups={{0,32,128,160},{64,96,192,224},{256,288,384,416},{320,352,448,480},{481..., dimensions={0} | all-to-all | bytes 786432 | tf_op jit(solution)/shard_map/all_to_all | solution.py:270
  45.5 4.7 %collective-permute-start.15 = (bf16[256,768]{1,0:T(8,128)(2,1)S(1)}, bf16[256,768]{1,0:T(8,128)(2,1)S(1)}, u32[]{:S(2)}, u32[]{:S(2)}) collective-permute-start(bf16[256,768]{1,0:T(8,128)(2,1)S(1)} %bitcast.13), channel_id=1, source_target_pairs={{0,480},{32,448},{64,416},{96,384},{128,352},{160,320},{192,288},{... | collective-permute-start | bytes 1179656 | tf_op jit(solution)/shard_map/ppermute | solution.py:292
  50.2 3.5 %all-to-all-start = ((bf16[4,72,768]{2,1,0:T(8,128)(2,1)}), bf16[4,72,768]{2,1,0:T(8,128)(2,1)S(1)}, u32[]{:S(2)}, u32[]{:S(2)}) async-start(bf16[4,72,768]{2,1,0:T(8,128)(2,1)} %get-tuple-element.25), calls=%async_computation | async-start | bytes 884736 | tf_op jit(solution)/shard_map/all_to_all | solution.py:270
  53.7 3.8 %collective-permute-start.14 = (bf16[256,768]{1,0:T(8,128)(2,1)S(1)}, bf16[256,768]{1,0:T(8,128)(2,1)}, u32[]{:S(2)}, u32[]{:S(2)}) collective-permute-start(bf16[256,768]{1,0:T(8,128)(2,1)S(1)} %bitcast.14), channel_id=1, source_target_pairs={{0,96},{32,64},{64,32},{96,0},{128,224},{160,192},{192,160},{224,1... | collective-permute-start | bytes 1179656 | tf_op jit(solution)/shard_map/ppermute | solution.py:292
  57.5 1.0 collective-permute-done.15.x_ref
  58.5 0.8 copy-done.4
  59.3 4.0 %collective-permute-start.13 = (bf16[256,768]{1,0:T(8,128)(2,1)S(1)}, bf16[256,768]{1,0:T(8,128)(2,1)S(1)}, u32[]{:S(2)}, u32[]{:S(2)}) collective-permute-start(bf16[256,768]{1,0:T(8,128)(2,1)S(1)} %bitcast.15), channel_id=1, source_target_pairs={{0,384},{32,416},{64,448},{96,480},{128,256},{160,288},{192,320},{... | collective-permute-start | bytes 1179656 | tf_op jit(solution)/shard_map/ppermute | solution.py:292
  63.3 3.3 %collective-permute-start.9 = (bf16[288,768]{1,0:T(8,128)(2,1)S(1)}, bf16[288,768]{1,0:T(8,128)(2,1)S(1)}, u32[]{:S(2)}, u32[]{:S(2)}) collective-permute-start(bf16[288,768]{1,0:T(8,128)(2,1)S(1)} %bitcast.9), channel_id=1, source_target_pairs={{0,480},{32,448},{64,416},{96,384},{128,352},{160,320},{192,288},{... | collective-permute-start | bytes 1327112 | tf_op jit(solution)/shard_map/ppermute | solution.py:292
  66.6 4.4 %collective-permute-start.8 = (bf16[288,768]{1,0:T(8,128)(2,1)S(1)}, bf16[288,768]{1,0:T(8,128)(2,1)S(1)}, u32[]{:S(2)}, u32[]{:S(2)}) collective-permute-start(bf16[288,768]{1,0:T(8,128)(2,1)S(1)} %bitcast.10), channel_id=1, source_target_pairs={{0,96},{32,64},{64,32},{96,0},{128,224},{160,192},{192,160},{224,1... | collective-permute-start | bytes 1327112 | tf_op jit(solution)/shard_map/ppermute | solution.py:292
  71.0 4.0 %collective-permute-start.4 = (bf16[288,768]{1,0:T(8,128)(2,1)S(1)}, bf16[288,768]{1,0:T(8,128)(2,1)S(1)}, u32[]{:S(2)}, u32[]{:S(2)}) collective-permute-start(bf16[288,768]{1,0:T(8,128)(2,1)S(1)} %bitcast.11), channel_id=1, source_target_pairs={{0,384},{32,416},{64,448},{96,480},{128,256},{160,288},{192,320},{... | collective-permute-start | bytes 1327112 | tf_op jit(solution)/shard_map/ppermute | solution.py:292
  75.0 1.2 copy-done.2
  76.2 2.3 %shard_map.66 = (bf16[768,3072]{1,0:T(8,128)(2,1)S(1)}, bf16[384,3072]{1,0:T(8,128)(2,1)S(1)}) custom-call(bf16[168,3072]{1,0:T(8,128)(2,1)S(1)} %bitcast.18, bf16[168,3072]{1,0:T(8,128)(2,1)S(1)} %bitcast.20, bf16[168,3072]{1,0:T(8,128)(2,1)S(1)} %bitcast.22, bf16[168,3072]{1,0:T(8,128)(2,1)} %collective-permute-done.5.gate1, ...), custom_call_target="tpu_custom_call" | custom-call | tf_op jit(solution)/shard_map/pallas_call | solution.py:253
  78.5 0.5 shard_map.74.sofar_ref
  79.5 0.5 shard_map.75.sofar_ref
  80.1 1.5 shard_map.76.sofar_ref
  81.6 2.0 %shard_map.77 = (bf16[4,384,128]{2,1,0:T(8,128)(2,1)S(1)}, bf16[4,384,128]{2,1,0:T(8,128)(2,1)S(1)}, bf16[4,384,128]{2,1,0:T(8,128)(2,1)S(1)}, bf16[4,384,128]{2,1,0:T(8,128)(2,1)S(1)}) custom-call(bf16[256,768]{1,0:T(8,128)(2,1)S(1)} %collective-permute-done.13.x_ref, bf16[768,3072]{1,0:T(8,128)(2,1)S(1)} %get-tuple-element.26.weights_ref, ...), custom_call_target="tpu_custom_call" | custom-call | tf_op jit(solution)/shard_map/pallas_call | solution.py:253
  83.6 3.3 %collective-permute-start.16 = (bf16[4,384,128]{2,1,0:T(8,128)(2,1)S(1)}, bf16[4,384,128]{2,1,0:T(8,128)(2,1)S(1)}, u32[]{:S(2)}, u32[]{:S(2)}) collective-permute-start(bf16[4,384,128]{2,1,0:T(8,128)(2,1)S(1)} %get-tuple-element.34), channel_id=1, source_target_pairs={{0,480},{32,448},{64,416},{96,384},{128,352},{160,320},{192,288},{... | collective-permute-start | bytes 1179656 | tf_op jit(solution)/shard_map/ppermute | solution.py:306
  86.9 4.4 %collective-permute-start.17 = (bf16[4,384,128]{2,1,0:T(8,128)(2,1)S(1)}, bf16[4,384,128]{2,1,0:T(8,128)(2,1)S(1)}, u32[]{:S(2)}, u32[]{:S(2)}) collective-permute-start(bf16[4,384,128]{2,1,0:T(8,128)(2,1)S(1)} %get-tuple-element.35), channel_id=1, source_target_pairs={{0,96},{32,64},{64,32},{96,0},{128,224},{160,192},{192,160},{224,1... | collective-permute-start | bytes 1179656 | tf_op jit(solution)/shard_map/ppermute | solution.py:306
  91.3 4.0 %collective-permute-start.18 = (bf16[4,384,128]{2,1,0:T(8,128)(2,1)S(1)}, bf16[4,384,128]{2,1,0:T(8,128)(2,1)S(1)}, u32[]{:S(2)}, u32[]{:S(2)}) collective-permute-start(bf16[4,384,128]{2,1,0:T(8,128)(2,1)S(1)} %get-tuple-element.36), channel_id=1, source_target_pairs={{0,384},{32,416},{64,448},{96,480},{128,256},{160,288},{192,320},{... | collective-permute-start | bytes 1179656 | tf_op jit(solution)/shard_map/ppermute | solution.py:306
  95.3 0.6 shard_map.67.sofar_ref
  95.9 0.6 shard_map.68.sofar_ref
  96.5 0.6 shard_map.69.sofar_ref
  97.1 2.7 %shard_map.70 = (bf16[4,432,128]{2,1,0:T(8,128)(2,1)}, bf16[4,432,128]{2,1,0:T(8,128)(2,1)S(1)}, bf16[4,432,128]{2,1,0:T(8,128)(2,1)S(1)}, bf16[4,432,128]{2,1,0:T(8,128)(2,1)S(1)}) custom-call(bf16[288,768]{1,0:T(8,128)(2,1)S(1)} %collective-permute-done.4.x_ref, bf16[768,3072]{1,0:T(8,128)(2,1)S(1)} %get-tuple-element.26.weights_ref, ...), custom_call_target="tpu_custom_call" | custom-call | tf_op jit(solution)/shard_map/pallas_call | solution.py:253
  99.8 3.2 %collective-permute-start.10 = (bf16[4,432,128]{2,1,0:T(8,128)(2,1)}, bf16[4,432,128]{2,1,0:T(8,128)(2,1)S(1)}, u32[]{:S(2)}, u32[]{:S(2)}) collective-permute-start(bf16[4,432,128]{2,1,0:T(8,128)(2,1)} %get-tuple-element.29), channel_id=1, source_target_pairs={{0,480},{32,448},{64,416},{96,384},{128,352},{160,320},{192,288},{... | collective-permute-start | bytes 1327112 | tf_op jit(solution)/shard_map/ppermute | solution.py:306
  103.0 4.4 %collective-permute-start.11 = (bf16[4,432,128]{2,1,0:T(8,128)(2,1)S(1)}, bf16[4,432,128]{2,1,0:T(8,128)(2,1)S(1)}, u32[]{:S(2)}, u32[]{:S(2)}) collective-permute-start(bf16[4,432,128]{2,1,0:T(8,128)(2,1)S(1)} %get-tuple-element.30), channel_id=1, source_target_pairs={{0,96},{32,64},{64,32},{96,0},{128,224},{160,192},{192,160},{224,1... | collective-permute-start | bytes 1327112 | tf_op jit(solution)/shard_map/ppermute | solution.py:306
  107.5 4.0 %collective-permute-start.12 = (bf16[4,432,128]{2,1,0:T(8,128)(2,1)S(1)}, bf16[4,432,128]{2,1,0:T(8,128)(2,1)S(1)}, u32[]{:S(2)}, u32[]{:S(2)}) collective-permute-start(bf16[4,432,128]{2,1,0:T(8,128)(2,1)S(1)} %get-tuple-element.31), channel_id=1, source_target_pairs={{0,384},{32,416},{64,448},{96,480},{128,256},{160,288},{192,320},{... | collective-permute-start | bytes 1327112 | tf_op jit(solution)/shard_map/ppermute | solution.py:306
  111.7 0.8 shard_map.80
  112.5 3.4 %all-to-all-start.3 = ((bf16[4,384,128]{2,1,0:T(8,128)(2,1)}), bf16[4,384,128]{2,1,0:T(8,128)(2,1)S(1)}, u32[]{:S(2)}, u32[]{:S(2)}) async-start(bf16[4,384,128]{2,1,0:T(8,128)(2,1)} %shard_map.80), calls=%async_computation.3 | async-start | bytes 786432 | tf_op jit(solution)/shard_map/all_to_all | solution.py:270
  116.0 2.8 %collective-permute-done.11.b = bf16[4,432,128]{2,1,0:T(8,128)(2,1)S(1)} collective-permute-done((bf16[4,432,128]{2,1,0:T(8,128)(2,1)S(1)}, bf16[4,432,128]{2,1,0:T(8,128)(2,1)S(1)}, u32[]{:S(2)}, u32[]{:S(2)}) %collective-permute-start.11) | collective-permute-done | bytes 442400 | tf_op jit(solution)/shard_map/ppermute | solution.py:306
  119.0 1.3 collective-permute-done.12.b
  120.4 0.7 all-to-all-done.3.refs_1_
  121.1 8.8 %all_to_all.26.refs_0_ = bf16[4,432,128]{2,1,0:T(8,128)(2,1)S(1)} all-to-all(bf16[4,432,128]{2,1,0:T(8,128)(2,1)S(1)} %shard_map.73), channel_id=1, replica_groups={{0,32,128,160},{64,96,192,224},{256,288,384,416},{320,352,448,480},{481..., dimensions={0} | all-to-all | bytes 884736 | tf_op jit(solution)/shard_map/all_to_all | solution.py:270
  129.9 0.9 shard_map.81
  130.8 9.6 %all-to-all-start.4 = ((bf16[16,56,128]{2,1,0:T(8,128)(2,1)}), bf16[16,56,128]{2,1,0:T(8,128)(2,1)S(1)}, u32[]{:S(2)}, u32[]{:S(2)}) async-start(bf16[16,56,128]{2,1,0:T(8,128)(2,1)} %shard_map.81), calls=%async_computation.4 | async-start | bytes 458752 | tf_op jit(solution)/shard_map/all_to_all | solution.py:270
  140.5 0.7 shard_map.82.gates_ref
  141.2 15.2 %all-to-all-done.4 = bf16[16,56,128]{2,1,0:T(8,128)(2,1)S(1)} async-done(((bf16[16,56,128]{2,1,0:T(8,128)(2,1)}), bf16[16,56,128]{2,1,0:T(8,128)(2,1)S(1)}, u32[]{:S(2)}, u32[]{:S(2)}) %all-to-all-start.4) | async-done | bytes 229408 | tf_op jit(solution)/shard_map/all_to_all | solution.py:270
  156.4 1.2 shard_map.83
  (36 shorter events, 0.9 us)
Async XLA Ops:
  0.0 75.0 %copy-start = (bf16[1,168,3072]{2,1,0:T(8,128)(2,1)S(1)}, bf16[1,168,3072]{2,1,0:T(8,128)(2,1)}, u32[]{:S(2)}) copy-start(bf16[1,168,3072]{2,1,0:T(8,128)(2,1)} %param.9) | copy-start | bytes 3096580
  0.0 75.0 %copy-start.1 = (bf16[1,168,3072]{2,1,0:T(8,128)(2,1)S(1)}, bf16[1,168,3072]{2,1,0:T(8,128)(2,1)}, u32[]{:S(2)}) copy-start(bf16[1,168,3072]{2,1,0:T(8,128)(2,1)} %param.10) | copy-start | bytes 3096580
  0.0 63.3 %collective-permute-start.5 = (bf16[168,3072]{1,0:T(8,128)(2,1)}, bf16[168,3072]{1,0:T(8,128)(2,1)}, u32[]{:S(2)}, u32[]{:S(2)}) collective-permute-start(bf16[168,3072]{1,0:T(8,128)(2,1)} %bitcast.17), channel_id=1, source_target_pairs={{0,1},{1,0},{2,3},{3,2},{4,5},{5,4},{6,7},{7,6},{8,9},{9,8},{10,11... | collective-permute-start | bytes 3096584 | tf_op jit(solution)/shard_map/ppermute | solution.py:266
  2.1 1.1 copy-start.3
  3.2 0.7 copy-start.6
  4.7 25.8 %collective-permute-start = (bf16[40,768]{1,0:T(8,128)(2,1)S(1)}, bf16[40,768]{1,0:T(8,128)(2,1)S(1)}, u32[]{:S(2)}, u32[]{:S(2)}) collective-permute-start(bf16[40,768]{1,0:T(8,128)(2,1)S(1)} %get-tuple-element.21), channel_id=1, source_target_pairs={{0,16},{1,11},{2,18},{3,13},{4,20},{5,15},{6,22},{7,17},{8,24},{9,... | collective-permute-start | bytes 184328 | tf_op jit(solution)/shard_map/ppermute | solution.py:284
  17.9 14.6 %collective-permute-start.1 = (bf16[40,768]{1,0:T(8,128)(2,1)S(1)}, bf16[40,768]{1,0:T(8,128)(2,1)S(1)}, u32[]{:S(2)}, u32[]{:S(2)}) collective-permute-start(bf16[40,768]{1,0:T(8,128)(2,1)S(1)} %get-tuple-element.22), channel_id=1, source_target_pairs={{0,8},{1,23},{2,10},{3,25},{4,12},{5,27},{6,14},{7,29},{8,16},{9,3... | collective-permute-start | bytes 184328 | tf_op jit(solution)/shard_map/ppermute | solution.py:284
  21.9 13.0 %collective-permute-start.2 = (bf16[40,768]{1,0:T(8,128)(2,1)S(1)}, bf16[40,768]{1,0:T(8,128)(2,1)S(1)}, u32[]{:S(2)}, u32[]{:S(2)}) collective-permute-start(bf16[40,768]{1,0:T(8,128)(2,1)S(1)} %get-tuple-element.23), channel_id=1, source_target_pairs={{0,24},{1,7},{2,26},{3,9},{4,28},{5,11},{6,30},{7,13},{8,0},{9,15}... | collective-permute-start | bytes 184328 | tf_op jit(solution)/shard_map/ppermute | solution.py:284
  24.8 10.0 %collective-permute-start.3 = (bf16[40,768]{1,0:T(8,128)(2,1)S(1)}, bf16[40,768]{1,0:T(8,128)(2,1)S(1)}, u32[]{:S(2)}, u32[]{:S(2)}) collective-permute-start(bf16[40,768]{1,0:T(8,128)(2,1)S(1)} %get-tuple-element.24), channel_id=1, source_target_pairs={{0,0},{1,27},{2,2},{3,29},{4,4},{5,31},{6,6},{7,1},{8,8},{9,3},{10... | collective-permute-start | bytes 184328 | tf_op jit(solution)/shard_map/ppermute | solution.py:284
  30.5 36.1 %collective-permute-start.6 = (bf16[168,3072]{1,0:T(8,128)(2,1)}, bf16[168,3072]{1,0:T(8,128)(2,1)}, u32[]{:S(2)}, u32[]{:S(2)}) collective-permute-start(bf16[168,3072]{1,0:T(8,128)(2,1)} %bitcast.19), channel_id=1, source_target_pairs={{0,1},{1,0},{2,3},{3,2},{4,5},{5,4},{6,7},{7,6},{8,9},{9,8},{10,11... | collective-permute-start | bytes 3096584 | tf_op jit(solution)/shard_map/ppermute | solution.py:266
  32.4 38.5 %collective-permute-start.7 = (bf16[168,3072]{1,0:T(8,128)(2,1)}, bf16[168,3072]{1,0:T(8,128)(2,1)}, u32[]{:S(2)}, u32[]{:S(2)}) collective-permute-start(bf16[168,3072]{1,0:T(8,128)(2,1)} %bitcast.21), channel_id=1, source_target_pairs={{0,1},{1,0},{2,3},{3,2},{4,5},{5,4},{6,7},{7,6},{8,9},{9,8},{10,11... | collective-permute-start | bytes 3096584 | tf_op jit(solution)/shard_map/ppermute | solution.py:266
  45.5 13.1 %collective-permute-start.15 = (bf16[256,768]{1,0:T(8,128)(2,1)S(1)}, bf16[256,768]{1,0:T(8,128)(2,1)S(1)}, u32[]{:S(2)}, u32[]{:S(2)}) collective-permute-start(bf16[256,768]{1,0:T(8,128)(2,1)S(1)} %bitcast.13), channel_id=1, source_target_pairs={{0,480},{32,448},{64,416},{96,384},{128,352},{160,320},{192,288},{... | collective-permute-start | bytes 1179656 | tf_op jit(solution)/shard_map/ppermute | solution.py:292
  50.2 13.1 %all-to-all-start = ((bf16[4,72,768]{2,1,0:T(8,128)(2,1)}), bf16[4,72,768]{2,1,0:T(8,128)(2,1)S(1)}, u32[]{:S(2)}, u32[]{:S(2)}) async-start(bf16[4,72,768]{2,1,0:T(8,128)(2,1)} %get-tuple-element.25), calls=%async_computation | async-start | bytes 884736 | tf_op jit(solution)/shard_map/all_to_all | solution.py:270
  53.7 26.4 %collective-permute-start.14 = (bf16[256,768]{1,0:T(8,128)(2,1)S(1)}, bf16[256,768]{1,0:T(8,128)(2,1)}, u32[]{:S(2)}, u32[]{:S(2)}) collective-permute-start(bf16[256,768]{1,0:T(8,128)(2,1)S(1)} %bitcast.14), channel_id=1, source_target_pairs={{0,96},{32,64},{64,32},{96,0},{128,224},{160,192},{192,160},{224,1... | collective-permute-start | bytes 1179656 | tf_op jit(solution)/shard_map/ppermute | solution.py:292
  58.5 0.8 copy-start.4
  59.3 22.3 %collective-permute-start.13 = (bf16[256,768]{1,0:T(8,128)(2,1)S(1)}, bf16[256,768]{1,0:T(8,128)(2,1)S(1)}, u32[]{:S(2)}, u32[]{:S(2)}) collective-permute-start(bf16[256,768]{1,0:T(8,128)(2,1)S(1)} %bitcast.15), channel_id=1, source_target_pairs={{0,384},{32,416},{64,448},{96,480},{128,256},{160,288},{192,320},{... | collective-permute-start | bytes 1179656 | tf_op jit(solution)/shard_map/ppermute | solution.py:292
  63.3 28.0 %collective-permute-start.9 = (bf16[288,768]{1,0:T(8,128)(2,1)S(1)}, bf16[288,768]{1,0:T(8,128)(2,1)S(1)}, u32[]{:S(2)}, u32[]{:S(2)}) collective-permute-start(bf16[288,768]{1,0:T(8,128)(2,1)S(1)} %bitcast.9), channel_id=1, source_target_pairs={{0,480},{32,448},{64,416},{96,384},{128,352},{160,320},{192,288},{... | collective-permute-start | bytes 1327112 | tf_op jit(solution)/shard_map/ppermute | solution.py:292
  66.6 29.9 %collective-permute-start.8 = (bf16[288,768]{1,0:T(8,128)(2,1)S(1)}, bf16[288,768]{1,0:T(8,128)(2,1)S(1)}, u32[]{:S(2)}, u32[]{:S(2)}) collective-permute-start(bf16[288,768]{1,0:T(8,128)(2,1)S(1)} %bitcast.10), channel_id=1, source_target_pairs={{0,96},{32,64},{64,32},{96,0},{128,224},{160,192},{192,160},{224,1... | collective-permute-start | bytes 1327112 | tf_op jit(solution)/shard_map/ppermute | solution.py:292
  71.0 26.1 %collective-permute-start.4 = (bf16[288,768]{1,0:T(8,128)(2,1)S(1)}, bf16[288,768]{1,0:T(8,128)(2,1)S(1)}, u32[]{:S(2)}, u32[]{:S(2)}) collective-permute-start(bf16[288,768]{1,0:T(8,128)(2,1)S(1)} %bitcast.11), channel_id=1, source_target_pairs={{0,384},{32,416},{64,448},{96,480},{128,256},{160,288},{192,320},{... | collective-permute-start | bytes 1327112 | tf_op jit(solution)/shard_map/ppermute | solution.py:292
  75.0 1.2 copy-start.2
  78.5 1.0 copy-start.5
  83.6 23.8 %collective-permute-start.16 = (bf16[4,384,128]{2,1,0:T(8,128)(2,1)S(1)}, bf16[4,384,128]{2,1,0:T(8,128)(2,1)S(1)}, u32[]{:S(2)}, u32[]{:S(2)}) collective-permute-start(bf16[4,384,128]{2,1,0:T(8,128)(2,1)S(1)} %get-tuple-element.34), channel_id=1, source_target_pairs={{0,480},{32,448},{64,416},{96,384},{128,352},{160,320},{192,288},{... | collective-permute-start | bytes 1179656 | tf_op jit(solution)/shard_map/ppermute | solution.py:306
  86.9 24.7 %collective-permute-start.17 = (bf16[4,384,128]{2,1,0:T(8,128)(2,1)S(1)}, bf16[4,384,128]{2,1,0:T(8,128)(2,1)S(1)}, u32[]{:S(2)}, u32[]{:S(2)}) collective-permute-start(bf16[4,384,128]{2,1,0:T(8,128)(2,1)S(1)} %get-tuple-element.35), channel_id=1, source_target_pairs={{0,96},{32,64},{64,32},{96,0},{128,224},{160,192},{192,160},{224,1... | collective-permute-start | bytes 1179656 | tf_op jit(solution)/shard_map/ppermute | solution.py:306
  91.3 20.3 %collective-permute-start.18 = (bf16[4,384,128]{2,1,0:T(8,128)(2,1)S(1)}, bf16[4,384,128]{2,1,0:T(8,128)(2,1)S(1)}, u32[]{:S(2)}, u32[]{:S(2)}) collective-permute-start(bf16[4,384,128]{2,1,0:T(8,128)(2,1)S(1)} %get-tuple-element.36), channel_id=1, source_target_pairs={{0,384},{32,416},{64,448},{96,480},{128,256},{160,288},{192,320},{... | collective-permute-start | bytes 1179656 | tf_op jit(solution)/shard_map/ppermute | solution.py:306
  99.8 16.1 %collective-permute-start.10 = (bf16[4,432,128]{2,1,0:T(8,128)(2,1)}, bf16[4,432,128]{2,1,0:T(8,128)(2,1)S(1)}, u32[]{:S(2)}, u32[]{:S(2)}) collective-permute-start(bf16[4,432,128]{2,1,0:T(8,128)(2,1)} %get-tuple-element.29), channel_id=1, source_target_pairs={{0,480},{32,448},{64,416},{96,384},{128,352},{160,320},{192,288},{... | collective-permute-start | bytes 1327112 | tf_op jit(solution)/shard_map/ppermute | solution.py:306
  103.0 15.8 %collective-permute-start.11 = (bf16[4,432,128]{2,1,0:T(8,128)(2,1)S(1)}, bf16[4,432,128]{2,1,0:T(8,128)(2,1)S(1)}, u32[]{:S(2)}, u32[]{:S(2)}) collective-permute-start(bf16[4,432,128]{2,1,0:T(8,128)(2,1)S(1)} %get-tuple-element.30), channel_id=1, source_target_pairs={{0,96},{32,64},{64,32},{96,0},{128,224},{160,192},{192,160},{224,1... | collective-permute-start | bytes 1327112 | tf_op jit(solution)/shard_map/ppermute | solution.py:306
  107.5 12.9 %collective-permute-start.12 = (bf16[4,432,128]{2,1,0:T(8,128)(2,1)S(1)}, bf16[4,432,128]{2,1,0:T(8,128)(2,1)S(1)}, u32[]{:S(2)}, u32[]{:S(2)}) collective-permute-start(bf16[4,432,128]{2,1,0:T(8,128)(2,1)S(1)} %get-tuple-element.31), channel_id=1, source_target_pairs={{0,384},{32,416},{64,448},{96,480},{128,256},{160,288},{192,320},{... | collective-permute-start | bytes 1327112 | tf_op jit(solution)/shard_map/ppermute | solution.py:306
  112.5 8.6 %all-to-all-start.3 = ((bf16[4,384,128]{2,1,0:T(8,128)(2,1)}), bf16[4,384,128]{2,1,0:T(8,128)(2,1)S(1)}, u32[]{:S(2)}, u32[]{:S(2)}) async-start(bf16[4,384,128]{2,1,0:T(8,128)(2,1)} %shard_map.80), calls=%async_computation.3 | async-start | bytes 786432 | tf_op jit(solution)/shard_map/all_to_all | solution.py:270
  119.0 21.5 %copy-start.7 = (s32[256,4]{0,1:T(4,128)S(1)}, s32[256,4]{0,1:T(4,128)}, u32[]{:S(2)}) copy-start(s32[256,4]{0,1:T(4,128)} %param.7) | copy-start | bytes 12292
  119.0 21.5 %copy-start.8 = (f32[256,4]{0,1:T(4,128)S(1)}, f32[256,4]{0,1:T(4,128)}, u32[]{:S(2)}) copy-start(f32[256,4]{0,1:T(4,128)} %param.8) | copy-start | bytes 12292
  130.8 25.6 %all-to-all-start.4 = ((bf16[16,56,128]{2,1,0:T(8,128)(2,1)}), bf16[16,56,128]{2,1,0:T(8,128)(2,1)S(1)}, u32[]{:S(2)}, u32[]{:S(2)}) async-start(bf16[16,56,128]{2,1,0:T(8,128)(2,1)} %shard_map.81), calls=%async_computation.4 | async-start | bytes 458752 | tf_op jit(solution)/shard_map/all_to_all | solution.py:270

commit v7 on v5

--- a/solution.py
+++ b/solution.py
@@ -177,12 +177,13 @@
     total_ref[...] = sofar_ref[...] + products(mask, x_ref, weights_ref)
 
 
-def last_kernel(mask, out_mask, x_ref, weights_ref, sofar_ref, down_ref, hidden_ref, out_ref):
+def last_kernel(mask, x_ref, weights_ref, sofar_ref, down_ref, hidden_ref, *out_refs):
     total = sofar_ref[...] + products(mask, x_ref, weights_ref)
     g, u = total[:, :WIDE], total[:, WIDE:]
     hidden = (g / (1.0 + jnp.exp(-g)) * u).astype(BF16)
     hidden_ref[...] = hidden
-    down_products(out_mask, hidden, down_ref, out_ref)
+    for to, out_ref in zip(MASKS, out_refs):
+        down_products(to, hidden, down_ref, out_ref)
 
 
 def down_kernel(mask, hidden_ref, down_ref, out_ref):
@@ -236,14 +237,12 @@
     out_ref[LANES:, :] = jnp.where(odd, first[HLANES:], rest).astype(BF16)
 
 
-def call(kernel, shape, *args, scratch=(), limit=16, flops=0):
+def call(kernel, shape, *args, scratch=(), limit=16):
     out = jax.ShapeDtypeStruct(shape, BF16) if isinstance(shape, tuple) else [pltpu.VMEM(s, d) for s, d in shape]
-    sizes = sum(v.size * v.dtype.itemsize for v in args)
     return pl.pallas_call(
         kernel,
         out_shape=out,
         scratch_shapes=scratch,
-        cost_estimate=pl.CostEstimate(flops=flops, transcendentals=0, bytes_accessed=sizes) if flops else None,
         compiler_params=pltpu.CompilerParams(vmem_limit_bytes=limit * 1024 * 1024),
     )(*args)
 
@@ -281,18 +280,14 @@
     (total,) = call(functools.partial(first_kernel, 0), [total_shape], rows, weights, limit=32)
     for mask, other in zip(MASKS[:2], others[:2]):
         (total,) = call(functools.partial(next_kernel, mask), [total_shape], other, weights, held(total), limit=32)
-    hidden, first = call(
-        functools.partial(last_kernel, MASKS[2], MASKS[0]),
-        [((2 * SIDE, WIDE), BF16), out_shape],
+    hidden, *outs = call(
+        functools.partial(last_kernel, MASKS[2]),
+        [((2 * SIDE, WIDE), BF16)] + [out_shape] * 3,
         *(others[2], weights, held(total), down),
         limit=32,
     )
-    hidden = held(hidden)
-    outs, work = [first], 2 * hidden.size * 8 * LANES
-    for mask in (*MASKS[1:], 0):
-        outs += call(functools.partial(down_kernel, mask), [out_shape], hidden, down, limit=32, flops=work)
-    others = [lax.ppermute(out, plane, across(mask)) for mask, out in zip(MASKS, outs[:3])]
-    partial = outs[3]
+    (partial,) = call(functools.partial(down_kernel, 0), [out_shape], held(hidden), down, limit=32)
+    others = [lax.ppermute(out, plane, across(mask)) for mask, out in zip(MASKS, outs)]
     for other, kind in zip(others, (F32, F32, BF16)):
         (partial,) = call(add_kernel, [((4, PART, LANES), kind)], held(partial), other, limit=24)
     partial = exchange(partial, plane, inside)

time: 151 us -> 144 us (0.954)
  waiting for transfers between devices: 65.3 us -> 59.2 us
    ppermute x3, waiting for transfers between devices: 24.3 us -> 18.2 us  [shards(): lax.ppermute(out, plane, across(mask))]
    pallas_call x16 -> x14, Pallas kernels: 15.6 us -> 15 us  [call(): pl.pallas_call(kernel, out_shape=out, scratch_shapes=scratch, compiler_pa...]
  transfers between devices with their start and end apart: 12 -> 12, of which waited for: 7 -> 8; matrix products, arithmetic and copies ran while one was open for 0% -> 0% of each run, Pallas kernels for 6% -> 6%
where the time goes in v7:
time: 144 us; the launch traced here: 142 us
  waiting for transfers between devices  59.2 us (41%)
  starting transfers between devices  54.2 us (38%)
  Pallas kernels  15 us (10%)
  blocking collectives  10.8 us (8%)
  local copies, waits for them, and re-layouts  3.05 us (2%)
    all_to_all x3, waiting for transfers between devices, exchange(): lax.all_to_all(value, axis, split_axis=0, concat_axis=0, tiled=True, axis...  31.7 us
    all_to_all x3, starting transfers between devices, exchange(): lax.all_to_all(value, axis, split_axis=0, concat_axis=0, tiled=True, axis...  24.7 us
    ppermute x3, waiting for transfers between devices, shards(): lax.ppermute(out, plane, across(mask))  18.2 us
    pallas_call x14, Pallas kernels, call(): pl.pallas_call(kernel, out_shape=out, scratch_shapes=scratch, compiler_pa...  15 us
    ppermute x3, starting transfers between devices, shards(): lax.ppermute(out, plane, across(mask))  11.6 us
    ppermute x3, starting transfers between devices, shards(): others = [lax.ppermute(rows, plane, across(mask)) for mask in MASKS]  11.6 us
    all_to_all x1, blocking collectives, exchange(): lax.all_to_all(value, axis, split_axis=0, concat_axis=0, tiled=True, axis...  10.8 us
    ppermute x3, waiting for transfers between devices, shards(): others = [lax.ppermute(rows, plane, across(mask)) for mask in MASKS]  9.3 us
  transfers between devices with their start and end apart: 12, of which 8 were waited for; matrix products, arithmetic and copies ran while one was open for 0% of the time, Pallas kernels for 6%

profile of v7, /device:TPU:6, one launch (start us, length us, event | category | flops | bytes accessed | tf_op | source)
XLA Modules:
  0.0 142.5 jit_solution(7424117317747539583)
XLA Ops:
  0.0 1.1 copy-done.3
  1.1 0.7 copy-done.4
  1.8 1.4 shard_map.64
  3.2 15.3 %all-to-all-start = ((bf16[16,56,128]{2,1,0:T(8,128)(2,1)}), bf16[16,56,128]{2,1,0:T(8,128)(2,1)S(1)}, u32[]{:S(2)}, u32[]{:S(2)}) async-start(bf16[16,56,128]{2,1,0:T(8,128)(2,1)} %bitcast.1), calls=%async_computation | async-start | bytes 458752 | tf_op jit(solution)/shard_map/all_to_all | solution.py:259
  18.5 1.9 %collective-permute-start.1 = (bf16[168,3072]{1,0:T(8,128)(2,1)}, bf16[168,3072]{1,0:T(8,128)(2,1)}, u32[]{:S(2)}, u32[]{:S(2)}) collective-permute-start(bf16[168,3072]{1,0:T(8,128)(2,1)} %bitcast.10), channel_id=1, source_target_pairs={{0,1},{1,0},{2,3},{3,2},{4,5},{5,4},{6,7},{7,6},{8,9},{9,8},{10,11... | collective-permute-start | bytes 3096584 | tf_op jit(solution)/shard_map/ppermute | solution.py:255
  20.5 15.5 %all-to-all-done = bf16[16,56,128]{2,1,0:T(8,128)(2,1)S(1)} async-done(((bf16[16,56,128]{2,1,0:T(8,128)(2,1)}), bf16[16,56,128]{2,1,0:T(8,128)(2,1)S(1)}, u32[]{:S(2)}, u32[]{:S(2)}) %all-to-all-start) | async-done | bytes 229408 | tf_op jit(solution)/shard_map/all_to_all | solution.py:259
  35.9 1.0 shard_map.65
  37.0 4.3 %all-to-all-start.1 = ((bf16[4,816,128]{2,1,0:T(8,128)(2,1)}), bf16[4,816,128]{2,1,0:T(8,128)(2,1)S(1)}, u32[]{:S(2)}, u32[]{:S(2)}) async-start(bf16[4,816,128]{2,1,0:T(8,128)(2,1)} %shard_map.65), calls=%async_computation.1 | async-start | bytes 1671168 | tf_op jit(solution)/shard_map/all_to_all | solution.py:259
  41.3 0.0 copy-done.1
  41.3 1.9 %collective-permute-start.2 = (bf16[168,3072]{1,0:T(8,128)(2,1)S(1)}, bf16[168,3072]{1,0:T(8,128)(2,1)}, u32[]{:S(2)}, u32[]{:S(2)}) collective-permute-start(bf16[168,3072]{1,0:T(8,128)(2,1)S(1)} %bitcast.12), channel_id=1, source_target_pairs={{0,1},{1,0},{2,3},{3,2},{4,5},{5,4},{6,7},{7,6},{8,9},{9,8},{10,11... | collective-permute-start | bytes 3096584 | tf_op jit(solution)/shard_map/ppermute | solution.py:255
  43.2 2.4 %collective-permute-start.3 = (bf16[168,3072]{1,0:T(8,128)(2,1)}, bf16[168,3072]{1,0:T(8,128)(2,1)}, u32[]{:S(2)}, u32[]{:S(2)}) collective-permute-start(bf16[168,3072]{1,0:T(8,128)(2,1)} %bitcast.14), channel_id=1, source_target_pairs={{0,1},{1,0},{2,3},{3,2},{4,5},{5,4},{6,7},{7,6},{8,9},{9,8},{10,11... | collective-permute-start | bytes 3096584 | tf_op jit(solution)/shard_map/ppermute | solution.py:255
  45.6 3.4 %all-to-all-done.1.x_ref = bf16[4,816,128]{2,1,0:T(8,128)(2,1)S(1)} async-done(((bf16[4,816,128]{2,1,0:T(8,128)(2,1)}), bf16[4,816,128]{2,1,0:T(8,128)(2,1)S(1)}, u32[]{:S(2)}, u32[]{:S(2)}) %all-to-all-start.1) | async-done | bytes 835616 | tf_op jit(solution)/shard_map/all_to_all | solution.py:259
  48.9 4.8 %collective-permute-start.5 = (bf16[4,816,128]{2,1,0:T(8,128)(2,1)S(1)}, bf16[4,816,128]{2,1,0:T(8,128)(2,1)S(1)}, u32[]{:S(2)}, u32[]{:S(2)}) collective-permute-start(bf16[4,816,128]{2,1,0:T(8,128)(2,1)S(1)} %all-to-all-done.1.x_ref), channel_id=1, source_target_pairs={{0,480},{32,448},{64,416},{96,384},{128,352},{160,320},{192,288},{... | collective-permute-start | bytes 2506760 | tf_op jit(solution)/shard_map/ppermute | solution.py:278
  53.7 4.0 %collective-permute-start.4 = (bf16[4,816,128]{2,1,0:T(8,128)(2,1)S(1)}, bf16[4,816,128]{2,1,0:T(8,128)(2,1)S(1)}, u32[]{:S(2)}, u32[]{:S(2)}) collective-permute-start(bf16[4,816,128]{2,1,0:T(8,128)(2,1)S(1)} %all-to-all-done.1.x_ref), channel_id=1, source_target_pairs={{0,96},{32,64},{64,32},{96,0},{128,224},{160,192},{192,160},{224,1... | collective-permute-start | bytes 2506760 | tf_op jit(solution)/shard_map/ppermute | solution.py:278
  57.7 0.0 collective-permute-done.1.gate1
  57.7 2.9 %collective-permute-start = (bf16[4,816,128]{2,1,0:T(8,128)(2,1)S(1)}, bf16[4,816,128]{2,1,0:T(8,128)(2,1)S(1)}, u32[]{:S(2)}, u32[]{:S(2)}) collective-permute-start(bf16[4,816,128]{2,1,0:T(8,128)(2,1)S(1)} %all-to-all-done.1.x_ref), channel_id=1, source_target_pairs={{0,384},{32,416},{64,448},{96,480},{128,256},{160,288},{192,320},{... | collective-permute-start | bytes 2506760 | tf_op jit(solution)/shard_map/ppermute | solution.py:278
  60.6 0.0 collective-permute-done.2.up1
  60.6 0.0 collective-permute-done.3.down1
  60.6 0.0 copy-done
  60.6 0.0 copy-start.2
  60.6 1.2 copy-done.2
  61.9 2.3 %shard_map.66 = (bf16[768,3072]{1,0:T(8,128)(2,1)S(1)}, bf16[384,3072]{1,0:T(8,128)(2,1)S(1)}) custom-call(bf16[168,3072]{1,0:T(8,128)(2,1)S(1)} %bitcast.11, bf16[168,3072]{1,0:T(8,128)(2,1)S(1)} %bitcast.13, bf16[168,3072]{1,0:T(8,128)(2,1)S(1)} %bitcast.15, bf16[168,3072]{1,0:T(8,128)(2,1)} %collective-permute-done.1.gate1, ...), custom_call_target="tpu_custom_call" | custom-call | tf_op jit(solution)/shard_map/pallas_call | solution.py:242
  64.2 0.9 shard_map.67.sofar_ref
  65.1 1.7 %collective-permute-done.5.x_ref = bf16[4,816,128]{2,1,0:T(8,128)(2,1)S(1)} collective-permute-done((bf16[4,816,128]{2,1,0:T(8,128)(2,1)S(1)}, bf16[4,816,128]{2,1,0:T(8,128)(2,1)S(1)}, u32[]{:S(2)}, u32[]{:S(2)}) %collective-permute-start.5) | collective-permute-done | bytes 835616 | tf_op jit(solution)/shard_map/ppermute | solution.py:278
  66.8 0.9 shard_map.68.sofar_ref
  67.7 7.6 %collective-permute-done.4.x_ref = bf16[4,816,128]{2,1,0:T(8,128)(2,1)S(1)} collective-permute-done((bf16[4,816,128]{2,1,0:T(8,128)(2,1)S(1)}, bf16[4,816,128]{2,1,0:T(8,128)(2,1)S(1)}, u32[]{:S(2)}, u32[]{:S(2)}) %collective-permute-start.4) | collective-permute-done | bytes 835616 | tf_op jit(solution)/shard_map/ppermute | solution.py:278
  75.3 0.9 shard_map.69.sofar_ref
  76.2 0.0 collective-permute-done.x_ref
  76.2 3.3 %shard_map.70 = (bf16[544,384]{1,0:T(8,128)(2,1)S(1)}, bf16[4,816,128]{2,1,0:T(8,128)(2,1)S(1)}, bf16[4,816,128]{2,1,0:T(8,128)(2,1)S(1)}, bf16[4,816,128]{2,1,0:T(8,128)(2,1)S(1)}) custom-call(bf16[4,816,128]{2,1,0:T(8,128)(2,1)S(1)} %collective-permute-done.x_ref, bf16[768,3072]{1,0:T(8,128)(2,1)S(1)} %get-tuple-element.11.weights_ref, ...), custom_call_target="tpu_custom_call" | custom-call | tf_op jit(solution)/shard_map/pallas_call | solution.py:242
  79.5 4.2 %collective-permute-start.6 = (bf16[4,816,128]{2,1,0:T(8,128)(2,1)S(1)}, bf16[4,816,128]{2,1,0:T(8,128)(2,1)S(1)}, u32[]{:S(2)}, u32[]{:S(2)}) collective-permute-start(bf16[4,816,128]{2,1,0:T(8,128)(2,1)S(1)} %get-tuple-element.14), channel_id=1, source_target_pairs={{0,480},{32,448},{64,416},{96,384},{128,352},{160,320},{192,288},{... | collective-permute-start | bytes 2506760 | tf_op jit(solution)/shard_map/ppermute | solution.py:290
  83.7 4.0 %collective-permute-start.7 = (bf16[4,816,128]{2,1,0:T(8,128)(2,1)S(1)}, bf16[4,816,128]{2,1,0:T(8,128)(2,1)S(1)}, u32[]{:S(2)}, u32[]{:S(2)}) collective-permute-start(bf16[4,816,128]{2,1,0:T(8,128)(2,1)S(1)} %get-tuple-element.15), channel_id=1, source_target_pairs={{0,96},{32,64},{64,32},{96,0},{128,224},{160,192},{192,160},{224,1... | collective-permute-start | bytes 2506760 | tf_op jit(solution)/shard_map/ppermute | solution.py:290
  87.7 3.4 %collective-permute-start.8 = (bf16[4,816,128]{2,1,0:T(8,128)(2,1)S(1)}, bf16[4,816,128]{2,1,0:T(8,128)(2,1)S(1)}, u32[]{:S(2)}, u32[]{:S(2)}) collective-permute-start(bf16[4,816,128]{2,1,0:T(8,128)(2,1)S(1)} %get-tuple-element.16), channel_id=1, source_target_pairs={{0,384},{32,416},{64,448},{96,480},{128,256},{160,288},{192,320},{... | collective-permute-start | bytes 2506760 | tf_op jit(solution)/shard_map/ppermute | solution.py:290
  91.2 0.9 shard_map.71.a
  92.1 5.3 %collective-permute-done.6.b = bf16[4,816,128]{2,1,0:T(8,128)(2,1)S(1)} collective-permute-done((bf16[4,816,128]{2,1,0:T(8,128)(2,1)S(1)}, bf16[4,816,128]{2,1,0:T(8,128)(2,1)S(1)}, u32[]{:S(2)}, u32[]{:S(2)}) %collective-permute-start.6) | collective-permute-done | bytes 835616 | tf_op jit(solution)/shard_map/ppermute | solution.py:290
  97.3 0.2 shard_map.72.a
  97.5 7.8 %collective-permute-done.7.b = bf16[4,816,128]{2,1,0:T(8,128)(2,1)S(1)} collective-permute-done((bf16[4,816,128]{2,1,0:T(8,128)(2,1)S(1)}, bf16[4,816,128]{2,1,0:T(8,128)(2,1)S(1)}, u32[]{:S(2)}, u32[]{:S(2)}) %collective-permute-start.7) | collective-permute-done | bytes 835616 | tf_op jit(solution)/shard_map/ppermute | solution.py:290
  105.3 0.2 shard_map.73.a
  105.5 5.2 %collective-permute-done.8.b = bf16[4,816,128]{2,1,0:T(8,128)(2,1)S(1)} collective-permute-done((bf16[4,816,128]{2,1,0:T(8,128)(2,1)S(1)}, bf16[4,816,128]{2,1,0:T(8,128)(2,1)S(1)}, u32[]{:S(2)}, u32[]{:S(2)}) %collective-permute-start.8) | collective-permute-done | bytes 835616 | tf_op jit(solution)/shard_map/ppermute | solution.py:290
  110.7 0.2 shard_map.74
  110.8 0.0 copy-start.5
  110.9 0.0 copy-start.6
  110.9 10.8 %all_to_all.20.parts_ref = bf16[4,816,128]{2,1,0:T(8,128)(2,1)S(1)} all-to-all(bf16[4,816,128]{2,1,0:T(8,128)(2,1)S(1)} %shard_map.74), channel_id=1, replica_groups={{0,32,128,160},{64,96,192,224},{256,288,384,416},{320,352,448,480},{481..., dimensions={0} | all-to-all | bytes 1671168 | tf_op jit(solution)/shard_map/all_to_all | solution.py:259
  121.7 0.9 shard_map.75
  122.5 5.0 %all-to-all-start.3 = ((bf16[16,56,128]{2,1,0:T(8,128)(2,1)}), bf16[16,56,128]{2,1,0:T(8,128)(2,1)S(1)}, u32[]{:S(2)}, u32[]{:S(2)}) async-start(bf16[16,56,128]{2,1,0:T(8,128)(2,1)} %bitcast.6), calls=%async_computation.3 | async-start | bytes 458752 | tf_op jit(solution)/shard_map/all_to_all | solution.py:259
  127.6 0.0 copy-done.5
  127.6 0.8 shard_map.76.gates_ref
  128.4 12.9 %all-to-all-done.3 = bf16[16,56,128]{2,1,0:T(8,128)(2,1)S(1)} async-done(((bf16[16,56,128]{2,1,0:T(8,128)(2,1)}), bf16[16,56,128]{2,1,0:T(8,128)(2,1)S(1)}, u32[]{:S(2)}, u32[]{:S(2)}) %all-to-all-start.3) | async-done | bytes 229408 | tf_op jit(solution)/shard_map/all_to_all | solution.py:259
  141.3 1.2 shard_map.77
  (5 shorter events, 0.0 us)
Async XLA Ops:
  0.0 1.1 copy-start.3
  1.1 0.7 copy-start.4
  3.2 38.1 %copy-start.1 = (bf16[1,168,3072]{2,1,0:T(8,128)(2,1)S(1)}, bf16[1,168,3072]{2,1,0:T(8,128)(2,1)}, u32[]{:S(2)}) copy-start(bf16[1,168,3072]{2,1,0:T(8,128)(2,1)} %param.10) | copy-start | bytes 3096580
  3.2 57.4 %copy-start = (bf16[1,168,3072]{2,1,0:T(8,128)(2,1)S(1)}, bf16[1,168,3072]{2,1,0:T(8,128)(2,1)}, u32[]{:S(2)}) copy-start(bf16[1,168,3072]{2,1,0:T(8,128)(2,1)} %param.9) | copy-start | bytes 3096580
  3.2 32.7 %all-to-all-start = ((bf16[16,56,128]{2,1,0:T(8,128)(2,1)}), bf16[16,56,128]{2,1,0:T(8,128)(2,1)S(1)}, u32[]{:S(2)}, u32[]{:S(2)}) async-start(bf16[16,56,128]{2,1,0:T(8,128)(2,1)} %bitcast.1), calls=%async_computation | async-start | bytes 458752 | tf_op jit(solution)/shard_map/all_to_all | solution.py:259
  18.5 39.2 %collective-permute-start.1 = (bf16[168,3072]{1,0:T(8,128)(2,1)}, bf16[168,3072]{1,0:T(8,128)(2,1)}, u32[]{:S(2)}, u32[]{:S(2)}) collective-permute-start(bf16[168,3072]{1,0:T(8,128)(2,1)} %bitcast.10), channel_id=1, source_target_pairs={{0,1},{1,0},{2,3},{3,2},{4,5},{5,4},{6,7},{7,6},{8,9},{9,8},{10,11... | collective-permute-start | bytes 3096584 | tf_op jit(solution)/shard_map/ppermute | solution.py:255
  37.0 12.0 %all-to-all-start.1 = ((bf16[4,816,128]{2,1,0:T(8,128)(2,1)}), bf16[4,816,128]{2,1,0:T(8,128)(2,1)S(1)}, u32[]{:S(2)}, u32[]{:S(2)}) async-start(bf16[4,816,128]{2,1,0:T(8,128)(2,1)} %shard_map.65), calls=%async_computation.1 | async-start | bytes 1671168 | tf_op jit(solution)/shard_map/all_to_all | solution.py:259
  41.3 19.3 %collective-permute-start.2 = (bf16[168,3072]{1,0:T(8,128)(2,1)S(1)}, bf16[168,3072]{1,0:T(8,128)(2,1)}, u32[]{:S(2)}, u32[]{:S(2)}) collective-permute-start(bf16[168,3072]{1,0:T(8,128)(2,1)S(1)} %bitcast.12), channel_id=1, source_target_pairs={{0,1},{1,0},{2,3},{3,2},{4,5},{5,4},{6,7},{7,6},{8,9},{9,8},{10,11... | collective-permute-start | bytes 3096584 | tf_op jit(solution)/shard_map/ppermute | solution.py:255
  43.2 17.4 %collective-permute-start.3 = (bf16[168,3072]{1,0:T(8,128)(2,1)}, bf16[168,3072]{1,0:T(8,128)(2,1)}, u32[]{:S(2)}, u32[]{:S(2)}) collective-permute-start(bf16[168,3072]{1,0:T(8,128)(2,1)} %bitcast.14), channel_id=1, source_target_pairs={{0,1},{1,0},{2,3},{3,2},{4,5},{5,4},{6,7},{7,6},{8,9},{9,8},{10,11... | collective-permute-start | bytes 3096584 | tf_op jit(solution)/shard_map/ppermute | solution.py:255
  48.9 17.8 %collective-permute-start.5 = (bf16[4,816,128]{2,1,0:T(8,128)(2,1)S(1)}, bf16[4,816,128]{2,1,0:T(8,128)(2,1)S(1)}, u32[]{:S(2)}, u32[]{:S(2)}) collective-permute-start(bf16[4,816,128]{2,1,0:T(8,128)(2,1)S(1)} %all-to-all-done.1.x_ref), channel_id=1, source_target_pairs={{0,480},{32,448},{64,416},{96,384},{128,352},{160,320},{192,288},{... | collective-permute-start | bytes 2506760 | tf_op jit(solution)/shard_map/ppermute | solution.py:278
  53.7 21.5 %collective-permute-start.4 = (bf16[4,816,128]{2,1,0:T(8,128)(2,1)S(1)}, bf16[4,816,128]{2,1,0:T(8,128)(2,1)S(1)}, u32[]{:S(2)}, u32[]{:S(2)}) collective-permute-start(bf16[4,816,128]{2,1,0:T(8,128)(2,1)S(1)} %all-to-all-done.1.x_ref), channel_id=1, source_target_pairs={{0,96},{32,64},{64,32},{96,0},{128,224},{160,192},{192,160},{224,1... | collective-permute-start | bytes 2506760 | tf_op jit(solution)/shard_map/ppermute | solution.py:278
  57.7 18.4 %collective-permute-start = (bf16[4,816,128]{2,1,0:T(8,128)(2,1)S(1)}, bf16[4,816,128]{2,1,0:T(8,128)(2,1)S(1)}, u32[]{:S(2)}, u32[]{:S(2)}) collective-permute-start(bf16[4,816,128]{2,1,0:T(8,128)(2,1)S(1)} %all-to-all-done.1.x_ref), channel_id=1, source_target_pairs={{0,384},{32,416},{64,448},{96,480},{128,256},{160,288},{192,320},{... | collective-permute-start | bytes 2506760 | tf_op jit(solution)/shard_map/ppermute | solution.py:278
  60.6 1.2 copy-start.2
  79.5 17.8 %collective-permute-start.6 = (bf16[4,816,128]{2,1,0:T(8,128)(2,1)S(1)}, bf16[4,816,128]{2,1,0:T(8,128)(2,1)S(1)}, u32[]{:S(2)}, u32[]{:S(2)}) collective-permute-start(bf16[4,816,128]{2,1,0:T(8,128)(2,1)S(1)} %get-tuple-element.14), channel_id=1, source_target_pairs={{0,480},{32,448},{64,416},{96,384},{128,352},{160,320},{192,288},{... | collective-permute-start | bytes 2506760 | tf_op jit(solution)/shard_map/ppermute | solution.py:290
  83.7 21.5 %collective-permute-start.7 = (bf16[4,816,128]{2,1,0:T(8,128)(2,1)S(1)}, bf16[4,816,128]{2,1,0:T(8,128)(2,1)S(1)}, u32[]{:S(2)}, u32[]{:S(2)}) collective-permute-start(bf16[4,816,128]{2,1,0:T(8,128)(2,1)S(1)} %get-tuple-element.15), channel_id=1, source_target_pairs={{0,96},{32,64},{64,32},{96,0},{128,224},{160,192},{192,160},{224,1... | collective-permute-start | bytes 2506760 | tf_op jit(solution)/shard_map/ppermute | solution.py:290
  87.7 22.9 %collective-permute-start.8 = (bf16[4,816,128]{2,1,0:T(8,128)(2,1)S(1)}, bf16[4,816,128]{2,1,0:T(8,128)(2,1)S(1)}, u32[]{:S(2)}, u32[]{:S(2)}) collective-permute-start(bf16[4,816,128]{2,1,0:T(8,128)(2,1)S(1)} %get-tuple-element.16), channel_id=1, source_target_pairs={{0,384},{32,416},{64,448},{96,480},{128,256},{160,288},{192,320},{... | collective-permute-start | bytes 2506760 | tf_op jit(solution)/shard_map/ppermute | solution.py:290
  110.8 16.7 %copy-start.5 = (s32[256,4]{0,1:T(4,128)S(1)}, s32[256,4]{0,1:T(4,128)}, u32[]{:S(2)}) copy-start(s32[256,4]{0,1:T(4,128)} %param.7) | copy-start | bytes 12292
  110.9 16.7 %copy-start.6 = (f32[256,4]{0,1:T(4,128)S(1)}, f32[256,4]{0,1:T(4,128)}, u32[]{:S(2)}) copy-start(f32[256,4]{0,1:T(4,128)} %param.8) | copy-start | bytes 12292
  122.5 18.7 %all-to-all-start.3 = ((bf16[16,56,128]{2,1,0:T(8,128)(2,1)}), bf16[16,56,128]{2,1,0:T(8,128)(2,1)S(1)}, u32[]{:S(2)}, u32[]{:S(2)}) async-start(bf16[16,56,128]{2,1,0:T(8,128)(2,1)} %bitcast.6), calls=%async_computation.3 | async-start | bytes 458752 | tf_op jit(solution)/shard_map/all_to_all | solution.py:259

commit v8 on v7

--- a/solution.py
+++ b/solution.py
@@ -19,7 +19,8 @@
 SIDE = EXPERTS * HALF
 PART = 3 * SIDE
 WIDE = 384
-MASKS = (3, 1, 2)
+SIDES = (1, 2)
+DIAGONAL = 3
 F32 = jnp.float32
 BF16 = jnp.bfloat16
 
@@ -109,7 +110,7 @@
     out_ref[...] = dot(picks, rows).astype(BF16)
 
 
-def pack_kernel(blocks_ref, out_ref, source, packed):
+def pack_kernel(blocks_ref, out_ref, one_ref, source, packed):
     source[...] = blocks_ref[...].astype(F32)
     for e in range(EXPERTS):
         for third in range(3):
@@ -119,6 +120,7 @@
     value = packed[...].astype(BF16)
     for copy in range(out_ref.shape[0]):
         out_ref[copy] = value
+    one_ref[...] = value
 
 
 def weights_kernel(gate0, up0, down0, gate1, up1, down1, weights_ref, down_ref):
@@ -138,12 +140,13 @@
 def products(mask, x_ref, weights_ref):
     _, q = place_of()
     q = q ^ mask
+    turn = DIAGONAL if mask == DIAGONAL else 0
     low = iota((SIDE, LANES), 1) < HLANES
-    main = jnp.concatenate([x_ref[at, : 2 * SIDE, :] for at in range(4)], axis=1)
+    main = jnp.concatenate([x_ref[at ^ turn, : 2 * SIDE, :] for at in range(4)], axis=1)
     halves = []
     for pair in range(2):
-        even = x_ref[2 * pair, 2 * SIDE :, :].astype(F32)
-        odd = x_ref[2 * pair + 1, 2 * SIDE :, :].astype(F32)
+        even = x_ref[2 * pair ^ turn, 2 * SIDE :, :].astype(F32)
+        odd = x_ref[2 * pair + 1 ^ turn, 2 * SIDE :, :].astype(F32)
         upper = jnp.where(low, even, pltpu.roll(odd, HLANES, 1)).astype(BF16)
         lower = jnp.where(low, pltpu.roll(even, HLANES, 1), odd).astype(BF16)
         halves.append(jnp.concatenate([upper, lower], axis=0))
@@ -156,17 +159,18 @@
 def down_products(mask, hidden, down_ref, out_ref):
     core, q = place_of()
     to = q ^ mask
+    turn = DIAGONAL if mask == DIAGONAL else 0
     low = iota((SIDE, LANES), 1) < HLANES
     for at in range(4):
         dp = (to // 2 * 2 + at // 2 - core) % SIZE * SIZE + (to % 2 * 2 + at % 2 - core) % SIZE
         odd = dp % 2 == 1
         y = dot(hidden, down_ref[:, pl.ds(pl.multiple_of((dp * 3 - dp % 2) // 2 * LANES, LANES), 2 * LANES)])
         first, second = y[:, :LANES], y[:, LANES:]
-        out_ref[at, : 2 * SIDE, :] = jnp.where(odd, second, first).astype(BF16)
+        out_ref[at ^ turn, : 2 * SIDE, :] = jnp.where(odd, second, first).astype(BF16)
         half = jnp.where(odd, first, second)
         turned = pltpu.roll(half, HLANES, 1)
         left, right = jnp.where(odd, turned, half), jnp.where(odd, half, turned)
-        out_ref[at, 2 * SIDE :, :] = jnp.where(low, left[:SIDE], right[SIDE:]).astype(BF16)
+        out_ref[at ^ turn, 2 * SIDE :, :] = jnp.where(low, left[:SIDE], right[SIDE:]).astype(BF16)
 
 
 def first_kernel(mask, x_ref, weights_ref, total_ref):
@@ -182,7 +186,7 @@
     g, u = total[:, :WIDE], total[:, WIDE:]
     hidden = (g / (1.0 + jnp.exp(-g)) * u).astype(BF16)
     hidden_ref[...] = hidden
-    for to, out_ref in zip(MASKS, out_refs):
+    for to, out_ref in zip((DIAGONAL, *SIDES), out_refs):
         down_products(to, hidden, down_ref, out_ref)
 
 
@@ -194,9 +198,16 @@
     out_ref[...] = (a[...].astype(F32) + b[...].astype(F32)).astype(out_ref.dtype)
 
 
-def add_blocks_kernel(parts_ref, out_ref, packed, blocks):
+def add_parts_kernel(parts_ref, out_ref):
     total = parts_ref[0].astype(F32)
     for i in range(1, parts_ref.shape[0]):
+        total += parts_ref[i].astype(F32)
+    out_ref[...] = total.astype(BF16)
+
+
+def add_blocks_kernel(parts_ref, more_ref, out_ref, packed, blocks):
+    total = more_ref[...].astype(F32)
+    for i in range(parts_ref.shape[0]):
         total += parts_ref[i].astype(F32)
     packed[...] = total
     for e in range(EXPERTS):
@@ -273,26 +284,35 @@
 
     sent = call(dispatch_kernel, (EXPERTS * BLOCK, LANES), ids, tokens)
     arrived = exchange(sent.reshape(EXPERTS, BLOCK, LANES), "expert").reshape(EXPERTS * BLOCK, LANES)
-    rows = call(pack_kernel, (4, PART, LANES), arrived, scratch=[block_scratch, part_scratch])
+    out_shape = (4, PART, LANES)
+    rows, one = call(
+        pack_kernel, [(out_shape, BF16), (out_shape[1:], BF16)], arrived, scratch=[block_scratch, part_scratch]
+    )
     rows = exchange(rows, plane, inside)
-    others = [lax.ppermute(rows, plane, across(mask)) for mask in MASKS]
-    total_shape, out_shape = ((2 * SIDE, 2 * WIDE), F32), ((4, PART, LANES), BF16)
-    (total,) = call(functools.partial(first_kernel, 0), [total_shape], rows, weights, limit=32)
-    for mask, other in zip(MASKS[:2], others[:2]):
-        (total,) = call(functools.partial(next_kernel, mask), [total_shape], other, weights, held(total), limit=32)
-    hidden, *outs = call(
-        functools.partial(last_kernel, MASKS[2]),
-        [((2 * SIDE, WIDE), BF16)] + [out_shape] * 3,
-        *(others[2], weights, held(total), down),
+    one = lax.ppermute(one, plane, across(DIAGONAL))
+    others = [lax.ppermute(rows, plane, across(mask)) for mask in SIDES]
+    diagonal = exchange(jnp.broadcast_to(one, out_shape), plane, inside)
+    total_shape = [((2 * SIDE, 2 * WIDE), F32)]
+    (total,) = call(functools.partial(first_kernel, 0), total_shape, rows, weights, limit=32)
+    for mask, other in zip(SIDES, others):
+        (total,) = call(functools.partial(next_kernel, mask), total_shape, other, weights, held(total), limit=32)
+    hidden, across_out, *outs = call(
+        functools.partial(last_kernel, DIAGONAL),
+        [((2 * SIDE, WIDE), BF16)] + [(out_shape, BF16)] * 3,
+        *(diagonal, weights, held(total), down),
         limit=32,
     )
-    (partial,) = call(functools.partial(down_kernel, 0), [out_shape], held(hidden), down, limit=32)
-    others = [lax.ppermute(out, plane, across(mask)) for mask, out in zip(MASKS, outs)]
-    for other, kind in zip(others, (F32, F32, BF16)):
-        (partial,) = call(add_kernel, [((4, PART, LANES), kind)], held(partial), other, limit=24)
+    (partial,) = call(functools.partial(down_kernel, 0), [(out_shape, BF16)], held(hidden), down, limit=32)
+    others = [lax.ppermute(out, plane, across(mask)) for mask, out in zip(SIDES, outs)]
+    one = call(add_parts_kernel, out_shape[1:], exchange(across_out, plane, inside))
+    one = lax.ppermute(one, plane, across(DIAGONAL))
+    for other, kind in zip(others, (F32, BF16)):
+        (partial,) = call(add_kernel, [(out_shape, kind)], held(partial), other, limit=24)
     partial = exchange(partial, plane, inside)
-    summed = call(add_blocks_kernel, (EXPERTS * BLOCK, LANES), partial, scratch=[part_scratch, block_scratch])
-    back = exchange(summed.reshape(EXPERTS, BLOCK, LANES), "expert").reshape(EXPERTS * BLOCK, LANES)
+    summed = call(
+        add_blocks_kernel, (EXPERTS * BLOCK, LANES), partial, one, scratch=[part_scratch, block_scratch]
+    ).reshape(EXPERTS, BLOCK, LANES)
+    back = exchange(summed, "expert").reshape(EXPERTS * BLOCK, LANES)
     (factors,) = call(gates_kernel, [((3, EXPERTS * BLOCK, 3 * n), BF16)], ids, gates)
     return call(combine_kernel, (width // DP, n), back, held(factors)).T
 

time: 144 us -> 154 us (1.069)
  the two profiles are of different devices: /device:TPU:6 before, /device:TPU:32 now
where the time goes in v8:
time: 154 us; the launch traced here: 153 us
  starting transfers between devices  50.3 us (33%)
  waiting for transfers between devices  35.3 us (23%)
  blocking collectives  31.9 us (21%)
  Pallas kernels  20.8 us (14%)
  local copies, waits for them, and re-layouts  14.3 us (9%)
    all_to_all x1, blocking collectives, exchange(): lax.all_to_all(value, axis, split_axis=0, concat_axis=0, tiled=True, axis...  31.9 us
    pallas_call x14, Pallas kernels, call(): pl.pallas_call(kernel, out_shape=out, scratch_shapes=scratch, compiler_pa...  20.8 us
    all_to_all x5, starting transfers between devices, exchange(): lax.all_to_all(value, axis, split_axis=0, concat_axis=0, tiled=True, axis...  20.8 us
    unnamed x34, local copies, waits for them, and re-layouts  13.2 us
    all_to_all x5, waiting for transfers between devices, exchange(): lax.all_to_all(value, axis, split_axis=0, concat_axis=0, tiled=True, axis...  13 us
    ppermute x2, waiting for transfers between devices, shards(): lax.ppermute(out, plane, across(mask))  11.8 us
    ppermute x2, starting transfers between devices, shards(): one = lax.ppermute(one, plane, across(DIAGONAL))  11.2 us
    ppermute x2, waiting for transfers between devices, shards(): one = lax.ppermute(one, plane, across(DIAGONAL))  7.66 us
  transfers between devices with their start and end apart: 14, of which 6 were waited for; matrix products, arithmetic and copies ran while one was open for 1% of the time, Pallas kernels for 8%

profile of v8, /device:TPU:32, one launch (start us, length us, event | category | flops | bytes accessed | tf_op | source)
XLA Modules:
  0.0 152.9 jit_solution(13323595079236800838)
XLA Ops:
  0.0 1.1 copy-done.11
  1.1 0.7 copy-done.14
  1.8 0.7 shard_map.64
  2.5 31.9 %all_to_all.30 = bf16[16,56,128]{2,1,0:T(8,128)(2,1)S(1)} all-to-all(bf16[16,56,128]{2,1,0:T(8,128)(2,1)S(1)} %bitcast.18), channel_id=1, replica_groups=mesh['dp'=16,'expert'=16,'tensor'=2] {'expert'}, dimensions={0} | all-to-all | bytes 458752 | tf_op jit(solution)/shard_map/all_to_all | solution.py:270
  34.4 0.1 shard_map.65
  34.6 0.9 copy-done.10
  35.5 3.8 %all-to-all-start.2 = ((bf16[4,816,128]{2,1,0:T(8,128)(2,1)}), bf16[4,816,128]{2,1,0:T(8,128)(2,1)S(1)}, u32[]{:S(2)}, u32[]{:S(2)}) async-start(bf16[4,816,128]{2,1,0:T(8,128)(2,1)} %copy-done.10), calls=%async_computation.2 | async-start | bytes 1671168 | tf_op jit(solution)/shard_map/all_to_all | solution.py:270
  39.2 7.8 %collective-permute-start = (bf16[816,128]{1,0:T(8,128)(2,1)S(1)}, bf16[816,128]{1,0:T(8,128)(2,1)S(1)}, u32[]{:S(2)}, u32[]{:S(2)}) collective-permute-start(bf16[816,128]{1,0:T(8,128)(2,1)S(1)} %get-tuple-element.13), channel_id=1, source_target_pairs={{0,480},{32,448},{64,416},{96,384},{128,352},{160,320},{192,288},{... | collective-permute-start | bytes 626696 | tf_op jit(solution)/shard_map/ppermute | solution.py:292
  47.1 1.9 %collective-permute-start.1 = (bf16[168,3072]{1,0:T(8,128)(2,1)S(1)}, bf16[168,3072]{1,0:T(8,128)(2,1)}, u32[]{:S(2)}, u32[]{:S(2)}) collective-permute-start(bf16[168,3072]{1,0:T(8,128)(2,1)S(1)} %bitcast.10), channel_id=1, source_target_pairs={{0,1},{1,0},{2,3},{3,2},{4,5},{5,4},{6,7},{7,6},{8,9},{9,8},{10,11... | collective-permute-start | bytes 3096584 | tf_op jit(solution)/shard_map/ppermute | solution.py:266
  49.0 2.4 %collective-permute-start.2 = (bf16[168,3072]{1,0:T(8,128)(2,1)S(1)}, bf16[168,3072]{1,0:T(8,128)(2,1)}, u32[]{:S(2)}, u32[]{:S(2)}) collective-permute-start(bf16[168,3072]{1,0:T(8,128)(2,1)S(1)} %bitcast.12), channel_id=1, source_target_pairs={{0,1},{1,0},{2,3},{3,2},{4,5},{5,4},{6,7},{7,6},{8,9},{9,8},{10,11... | collective-permute-start | bytes 3096584 | tf_op jit(solution)/shard_map/ppermute | solution.py:266
  51.4 1.9 %collective-permute-start.3 = (bf16[168,3072]{1,0:T(8,128)(2,1)}, bf16[168,3072]{1,0:T(8,128)(2,1)}, u32[]{:S(2)}, u32[]{:S(2)}) collective-permute-start(bf16[168,3072]{1,0:T(8,128)(2,1)} %bitcast.14), channel_id=1, source_target_pairs={{0,1},{1,0},{2,3},{3,2},{4,5},{5,4},{6,7},{7,6},{8,9},{9,8},{10,11... | collective-permute-start | bytes 3096584 | tf_op jit(solution)/shard_map/ppermute | solution.py:266
  53.4 2.1 %collective-permute-start.5 = (bf16[4,816,128]{2,1,0:T(8,128)(2,1)S(1)}, bf16[4,816,128]{2,1,0:T(8,128)(2,1)}, u32[]{:S(2)}, u32[]{:S(2)}) collective-permute-start(bf16[4,816,128]{2,1,0:T(8,128)(2,1)S(1)} %all-to-all-done.2.x_ref), channel_id=1, source_target_pairs={{0,96},{32,64},{64,32},{96,0},{128,224},{160,192},{192,160},{224,1... | collective-permute-start | bytes 2506760 | tf_op jit(solution)/shard_map/ppermute | solution.py:293
  55.5 3.0 %collective-permute-start.4 = (bf16[4,816,128]{2,1,0:T(8,128)(2,1)S(1)}, bf16[4,816,128]{2,1,0:T(8,128)(2,1)}, u32[]{:S(2)}, u32[]{:S(2)}) collective-permute-start(bf16[4,816,128]{2,1,0:T(8,128)(2,1)S(1)} %all-to-all-done.2.x_ref), channel_id=1, source_target_pairs={{0,384},{32,416},{64,448},{96,480},{128,256},{160,288},{192,320},{... | collective-permute-start | bytes 2506760 | tf_op jit(solution)/shard_map/ppermute | solution.py:293
  58.6 1.1 broadcast_in_dim.3
  59.7 4.2 %all-to-all-start.1 = ((bf16[4,816,128]{2,1,0:T(8,128)(2,1)}), bf16[4,816,128]{2,1,0:T(8,128)(2,1)}, u32[]{:S(2)}, u32[]{:S(2)}) async-start(bf16[4,816,128]{2,1,0:T(8,128)(2,1)} %broadcast_in_dim.3), calls=%async_computation.1 | async-start | bytes 1671168 | tf_op jit(solution)/shard_map/all_to_all | solution.py:270
  63.9 1.2 copy-done.5
  65.1 1.2 copy-done.7
  66.3 1.2 copy-done.8
  67.6 2.3 %shard_map.66 = (bf16[768,3072]{1,0:T(8,128)(2,1)S(1)}, bf16[384,3072]{1,0:T(8,128)(2,1)S(1)}) custom-call(bf16[168,3072]{1,0:T(8,128)(2,1)S(1)} %bitcast.11, bf16[168,3072]{1,0:T(8,128)(2,1)S(1)} %bitcast.13, bf16[168,3072]{1,0:T(8,128)(2,1)S(1)} %bitcast.15, bf16[168,3072]{1,0:T(8,128)(2,1)} %collective-permute-done.1.gate1, ...), custom_call_target="tpu_custom_call" | custom-call | tf_op jit(solution)/shard_map/pallas_call | solution.py:253
  69.9 0.9 shard_map.67.sofar_ref
  70.8 0.6 collective-permute-done.5.x_ref
  71.4 2.1 %shard_map.68.sofar_ref = f32[544,768]{1,0:T(8,128)S(1)} custom-call(bf16[4,816,128]{2,1,0:T(8,128)(2,1)} %collective-permute-done.5.x_ref, bf16[768,3072]{1,0:T(8,128)(2,1)S(1)} %get-tuple-element.14.weights_ref, f32[544,768]{1,0:T(8,128)S(1)} %shard_map.67.sofar_ref), custom_call_target="tpu_custom_call" | custom-call | tf_op jit(solution)/shard_map/pallas_call | solution.py:253
  73.5 2.2 %collective-permute-done.4.x_ref = bf16[4,816,128]{2,1,0:T(8,128)(2,1)} collective-permute-done((bf16[4,816,128]{2,1,0:T(8,128)(2,1)S(1)}, bf16[4,816,128]{2,1,0:T(8,128)(2,1)}, u32[]{:S(2)}, u32[]{:S(2)}) %collective-permute-start.4) | collective-permute-done | bytes 835616 | tf_op jit(solution)/shard_map/ppermute | solution.py:293
  75.7 2.0 %shard_map.69.sofar_ref = f32[544,768]{1,0:T(8,128)S(1)} custom-call(bf16[4,816,128]{2,1,0:T(8,128)(2,1)} %collective-permute-done.4.x_ref, bf16[768,3072]{1,0:T(8,128)(2,1)S(1)} %get-tuple-element.14.weights_ref, f32[544,768]{1,0:T(8,128)S(1)} %shard_map.68.sofar_ref), custom_call_target="tpu_custom_call" | custom-call | tf_op jit(solution)/shard_map/pallas_call | solution.py:253
  77.8 1.2 copy-done.2
  79.0 2.3 %copy-done.1 = bf16[768,3072]{1,0:T(8,128)(2,1)S(1)} copy-done((bf16[768,3072]{1,0:T(8,128)(2,1)S(1)}, bf16[768,3072]{1,0:T(8,128)(2,1)}, u32[]{:S(2)}) %copy-start.1) | copy-done | bytes 4718616
  81.4 1.4 copy-done.3
  82.8 5.4 %shard_map.70 = (bf16[544,384]{1,0:T(8,128)(2,1)S(1)}, bf16[4,816,128]{2,1,0:T(8,128)(2,1)S(1)}, bf16[4,816,128]{2,1,0:T(8,128)(2,1)}, bf16[4,816,128]{2,1,0:T(8,128)(2,1)}) custom-call(bf16[4,816,128]{2,1,0:T(8,128)(2,1)} %all-to-all-done.1.x_ref, bf16[768,3072]{1,0:T(8,128)(2,1)S(1)} %copy-done.1, f32[544,768]{1,0:T(8,128)S(1)} %copy-done.3, ...), custom_call_target="tpu_custom_call" | custom-call | tf_op jit(solution)/shard_map/pallas_call | solution.py:253
  88.2 0.8 copy-done.12
  89.0 4.9 %collective-permute-start.6 = (bf16[4,816,128]{2,1,0:T(8,128)(2,1)}, bf16[4,816,128]{2,1,0:T(8,128)(2,1)}, u32[]{:S(2)}, u32[]{:S(2)}) collective-permute-start(bf16[4,816,128]{2,1,0:T(8,128)(2,1)} %get-tuple-element.18), channel_id=1, source_target_pairs={{0,96},{32,64},{64,32},{96,0},{128,224},{160,192},{192,160},{224,1... | collective-permute-start | bytes 2506760 | tf_op jit(solution)/shard_map/ppermute | solution.py:306
  93.9 2.0 %collective-permute-start.7 = (bf16[4,816,128]{2,1,0:T(8,128)(2,1)}, bf16[4,816,128]{2,1,0:T(8,128)(2,1)}, u32[]{:S(2)}, u32[]{:S(2)}) collective-permute-start(bf16[4,816,128]{2,1,0:T(8,128)(2,1)} %get-tuple-element.19), channel_id=1, source_target_pairs={{0,384},{32,416},{64,448},{96,480},{128,256},{160,288},{192,320},{... | collective-permute-start | bytes 2506760 | tf_op jit(solution)/shard_map/ppermute | solution.py:306
  95.9 3.5 %all-to-all-start.4 = ((bf16[4,816,128]{2,1,0:T(8,128)(2,1)}), bf16[4,816,128]{2,1,0:T(8,128)(2,1)S(1)}, u32[]{:S(2)}, u32[]{:S(2)}) async-start(bf16[4,816,128]{2,1,0:T(8,128)(2,1)} %copy-done.9), calls=%async_computation.4 | async-start | bytes 1671168 | tf_op jit(solution)/shard_map/all_to_all | solution.py:270
  99.4 1.0 copy-done.13
  100.4 0.8 shard_map.71.a
  101.2 7.2 %collective-permute-done.6.b = bf16[4,816,128]{2,1,0:T(8,128)(2,1)} collective-permute-done((bf16[4,816,128]{2,1,0:T(8,128)(2,1)}, bf16[4,816,128]{2,1,0:T(8,128)(2,1)}, u32[]{:S(2)}, u32[]{:S(2)}) %collective-permute-start.6) | collective-permute-done | bytes 835616 | tf_op jit(solution)/shard_map/ppermute | solution.py:306
  108.4 1.3 shard_map.72.a
  109.7 4.6 %collective-permute-done.7.b = bf16[4,816,128]{2,1,0:T(8,128)(2,1)} collective-permute-done((bf16[4,816,128]{2,1,0:T(8,128)(2,1)}, bf16[4,816,128]{2,1,0:T(8,128)(2,1)}, u32[]{:S(2)}, u32[]{:S(2)}) %collective-permute-start.7) | collective-permute-done | bytes 835616 | tf_op jit(solution)/shard_map/ppermute | solution.py:306
  114.3 2.2 %shard_map.73 = bf16[4,816,128]{2,1,0:T(8,128)(2,1)} custom-call(f32[4,816,128]{2,1,0:T(8,128)S(1)} %shard_map.72.a, bf16[4,816,128]{2,1,0:T(8,128)(2,1)} %collective-permute-done.7.b), custom_call_target="tpu_custom_call" | custom-call | tf_op jit(solution)/shard_map/pallas_call | solution.py:253
  116.5 3.5 %all-to-all-start.3 = ((bf16[4,816,128]{2,1,0:T(8,128)(2,1)}), bf16[4,816,128]{2,1,0:T(8,128)(2,1)S(1)}, u32[]{:S(2)}, u32[]{:S(2)}) async-start(bf16[4,816,128]{2,1,0:T(8,128)(2,1)} %shard_map.73), calls=%async_computation.3 | async-start | bytes 1671168 | tf_op jit(solution)/shard_map/all_to_all | solution.py:270
  120.0 0.0 copy-start.15
  120.0 0.1 shard_map.74
  120.2 3.3 %collective-permute-start.8 = (bf16[816,128]{1,0:T(8,128)(2,1)S(1)}, bf16[816,128]{1,0:T(8,128)(2,1)S(1)}, u32[]{:S(2)}, u32[]{:S(2)}) collective-permute-start(bf16[816,128]{1,0:T(8,128)(2,1)S(1)} %shard_map.74), channel_id=1, source_target_pairs={{0,480},{32,448},{64,416},{96,384},{128,352},{160,320},{192,288},{... | collective-permute-start | bytes 626696 | tf_op jit(solution)/shard_map/ppermute | solution.py:308
  123.5 7.7 %collective-permute-done.8.more_ref = bf16[816,128]{1,0:T(8,128)(2,1)S(1)} collective-permute-done((bf16[816,128]{1,0:T(8,128)(2,1)S(1)}, bf16[816,128]{1,0:T(8,128)(2,1)S(1)}, u32[]{:S(2)}, u32[]{:S(2)}) %collective-permute-start.8) | collective-permute-done | bytes 208928 | tf_op jit(solution)/shard_map/ppermute | solution.py:308
  131.2 0.9 shard_map.75
  132.1 5.8 %all-to-all-start.5 = ((bf16[16,56,128]{2,1,0:T(8,128)(2,1)}), bf16[16,56,128]{2,1,0:T(8,128)(2,1)S(1)}, u32[]{:S(2)}, u32[]{:S(2)}) async-start(bf16[16,56,128]{2,1,0:T(8,128)(2,1)} %bitcast.6), calls=%async_computation.5 | async-start | bytes 458752 | tf_op jit(solution)/shard_map/all_to_all | solution.py:270
  137.9 0.8 shard_map.76.gates_ref
  138.7 13.0 %all-to-all-done.5 = bf16[16,56,128]{2,1,0:T(8,128)(2,1)S(1)} async-done(((bf16[16,56,128]{2,1,0:T(8,128)(2,1)}), bf16[16,56,128]{2,1,0:T(8,128)(2,1)S(1)}, u32[]{:S(2)}, u32[]{:S(2)}) %all-to-all-start.5) | async-done | bytes 229408 | tf_op jit(solution)/shard_map/all_to_all | solution.py:270
  151.7 1.2 shard_map.77
  (30 shorter events, 0.1 us)
Async XLA Ops:
  0.0 1.1 copy-start.11
  1.1 0.7 copy-start.14
  1.8 45.2 %copy-start.4 = (bf16[1,168,3072]{2,1,0:T(8,128)(2,1)S(1)}, bf16[1,168,3072]{2,1,0:T(8,128)(2,1)}, u32[]{:S(2)}) copy-start(bf16[1,168,3072]{2,1,0:T(8,128)(2,1)} %param.9) | copy-start | bytes 3096580
  1.8 47.2 %copy-start.6 = (bf16[1,168,3072]{2,1,0:T(8,128)(2,1)S(1)}, bf16[1,168,3072]{2,1,0:T(8,128)(2,1)}, u32[]{:S(2)}) copy-start(bf16[1,168,3072]{2,1,0:T(8,128)(2,1)} %param.10) | copy-start | bytes 3096580
  34.6 0.9 copy-start.10
  35.5 17.9 %all-to-all-start.2 = ((bf16[4,816,128]{2,1,0:T(8,128)(2,1)}), bf16[4,816,128]{2,1,0:T(8,128)(2,1)S(1)}, u32[]{:S(2)}, u32[]{:S(2)}) async-start(bf16[4,816,128]{2,1,0:T(8,128)(2,1)} %copy-done.10), calls=%async_computation.2 | async-start | bytes 1671168 | tf_op jit(solution)/shard_map/all_to_all | solution.py:270
  39.2 16.3 %collective-permute-start = (bf16[816,128]{1,0:T(8,128)(2,1)S(1)}, bf16[816,128]{1,0:T(8,128)(2,1)S(1)}, u32[]{:S(2)}, u32[]{:S(2)}) collective-permute-start(bf16[816,128]{1,0:T(8,128)(2,1)S(1)} %get-tuple-element.13), channel_id=1, source_target_pairs={{0,480},{32,448},{64,416},{96,384},{128,352},{160,320},{192,288},{... | collective-permute-start | bytes 626696 | tf_op jit(solution)/shard_map/ppermute | solution.py:292
  47.1 16.8 %collective-permute-start.1 = (bf16[168,3072]{1,0:T(8,128)(2,1)S(1)}, bf16[168,3072]{1,0:T(8,128)(2,1)}, u32[]{:S(2)}, u32[]{:S(2)}) collective-permute-start(bf16[168,3072]{1,0:T(8,128)(2,1)S(1)} %bitcast.10), channel_id=1, source_target_pairs={{0,1},{1,0},{2,3},{3,2},{4,5},{5,4},{6,7},{7,6},{8,9},{9,8},{10,11... | collective-permute-start | bytes 3096584 | tf_op jit(solution)/shard_map/ppermute | solution.py:266
  49.0 14.9 %collective-permute-start.2 = (bf16[168,3072]{1,0:T(8,128)(2,1)S(1)}, bf16[168,3072]{1,0:T(8,128)(2,1)}, u32[]{:S(2)}, u32[]{:S(2)}) collective-permute-start(bf16[168,3072]{1,0:T(8,128)(2,1)S(1)} %bitcast.12), channel_id=1, source_target_pairs={{0,1},{1,0},{2,3},{3,2},{4,5},{5,4},{6,7},{7,6},{8,9},{9,8},{10,11... | collective-permute-start | bytes 3096584 | tf_op jit(solution)/shard_map/ppermute | solution.py:266
  51.4 12.4 %collective-permute-start.3 = (bf16[168,3072]{1,0:T(8,128)(2,1)}, bf16[168,3072]{1,0:T(8,128)(2,1)}, u32[]{:S(2)}, u32[]{:S(2)}) collective-permute-start(bf16[168,3072]{1,0:T(8,128)(2,1)} %bitcast.14), channel_id=1, source_target_pairs={{0,1},{1,0},{2,3},{3,2},{4,5},{5,4},{6,7},{7,6},{8,9},{9,8},{10,11... | collective-permute-start | bytes 3096584 | tf_op jit(solution)/shard_map/ppermute | solution.py:266
  53.4 18.0 %collective-permute-start.5 = (bf16[4,816,128]{2,1,0:T(8,128)(2,1)S(1)}, bf16[4,816,128]{2,1,0:T(8,128)(2,1)}, u32[]{:S(2)}, u32[]{:S(2)}) collective-permute-start(bf16[4,816,128]{2,1,0:T(8,128)(2,1)S(1)} %all-to-all-done.2.x_ref), channel_id=1, source_target_pairs={{0,96},{32,64},{64,32},{96,0},{128,224},{160,192},{192,160},{224,1... | collective-permute-start | bytes 2506760 | tf_op jit(solution)/shard_map/ppermute | solution.py:293
  55.5 20.2 %collective-permute-start.4 = (bf16[4,816,128]{2,1,0:T(8,128)(2,1)S(1)}, bf16[4,816,128]{2,1,0:T(8,128)(2,1)}, u32[]{:S(2)}, u32[]{:S(2)}) collective-permute-start(bf16[4,816,128]{2,1,0:T(8,128)(2,1)S(1)} %all-to-all-done.2.x_ref), channel_id=1, source_target_pairs={{0,384},{32,416},{64,448},{96,480},{128,256},{160,288},{192,320},{... | collective-permute-start | bytes 2506760 | tf_op jit(solution)/shard_map/ppermute | solution.py:293
  59.7 19.4 %all-to-all-start.1 = ((bf16[4,816,128]{2,1,0:T(8,128)(2,1)}), bf16[4,816,128]{2,1,0:T(8,128)(2,1)}, u32[]{:S(2)}, u32[]{:S(2)}) async-start(bf16[4,816,128]{2,1,0:T(8,128)(2,1)} %broadcast_in_dim.3), calls=%async_computation.1 | async-start | bytes 1671168 | tf_op jit(solution)/shard_map/all_to_all | solution.py:270
  63.9 1.2 copy-start.5
  65.1 1.2 copy-start.7
  66.3 1.2 copy-start.8
  69.8 5.9 %copy-start = (bf16[768,3072]{1,0:T(8,128)(2,1)}, bf16[768,3072]{1,0:T(8,128)(2,1)S(1)}, u32[]{:S(2)}) copy-start(bf16[768,3072]{1,0:T(8,128)(2,1)S(1)} %get-tuple-element.14.weights_ref) | copy-start | bytes 14155780
  77.8 1.2 copy-start.2
  79.0 2.3 %copy-start.1 = (bf16[768,3072]{1,0:T(8,128)(2,1)S(1)}, bf16[768,3072]{1,0:T(8,128)(2,1)}, u32[]{:S(2)}) copy-start(bf16[768,3072]{1,0:T(8,128)(2,1)} %copy-done) | copy-start | bytes 14155780
  81.4 1.4 copy-start.3
  88.2 0.8 copy-start.12
  89.0 6.9 %copy-start.9 = (bf16[4,816,128]{2,1,0:T(8,128)(2,1)}, bf16[4,816,128]{2,1,0:T(8,128)(2,1)S(1)}, u32[]{:S(2)}) copy-start(bf16[4,816,128]{2,1,0:T(8,128)(2,1)S(1)} %get-tuple-element.20) | copy-start | bytes 2506756
  89.0 19.4 %collective-permute-start.6 = (bf16[4,816,128]{2,1,0:T(8,128)(2,1)}, bf16[4,816,128]{2,1,0:T(8,128)(2,1)}, u32[]{:S(2)}, u32[]{:S(2)}) collective-permute-start(bf16[4,816,128]{2,1,0:T(8,128)(2,1)} %get-tuple-element.18), channel_id=1, source_target_pairs={{0,96},{32,64},{64,32},{96,0},{128,224},{160,192},{192,160},{224,1... | collective-permute-start | bytes 2506760 | tf_op jit(solution)/shard_map/ppermute | solution.py:306
  93.9 20.4 %collective-permute-start.7 = (bf16[4,816,128]{2,1,0:T(8,128)(2,1)}, bf16[4,816,128]{2,1,0:T(8,128)(2,1)}, u32[]{:S(2)}, u32[]{:S(2)}) collective-permute-start(bf16[4,816,128]{2,1,0:T(8,128)(2,1)} %get-tuple-element.19), channel_id=1, source_target_pairs={{0,384},{32,416},{64,448},{96,480},{128,256},{160,288},{192,320},{... | collective-permute-start | bytes 2506760 | tf_op jit(solution)/shard_map/ppermute | solution.py:306
  95.9 20.6 %all-to-all-start.4 = ((bf16[4,816,128]{2,1,0:T(8,128)(2,1)}), bf16[4,816,128]{2,1,0:T(8,128)(2,1)S(1)}, u32[]{:S(2)}, u32[]{:S(2)}) async-start(bf16[4,816,128]{2,1,0:T(8,128)(2,1)} %copy-done.9), calls=%async_computation.4 | async-start | bytes 1671168 | tf_op jit(solution)/shard_map/all_to_all | solution.py:270
  99.4 1.0 copy-start.13
  116.5 14.7 %all-to-all-start.3 = ((bf16[4,816,128]{2,1,0:T(8,128)(2,1)}), bf16[4,816,128]{2,1,0:T(8,128)(2,1)S(1)}, u32[]{:S(2)}, u32[]{:S(2)}) async-start(bf16[4,816,128]{2,1,0:T(8,128)(2,1)} %shard_map.73), calls=%async_computation.3 | async-start | bytes 1671168 | tf_op jit(solution)/shard_map/all_to_all | solution.py:270
  120.0 17.9 %copy-start.15 = (s32[256,4]{0,1:T(4,128)S(1)}, s32[256,4]{0,1:T(4,128)}, u32[]{:S(2)}) copy-start(s32[256,4]{0,1:T(4,128)} %param.7) | copy-start | bytes 12292
  120.0 17.9 %copy-start.16 = (f32[256,4]{0,1:T(4,128)S(1)}, f32[256,4]{0,1:T(4,128)}, u32[]{:S(2)}) copy-start(f32[256,4]{0,1:T(4,128)} %param.8) | copy-start | bytes 12292
  120.2 11.0 %collective-permute-start.8 = (bf16[816,128]{1,0:T(8,128)(2,1)S(1)}, bf16[816,128]{1,0:T(8,128)(2,1)S(1)}, u32[]{:S(2)}, u32[]{:S(2)}) collective-permute-start(bf16[816,128]{1,0:T(8,128)(2,1)S(1)} %shard_map.74), channel_id=1, source_target_pairs={{0,480},{32,448},{64,416},{96,384},{128,352},{160,320},{192,288},{... | collective-permute-start | bytes 626696 | tf_op jit(solution)/shard_map/ppermute | solution.py:308
  132.1 19.6 %all-to-all-start.5 = ((bf16[16,56,128]{2,1,0:T(8,128)(2,1)}), bf16[16,56,128]{2,1,0:T(8,128)(2,1)S(1)}, u32[]{:S(2)}, u32[]{:S(2)}) async-start(bf16[16,56,128]{2,1,0:T(8,128)(2,1)} %bitcast.6), calls=%async_computation.5 | async-start | bytes 458752 | tf_op jit(solution)/shard_map/all_to_all | solution.py:270

commit v9 on v7

--- a/solution.py
+++ b/solution.py
@@ -24,8 +24,8 @@
 BF16 = jnp.bfloat16
 
 
-def quarter(y, x, core):
-    a, b = (y + core) % SIZE, (x + core) % SIZE
+def quarter(y, x, cut):
+    a, b = (y + cut) % SIZE, (x + cut) % SIZE
     return a // 2 * 2 + b // 2, a % 2 * 2 + b % 2
 
 
@@ -33,23 +33,24 @@
     return (y % SIZE * SIZE + x % SIZE) * 2 + core
 
 
-def quarter_groups():
+def quarter_groups(back):
     groups = {}
     for core in range(2):
         for y in range(SIZE):
             for x in range(SIZE):
-                q, at = quarter(y, x, core)
+                q, at = quarter(y, x, core ^ back)
                 groups.setdefault((core, q), [0] * 4)[at] = device(y, x, core)
     return [groups[key] for key in sorted(groups)]
 
 
-def across(mask):
+def across(mask, back):
     pairs = []
     for core in range(2):
+        cut = core ^ back
         for y in range(SIZE):
             for x in range(SIZE):
-                up = y + 1 if (y + core) % 2 else y - 1
-                right = x + 1 if (x + core) % 2 else x - 1
+                up = y + 1 if (y + cut) % 2 else y - 1
+                right = x + 1 if (x + cut) % 2 else x - 1
                 pairs.append((device(y, x, core), device(up if mask & 2 else y, right if mask & 1 else x, core)))
     return pairs
 
@@ -130,13 +131,13 @@
             out_ref[at + start + hidden : at + end, :] = jnp.zeros((end - start - hidden, width), BF16)
 
 
-def place_of():
-    core, dp = lax.axis_index("tensor"), lax.axis_index("dp")
-    return core, quarter(dp // SIZE, dp % SIZE, core)[0]
+def place_of(back):
+    cut, dp = lax.axis_index("tensor") ^ back, lax.axis_index("dp")
+    return cut, quarter(dp // SIZE, dp % SIZE, cut)[0]
 
 
 def products(mask, x_ref, weights_ref):
-    _, q = place_of()
+    _, q = place_of(0)
     q = q ^ mask
     low = iota((SIDE, LANES), 1) < HLANES
     main = jnp.concatenate([x_ref[at, : 2 * SIDE, :] for at in range(4)], axis=1)
@@ -154,11 +155,11 @@
 
 
 def down_products(mask, hidden, down_ref, out_ref):
-    core, q = place_of()
+    cut, q = place_of(1)
     to = q ^ mask
     low = iota((SIDE, LANES), 1) < HLANES
     for at in range(4):
-        dp = (to // 2 * 2 + at // 2 - core) % SIZE * SIZE + (to % 2 * 2 + at % 2 - core) % SIZE
+        dp = (to // 2 * 2 + at // 2 - cut) % SIZE * SIZE + (to % 2 * 2 + at % 2 - cut) % SIZE
         odd = dp % 2 == 1
         y = dot(hidden, down_ref[:, pl.ds(pl.multiple_of((dp * 3 - dp % 2) // 2 * LANES, LANES), 2 * LANES)])
         first, second = y[:, :LANES], y[:, LANES:]
@@ -261,7 +262,7 @@
 
 def shards(tokens, expert_ids, gate_values, w_gate, w_up, w_down):
     n, width = tokens.shape
-    plane, inside = ("dp", "tensor"), quarter_groups()
+    plane = ("dp", "tensor")
     ids, gates = expert_ids.T, gate_values.T
     own = [w_gate[0], w_up[0], w_down[0]]
     weights, down = call(
@@ -274,8 +275,8 @@
     sent = call(dispatch_kernel, (EXPERTS * BLOCK, LANES), ids, tokens)
     arrived = exchange(sent.reshape(EXPERTS, BLOCK, LANES), "expert").reshape(EXPERTS * BLOCK, LANES)
     rows = call(pack_kernel, (4, PART, LANES), arrived, scratch=[block_scratch, part_scratch])
-    rows = exchange(rows, plane, inside)
-    others = [lax.ppermute(rows, plane, across(mask)) for mask in MASKS]
+    rows = exchange(rows, plane, quarter_groups(0))
+    others = [lax.ppermute(rows, plane, across(mask, 0)) for mask in MASKS]
     total_shape, out_shape = ((2 * SIDE, 2 * WIDE), F32), ((4, PART, LANES), BF16)
     (total,) = call(functools.partial(first_kernel, 0), [total_shape], rows, weights, limit=32)
     for mask, other in zip(MASKS[:2], others[:2]):
@@ -287,10 +288,10 @@
         limit=32,
     )
     (partial,) = call(functools.partial(down_kernel, 0), [out_shape], held(hidden), down, limit=32)
-    others = [lax.ppermute(out, plane, across(mask)) for mask, out in zip(MASKS, outs)]
+    others = [lax.ppermute(out, plane, across(mask, 1)) for mask, out in zip(MASKS, outs)]
     for other, kind in zip(others, (F32, F32, BF16)):
         (partial,) = call(add_kernel, [((4, PART, LANES), kind)], held(partial), other, limit=24)
-    partial = exchange(partial, plane, inside)
+    partial = exchange(partial, plane, quarter_groups(1))
     summed = call(add_blocks_kernel, (EXPERTS * BLOCK, LANES), partial, scratch=[part_scratch, block_scratch])
     back = exchange(summed.reshape(EXPERTS, BLOCK, LANES), "expert").reshape(EXPERTS * BLOCK, LANES)
     (factors,) = call(gates_kernel, [((3, EXPERTS * BLOCK, 3 * n), BF16)], ids, gates)

time: 144 us -> 141 us (0.979)
  waiting for transfers between devices: 59.2 us -> 54.9 us
  blocking collectives: 10.8 us -> 13.9 us
  starting transfers between devices: 54.2 us -> 51.9 us
    ppermute x6, waiting for transfers between devices: 27.5 us -> 23.1 us  [the longest x3 13.8 us: shards(): lax.ppermute(out, plane, across(mask, 1))]
    all_to_all x1, blocking collectives: 10.8 us -> 13.9 us  [exchange(): lax.all_to_all(value, axis, split_axis=0, concat_axis=0, tiled=True, axis...]
    ppermute x6, starting transfers between devices: 23.3 us -> 20.8 us  [the longest x3 11.6 us: shards(): others = [lax.ppermute(rows, plane, across(mask, 0)) for mask in MASKS]]
where the time goes in v9:
time: 141 us; the launch traced here: 139 us
  waiting for transfers between devices  54.9 us (39%)
  starting transfers between devices  51.9 us (37%)
  Pallas kernels  15 us (11%)
  blocking collectives  13.9 us (10%)
  local copies, waits for them, and re-layouts  3.05 us (2%)
    all_to_all x3, waiting for transfers between devices, exchange(): lax.all_to_all(value, axis, split_axis=0, concat_axis=0, tiled=True, axis...  31.9 us
    all_to_all x3, starting transfers between devices, exchange(): lax.all_to_all(value, axis, split_axis=0, concat_axis=0, tiled=True, axis...  24.9 us
    pallas_call x14, Pallas kernels, call(): pl.pallas_call(kernel, out_shape=out, scratch_shapes=scratch, compiler_pa...  15 us
    all_to_all x1, blocking collectives, exchange(): lax.all_to_all(value, axis, split_axis=0, concat_axis=0, tiled=True, axis...  13.9 us
    ppermute x3, waiting for transfers between devices, shards(): lax.ppermute(out, plane, across(mask, 1))  13.8 us
    ppermute x3, starting transfers between devices, shards(): others = [lax.ppermute(rows, plane, across(mask, 0)) for mask in MASKS]  11.6 us
    ppermute x3, waiting for transfers between devices, shards(): others = [lax.ppermute(rows, plane, across(mask, 0)) for mask in MASKS]  9.3 us
    ppermute x3, starting transfers between devices, shards(): lax.ppermute(out, plane, across(mask, 1))  9.21 us
  transfers between devices with their start and end apart: 12, of which 8 were waited for; matrix products, arithmetic and copies ran while one was open for 0% of the time, Pallas kernels for 6%

profile of v9, /device:TPU:6, one launch (start us, length us, event | category | flops | bytes accessed | tf_op | source)
XLA Modules:
  0.0 139.1 jit_solution(12755751431725151295)
XLA Ops:
  0.0 1.1 copy-done.3
  1.1 0.7 copy-done.4
  1.8 1.4 shard_map.64
  3.2 15.3 %all-to-all-start = ((bf16[16,56,128]{2,1,0:T(8,128)(2,1)}), bf16[16,56,128]{2,1,0:T(8,128)(2,1)S(1)}, u32[]{:S(2)}, u32[]{:S(2)}) async-start(bf16[16,56,128]{2,1,0:T(8,128)(2,1)} %bitcast.1), calls=%async_computation | async-start | bytes 458752 | tf_op jit(solution)/shard_map/all_to_all | solution.py:260
  18.5 1.9 %collective-permute-start.1 = (bf16[168,3072]{1,0:T(8,128)(2,1)}, bf16[168,3072]{1,0:T(8,128)(2,1)}, u32[]{:S(2)}, u32[]{:S(2)}) collective-permute-start(bf16[168,3072]{1,0:T(8,128)(2,1)} %bitcast.10), channel_id=1, source_target_pairs={{0,1},{1,0},{2,3},{3,2},{4,5},{5,4},{6,7},{7,6},{8,9},{9,8},{10,11... | collective-permute-start | bytes 3096584 | tf_op jit(solution)/shard_map/ppermute | solution.py:256
  20.5 15.5 %all-to-all-done = bf16[16,56,128]{2,1,0:T(8,128)(2,1)S(1)} async-done(((bf16[16,56,128]{2,1,0:T(8,128)(2,1)}), bf16[16,56,128]{2,1,0:T(8,128)(2,1)S(1)}, u32[]{:S(2)}, u32[]{:S(2)}) %all-to-all-start) | async-done | bytes 229408 | tf_op jit(solution)/shard_map/all_to_all | solution.py:260
  35.9 1.0 shard_map.65
  37.0 4.3 %all-to-all-start.1 = ((bf16[4,816,128]{2,1,0:T(8,128)(2,1)}), bf16[4,816,128]{2,1,0:T(8,128)(2,1)S(1)}, u32[]{:S(2)}, u32[]{:S(2)}) async-start(bf16[4,816,128]{2,1,0:T(8,128)(2,1)} %shard_map.65), calls=%async_computation.1 | async-start | bytes 1671168 | tf_op jit(solution)/shard_map/all_to_all | solution.py:260
  41.3 0.0 copy-done.1
  41.3 1.9 %collective-permute-start.2 = (bf16[168,3072]{1,0:T(8,128)(2,1)S(1)}, bf16[168,3072]{1,0:T(8,128)(2,1)}, u32[]{:S(2)}, u32[]{:S(2)}) collective-permute-start(bf16[168,3072]{1,0:T(8,128)(2,1)S(1)} %bitcast.12), channel_id=1, source_target_pairs={{0,1},{1,0},{2,3},{3,2},{4,5},{5,4},{6,7},{7,6},{8,9},{9,8},{10,11... | collective-permute-start | bytes 3096584 | tf_op jit(solution)/shard_map/ppermute | solution.py:256
  43.2 2.4 %collective-permute-start.3 = (bf16[168,3072]{1,0:T(8,128)(2,1)}, bf16[168,3072]{1,0:T(8,128)(2,1)}, u32[]{:S(2)}, u32[]{:S(2)}) collective-permute-start(bf16[168,3072]{1,0:T(8,128)(2,1)} %bitcast.14), channel_id=1, source_target_pairs={{0,1},{1,0},{2,3},{3,2},{4,5},{5,4},{6,7},{7,6},{8,9},{9,8},{10,11... | collective-permute-start | bytes 3096584 | tf_op jit(solution)/shard_map/ppermute | solution.py:256
  45.6 3.4 %all-to-all-done.1.x_ref = bf16[4,816,128]{2,1,0:T(8,128)(2,1)S(1)} async-done(((bf16[4,816,128]{2,1,0:T(8,128)(2,1)}), bf16[4,816,128]{2,1,0:T(8,128)(2,1)S(1)}, u32[]{:S(2)}, u32[]{:S(2)}) %all-to-all-start.1) | async-done | bytes 835616 | tf_op jit(solution)/shard_map/all_to_all | solution.py:260
  48.9 4.8 %collective-permute-start.5 = (bf16[4,816,128]{2,1,0:T(8,128)(2,1)S(1)}, bf16[4,816,128]{2,1,0:T(8,128)(2,1)S(1)}, u32[]{:S(2)}, u32[]{:S(2)}) collective-permute-start(bf16[4,816,128]{2,1,0:T(8,128)(2,1)S(1)} %all-to-all-done.1.x_ref), channel_id=1, source_target_pairs={{0,480},{32,448},{64,416},{96,384},{128,352},{160,320},{192,288},{... | collective-permute-start | bytes 2506760 | tf_op jit(solution)/shard_map/ppermute | solution.py:279
  53.7 4.0 %collective-permute-start.4 = (bf16[4,816,128]{2,1,0:T(8,128)(2,1)S(1)}, bf16[4,816,128]{2,1,0:T(8,128)(2,1)S(1)}, u32[]{:S(2)}, u32[]{:S(2)}) collective-permute-start(bf16[4,816,128]{2,1,0:T(8,128)(2,1)S(1)} %all-to-all-done.1.x_ref), channel_id=1, source_target_pairs={{0,96},{32,64},{64,32},{96,0},{128,224},{160,192},{192,160},{224,1... | collective-permute-start | bytes 2506760 | tf_op jit(solution)/shard_map/ppermute | solution.py:279
  57.7 0.0 collective-permute-done.1.gate1
  57.7 2.9 %collective-permute-start = (bf16[4,816,128]{2,1,0:T(8,128)(2,1)S(1)}, bf16[4,816,128]{2,1,0:T(8,128)(2,1)S(1)}, u32[]{:S(2)}, u32[]{:S(2)}) collective-permute-start(bf16[4,816,128]{2,1,0:T(8,128)(2,1)S(1)} %all-to-all-done.1.x_ref), channel_id=1, source_target_pairs={{0,384},{32,416},{64,448},{96,480},{128,256},{160,288},{192,320},{... | collective-permute-start | bytes 2506760 | tf_op jit(solution)/shard_map/ppermute | solution.py:279
  60.6 0.0 collective-permute-done.2.up1
  60.6 0.0 collective-permute-done.3.down1
  60.6 0.0 copy-done
  60.6 0.0 copy-start.2
  60.6 1.2 copy-done.2
  61.9 2.3 %shard_map.66 = (bf16[768,3072]{1,0:T(8,128)(2,1)S(1)}, bf16[384,3072]{1,0:T(8,128)(2,1)S(1)}) custom-call(bf16[168,3072]{1,0:T(8,128)(2,1)S(1)} %bitcast.11, bf16[168,3072]{1,0:T(8,128)(2,1)S(1)} %bitcast.13, bf16[168,3072]{1,0:T(8,128)(2,1)S(1)} %bitcast.15, bf16[168,3072]{1,0:T(8,128)(2,1)} %collective-permute-done.1.gate1, ...), custom_call_target="tpu_custom_call" | custom-call | tf_op jit(solution)/shard_map/pallas_call | solution.py:243
  64.2 0.9 shard_map.67.sofar_ref
  65.1 1.7 %collective-permute-done.5.x_ref = bf16[4,816,128]{2,1,0:T(8,128)(2,1)S(1)} collective-permute-done((bf16[4,816,128]{2,1,0:T(8,128)(2,1)S(1)}, bf16[4,816,128]{2,1,0:T(8,128)(2,1)S(1)}, u32[]{:S(2)}, u32[]{:S(2)}) %collective-permute-start.5) | collective-permute-done | bytes 835616 | tf_op jit(solution)/shard_map/ppermute | solution.py:279
  66.8 0.9 shard_map.68.sofar_ref
  67.7 7.6 %collective-permute-done.4.x_ref = bf16[4,816,128]{2,1,0:T(8,128)(2,1)S(1)} collective-permute-done((bf16[4,816,128]{2,1,0:T(8,128)(2,1)S(1)}, bf16[4,816,128]{2,1,0:T(8,128)(2,1)S(1)}, u32[]{:S(2)}, u32[]{:S(2)}) %collective-permute-start.4) | collective-permute-done | bytes 835616 | tf_op jit(solution)/shard_map/ppermute | solution.py:279
  75.3 0.9 shard_map.69.sofar_ref
  76.2 0.0 collective-permute-done.x_ref
  76.2 3.3 %shard_map.70 = (bf16[544,384]{1,0:T(8,128)(2,1)S(1)}, bf16[4,816,128]{2,1,0:T(8,128)(2,1)S(1)}, bf16[4,816,128]{2,1,0:T(8,128)(2,1)S(1)}, bf16[4,816,128]{2,1,0:T(8,128)(2,1)S(1)}) custom-call(bf16[4,816,128]{2,1,0:T(8,128)(2,1)S(1)} %collective-permute-done.x_ref, bf16[768,3072]{1,0:T(8,128)(2,1)S(1)} %get-tuple-element.11.weights_ref, ...), custom_call_target="tpu_custom_call" | custom-call | tf_op jit(solution)/shard_map/pallas_call | solution.py:243
  79.5 1.9 %collective-permute-start.6 = (bf16[4,816,128]{2,1,0:T(8,128)(2,1)S(1)}, bf16[4,816,128]{2,1,0:T(8,128)(2,1)S(1)}, u32[]{:S(2)}, u32[]{:S(2)}) collective-permute-start(bf16[4,816,128]{2,1,0:T(8,128)(2,1)S(1)} %get-tuple-element.14), channel_id=1, source_target_pairs={{0,160},{32,128},{64,224},{96,192},{128,32},{160,0},{192,96},{224,... | collective-permute-start | bytes 2506760 | tf_op jit(solution)/shard_map/ppermute | solution.py:291
  81.5 4.2 %collective-permute-start.7 = (bf16[4,816,128]{2,1,0:T(8,128)(2,1)S(1)}, bf16[4,816,128]{2,1,0:T(8,128)(2,1)S(1)}, u32[]{:S(2)}, u32[]{:S(2)}) collective-permute-start(bf16[4,816,128]{2,1,0:T(8,128)(2,1)S(1)} %get-tuple-element.15), channel_id=1, source_target_pairs={{0,32},{32,0},{64,96},{96,64},{128,160},{160,128},{192,224},{224,1... | collective-permute-start | bytes 2506760 | tf_op jit(solution)/shard_map/ppermute | solution.py:291
  85.7 3.1 %collective-permute-start.8 = (bf16[4,816,128]{2,1,0:T(8,128)(2,1)S(1)}, bf16[4,816,128]{2,1,0:T(8,128)(2,1)S(1)}, u32[]{:S(2)}, u32[]{:S(2)}) collective-permute-start(bf16[4,816,128]{2,1,0:T(8,128)(2,1)S(1)} %get-tuple-element.16), channel_id=1, source_target_pairs={{0,128},{32,160},{64,192},{96,224},{128,0},{160,32},{192,64},{224,... | collective-permute-start | bytes 2506760 | tf_op jit(solution)/shard_map/ppermute | solution.py:291
  88.8 0.9 shard_map.71.a
  89.7 5.3 %collective-permute-done.6.b = bf16[4,816,128]{2,1,0:T(8,128)(2,1)S(1)} collective-permute-done((bf16[4,816,128]{2,1,0:T(8,128)(2,1)S(1)}, bf16[4,816,128]{2,1,0:T(8,128)(2,1)S(1)}, u32[]{:S(2)}, u32[]{:S(2)}) %collective-permute-start.6) | collective-permute-done | bytes 835616 | tf_op jit(solution)/shard_map/ppermute | solution.py:291
  94.9 0.2 shard_map.72.a
  95.1 8.2 %collective-permute-done.7.b = bf16[4,816,128]{2,1,0:T(8,128)(2,1)S(1)} collective-permute-done((bf16[4,816,128]{2,1,0:T(8,128)(2,1)S(1)}, bf16[4,816,128]{2,1,0:T(8,128)(2,1)S(1)}, u32[]{:S(2)}, u32[]{:S(2)}) %collective-permute-start.7) | collective-permute-done | bytes 835616 | tf_op jit(solution)/shard_map/ppermute | solution.py:291
  103.3 0.2 shard_map.73.a
  103.5 0.3 collective-permute-done.8.b
  103.8 0.2 shard_map.74
  104.0 0.0 copy-start.5
  104.0 0.0 copy-start.6
  104.0 13.9 %all_to_all.20.parts_ref = bf16[4,816,128]{2,1,0:T(8,128)(2,1)S(1)} all-to-all(bf16[4,816,128]{2,1,0:T(8,128)(2,1)S(1)} %shard_map.74), channel_id=1, replica_groups={{480,384,96,0},{416,448,32,64},{224,128,352,256},{160,192,288,320},{1,3..., dimensions={0} | all-to-all | bytes 1671168 | tf_op jit(solution)/shard_map/all_to_all | solution.py:260
  117.9 0.9 shard_map.75
  118.8 5.2 %all-to-all-start.3 = ((bf16[16,56,128]{2,1,0:T(8,128)(2,1)}), bf16[16,56,128]{2,1,0:T(8,128)(2,1)S(1)}, u32[]{:S(2)}, u32[]{:S(2)}) async-start(bf16[16,56,128]{2,1,0:T(8,128)(2,1)} %bitcast.6), calls=%async_computation.3 | async-start | bytes 458752 | tf_op jit(solution)/shard_map/all_to_all | solution.py:260
  124.1 0.0 copy-done.5
  124.1 0.8 shard_map.76.gates_ref
  124.8 13.0 %all-to-all-done.3 = bf16[16,56,128]{2,1,0:T(8,128)(2,1)S(1)} async-done(((bf16[16,56,128]{2,1,0:T(8,128)(2,1)}), bf16[16,56,128]{2,1,0:T(8,128)(2,1)S(1)}, u32[]{:S(2)}, u32[]{:S(2)}) %all-to-all-start.3) | async-done | bytes 229408 | tf_op jit(solution)/shard_map/all_to_all | solution.py:260
  137.9 1.2 shard_map.77
  (5 shorter events, 0.0 us)
Async XLA Ops:
  0.0 1.1 copy-start.3
  1.1 0.7 copy-start.4
  3.2 38.1 %copy-start.1 = (bf16[1,168,3072]{2,1,0:T(8,128)(2,1)S(1)}, bf16[1,168,3072]{2,1,0:T(8,128)(2,1)}, u32[]{:S(2)}) copy-start(bf16[1,168,3072]{2,1,0:T(8,128)(2,1)} %param.10) | copy-start | bytes 3096580
  3.2 57.4 %copy-start = (bf16[1,168,3072]{2,1,0:T(8,128)(2,1)S(1)}, bf16[1,168,3072]{2,1,0:T(8,128)(2,1)}, u32[]{:S(2)}) copy-start(bf16[1,168,3072]{2,1,0:T(8,128)(2,1)} %param.9) | copy-start | bytes 3096580
  3.2 32.7 %all-to-all-start = ((bf16[16,56,128]{2,1,0:T(8,128)(2,1)}), bf16[16,56,128]{2,1,0:T(8,128)(2,1)S(1)}, u32[]{:S(2)}, u32[]{:S(2)}) async-start(bf16[16,56,128]{2,1,0:T(8,128)(2,1)} %bitcast.1), calls=%async_computation | async-start | bytes 458752 | tf_op jit(solution)/shard_map/all_to_all | solution.py:260
  18.5 39.2 %collective-permute-start.1 = (bf16[168,3072]{1,0:T(8,128)(2,1)}, bf16[168,3072]{1,0:T(8,128)(2,1)}, u32[]{:S(2)}, u32[]{:S(2)}) collective-permute-start(bf16[168,3072]{1,0:T(8,128)(2,1)} %bitcast.10), channel_id=1, source_target_pairs={{0,1},{1,0},{2,3},{3,2},{4,5},{5,4},{6,7},{7,6},{8,9},{9,8},{10,11... | collective-permute-start | bytes 3096584 | tf_op jit(solution)/shard_map/ppermute | solution.py:256
  37.0 12.0 %all-to-all-start.1 = ((bf16[4,816,128]{2,1,0:T(8,128)(2,1)}), bf16[4,816,128]{2,1,0:T(8,128)(2,1)S(1)}, u32[]{:S(2)}, u32[]{:S(2)}) async-start(bf16[4,816,128]{2,1,0:T(8,128)(2,1)} %shard_map.65), calls=%async_computation.1 | async-start | bytes 1671168 | tf_op jit(solution)/shard_map/all_to_all | solution.py:260
  41.3 19.3 %collective-permute-start.2 = (bf16[168,3072]{1,0:T(8,128)(2,1)S(1)}, bf16[168,3072]{1,0:T(8,128)(2,1)}, u32[]{:S(2)}, u32[]{:S(2)}) collective-permute-start(bf16[168,3072]{1,0:T(8,128)(2,1)S(1)} %bitcast.12), channel_id=1, source_target_pairs={{0,1},{1,0},{2,3},{3,2},{4,5},{5,4},{6,7},{7,6},{8,9},{9,8},{10,11... | collective-permute-start | bytes 3096584 | tf_op jit(solution)/shard_map/ppermute | solution.py:256
  43.2 17.4 %collective-permute-start.3 = (bf16[168,3072]{1,0:T(8,128)(2,1)}, bf16[168,3072]{1,0:T(8,128)(2,1)}, u32[]{:S(2)}, u32[]{:S(2)}) collective-permute-start(bf16[168,3072]{1,0:T(8,128)(2,1)} %bitcast.14), channel_id=1, source_target_pairs={{0,1},{1,0},{2,3},{3,2},{4,5},{5,4},{6,7},{7,6},{8,9},{9,8},{10,11... | collective-permute-start | bytes 3096584 | tf_op jit(solution)/shard_map/ppermute | solution.py:256
  48.9 17.8 %collective-permute-start.5 = (bf16[4,816,128]{2,1,0:T(8,128)(2,1)S(1)}, bf16[4,816,128]{2,1,0:T(8,128)(2,1)S(1)}, u32[]{:S(2)}, u32[]{:S(2)}) collective-permute-start(bf16[4,816,128]{2,1,0:T(8,128)(2,1)S(1)} %all-to-all-done.1.x_ref), channel_id=1, source_target_pairs={{0,480},{32,448},{64,416},{96,384},{128,352},{160,320},{192,288},{... | collective-permute-start | bytes 2506760 | tf_op jit(solution)/shard_map/ppermute | solution.py:279
  53.7 21.5 %collective-permute-start.4 = (bf16[4,816,128]{2,1,0:T(8,128)(2,1)S(1)}, bf16[4,816,128]{2,1,0:T(8,128)(2,1)S(1)}, u32[]{:S(2)}, u32[]{:S(2)}) collective-permute-start(bf16[4,816,128]{2,1,0:T(8,128)(2,1)S(1)} %all-to-all-done.1.x_ref), channel_id=1, source_target_pairs={{0,96},{32,64},{64,32},{96,0},{128,224},{160,192},{192,160},{224,1... | collective-permute-start | bytes 2506760 | tf_op jit(solution)/shard_map/ppermute | solution.py:279
  57.7 18.4 %collective-permute-start = (bf16[4,816,128]{2,1,0:T(8,128)(2,1)S(1)}, bf16[4,816,128]{2,1,0:T(8,128)(2,1)S(1)}, u32[]{:S(2)}, u32[]{:S(2)}) collective-permute-start(bf16[4,816,128]{2,1,0:T(8,128)(2,1)S(1)} %all-to-all-done.1.x_ref), channel_id=1, source_target_pairs={{0,384},{32,416},{64,448},{96,480},{128,256},{160,288},{192,320},{... | collective-permute-start | bytes 2506760 | tf_op jit(solution)/shard_map/ppermute | solution.py:279
  60.6 1.2 copy-start.2
  79.5 15.4 %collective-permute-start.6 = (bf16[4,816,128]{2,1,0:T(8,128)(2,1)S(1)}, bf16[4,816,128]{2,1,0:T(8,128)(2,1)S(1)}, u32[]{:S(2)}, u32[]{:S(2)}) collective-permute-start(bf16[4,816,128]{2,1,0:T(8,128)(2,1)S(1)} %get-tuple-element.14), channel_id=1, source_target_pairs={{0,160},{32,128},{64,224},{96,192},{128,32},{160,0},{192,96},{224,... | collective-permute-start | bytes 2506760 | tf_op jit(solution)/shard_map/ppermute | solution.py:291
  81.5 21.8 %collective-permute-start.7 = (bf16[4,816,128]{2,1,0:T(8,128)(2,1)S(1)}, bf16[4,816,128]{2,1,0:T(8,128)(2,1)S(1)}, u32[]{:S(2)}, u32[]{:S(2)}) collective-permute-start(bf16[4,816,128]{2,1,0:T(8,128)(2,1)S(1)} %get-tuple-element.15), channel_id=1, source_target_pairs={{0,32},{32,0},{64,96},{96,64},{128,160},{160,128},{192,224},{224,1... | collective-permute-start | bytes 2506760 | tf_op jit(solution)/shard_map/ppermute | solution.py:291
  85.7 18.1 %collective-permute-start.8 = (bf16[4,816,128]{2,1,0:T(8,128)(2,1)S(1)}, bf16[4,816,128]{2,1,0:T(8,128)(2,1)S(1)}, u32[]{:S(2)}, u32[]{:S(2)}) collective-permute-start(bf16[4,816,128]{2,1,0:T(8,128)(2,1)S(1)} %get-tuple-element.16), channel_id=1, source_target_pairs={{0,128},{32,160},{64,192},{96,224},{128,0},{160,32},{192,64},{224,... | collective-permute-start | bytes 2506760 | tf_op jit(solution)/shard_map/ppermute | solution.py:291
  104.0 20.1 %copy-start.5 = (s32[256,4]{0,1:T(4,128)S(1)}, s32[256,4]{0,1:T(4,128)}, u32[]{:S(2)}) copy-start(s32[256,4]{0,1:T(4,128)} %param.7) | copy-start | bytes 12292
  104.0 20.1 %copy-start.6 = (f32[256,4]{0,1:T(4,128)S(1)}, f32[256,4]{0,1:T(4,128)}, u32[]{:S(2)}) copy-start(f32[256,4]{0,1:T(4,128)} %param.8) | copy-start | bytes 12292
  118.8 19.1 %all-to-all-start.3 = ((bf16[16,56,128]{2,1,0:T(8,128)(2,1)}), bf16[16,56,128]{2,1,0:T(8,128)(2,1)S(1)}, u32[]{:S(2)}, u32[]{:S(2)}) async-start(bf16[16,56,128]{2,1,0:T(8,128)(2,1)} %bitcast.6), calls=%async_computation.3 | async-start | bytes 458752 | tf_op jit(solution)/shard_map/all_to_all | solution.py:260

commit v10 on v9

--- a/solution.py
+++ b/solution.py
@@ -33,20 +33,20 @@
     return (y % SIZE * SIZE + x % SIZE) * 2 + core
 
 
-def quarter_groups(back):
+def quarter_groups():
     groups = {}
     for core in range(2):
         for y in range(SIZE):
             for x in range(SIZE):
-                q, at = quarter(y, x, core ^ back)
+                q, at = quarter(y, x, 1 - core)
                 groups.setdefault((core, q), [0] * 4)[at] = device(y, x, core)
     return [groups[key] for key in sorted(groups)]
 
 
-def across(mask, back):
+def across(mask):
     pairs = []
     for core in range(2):
-        cut = core ^ back
+        cut = 1 - core
         for y in range(SIZE):
             for x in range(SIZE):
                 up = y + 1 if (y + cut) % 2 else y - 1
@@ -93,7 +93,7 @@
 def dispatch_kernel(ids_ref, tokens_ref, out_ref):
     n = tokens_ref.shape[0]
     core, dp = lax.axis_index("tensor"), lax.axis_index("dp")
-    q, at = quarter(dp // SIZE, dp % SIZE, core)
+    q, at = quarter(dp // SIZE, dp % SIZE, 1 - core)
     part = 4 * q + at
     picks, _ = slot_picks(ids_ref[:, pl.ds(pl.multiple_of(core * n, n), n)])
     picks = jnp.concatenate([p.astype(BF16) for p in picks], axis=1)
@@ -131,13 +131,13 @@
             out_ref[at + start + hidden : at + end, :] = jnp.zeros((end - start - hidden, width), BF16)
 
 
-def place_of(back):
-    cut, dp = lax.axis_index("tensor") ^ back, lax.axis_index("dp")
+def place_of():
+    cut, dp = 1 - lax.axis_index("tensor"), lax.axis_index("dp")
     return cut, quarter(dp // SIZE, dp % SIZE, cut)[0]
 
 
 def products(mask, x_ref, weights_ref):
-    _, q = place_of(0)
+    _, q = place_of()
     q = q ^ mask
     low = iota((SIDE, LANES), 1) < HLANES
     main = jnp.concatenate([x_ref[at, : 2 * SIDE, :] for at in range(4)], axis=1)
@@ -155,7 +155,7 @@
 
 
 def down_products(mask, hidden, down_ref, out_ref):
-    cut, q = place_of(1)
+    cut, q = place_of()
     to = q ^ mask
     low = iota((SIDE, LANES), 1) < HLANES
     for at in range(4):
@@ -275,8 +275,8 @@
     sent = call(dispatch_kernel, (EXPERTS * BLOCK, LANES), ids, tokens)
     arrived = exchange(sent.reshape(EXPERTS, BLOCK, LANES), "expert").reshape(EXPERTS * BLOCK, LANES)
     rows = call(pack_kernel, (4, PART, LANES), arrived, scratch=[block_scratch, part_scratch])
-    rows = exchange(rows, plane, quarter_groups(0))
-    others = [lax.ppermute(rows, plane, across(mask, 0)) for mask in MASKS]
+    rows = exchange(rows, plane, quarter_groups())
+    others = [lax.ppermute(rows, plane, across(mask)) for mask in MASKS]
     total_shape, out_shape = ((2 * SIDE, 2 * WIDE), F32), ((4, PART, LANES), BF16)
     (total,) = call(functools.partial(first_kernel, 0), [total_shape], rows, weights, limit=32)
     for mask, other in zip(MASKS[:2], others[:2]):
@@ -288,10 +288,10 @@
         limit=32,
     )
     (partial,) = call(functools.partial(down_kernel, 0), [out_shape], held(hidden), down, limit=32)
-    others = [lax.ppermute(out, plane, across(mask, 1)) for mask, out in zip(MASKS, outs)]
+    others = [lax.ppermute(out, plane, across(mask)) for mask, out in zip(MASKS, outs)]
     for other, kind in zip(others, (F32, F32, BF16)):
         (partial,) = call(add_kernel, [((4, PART, LANES), kind)], held(partial), other, limit=24)
-    partial = exchange(partial, plane, quarter_groups(1))
+    partial = exchange(partial, plane, quarter_groups())
     summed = call(add_blocks_kernel, (EXPERTS * BLOCK, LANES), partial, scratch=[part_scratch, block_scratch])
     back = exchange(summed.reshape(EXPERTS, BLOCK, LANES), "expert").reshape(EXPERTS * BLOCK, LANES)
     (factors,) = call(gates_kernel, [((3, EXPERTS * BLOCK, 3 * n), BF16)], ids, gates)

time: 141 us -> 142 us (level)
    ppermute x6, starting transfers between devices: 20.8 us -> 18.4 us  [the longest x3 9.21 us: shards(): lax.ppermute(out, plane, across(mask))]
    all_to_all x3, starting transfers between devices: 24.9 us -> 27.2 us  [exchange(): lax.all_to_all(value, axis, split_axis=0, concat_axis=0, tiled=True, axis...]
where the time goes in v10:
time: 142 us; the launch traced here: 139 us
  waiting for transfers between devices  55.9 us (39%)
  starting transfers between devices  51.8 us (36%)
  Pallas kernels  15 us (11%)
  blocking collectives  13.2 us (9%)
  local copies, waits for them, and re-layouts  3.05 us (2%)
    all_to_all x3, waiting for transfers between devices, exchange(): lax.all_to_all(value, axis, split_axis=0, concat_axis=0, tiled=True, axis...  33.1 us
    all_to_all x3, starting transfers between devices, exchange(): lax.all_to_all(value, axis, split_axis=0, concat_axis=0, tiled=True, axis...  27.2 us
    pallas_call x14, Pallas kernels, call(): pl.pallas_call(kernel, out_shape=out, scratch_shapes=scratch, compiler_pa...  15 us
    ppermute x3, waiting for transfers between devices, shards(): lax.ppermute(out, plane, across(mask))  14.1 us
    all_to_all x1, blocking collectives, exchange(): lax.all_to_all(value, axis, split_axis=0, concat_axis=0, tiled=True, axis...  13.2 us
    ppermute x3, starting transfers between devices, shards(): lax.ppermute(out, plane, across(mask))  9.21 us
    ppermute x3, starting transfers between devices, shards(): others = [lax.ppermute(rows, plane, across(mask)) for mask in MASKS]  9.2 us
    ppermute x3, waiting for transfers between devices, shards(): others = [lax.ppermute(rows, plane, across(mask)) for mask in MASKS]  8.74 us
  transfers between devices with their start and end apart: 12, of which 8 were waited for; matrix products, arithmetic and copies ran while one was open for 0% of the time, Pallas kernels for 6%

profile of v10, /device:TPU:6, one launch (start us, length us, event | category | flops | bytes accessed | tf_op | source)
XLA Modules:
  0.0 139.2 jit_solution(4943731218379262460)
XLA Ops:
  0.0 1.1 copy-done.3
  1.1 0.7 copy-done.4
  1.8 1.4 shard_map.64
  3.2 15.3 %all-to-all-start = ((bf16[16,56,128]{2,1,0:T(8,128)(2,1)}), bf16[16,56,128]{2,1,0:T(8,128)(2,1)S(1)}, u32[]{:S(2)}, u32[]{:S(2)}) async-start(bf16[16,56,128]{2,1,0:T(8,128)(2,1)} %bitcast.1), calls=%async_computation | async-start | bytes 458752 | tf_op jit(solution)/shard_map/all_to_all | solution.py:260
  18.5 1.9 %collective-permute-start.1 = (bf16[168,3072]{1,0:T(8,128)(2,1)}, bf16[168,3072]{1,0:T(8,128)(2,1)}, u32[]{:S(2)}, u32[]{:S(2)}) collective-permute-start(bf16[168,3072]{1,0:T(8,128)(2,1)} %bitcast.10), channel_id=1, source_target_pairs={{0,1},{1,0},{2,3},{3,2},{4,5},{5,4},{6,7},{7,6},{8,9},{9,8},{10,11... | collective-permute-start | bytes 3096584 | tf_op jit(solution)/shard_map/ppermute | solution.py:256
  20.5 15.4 %all-to-all-done = bf16[16,56,128]{2,1,0:T(8,128)(2,1)S(1)} async-done(((bf16[16,56,128]{2,1,0:T(8,128)(2,1)}), bf16[16,56,128]{2,1,0:T(8,128)(2,1)S(1)}, u32[]{:S(2)}, u32[]{:S(2)}) %all-to-all-start) | async-done | bytes 229408 | tf_op jit(solution)/shard_map/all_to_all | solution.py:260
  35.9 1.0 shard_map.65
  36.9 6.5 %all-to-all-start.1 = ((bf16[4,816,128]{2,1,0:T(8,128)(2,1)}), bf16[4,816,128]{2,1,0:T(8,128)(2,1)S(1)}, u32[]{:S(2)}, u32[]{:S(2)}) async-start(bf16[4,816,128]{2,1,0:T(8,128)(2,1)} %shard_map.65), calls=%async_computation.1 | async-start | bytes 1671168 | tf_op jit(solution)/shard_map/all_to_all | solution.py:260
  43.4 0.0 copy-done.1
  43.4 1.9 %collective-permute-start.2 = (bf16[168,3072]{1,0:T(8,128)(2,1)S(1)}, bf16[168,3072]{1,0:T(8,128)(2,1)}, u32[]{:S(2)}, u32[]{:S(2)}) collective-permute-start(bf16[168,3072]{1,0:T(8,128)(2,1)S(1)} %bitcast.12), channel_id=1, source_target_pairs={{0,1},{1,0},{2,3},{3,2},{4,5},{5,4},{6,7},{7,6},{8,9},{9,8},{10,11... | collective-permute-start | bytes 3096584 | tf_op jit(solution)/shard_map/ppermute | solution.py:256
  45.3 2.4 %collective-permute-start.3 = (bf16[168,3072]{1,0:T(8,128)(2,1)}, bf16[168,3072]{1,0:T(8,128)(2,1)}, u32[]{:S(2)}, u32[]{:S(2)}) collective-permute-start(bf16[168,3072]{1,0:T(8,128)(2,1)} %bitcast.14), channel_id=1, source_target_pairs={{0,1},{1,0},{2,3},{3,2},{4,5},{5,4},{6,7},{7,6},{8,9},{9,8},{10,11... | collective-permute-start | bytes 3096584 | tf_op jit(solution)/shard_map/ppermute | solution.py:256
  47.8 4.6 %all-to-all-done.1.x_ref = bf16[4,816,128]{2,1,0:T(8,128)(2,1)S(1)} async-done(((bf16[4,816,128]{2,1,0:T(8,128)(2,1)}), bf16[4,816,128]{2,1,0:T(8,128)(2,1)S(1)}, u32[]{:S(2)}, u32[]{:S(2)}) %all-to-all-start.1) | async-done | bytes 835616 | tf_op jit(solution)/shard_map/all_to_all | solution.py:260
  52.4 1.9 %collective-permute-start.5 = (bf16[4,816,128]{2,1,0:T(8,128)(2,1)S(1)}, bf16[4,816,128]{2,1,0:T(8,128)(2,1)S(1)}, u32[]{:S(2)}, u32[]{:S(2)}) collective-permute-start(bf16[4,816,128]{2,1,0:T(8,128)(2,1)S(1)} %all-to-all-done.1.x_ref), channel_id=1, source_target_pairs={{0,160},{32,128},{64,224},{96,192},{128,32},{160,0},{192,96},{224,... | collective-permute-start | bytes 2506760 | tf_op jit(solution)/shard_map/ppermute | solution.py:279
  54.3 2.4 %collective-permute-start.4 = (bf16[4,816,128]{2,1,0:T(8,128)(2,1)S(1)}, bf16[4,816,128]{2,1,0:T(8,128)(2,1)S(1)}, u32[]{:S(2)}, u32[]{:S(2)}) collective-permute-start(bf16[4,816,128]{2,1,0:T(8,128)(2,1)S(1)} %all-to-all-done.1.x_ref), channel_id=1, source_target_pairs={{0,32},{32,0},{64,96},{96,64},{128,160},{160,128},{192,224},{224,1... | collective-permute-start | bytes 2506760 | tf_op jit(solution)/shard_map/ppermute | solution.py:279
  56.7 0.0 collective-permute-done.1.gate1
  56.7 4.9 %collective-permute-start = (bf16[4,816,128]{2,1,0:T(8,128)(2,1)S(1)}, bf16[4,816,128]{2,1,0:T(8,128)(2,1)S(1)}, u32[]{:S(2)}, u32[]{:S(2)}) collective-permute-start(bf16[4,816,128]{2,1,0:T(8,128)(2,1)S(1)} %all-to-all-done.1.x_ref), channel_id=1, source_target_pairs={{0,128},{32,160},{64,192},{96,224},{128,0},{160,32},{192,64},{224,... | collective-permute-start | bytes 2506760 | tf_op jit(solution)/shard_map/ppermute | solution.py:279
  61.6 0.0 collective-permute-done.2.up1
  61.6 0.0 collective-permute-done.3.down1
  61.6 0.0 copy-done
  61.6 0.0 copy-start.2
  61.6 1.2 copy-done.2
  62.9 2.3 %shard_map.66 = (bf16[768,3072]{1,0:T(8,128)(2,1)S(1)}, bf16[384,3072]{1,0:T(8,128)(2,1)S(1)}) custom-call(bf16[168,3072]{1,0:T(8,128)(2,1)S(1)} %bitcast.11, bf16[168,3072]{1,0:T(8,128)(2,1)S(1)} %bitcast.13, bf16[168,3072]{1,0:T(8,128)(2,1)S(1)} %bitcast.15, bf16[168,3072]{1,0:T(8,128)(2,1)} %collective-permute-done.1.gate1, ...), custom_call_target="tpu_custom_call" | custom-call | tf_op jit(solution)/shard_map/pallas_call | solution.py:243
  65.2 0.9 shard_map.67.sofar_ref
  66.1 1.7 %collective-permute-done.5.x_ref = bf16[4,816,128]{2,1,0:T(8,128)(2,1)S(1)} collective-permute-done((bf16[4,816,128]{2,1,0:T(8,128)(2,1)S(1)}, bf16[4,816,128]{2,1,0:T(8,128)(2,1)S(1)}, u32[]{:S(2)}, u32[]{:S(2)}) %collective-permute-start.5) | collective-permute-done | bytes 835616 | tf_op jit(solution)/shard_map/ppermute | solution.py:279
  67.8 0.9 shard_map.68.sofar_ref
  68.7 5.6 %collective-permute-done.4.x_ref = bf16[4,816,128]{2,1,0:T(8,128)(2,1)S(1)} collective-permute-done((bf16[4,816,128]{2,1,0:T(8,128)(2,1)S(1)}, bf16[4,816,128]{2,1,0:T(8,128)(2,1)S(1)}, u32[]{:S(2)}, u32[]{:S(2)}) %collective-permute-start.4) | collective-permute-done | bytes 835616 | tf_op jit(solution)/shard_map/ppermute | solution.py:279
  74.2 0.9 shard_map.69.sofar_ref
  75.2 1.5 %collective-permute-done.x_ref = bf16[4,816,128]{2,1,0:T(8,128)(2,1)S(1)} collective-permute-done((bf16[4,816,128]{2,1,0:T(8,128)(2,1)S(1)}, bf16[4,816,128]{2,1,0:T(8,128)(2,1)S(1)}, u32[]{:S(2)}, u32[]{:S(2)}) %collective-permute-start) | collective-permute-done | bytes 835616 | tf_op jit(solution)/shard_map/ppermute | solution.py:279
  76.6 3.3 %shard_map.70 = (bf16[544,384]{1,0:T(8,128)(2,1)S(1)}, bf16[4,816,128]{2,1,0:T(8,128)(2,1)S(1)}, bf16[4,816,128]{2,1,0:T(8,128)(2,1)S(1)}, bf16[4,816,128]{2,1,0:T(8,128)(2,1)S(1)}) custom-call(bf16[4,816,128]{2,1,0:T(8,128)(2,1)S(1)} %collective-permute-done.x_ref, bf16[768,3072]{1,0:T(8,128)(2,1)S(1)} %get-tuple-element.11.weights_ref, ...), custom_call_target="tpu_custom_call" | custom-call | tf_op jit(solution)/shard_map/pallas_call | solution.py:243
  79.9 2.4 %collective-permute-start.6 = (bf16[4,816,128]{2,1,0:T(8,128)(2,1)S(1)}, bf16[4,816,128]{2,1,0:T(8,128)(2,1)S(1)}, u32[]{:S(2)}, u32[]{:S(2)}) collective-permute-start(bf16[4,816,128]{2,1,0:T(8,128)(2,1)S(1)} %get-tuple-element.14), channel_id=1, source_target_pairs={{0,160},{32,128},{64,224},{96,192},{128,32},{160,0},{192,96},{224,... | collective-permute-start | bytes 2506760 | tf_op jit(solution)/shard_map/ppermute | solution.py:291
  82.4 4.4 %collective-permute-start.7 = (bf16[4,816,128]{2,1,0:T(8,128)(2,1)S(1)}, bf16[4,816,128]{2,1,0:T(8,128)(2,1)S(1)}, u32[]{:S(2)}, u32[]{:S(2)}) collective-permute-start(bf16[4,816,128]{2,1,0:T(8,128)(2,1)S(1)} %get-tuple-element.15), channel_id=1, source_target_pairs={{0,32},{32,0},{64,96},{96,64},{128,160},{160,128},{192,224},{224,1... | collective-permute-start | bytes 2506760 | tf_op jit(solution)/shard_map/ppermute | solution.py:291
  86.8 2.4 %collective-permute-start.8 = (bf16[4,816,128]{2,1,0:T(8,128)(2,1)S(1)}, bf16[4,816,128]{2,1,0:T(8,128)(2,1)S(1)}, u32[]{:S(2)}, u32[]{:S(2)}) collective-permute-start(bf16[4,816,128]{2,1,0:T(8,128)(2,1)S(1)} %get-tuple-element.16), channel_id=1, source_target_pairs={{0,128},{32,160},{64,192},{96,224},{128,0},{160,32},{192,64},{224,... | collective-permute-start | bytes 2506760 | tf_op jit(solution)/shard_map/ppermute | solution.py:291
  89.2 0.9 shard_map.71.a
  90.1 5.3 %collective-permute-done.6.b = bf16[4,816,128]{2,1,0:T(8,128)(2,1)S(1)} collective-permute-done((bf16[4,816,128]{2,1,0:T(8,128)(2,1)S(1)}, bf16[4,816,128]{2,1,0:T(8,128)(2,1)S(1)}, u32[]{:S(2)}, u32[]{:S(2)}) %collective-permute-start.6) | collective-permute-done | bytes 835616 | tf_op jit(solution)/shard_map/ppermute | solution.py:291
  95.4 0.2 shard_map.72.a
  95.5 8.8 %collective-permute-done.7.b = bf16[4,816,128]{2,1,0:T(8,128)(2,1)S(1)} collective-permute-done((bf16[4,816,128]{2,1,0:T(8,128)(2,1)S(1)}, bf16[4,816,128]{2,1,0:T(8,128)(2,1)S(1)}, u32[]{:S(2)}, u32[]{:S(2)}) %collective-permute-start.7) | collective-permute-done | bytes 835616 | tf_op jit(solution)/shard_map/ppermute | solution.py:291
  104.3 0.2 shard_map.73.a
  104.5 0.0 collective-permute-done.8.b
  104.5 0.2 shard_map.74
  104.7 0.0 copy-start.5
  104.7 0.0 copy-start.6
  104.7 13.2 %all_to_all.20.parts_ref = bf16[4,816,128]{2,1,0:T(8,128)(2,1)S(1)} all-to-all(bf16[4,816,128]{2,1,0:T(8,128)(2,1)S(1)} %shard_map.74), channel_id=1, replica_groups={{480,384,96,0},{416,448,32,64},{224,128,352,256},{160,192,288,320},{1,3..., dimensions={0} | all-to-all | bytes 1671168 | tf_op jit(solution)/shard_map/all_to_all | solution.py:260
  117.9 0.9 shard_map.75
  118.8 5.4 %all-to-all-start.3 = ((bf16[16,56,128]{2,1,0:T(8,128)(2,1)}), bf16[16,56,128]{2,1,0:T(8,128)(2,1)S(1)}, u32[]{:S(2)}, u32[]{:S(2)}) async-start(bf16[16,56,128]{2,1,0:T(8,128)(2,1)} %bitcast.6), calls=%async_computation.3 | async-start | bytes 458752 | tf_op jit(solution)/shard_map/all_to_all | solution.py:260
  124.2 0.0 copy-done.5
  124.2 0.8 shard_map.76.gates_ref
  125.0 13.0 %all-to-all-done.3 = bf16[16,56,128]{2,1,0:T(8,128)(2,1)S(1)} async-done(((bf16[16,56,128]{2,1,0:T(8,128)(2,1)}), bf16[16,56,128]{2,1,0:T(8,128)(2,1)S(1)}, u32[]{:S(2)}, u32[]{:S(2)}) %all-to-all-start.3) | async-done | bytes 229408 | tf_op jit(solution)/shard_map/all_to_all | solution.py:260
  138.0 1.2 shard_map.77
  (5 shorter events, 0.0 us)
Async XLA Ops:
  0.0 1.1 copy-start.3
  1.1 0.7 copy-start.4
  3.2 40.2 %copy-start.1 = (bf16[1,168,3072]{2,1,0:T(8,128)(2,1)S(1)}, bf16[1,168,3072]{2,1,0:T(8,128)(2,1)}, u32[]{:S(2)}) copy-start(bf16[1,168,3072]{2,1,0:T(8,128)(2,1)} %param.10) | copy-start | bytes 3096580
  3.2 58.4 %copy-start = (bf16[1,168,3072]{2,1,0:T(8,128)(2,1)S(1)}, bf16[1,168,3072]{2,1,0:T(8,128)(2,1)}, u32[]{:S(2)}) copy-start(bf16[1,168,3072]{2,1,0:T(8,128)(2,1)} %param.9) | copy-start | bytes 3096580
  3.2 32.7 %all-to-all-start = ((bf16[16,56,128]{2,1,0:T(8,128)(2,1)}), bf16[16,56,128]{2,1,0:T(8,128)(2,1)S(1)}, u32[]{:S(2)}, u32[]{:S(2)}) async-start(bf16[16,56,128]{2,1,0:T(8,128)(2,1)} %bitcast.1), calls=%async_computation | async-start | bytes 458752 | tf_op jit(solution)/shard_map/all_to_all | solution.py:260
  18.5 38.2 %collective-permute-start.1 = (bf16[168,3072]{1,0:T(8,128)(2,1)}, bf16[168,3072]{1,0:T(8,128)(2,1)}, u32[]{:S(2)}, u32[]{:S(2)}) collective-permute-start(bf16[168,3072]{1,0:T(8,128)(2,1)} %bitcast.10), channel_id=1, source_target_pairs={{0,1},{1,0},{2,3},{3,2},{4,5},{5,4},{6,7},{7,6},{8,9},{9,8},{10,11... | collective-permute-start | bytes 3096584 | tf_op jit(solution)/shard_map/ppermute | solution.py:256
  36.9 15.4 %all-to-all-start.1 = ((bf16[4,816,128]{2,1,0:T(8,128)(2,1)}), bf16[4,816,128]{2,1,0:T(8,128)(2,1)S(1)}, u32[]{:S(2)}, u32[]{:S(2)}) async-start(bf16[4,816,128]{2,1,0:T(8,128)(2,1)} %shard_map.65), calls=%async_computation.1 | async-start | bytes 1671168 | tf_op jit(solution)/shard_map/all_to_all | solution.py:260
  43.4 18.2 %collective-permute-start.2 = (bf16[168,3072]{1,0:T(8,128)(2,1)S(1)}, bf16[168,3072]{1,0:T(8,128)(2,1)}, u32[]{:S(2)}, u32[]{:S(2)}) collective-permute-start(bf16[168,3072]{1,0:T(8,128)(2,1)S(1)} %bitcast.12), channel_id=1, source_target_pairs={{0,1},{1,0},{2,3},{3,2},{4,5},{5,4},{6,7},{7,6},{8,9},{9,8},{10,11... | collective-permute-start | bytes 3096584 | tf_op jit(solution)/shard_map/ppermute | solution.py:256
  45.3 16.3 %collective-permute-start.3 = (bf16[168,3072]{1,0:T(8,128)(2,1)}, bf16[168,3072]{1,0:T(8,128)(2,1)}, u32[]{:S(2)}, u32[]{:S(2)}) collective-permute-start(bf16[168,3072]{1,0:T(8,128)(2,1)} %bitcast.14), channel_id=1, source_target_pairs={{0,1},{1,0},{2,3},{3,2},{4,5},{5,4},{6,7},{7,6},{8,9},{9,8},{10,11... | collective-permute-start | bytes 3096584 | tf_op jit(solution)/shard_map/ppermute | solution.py:256
  52.4 15.4 %collective-permute-start.5 = (bf16[4,816,128]{2,1,0:T(8,128)(2,1)S(1)}, bf16[4,816,128]{2,1,0:T(8,128)(2,1)S(1)}, u32[]{:S(2)}, u32[]{:S(2)}) collective-permute-start(bf16[4,816,128]{2,1,0:T(8,128)(2,1)S(1)} %all-to-all-done.1.x_ref), channel_id=1, source_target_pairs={{0,160},{32,128},{64,224},{96,192},{128,32},{160,0},{192,96},{224,... | collective-permute-start | bytes 2506760 | tf_op jit(solution)/shard_map/ppermute | solution.py:279
  54.3 20.0 %collective-permute-start.4 = (bf16[4,816,128]{2,1,0:T(8,128)(2,1)S(1)}, bf16[4,816,128]{2,1,0:T(8,128)(2,1)S(1)}, u32[]{:S(2)}, u32[]{:S(2)}) collective-permute-start(bf16[4,816,128]{2,1,0:T(8,128)(2,1)S(1)} %all-to-all-done.1.x_ref), channel_id=1, source_target_pairs={{0,32},{32,0},{64,96},{96,64},{128,160},{160,128},{192,224},{224,1... | collective-permute-start | bytes 2506760 | tf_op jit(solution)/shard_map/ppermute | solution.py:279
  56.7 19.9 %collective-permute-start = (bf16[4,816,128]{2,1,0:T(8,128)(2,1)S(1)}, bf16[4,816,128]{2,1,0:T(8,128)(2,1)S(1)}, u32[]{:S(2)}, u32[]{:S(2)}) collective-permute-start(bf16[4,816,128]{2,1,0:T(8,128)(2,1)S(1)} %all-to-all-done.1.x_ref), channel_id=1, source_target_pairs={{0,128},{32,160},{64,192},{96,224},{128,0},{160,32},{192,64},{224,... | collective-permute-start | bytes 2506760 | tf_op jit(solution)/shard_map/ppermute | solution.py:279
  61.6 1.2 copy-start.2
  79.9 15.4 %collective-permute-start.6 = (bf16[4,816,128]{2,1,0:T(8,128)(2,1)S(1)}, bf16[4,816,128]{2,1,0:T(8,128)(2,1)S(1)}, u32[]{:S(2)}, u32[]{:S(2)}) collective-permute-start(bf16[4,816,128]{2,1,0:T(8,128)(2,1)S(1)} %get-tuple-element.14), channel_id=1, source_target_pairs={{0,160},{32,128},{64,224},{96,192},{128,32},{160,0},{192,96},{224,... | collective-permute-start | bytes 2506760 | tf_op jit(solution)/shard_map/ppermute | solution.py:291
  82.4 22.0 %collective-permute-start.7 = (bf16[4,816,128]{2,1,0:T(8,128)(2,1)S(1)}, bf16[4,816,128]{2,1,0:T(8,128)(2,1)S(1)}, u32[]{:S(2)}, u32[]{:S(2)}) collective-permute-start(bf16[4,816,128]{2,1,0:T(8,128)(2,1)S(1)} %get-tuple-element.15), channel_id=1, source_target_pairs={{0,32},{32,0},{64,96},{96,64},{128,160},{160,128},{192,224},{224,1... | collective-permute-start | bytes 2506760 | tf_op jit(solution)/shard_map/ppermute | solution.py:291
  86.8 17.8 %collective-permute-start.8 = (bf16[4,816,128]{2,1,0:T(8,128)(2,1)S(1)}, bf16[4,816,128]{2,1,0:T(8,128)(2,1)S(1)}, u32[]{:S(2)}, u32[]{:S(2)}) collective-permute-start(bf16[4,816,128]{2,1,0:T(8,128)(2,1)S(1)} %get-tuple-element.16), channel_id=1, source_target_pairs={{0,128},{32,160},{64,192},{96,224},{128,0},{160,32},{192,64},{224,... | collective-permute-start | bytes 2506760 | tf_op jit(solution)/shard_map/ppermute | solution.py:291
  104.7 19.5 %copy-start.5 = (s32[256,4]{0,1:T(4,128)S(1)}, s32[256,4]{0,1:T(4,128)}, u32[]{:S(2)}) copy-start(s32[256,4]{0,1:T(4,128)} %param.7) | copy-start | bytes 12292
  104.7 19.5 %copy-start.6 = (f32[256,4]{0,1:T(4,128)S(1)}, f32[256,4]{0,1:T(4,128)}, u32[]{:S(2)}) copy-start(f32[256,4]{0,1:T(4,128)} %param.8) | copy-start | bytes 12292
  118.8 19.2 %all-to-all-start.3 = ((bf16[16,56,128]{2,1,0:T(8,128)(2,1)}), bf16[16,56,128]{2,1,0:T(8,128)(2,1)S(1)}, u32[]{:S(2)}, u32[]{:S(2)}) async-start(bf16[16,56,128]{2,1,0:T(8,128)(2,1)} %bitcast.6), calls=%async_computation.3 | async-start | bytes 458752 | tf_op jit(solution)/shard_map/all_to_all | solution.py:260

commit v11 on v9

--- a/solution.py
+++ b/solution.py
@@ -90,15 +90,21 @@
     return [main & (wide == at), half & (wide == at - CAP), half & (wide == at - HALF)], spread
 
 
-def dispatch_kernel(ids_ref, tokens_ref, out_ref):
+def dispatch_kernel(ids_ref, tokens_ref, out_ref, columns, sems):
     n = tokens_ref.shape[0]
     core, dp = lax.axis_index("tensor"), lax.axis_index("dp")
     q, at = quarter(dp // SIZE, dp % SIZE, core)
     part = 4 * q + at
+    copies = []
+    for i, block in enumerate((part, DP + part // 2)):
+        lanes = pl.ds(pl.multiple_of(block * LANES, LANES), LANES)
+        copies.append(pltpu.make_async_copy(tokens_ref.at[:, lanes], columns.at[i], sems.at[i]))
+        copies[i].start()
     picks, _ = slot_picks(ids_ref[:, pl.ds(pl.multiple_of(core * n, n), n)])
     picks = jnp.concatenate([p.astype(BF16) for p in picks], axis=1)
-    first = tokens_ref[:, pl.ds(pl.multiple_of(part * LANES, LANES), LANES)]
-    rest = tokens_ref[:, pl.ds(pl.multiple_of((DP + part // 2) * LANES, LANES), LANES)].astype(F32)
+    for copy in copies:
+        copy.wait()
+    first, rest = columns[0], columns[1].astype(F32)
     low = iota((n, LANES), 1) < HLANES
     turned = pltpu.roll(rest, HLANES, 1)
     odd = part % 2 == 1
@@ -157,17 +163,18 @@
 def down_products(mask, hidden, down_ref, out_ref):
     cut, q = place_of(1)
     to = q ^ mask
-    low = iota((SIDE, LANES), 1) < HLANES
+    lane = iota((SIDE, LANES), 1)
     for at in range(4):
         dp = (to // 2 * 2 + at // 2 - cut) % SIZE * SIZE + (to % 2 * 2 + at % 2 - cut) % SIZE
-        odd = dp % 2 == 1
-        y = dot(hidden, down_ref[:, pl.ds(pl.multiple_of((dp * 3 - dp % 2) // 2 * LANES, LANES), 2 * LANES)])
-        first, second = y[:, :LANES], y[:, LANES:]
-        out_ref[at, : 2 * SIDE, :] = jnp.where(odd, second, first).astype(BF16)
-        half = jnp.where(odd, first, second)
-        turned = pltpu.roll(half, HLANES, 1)
-        left, right = jnp.where(odd, turned, half), jnp.where(odd, half, turned)
-        out_ref[at, 2 * SIDE :, :] = jnp.where(low, left[:SIDE], right[SIDE:]).astype(BF16)
+        odd = dp % 2
+        main = (3 * dp + odd) // 2
+        blocks = [pl.ds(pl.multiple_of(i * LANES, LANES), LANES) for i in (main, main + 1 - 2 * odd)]
+        y = dot(hidden, jnp.concatenate([down_ref[:, lanes] for lanes in blocks], axis=1))
+        out_ref[at, : 2 * SIDE, :] = y[:, :LANES].astype(BF16)
+        upper, lower = y[:SIDE, LANES:], y[SIDE:, LANES:]
+        stays = jnp.where(odd == 1, lower, upper)
+        turned = pltpu.roll(jnp.where(odd == 1, upper, lower), HLANES, 1)
+        out_ref[at, 2 * SIDE :, :] = jnp.where(lane ^ (odd * HLANES) < HLANES, stays, turned).astype(BF16)
 
 
 def first_kernel(mask, x_ref, weights_ref, total_ref):
@@ -238,11 +245,13 @@
     out_ref[LANES:, :] = jnp.where(odd, first[HLANES:], rest).astype(BF16)
 
 
-def call(kernel, shape, *args, scratch=(), limit=16):
+def call(kernel, shape, *args, scratch=(), limit=16, specs=None):
     out = jax.ShapeDtypeStruct(shape, BF16) if isinstance(shape, tuple) else [pltpu.VMEM(s, d) for s, d in shape]
+    places = {} if specs is None else {"in_specs": [pl.BlockSpec(memory_space=space) for space in specs]}
     return pl.pallas_call(
         kernel,
         out_shape=out,
+        **places,
         scratch_shapes=scratch,
         compiler_params=pltpu.CompilerParams(vmem_limit_bytes=limit * 1024 * 1024),
     )(*args)
@@ -272,7 +281,13 @@
     part_scratch = pltpu.VMEM((PART, LANES), F32)
     block_scratch = pltpu.VMEM((EXPERTS * BLOCK, LANES), F32)
 
-    sent = call(dispatch_kernel, (EXPERTS * BLOCK, LANES), ids, tokens)
+    sent = call(
+        dispatch_kernel,
+        (EXPERTS * BLOCK, LANES),
+        *(ids, tokens),
+        scratch=[pltpu.VMEM((2, n, LANES), BF16), pltpu.SemaphoreType.DMA((2,))],
+        specs=(pltpu.VMEM, pltpu.HBM),
+    )
     arrived = exchange(sent.reshape(EXPERTS, BLOCK, LANES), "expert").reshape(EXPERTS * BLOCK, LANES)
     rows = call(pack_kernel, (4, PART, LANES), arrived, scratch=[block_scratch, part_scratch])
     rows = exchange(rows, plane, quarter_groups(0))

time: 141 us -> 141 us (level)
  no operation moved by 1% of the time
where the time goes in v11:
time: 141 us; the launch traced here: 139 us
  waiting for transfers between devices  54.9 us (39%)
  starting transfers between devices  52 us (37%)
  Pallas kernels  15.3 us (11%)
  blocking collectives  13.9 us (10%)
  local copies, waits for them, and re-layouts  3.06 us (2%)
    all_to_all x3, waiting for transfers between devices, exchange(): lax.all_to_all(value, axis, split_axis=0, concat_axis=0, tiled=True, axis...  31.8 us
    all_to_all x3, starting transfers between devices, exchange(): lax.all_to_all(value, axis, split_axis=0, concat_axis=0, tiled=True, axis...  24.9 us
    pallas_call x14, Pallas kernels, call(): pl.pallas_call(kernel, out_shape=out, **places, scratch_shapes=scratch, c...  15.3 us
    all_to_all x1, blocking collectives, exchange(): lax.all_to_all(value, axis, split_axis=0, concat_axis=0, tiled=True, axis...  13.9 us
    ppermute x3, waiting for transfers between devices, shards(): lax.ppermute(out, plane, across(mask, 1))  13.7 us
    ppermute x3, starting transfers between devices, shards(): others = [lax.ppermute(rows, plane, across(mask, 0)) for mask in MASKS]  11.6 us
    ppermute x3, waiting for transfers between devices, shards(): others = [lax.ppermute(rows, plane, across(mask, 0)) for mask in MASKS]  9.32 us
    ppermute x3, starting transfers between devices, shards(): lax.ppermute(out, plane, across(mask, 1))  9.21 us
  transfers between devices with their start and end apart: 12, of which 8 were waited for; matrix products, arithmetic and copies ran while one was open for 0% of the time, Pallas kernels for 6%

profile of v11, /device:TPU:6, one launch (start us, length us, event | category | flops | bytes accessed | tf_op | source)
XLA Modules:
  0.0 139.4 jit_solution(2882462918259965274)
XLA Ops:
  0.0 1.1 copy-done.3
  1.1 0.7 copy-done.4
  1.8 1.6 %shard_map.64 = bf16[896,128]{1,0:T(8,128)(2,1)} custom-call(s32[4,256]{1,0:T(4,128)S(1)} %bitcast.18, bf16[128,3072]{1,0:T(8,128)(2,1)S(1)} %copy-done.3), custom_call_target="tpu_custom_call" | custom-call | tf_op jit(solution)/shard_map/pallas_call | solution.py:251
  3.4 0.0 copy-start.1
  3.4 0.0 copy-start
  3.4 15.3 %all-to-all-start = ((bf16[16,56,128]{2,1,0:T(8,128)(2,1)}), bf16[16,56,128]{2,1,0:T(8,128)(2,1)S(1)}, u32[]{:S(2)}, u32[]{:S(2)}) async-start(bf16[16,56,128]{2,1,0:T(8,128)(2,1)} %bitcast.1), calls=%async_computation | async-start | bytes 458752 | tf_op jit(solution)/shard_map/all_to_all | solution.py:269
  18.8 1.9 %collective-permute-start.1 = (bf16[168,3072]{1,0:T(8,128)(2,1)}, bf16[168,3072]{1,0:T(8,128)(2,1)}, u32[]{:S(2)}, u32[]{:S(2)}) collective-permute-start(bf16[168,3072]{1,0:T(8,128)(2,1)} %bitcast.10), channel_id=1, source_target_pairs={{0,1},{1,0},{2,3},{3,2},{4,5},{5,4},{6,7},{7,6},{8,9},{9,8},{10,11... | collective-permute-start | bytes 3096584 | tf_op jit(solution)/shard_map/ppermute | solution.py:265
  20.7 15.4 %all-to-all-done = bf16[16,56,128]{2,1,0:T(8,128)(2,1)S(1)} async-done(((bf16[16,56,128]{2,1,0:T(8,128)(2,1)}), bf16[16,56,128]{2,1,0:T(8,128)(2,1)S(1)}, u32[]{:S(2)}, u32[]{:S(2)}) %all-to-all-start) | async-done | bytes 229408 | tf_op jit(solution)/shard_map/all_to_all | solution.py:269
  36.1 1.0 shard_map.65
  37.2 4.3 %all-to-all-start.1 = ((bf16[4,816,128]{2,1,0:T(8,128)(2,1)}), bf16[4,816,128]{2,1,0:T(8,128)(2,1)S(1)}, u32[]{:S(2)}, u32[]{:S(2)}) async-start(bf16[4,816,128]{2,1,0:T(8,128)(2,1)} %shard_map.65), calls=%async_computation.1 | async-start | bytes 1671168 | tf_op jit(solution)/shard_map/all_to_all | solution.py:269
  41.5 1.9 %collective-permute-start.2 = (bf16[168,3072]{1,0:T(8,128)(2,1)S(1)}, bf16[168,3072]{1,0:T(8,128)(2,1)}, u32[]{:S(2)}, u32[]{:S(2)}) collective-permute-start(bf16[168,3072]{1,0:T(8,128)(2,1)S(1)} %bitcast.12), channel_id=1, source_target_pairs={{0,1},{1,0},{2,3},{3,2},{4,5},{5,4},{6,7},{7,6},{8,9},{9,8},{10,11... | collective-permute-start | bytes 3096584 | tf_op jit(solution)/shard_map/ppermute | solution.py:265
  43.4 2.4 %collective-permute-start.3 = (bf16[168,3072]{1,0:T(8,128)(2,1)}, bf16[168,3072]{1,0:T(8,128)(2,1)}, u32[]{:S(2)}, u32[]{:S(2)}) collective-permute-start(bf16[168,3072]{1,0:T(8,128)(2,1)} %bitcast.14), channel_id=1, source_target_pairs={{0,1},{1,0},{2,3},{3,2},{4,5},{5,4},{6,7},{7,6},{8,9},{9,8},{10,11... | collective-permute-start | bytes 3096584 | tf_op jit(solution)/shard_map/ppermute | solution.py:265
  45.8 3.4 %all-to-all-done.1.x_ref = bf16[4,816,128]{2,1,0:T(8,128)(2,1)S(1)} async-done(((bf16[4,816,128]{2,1,0:T(8,128)(2,1)}), bf16[4,816,128]{2,1,0:T(8,128)(2,1)S(1)}, u32[]{:S(2)}, u32[]{:S(2)}) %all-to-all-start.1) | async-done | bytes 835616 | tf_op jit(solution)/shard_map/all_to_all | solution.py:269
  49.2 4.8 %collective-permute-start.5 = (bf16[4,816,128]{2,1,0:T(8,128)(2,1)S(1)}, bf16[4,816,128]{2,1,0:T(8,128)(2,1)S(1)}, u32[]{:S(2)}, u32[]{:S(2)}) collective-permute-start(bf16[4,816,128]{2,1,0:T(8,128)(2,1)S(1)} %all-to-all-done.1.x_ref), channel_id=1, source_target_pairs={{0,480},{32,448},{64,416},{96,384},{128,352},{160,320},{192,288},{... | collective-permute-start | bytes 2506760 | tf_op jit(solution)/shard_map/ppermute | solution.py:294
  54.0 4.0 %collective-permute-start.4 = (bf16[4,816,128]{2,1,0:T(8,128)(2,1)S(1)}, bf16[4,816,128]{2,1,0:T(8,128)(2,1)S(1)}, u32[]{:S(2)}, u32[]{:S(2)}) collective-permute-start(bf16[4,816,128]{2,1,0:T(8,128)(2,1)S(1)} %all-to-all-done.1.x_ref), channel_id=1, source_target_pairs={{0,96},{32,64},{64,32},{96,0},{128,224},{160,192},{192,160},{224,1... | collective-permute-start | bytes 2506760 | tf_op jit(solution)/shard_map/ppermute | solution.py:294
  58.0 0.0 collective-permute-done.1.gate1
  58.0 2.8 %collective-permute-start = (bf16[4,816,128]{2,1,0:T(8,128)(2,1)S(1)}, bf16[4,816,128]{2,1,0:T(8,128)(2,1)S(1)}, u32[]{:S(2)}, u32[]{:S(2)}) collective-permute-start(bf16[4,816,128]{2,1,0:T(8,128)(2,1)S(1)} %all-to-all-done.1.x_ref), channel_id=1, source_target_pairs={{0,384},{32,416},{64,448},{96,480},{128,256},{160,288},{192,320},{... | collective-permute-start | bytes 2506760 | tf_op jit(solution)/shard_map/ppermute | solution.py:294
  60.8 0.0 collective-permute-done.2.up1
  60.8 0.0 collective-permute-done.3.down1
  60.9 0.0 copy-done
  60.9 0.0 copy-start.2
  60.9 1.2 copy-done.2
  62.1 2.3 %shard_map.66 = (bf16[768,3072]{1,0:T(8,128)(2,1)S(1)}, bf16[384,3072]{1,0:T(8,128)(2,1)S(1)}) custom-call(bf16[168,3072]{1,0:T(8,128)(2,1)S(1)} %bitcast.11, bf16[168,3072]{1,0:T(8,128)(2,1)S(1)} %bitcast.13, bf16[168,3072]{1,0:T(8,128)(2,1)S(1)} %bitcast.15, bf16[168,3072]{1,0:T(8,128)(2,1)} %collective-permute-done.1.gate1, ...), custom_call_target="tpu_custom_call" | custom-call | tf_op jit(solution)/shard_map/pallas_call | solution.py:251
  64.4 0.9 shard_map.67.sofar_ref
  65.3 1.7 %collective-permute-done.5.x_ref = bf16[4,816,128]{2,1,0:T(8,128)(2,1)S(1)} collective-permute-done((bf16[4,816,128]{2,1,0:T(8,128)(2,1)S(1)}, bf16[4,816,128]{2,1,0:T(8,128)(2,1)S(1)}, u32[]{:S(2)}, u32[]{:S(2)}) %collective-permute-start.5) | collective-permute-done | bytes 835616 | tf_op jit(solution)/shard_map/ppermute | solution.py:294
  67.0 0.9 shard_map.68.sofar_ref
  67.9 7.6 %collective-permute-done.4.x_ref = bf16[4,816,128]{2,1,0:T(8,128)(2,1)S(1)} collective-permute-done((bf16[4,816,128]{2,1,0:T(8,128)(2,1)S(1)}, bf16[4,816,128]{2,1,0:T(8,128)(2,1)S(1)}, u32[]{:S(2)}, u32[]{:S(2)}) %collective-permute-start.4) | collective-permute-done | bytes 835616 | tf_op jit(solution)/shard_map/ppermute | solution.py:294
  75.5 0.9 shard_map.69.sofar_ref
  76.4 0.0 collective-permute-done.x_ref
  76.5 3.4 %shard_map.70 = (bf16[544,384]{1,0:T(8,128)(2,1)S(1)}, bf16[4,816,128]{2,1,0:T(8,128)(2,1)S(1)}, bf16[4,816,128]{2,1,0:T(8,128)(2,1)S(1)}, bf16[4,816,128]{2,1,0:T(8,128)(2,1)S(1)}) custom-call(bf16[4,816,128]{2,1,0:T(8,128)(2,1)S(1)} %collective-permute-done.x_ref, bf16[768,3072]{1,0:T(8,128)(2,1)S(1)} %get-tuple-element.11.weights_ref, ...), custom_call_target="tpu_custom_call" | custom-call | tf_op jit(solution)/shard_map/pallas_call | solution.py:251
  79.8 1.9 %collective-permute-start.6 = (bf16[4,816,128]{2,1,0:T(8,128)(2,1)S(1)}, bf16[4,816,128]{2,1,0:T(8,128)(2,1)S(1)}, u32[]{:S(2)}, u32[]{:S(2)}) collective-permute-start(bf16[4,816,128]{2,1,0:T(8,128)(2,1)S(1)} %get-tuple-element.14), channel_id=1, source_target_pairs={{0,160},{32,128},{64,224},{96,192},{128,32},{160,0},{192,96},{224,... | collective-permute-start | bytes 2506760 | tf_op jit(solution)/shard_map/ppermute | solution.py:306
  81.7 4.2 %collective-permute-start.7 = (bf16[4,816,128]{2,1,0:T(8,128)(2,1)S(1)}, bf16[4,816,128]{2,1,0:T(8,128)(2,1)S(1)}, u32[]{:S(2)}, u32[]{:S(2)}) collective-permute-start(bf16[4,816,128]{2,1,0:T(8,128)(2,1)S(1)} %get-tuple-element.15), channel_id=1, source_target_pairs={{0,32},{32,0},{64,96},{96,64},{128,160},{160,128},{192,224},{224,1... | collective-permute-start | bytes 2506760 | tf_op jit(solution)/shard_map/ppermute | solution.py:306
  85.9 3.1 %collective-permute-start.8 = (bf16[4,816,128]{2,1,0:T(8,128)(2,1)S(1)}, bf16[4,816,128]{2,1,0:T(8,128)(2,1)S(1)}, u32[]{:S(2)}, u32[]{:S(2)}) collective-permute-start(bf16[4,816,128]{2,1,0:T(8,128)(2,1)S(1)} %get-tuple-element.16), channel_id=1, source_target_pairs={{0,128},{32,160},{64,192},{96,224},{128,0},{160,32},{192,64},{224,... | collective-permute-start | bytes 2506760 | tf_op jit(solution)/shard_map/ppermute | solution.py:306
  89.0 0.9 shard_map.71.a
  90.0 5.3 %collective-permute-done.6.b = bf16[4,816,128]{2,1,0:T(8,128)(2,1)S(1)} collective-permute-done((bf16[4,816,128]{2,1,0:T(8,128)(2,1)S(1)}, bf16[4,816,128]{2,1,0:T(8,128)(2,1)S(1)}, u32[]{:S(2)}, u32[]{:S(2)}) %collective-permute-start.6) | collective-permute-done | bytes 835616 | tf_op jit(solution)/shard_map/ppermute | solution.py:306
  95.2 0.2 shard_map.72.a
  95.4 8.1 %collective-permute-done.7.b = bf16[4,816,128]{2,1,0:T(8,128)(2,1)S(1)} collective-permute-done((bf16[4,816,128]{2,1,0:T(8,128)(2,1)S(1)}, bf16[4,816,128]{2,1,0:T(8,128)(2,1)S(1)}, u32[]{:S(2)}, u32[]{:S(2)}) %collective-permute-start.7) | collective-permute-done | bytes 835616 | tf_op jit(solution)/shard_map/ppermute | solution.py:306
  103.5 0.2 shard_map.73.a
  103.7 0.3 collective-permute-done.8.b
  104.1 0.2 shard_map.74
  104.2 0.0 copy-start.5
  104.3 0.0 copy-start.6
  104.3 13.9 %all_to_all.20.parts_ref = bf16[4,816,128]{2,1,0:T(8,128)(2,1)S(1)} all-to-all(bf16[4,816,128]{2,1,0:T(8,128)(2,1)S(1)} %shard_map.74), channel_id=1, replica_groups={{480,384,96,0},{416,448,32,64},{224,128,352,256},{160,192,288,320},{1,3..., dimensions={0} | all-to-all | bytes 1671168 | tf_op jit(solution)/shard_map/all_to_all | solution.py:269
  118.2 0.9 shard_map.75
  119.1 5.3 %all-to-all-start.3 = ((bf16[16,56,128]{2,1,0:T(8,128)(2,1)}), bf16[16,56,128]{2,1,0:T(8,128)(2,1)S(1)}, u32[]{:S(2)}, u32[]{:S(2)}) async-start(bf16[16,56,128]{2,1,0:T(8,128)(2,1)} %bitcast.6), calls=%async_computation.3 | async-start | bytes 458752 | tf_op jit(solution)/shard_map/all_to_all | solution.py:269
  124.4 0.8 shard_map.76.gates_ref
  125.1 13.0 %all-to-all-done.3 = bf16[16,56,128]{2,1,0:T(8,128)(2,1)S(1)} async-done(((bf16[16,56,128]{2,1,0:T(8,128)(2,1)}), bf16[16,56,128]{2,1,0:T(8,128)(2,1)S(1)}, u32[]{:S(2)}, u32[]{:S(2)}) %all-to-all-start.3) | async-done | bytes 229408 | tf_op jit(solution)/shard_map/all_to_all | solution.py:269
  138.2 1.2 shard_map.77
  (5 shorter events, 0.0 us)
Async XLA Ops:
  0.0 1.1 copy-start.3
  1.1 0.7 copy-start.4
  3.4 38.1 %copy-start.1 = (bf16[1,168,3072]{2,1,0:T(8,128)(2,1)S(1)}, bf16[1,168,3072]{2,1,0:T(8,128)(2,1)}, u32[]{:S(2)}) copy-start(bf16[1,168,3072]{2,1,0:T(8,128)(2,1)} %param.10) | copy-start | bytes 3096580
  3.4 57.4 %copy-start = (bf16[1,168,3072]{2,1,0:T(8,128)(2,1)S(1)}, bf16[1,168,3072]{2,1,0:T(8,128)(2,1)}, u32[]{:S(2)}) copy-start(bf16[1,168,3072]{2,1,0:T(8,128)(2,1)} %param.9) | copy-start | bytes 3096580
  3.4 32.7 %all-to-all-start = ((bf16[16,56,128]{2,1,0:T(8,128)(2,1)}), bf16[16,56,128]{2,1,0:T(8,128)(2,1)S(1)}, u32[]{:S(2)}, u32[]{:S(2)}) async-start(bf16[16,56,128]{2,1,0:T(8,128)(2,1)} %bitcast.1), calls=%async_computation | async-start | bytes 458752 | tf_op jit(solution)/shard_map/all_to_all | solution.py:269
  18.8 39.2 %collective-permute-start.1 = (bf16[168,3072]{1,0:T(8,128)(2,1)}, bf16[168,3072]{1,0:T(8,128)(2,1)}, u32[]{:S(2)}, u32[]{:S(2)}) collective-permute-start(bf16[168,3072]{1,0:T(8,128)(2,1)} %bitcast.10), channel_id=1, source_target_pairs={{0,1},{1,0},{2,3},{3,2},{4,5},{5,4},{6,7},{7,6},{8,9},{9,8},{10,11... | collective-permute-start | bytes 3096584 | tf_op jit(solution)/shard_map/ppermute | solution.py:265
  37.2 12.0 %all-to-all-start.1 = ((bf16[4,816,128]{2,1,0:T(8,128)(2,1)}), bf16[4,816,128]{2,1,0:T(8,128)(2,1)S(1)}, u32[]{:S(2)}, u32[]{:S(2)}) async-start(bf16[4,816,128]{2,1,0:T(8,128)(2,1)} %shard_map.65), calls=%async_computation.1 | async-start | bytes 1671168 | tf_op jit(solution)/shard_map/all_to_all | solution.py:269
  41.5 19.3 %collective-permute-start.2 = (bf16[168,3072]{1,0:T(8,128)(2,1)S(1)}, bf16[168,3072]{1,0:T(8,128)(2,1)}, u32[]{:S(2)}, u32[]{:S(2)}) collective-permute-start(bf16[168,3072]{1,0:T(8,128)(2,1)S(1)} %bitcast.12), channel_id=1, source_target_pairs={{0,1},{1,0},{2,3},{3,2},{4,5},{5,4},{6,7},{7,6},{8,9},{9,8},{10,11... | collective-permute-start | bytes 3096584 | tf_op jit(solution)/shard_map/ppermute | solution.py:265
  43.4 17.4 %collective-permute-start.3 = (bf16[168,3072]{1,0:T(8,128)(2,1)}, bf16[168,3072]{1,0:T(8,128)(2,1)}, u32[]{:S(2)}, u32[]{:S(2)}) collective-permute-start(bf16[168,3072]{1,0:T(8,128)(2,1)} %bitcast.14), channel_id=1, source_target_pairs={{0,1},{1,0},{2,3},{3,2},{4,5},{5,4},{6,7},{7,6},{8,9},{9,8},{10,11... | collective-permute-start | bytes 3096584 | tf_op jit(solution)/shard_map/ppermute | solution.py:265
  49.2 17.8 %collective-permute-start.5 = (bf16[4,816,128]{2,1,0:T(8,128)(2,1)S(1)}, bf16[4,816,128]{2,1,0:T(8,128)(2,1)S(1)}, u32[]{:S(2)}, u32[]{:S(2)}) collective-permute-start(bf16[4,816,128]{2,1,0:T(8,128)(2,1)S(1)} %all-to-all-done.1.x_ref), channel_id=1, source_target_pairs={{0,480},{32,448},{64,416},{96,384},{128,352},{160,320},{192,288},{... | collective-permute-start | bytes 2506760 | tf_op jit(solution)/shard_map/ppermute | solution.py:294
  54.0 21.5 %collective-permute-start.4 = (bf16[4,816,128]{2,1,0:T(8,128)(2,1)S(1)}, bf16[4,816,128]{2,1,0:T(8,128)(2,1)S(1)}, u32[]{:S(2)}, u32[]{:S(2)}) collective-permute-start(bf16[4,816,128]{2,1,0:T(8,128)(2,1)S(1)} %all-to-all-done.1.x_ref), channel_id=1, source_target_pairs={{0,96},{32,64},{64,32},{96,0},{128,224},{160,192},{192,160},{224,1... | collective-permute-start | bytes 2506760 | tf_op jit(solution)/shard_map/ppermute | solution.py:294
  58.0 18.4 %collective-permute-start = (bf16[4,816,128]{2,1,0:T(8,128)(2,1)S(1)}, bf16[4,816,128]{2,1,0:T(8,128)(2,1)S(1)}, u32[]{:S(2)}, u32[]{:S(2)}) collective-permute-start(bf16[4,816,128]{2,1,0:T(8,128)(2,1)S(1)} %all-to-all-done.1.x_ref), channel_id=1, source_target_pairs={{0,384},{32,416},{64,448},{96,480},{128,256},{160,288},{192,320},{... | collective-permute-start | bytes 2506760 | tf_op jit(solution)/shard_map/ppermute | solution.py:294
  60.9 1.2 copy-start.2
  79.8 15.4 %collective-permute-start.6 = (bf16[4,816,128]{2,1,0:T(8,128)(2,1)S(1)}, bf16[4,816,128]{2,1,0:T(8,128)(2,1)S(1)}, u32[]{:S(2)}, u32[]{:S(2)}) collective-permute-start(bf16[4,816,128]{2,1,0:T(8,128)(2,1)S(1)} %get-tuple-element.14), channel_id=1, source_target_pairs={{0,160},{32,128},{64,224},{96,192},{128,32},{160,0},{192,96},{224,... | collective-permute-start | bytes 2506760 | tf_op jit(solution)/shard_map/ppermute | solution.py:306
  81.7 21.8 %collective-permute-start.7 = (bf16[4,816,128]{2,1,0:T(8,128)(2,1)S(1)}, bf16[4,816,128]{2,1,0:T(8,128)(2,1)S(1)}, u32[]{:S(2)}, u32[]{:S(2)}) collective-permute-start(bf16[4,816,128]{2,1,0:T(8,128)(2,1)S(1)} %get-tuple-element.15), channel_id=1, source_target_pairs={{0,32},{32,0},{64,96},{96,64},{128,160},{160,128},{192,224},{224,1... | collective-permute-start | bytes 2506760 | tf_op jit(solution)/shard_map/ppermute | solution.py:306
  85.9 18.1 %collective-permute-start.8 = (bf16[4,816,128]{2,1,0:T(8,128)(2,1)S(1)}, bf16[4,816,128]{2,1,0:T(8,128)(2,1)S(1)}, u32[]{:S(2)}, u32[]{:S(2)}) collective-permute-start(bf16[4,816,128]{2,1,0:T(8,128)(2,1)S(1)} %get-tuple-element.16), channel_id=1, source_target_pairs={{0,128},{32,160},{64,192},{96,224},{128,0},{160,32},{192,64},{224,... | collective-permute-start | bytes 2506760 | tf_op jit(solution)/shard_map/ppermute | solution.py:306
  104.2 20.1 %copy-start.5 = (s32[256,4]{0,1:T(4,128)S(1)}, s32[256,4]{0,1:T(4,128)}, u32[]{:S(2)}) copy-start(s32[256,4]{0,1:T(4,128)} %param.7) | copy-start | bytes 12292
  104.3 20.1 %copy-start.6 = (f32[256,4]{0,1:T(4,128)S(1)}, f32[256,4]{0,1:T(4,128)}, u32[]{:S(2)}) copy-start(f32[256,4]{0,1:T(4,128)} %param.8) | copy-start | bytes 12292
  119.1 19.1 %all-to-all-start.3 = ((bf16[16,56,128]{2,1,0:T(8,128)(2,1)}), bf16[16,56,128]{2,1,0:T(8,128)(2,1)S(1)}, u32[]{:S(2)}, u32[]{:S(2)}) async-start(bf16[16,56,128]{2,1,0:T(8,128)(2,1)} %bitcast.6), calls=%async_computation.3 | async-start | bytes 458752 | tf_op jit(solution)/shard_map/all_to_all | solution.py:269

commit v12 on v11

--- a/solution.py
+++ b/solution.py
@@ -284,7 +284,7 @@
     sent = call(
         dispatch_kernel,
         (EXPERTS * BLOCK, LANES),
-        *(ids, tokens),
+        *(ids, pltpu.with_memory_space_constraint(tokens, pltpu.HBM)),
         scratch=[pltpu.VMEM((2, n, LANES), BF16), pltpu.SemaphoreType.DMA((2,))],
         specs=(pltpu.VMEM, pltpu.HBM),
     )

time: 141 us -> 140 us (level)
    unnamed x14 -> x12, local copies, waits for them, and re-layouts: 3.06 us -> 1.93 us
where the time goes in v12:
time: 140 us; the launch traced here: 139 us
  waiting for transfers between devices  54.9 us (39%)
  starting transfers between devices  51.9 us (37%)
  Pallas kernels  15.7 us (11%)
  blocking collectives  13.9 us (10%)
  local copies, waits for them, and re-layouts  1.93 us (1%)
    all_to_all x3, waiting for transfers between devices, exchange(): lax.all_to_all(value, axis, split_axis=0, concat_axis=0, tiled=True, axis...  31.8 us
    all_to_all x3, starting transfers between devices, exchange(): lax.all_to_all(value, axis, split_axis=0, concat_axis=0, tiled=True, axis...  24.9 us
    pallas_call x14, Pallas kernels, call(): pl.pallas_call(kernel, out_shape=out, **places, scratch_shapes=scratch, c...  15.7 us
    all_to_all x1, blocking collectives, exchange(): lax.all_to_all(value, axis, split_axis=0, concat_axis=0, tiled=True, axis...  13.9 us
    ppermute x3, waiting for transfers between devices, shards(): lax.ppermute(out, plane, across(mask, 1))  13.7 us
    ppermute x3, starting transfers between devices, shards(): others = [lax.ppermute(rows, plane, across(mask, 0)) for mask in MASKS]  11.6 us
    ppermute x3, waiting for transfers between devices, shards(): others = [lax.ppermute(rows, plane, across(mask, 0)) for mask in MASKS]  9.3 us
    ppermute x3, starting transfers between devices, shards(): lax.ppermute(out, plane, across(mask, 1))  9.21 us
  transfers between devices with their start and end apart: 12, of which 8 were waited for; matrix products, arithmetic and copies ran while one was open for 0% of the time, Pallas kernels for 6%

profile of v12, /device:TPU:6, one launch (start us, length us, event | category | flops | bytes accessed | tf_op | source)
XLA Modules:
  0.0 138.6 jit_solution(6799471180626287467)
XLA Ops:
  0.0 0.7 copy-done.3
  0.7 2.0 %shard_map.64 = bf16[896,128]{1,0:T(8,128)(2,1)} custom-call(s32[4,256]{1,0:T(4,128)S(1)} %bitcast.18, bf16[128,3072]{1,0:T(8,128)(2,1)} %tokens_ref.1), custom_call_target="tpu_custom_call" | custom-call | tf_op jit(solution)/shard_map/pallas_call | solution.py:251
  2.7 0.0 copy-start.1
  2.7 0.0 copy-start
  2.7 15.3 %all-to-all-start = ((bf16[16,56,128]{2,1,0:T(8,128)(2,1)}), bf16[16,56,128]{2,1,0:T(8,128)(2,1)S(1)}, u32[]{:S(2)}, u32[]{:S(2)}) async-start(bf16[16,56,128]{2,1,0:T(8,128)(2,1)} %bitcast.1), calls=%async_computation | async-start | bytes 458752 | tf_op jit(solution)/shard_map/all_to_all | solution.py:269
  18.0 1.9 %collective-permute-start.1 = (bf16[168,3072]{1,0:T(8,128)(2,1)}, bf16[168,3072]{1,0:T(8,128)(2,1)}, u32[]{:S(2)}, u32[]{:S(2)}) collective-permute-start(bf16[168,3072]{1,0:T(8,128)(2,1)} %bitcast.10), channel_id=1, source_target_pairs={{0,1},{1,0},{2,3},{3,2},{4,5},{5,4},{6,7},{7,6},{8,9},{9,8},{10,11... | collective-permute-start | bytes 3096584 | tf_op jit(solution)/shard_map/ppermute | solution.py:265
  20.0 15.4 %all-to-all-done = bf16[16,56,128]{2,1,0:T(8,128)(2,1)S(1)} async-done(((bf16[16,56,128]{2,1,0:T(8,128)(2,1)}), bf16[16,56,128]{2,1,0:T(8,128)(2,1)S(1)}, u32[]{:S(2)}, u32[]{:S(2)}) %all-to-all-start) | async-done | bytes 229408 | tf_op jit(solution)/shard_map/all_to_all | solution.py:269
  35.4 1.0 shard_map.65
  36.5 4.3 %all-to-all-start.1 = ((bf16[4,816,128]{2,1,0:T(8,128)(2,1)}), bf16[4,816,128]{2,1,0:T(8,128)(2,1)S(1)}, u32[]{:S(2)}, u32[]{:S(2)}) async-start(bf16[4,816,128]{2,1,0:T(8,128)(2,1)} %shard_map.65), calls=%async_computation.1 | async-start | bytes 1671168 | tf_op jit(solution)/shard_map/all_to_all | solution.py:269
  40.8 0.0 copy-done.1
  40.8 1.9 %collective-permute-start.2 = (bf16[168,3072]{1,0:T(8,128)(2,1)S(1)}, bf16[168,3072]{1,0:T(8,128)(2,1)}, u32[]{:S(2)}, u32[]{:S(2)}) collective-permute-start(bf16[168,3072]{1,0:T(8,128)(2,1)S(1)} %bitcast.12), channel_id=1, source_target_pairs={{0,1},{1,0},{2,3},{3,2},{4,5},{5,4},{6,7},{7,6},{8,9},{9,8},{10,11... | collective-permute-start | bytes 3096584 | tf_op jit(solution)/shard_map/ppermute | solution.py:265
  42.7 2.4 %collective-permute-start.3 = (bf16[168,3072]{1,0:T(8,128)(2,1)}, bf16[168,3072]{1,0:T(8,128)(2,1)}, u32[]{:S(2)}, u32[]{:S(2)}) collective-permute-start(bf16[168,3072]{1,0:T(8,128)(2,1)} %bitcast.14), channel_id=1, source_target_pairs={{0,1},{1,0},{2,3},{3,2},{4,5},{5,4},{6,7},{7,6},{8,9},{9,8},{10,11... | collective-permute-start | bytes 3096584 | tf_op jit(solution)/shard_map/ppermute | solution.py:265
  45.1 3.4 %all-to-all-done.1.x_ref = bf16[4,816,128]{2,1,0:T(8,128)(2,1)S(1)} async-done(((bf16[4,816,128]{2,1,0:T(8,128)(2,1)}), bf16[4,816,128]{2,1,0:T(8,128)(2,1)S(1)}, u32[]{:S(2)}, u32[]{:S(2)}) %all-to-all-start.1) | async-done | bytes 835616 | tf_op jit(solution)/shard_map/all_to_all | solution.py:269
  48.5 4.8 %collective-permute-start.5 = (bf16[4,816,128]{2,1,0:T(8,128)(2,1)S(1)}, bf16[4,816,128]{2,1,0:T(8,128)(2,1)S(1)}, u32[]{:S(2)}, u32[]{:S(2)}) collective-permute-start(bf16[4,816,128]{2,1,0:T(8,128)(2,1)S(1)} %all-to-all-done.1.x_ref), channel_id=1, source_target_pairs={{0,480},{32,448},{64,416},{96,384},{128,352},{160,320},{192,288},{... | collective-permute-start | bytes 2506760 | tf_op jit(solution)/shard_map/ppermute | solution.py:294
  53.2 4.0 %collective-permute-start.4 = (bf16[4,816,128]{2,1,0:T(8,128)(2,1)S(1)}, bf16[4,816,128]{2,1,0:T(8,128)(2,1)S(1)}, u32[]{:S(2)}, u32[]{:S(2)}) collective-permute-start(bf16[4,816,128]{2,1,0:T(8,128)(2,1)S(1)} %all-to-all-done.1.x_ref), channel_id=1, source_target_pairs={{0,96},{32,64},{64,32},{96,0},{128,224},{160,192},{192,160},{224,1... | collective-permute-start | bytes 2506760 | tf_op jit(solution)/shard_map/ppermute | solution.py:294
  57.2 0.0 collective-permute-done.1.gate1
  57.3 2.9 %collective-permute-start = (bf16[4,816,128]{2,1,0:T(8,128)(2,1)S(1)}, bf16[4,816,128]{2,1,0:T(8,128)(2,1)S(1)}, u32[]{:S(2)}, u32[]{:S(2)}) collective-permute-start(bf16[4,816,128]{2,1,0:T(8,128)(2,1)S(1)} %all-to-all-done.1.x_ref), channel_id=1, source_target_pairs={{0,384},{32,416},{64,448},{96,480},{128,256},{160,288},{192,320},{... | collective-permute-start | bytes 2506760 | tf_op jit(solution)/shard_map/ppermute | solution.py:294
  60.1 0.0 collective-permute-done.2.up1
  60.1 0.0 collective-permute-done.3.down1
  60.1 0.0 copy-done
  60.1 0.0 copy-start.2
  60.2 1.2 copy-done.2
  61.4 2.3 %shard_map.66 = (bf16[768,3072]{1,0:T(8,128)(2,1)S(1)}, bf16[384,3072]{1,0:T(8,128)(2,1)S(1)}) custom-call(bf16[168,3072]{1,0:T(8,128)(2,1)S(1)} %bitcast.11, bf16[168,3072]{1,0:T(8,128)(2,1)S(1)} %bitcast.13, bf16[168,3072]{1,0:T(8,128)(2,1)S(1)} %bitcast.15, bf16[168,3072]{1,0:T(8,128)(2,1)} %collective-permute-done.1.gate1, ...), custom_call_target="tpu_custom_call" | custom-call | tf_op jit(solution)/shard_map/pallas_call | solution.py:251
  63.7 0.9 shard_map.67.sofar_ref
  64.6 1.7 %collective-permute-done.5.x_ref = bf16[4,816,128]{2,1,0:T(8,128)(2,1)S(1)} collective-permute-done((bf16[4,816,128]{2,1,0:T(8,128)(2,1)S(1)}, bf16[4,816,128]{2,1,0:T(8,128)(2,1)S(1)}, u32[]{:S(2)}, u32[]{:S(2)}) %collective-permute-start.5) | collective-permute-done | bytes 835616 | tf_op jit(solution)/shard_map/ppermute | solution.py:294
  66.3 0.9 shard_map.68.sofar_ref
  67.2 7.6 %collective-permute-done.4.x_ref = bf16[4,816,128]{2,1,0:T(8,128)(2,1)S(1)} collective-permute-done((bf16[4,816,128]{2,1,0:T(8,128)(2,1)S(1)}, bf16[4,816,128]{2,1,0:T(8,128)(2,1)S(1)}, u32[]{:S(2)}, u32[]{:S(2)}) %collective-permute-start.4) | collective-permute-done | bytes 835616 | tf_op jit(solution)/shard_map/ppermute | solution.py:294
  74.8 0.9 shard_map.69.sofar_ref
  75.7 0.0 collective-permute-done.x_ref
  75.7 3.4 %shard_map.70 = (bf16[544,384]{1,0:T(8,128)(2,1)S(1)}, bf16[4,816,128]{2,1,0:T(8,128)(2,1)S(1)}, bf16[4,816,128]{2,1,0:T(8,128)(2,1)S(1)}, bf16[4,816,128]{2,1,0:T(8,128)(2,1)S(1)}) custom-call(bf16[4,816,128]{2,1,0:T(8,128)(2,1)S(1)} %collective-permute-done.x_ref, bf16[768,3072]{1,0:T(8,128)(2,1)S(1)} %get-tuple-element.11.weights_ref, ...), custom_call_target="tpu_custom_call" | custom-call | tf_op jit(solution)/shard_map/pallas_call | solution.py:251
  79.1 1.9 %collective-permute-start.6 = (bf16[4,816,128]{2,1,0:T(8,128)(2,1)S(1)}, bf16[4,816,128]{2,1,0:T(8,128)(2,1)S(1)}, u32[]{:S(2)}, u32[]{:S(2)}) collective-permute-start(bf16[4,816,128]{2,1,0:T(8,128)(2,1)S(1)} %get-tuple-element.14), channel_id=1, source_target_pairs={{0,160},{32,128},{64,224},{96,192},{128,32},{160,0},{192,96},{224,... | collective-permute-start | bytes 2506760 | tf_op jit(solution)/shard_map/ppermute | solution.py:306
  81.0 4.2 %collective-permute-start.7 = (bf16[4,816,128]{2,1,0:T(8,128)(2,1)S(1)}, bf16[4,816,128]{2,1,0:T(8,128)(2,1)S(1)}, u32[]{:S(2)}, u32[]{:S(2)}) collective-permute-start(bf16[4,816,128]{2,1,0:T(8,128)(2,1)S(1)} %get-tuple-element.15), channel_id=1, source_target_pairs={{0,32},{32,0},{64,96},{96,64},{128,160},{160,128},{192,224},{224,1... | collective-permute-start | bytes 2506760 | tf_op jit(solution)/shard_map/ppermute | solution.py:306
  85.2 3.1 %collective-permute-start.8 = (bf16[4,816,128]{2,1,0:T(8,128)(2,1)S(1)}, bf16[4,816,128]{2,1,0:T(8,128)(2,1)S(1)}, u32[]{:S(2)}, u32[]{:S(2)}) collective-permute-start(bf16[4,816,128]{2,1,0:T(8,128)(2,1)S(1)} %get-tuple-element.16), channel_id=1, source_target_pairs={{0,128},{32,160},{64,192},{96,224},{128,0},{160,32},{192,64},{224,... | collective-permute-start | bytes 2506760 | tf_op jit(solution)/shard_map/ppermute | solution.py:306
  88.3 0.9 shard_map.71.a
  89.2 5.3 %collective-permute-done.6.b = bf16[4,816,128]{2,1,0:T(8,128)(2,1)S(1)} collective-permute-done((bf16[4,816,128]{2,1,0:T(8,128)(2,1)S(1)}, bf16[4,816,128]{2,1,0:T(8,128)(2,1)S(1)}, u32[]{:S(2)}, u32[]{:S(2)}) %collective-permute-start.6) | collective-permute-done | bytes 835616 | tf_op jit(solution)/shard_map/ppermute | solution.py:306
  94.5 0.2 shard_map.72.a
  94.6 8.1 %collective-permute-done.7.b = bf16[4,816,128]{2,1,0:T(8,128)(2,1)S(1)} collective-permute-done((bf16[4,816,128]{2,1,0:T(8,128)(2,1)S(1)}, bf16[4,816,128]{2,1,0:T(8,128)(2,1)S(1)}, u32[]{:S(2)}, u32[]{:S(2)}) %collective-permute-start.7) | collective-permute-done | bytes 835616 | tf_op jit(solution)/shard_map/ppermute | solution.py:306
  102.8 0.2 shard_map.73.a
  103.0 0.3 collective-permute-done.8.b
  103.3 0.2 shard_map.74
  103.5 0.0 copy-start.4
  103.5 0.0 copy-start.5
  103.5 13.9 %all_to_all.20.parts_ref = bf16[4,816,128]{2,1,0:T(8,128)(2,1)S(1)} all-to-all(bf16[4,816,128]{2,1,0:T(8,128)(2,1)S(1)} %shard_map.74), channel_id=1, replica_groups={{480,384,96,0},{416,448,32,64},{224,128,352,256},{160,192,288,320},{1,3..., dimensions={0} | all-to-all | bytes 1671168 | tf_op jit(solution)/shard_map/all_to_all | solution.py:269
  117.5 0.9 shard_map.75
  118.4 5.2 %all-to-all-start.3 = ((bf16[16,56,128]{2,1,0:T(8,128)(2,1)}), bf16[16,56,128]{2,1,0:T(8,128)(2,1)S(1)}, u32[]{:S(2)}, u32[]{:S(2)}) async-start(bf16[16,56,128]{2,1,0:T(8,128)(2,1)} %bitcast.6), calls=%async_computation.3 | async-start | bytes 458752 | tf_op jit(solution)/shard_map/all_to_all | solution.py:269
  123.6 0.8 shard_map.76.gates_ref
  124.4 13.0 %all-to-all-done.3 = bf16[16,56,128]{2,1,0:T(8,128)(2,1)S(1)} async-done(((bf16[16,56,128]{2,1,0:T(8,128)(2,1)}), bf16[16,56,128]{2,1,0:T(8,128)(2,1)S(1)}, u32[]{:S(2)}, u32[]{:S(2)}) %all-to-all-start.3) | async-done | bytes 229408 | tf_op jit(solution)/shard_map/all_to_all | solution.py:269
  137.4 1.2 shard_map.77
  (3 shorter events, 0.0 us)
Async XLA Ops:
  0.0 0.7 copy-start.3
  2.7 38.1 %copy-start.1 = (bf16[1,168,3072]{2,1,0:T(8,128)(2,1)S(1)}, bf16[1,168,3072]{2,1,0:T(8,128)(2,1)}, u32[]{:S(2)}) copy-start(bf16[1,168,3072]{2,1,0:T(8,128)(2,1)} %param.10) | copy-start | bytes 3096580
  2.7 57.4 %copy-start = (bf16[1,168,3072]{2,1,0:T(8,128)(2,1)S(1)}, bf16[1,168,3072]{2,1,0:T(8,128)(2,1)}, u32[]{:S(2)}) copy-start(bf16[1,168,3072]{2,1,0:T(8,128)(2,1)} %param.9) | copy-start | bytes 3096580
  2.7 32.7 %all-to-all-start = ((bf16[16,56,128]{2,1,0:T(8,128)(2,1)}), bf16[16,56,128]{2,1,0:T(8,128)(2,1)S(1)}, u32[]{:S(2)}, u32[]{:S(2)}) async-start(bf16[16,56,128]{2,1,0:T(8,128)(2,1)} %bitcast.1), calls=%async_computation | async-start | bytes 458752 | tf_op jit(solution)/shard_map/all_to_all | solution.py:269
  18.0 39.2 %collective-permute-start.1 = (bf16[168,3072]{1,0:T(8,128)(2,1)}, bf16[168,3072]{1,0:T(8,128)(2,1)}, u32[]{:S(2)}, u32[]{:S(2)}) collective-permute-start(bf16[168,3072]{1,0:T(8,128)(2,1)} %bitcast.10), channel_id=1, source_target_pairs={{0,1},{1,0},{2,3},{3,2},{4,5},{5,4},{6,7},{7,6},{8,9},{9,8},{10,11... | collective-permute-start | bytes 3096584 | tf_op jit(solution)/shard_map/ppermute | solution.py:265
  36.5 12.0 %all-to-all-start.1 = ((bf16[4,816,128]{2,1,0:T(8,128)(2,1)}), bf16[4,816,128]{2,1,0:T(8,128)(2,1)S(1)}, u32[]{:S(2)}, u32[]{:S(2)}) async-start(bf16[4,816,128]{2,1,0:T(8,128)(2,1)} %shard_map.65), calls=%async_computation.1 | async-start | bytes 1671168 | tf_op jit(solution)/shard_map/all_to_all | solution.py:269
  40.8 19.3 %collective-permute-start.2 = (bf16[168,3072]{1,0:T(8,128)(2,1)S(1)}, bf16[168,3072]{1,0:T(8,128)(2,1)}, u32[]{:S(2)}, u32[]{:S(2)}) collective-permute-start(bf16[168,3072]{1,0:T(8,128)(2,1)S(1)} %bitcast.12), channel_id=1, source_target_pairs={{0,1},{1,0},{2,3},{3,2},{4,5},{5,4},{6,7},{7,6},{8,9},{9,8},{10,11... | collective-permute-start | bytes 3096584 | tf_op jit(solution)/shard_map/ppermute | solution.py:265
  42.7 17.4 %collective-permute-start.3 = (bf16[168,3072]{1,0:T(8,128)(2,1)}, bf16[168,3072]{1,0:T(8,128)(2,1)}, u32[]{:S(2)}, u32[]{:S(2)}) collective-permute-start(bf16[168,3072]{1,0:T(8,128)(2,1)} %bitcast.14), channel_id=1, source_target_pairs={{0,1},{1,0},{2,3},{3,2},{4,5},{5,4},{6,7},{7,6},{8,9},{9,8},{10,11... | collective-permute-start | bytes 3096584 | tf_op jit(solution)/shard_map/ppermute | solution.py:265
  48.5 17.8 %collective-permute-start.5 = (bf16[4,816,128]{2,1,0:T(8,128)(2,1)S(1)}, bf16[4,816,128]{2,1,0:T(8,128)(2,1)S(1)}, u32[]{:S(2)}, u32[]{:S(2)}) collective-permute-start(bf16[4,816,128]{2,1,0:T(8,128)(2,1)S(1)} %all-to-all-done.1.x_ref), channel_id=1, source_target_pairs={{0,480},{32,448},{64,416},{96,384},{128,352},{160,320},{192,288},{... | collective-permute-start | bytes 2506760 | tf_op jit(solution)/shard_map/ppermute | solution.py:294
  53.2 21.5 %collective-permute-start.4 = (bf16[4,816,128]{2,1,0:T(8,128)(2,1)S(1)}, bf16[4,816,128]{2,1,0:T(8,128)(2,1)S(1)}, u32[]{:S(2)}, u32[]{:S(2)}) collective-permute-start(bf16[4,816,128]{2,1,0:T(8,128)(2,1)S(1)} %all-to-all-done.1.x_ref), channel_id=1, source_target_pairs={{0,96},{32,64},{64,32},{96,0},{128,224},{160,192},{192,160},{224,1... | collective-permute-start | bytes 2506760 | tf_op jit(solution)/shard_map/ppermute | solution.py:294
  57.3 18.4 %collective-permute-start = (bf16[4,816,128]{2,1,0:T(8,128)(2,1)S(1)}, bf16[4,816,128]{2,1,0:T(8,128)(2,1)S(1)}, u32[]{:S(2)}, u32[]{:S(2)}) collective-permute-start(bf16[4,816,128]{2,1,0:T(8,128)(2,1)S(1)} %all-to-all-done.1.x_ref), channel_id=1, source_target_pairs={{0,384},{32,416},{64,448},{96,480},{128,256},{160,288},{192,320},{... | collective-permute-start | bytes 2506760 | tf_op jit(solution)/shard_map/ppermute | solution.py:294
  60.1 1.2 copy-start.2
  79.1 15.4 %collective-permute-start.6 = (bf16[4,816,128]{2,1,0:T(8,128)(2,1)S(1)}, bf16[4,816,128]{2,1,0:T(8,128)(2,1)S(1)}, u32[]{:S(2)}, u32[]{:S(2)}) collective-permute-start(bf16[4,816,128]{2,1,0:T(8,128)(2,1)S(1)} %get-tuple-element.14), channel_id=1, source_target_pairs={{0,160},{32,128},{64,224},{96,192},{128,32},{160,0},{192,96},{224,... | collective-permute-start | bytes 2506760 | tf_op jit(solution)/shard_map/ppermute | solution.py:306
  81.0 21.8 %collective-permute-start.7 = (bf16[4,816,128]{2,1,0:T(8,128)(2,1)S(1)}, bf16[4,816,128]{2,1,0:T(8,128)(2,1)S(1)}, u32[]{:S(2)}, u32[]{:S(2)}) collective-permute-start(bf16[4,816,128]{2,1,0:T(8,128)(2,1)S(1)} %get-tuple-element.15), channel_id=1, source_target_pairs={{0,32},{32,0},{64,96},{96,64},{128,160},{160,128},{192,224},{224,1... | collective-permute-start | bytes 2506760 | tf_op jit(solution)/shard_map/ppermute | solution.py:306
  85.2 18.1 %collective-permute-start.8 = (bf16[4,816,128]{2,1,0:T(8,128)(2,1)S(1)}, bf16[4,816,128]{2,1,0:T(8,128)(2,1)S(1)}, u32[]{:S(2)}, u32[]{:S(2)}) collective-permute-start(bf16[4,816,128]{2,1,0:T(8,128)(2,1)S(1)} %get-tuple-element.16), channel_id=1, source_target_pairs={{0,128},{32,160},{64,192},{96,224},{128,0},{160,32},{192,64},{224,... | collective-permute-start | bytes 2506760 | tf_op jit(solution)/shard_map/ppermute | solution.py:306
  103.5 20.1 %copy-start.4 = (s32[256,4]{0,1:T(4,128)S(1)}, s32[256,4]{0,1:T(4,128)}, u32[]{:S(2)}) copy-start(s32[256,4]{0,1:T(4,128)} %param.7) | copy-start | bytes 12292
  103.5 20.1 %copy-start.5 = (f32[256,4]{0,1:T(4,128)S(1)}, f32[256,4]{0,1:T(4,128)}, u32[]{:S(2)}) copy-start(f32[256,4]{0,1:T(4,128)} %param.8) | copy-start | bytes 12292
  118.4 19.1 %all-to-all-start.3 = ((bf16[16,56,128]{2,1,0:T(8,128)(2,1)}), bf16[16,56,128]{2,1,0:T(8,128)(2,1)S(1)}, u32[]{:S(2)}, u32[]{:S(2)}) async-start(bf16[16,56,128]{2,1,0:T(8,128)(2,1)} %bitcast.6), calls=%async_computation.3 | async-start | bytes 458752 | tf_op jit(solution)/shard_map/all_to_all | solution.py:269

commit v13 on v12

--- a/solution.py
+++ b/solution.py
@@ -19,7 +19,7 @@
 SIDE = EXPERTS * HALF
 PART = 3 * SIDE
 WIDE = 384
-MASKS = (3, 1, 2)
+MASKS = (3, 2, 1)
 F32 = jnp.float32
 BF16 = jnp.bfloat16
 

time: 140 us -> 141 us (level)
  transfers between devices with their start and end apart: 12 -> 12, of which waited for: 8 -> 7; matrix products, arithmetic and copies ran while one was open for 0% -> 0% of each run, Pallas kernels for 6% -> 6%
where the time goes in v13:
time: 141 us; the launch traced here: 139 us
  waiting for transfers between devices  55.7 us (40%)
  starting transfers between devices  51.2 us (36%)
  Pallas kernels  15.7 us (11%)
  blocking collectives  14.4 us (10%)
  local copies, waits for them, and re-layouts  1.93 us (1%)
    all_to_all x3, waiting for transfers between devices, exchange(): lax.all_to_all(value, axis, split_axis=0, concat_axis=0, tiled=True, axis...  32.1 us
    all_to_all x3, starting transfers between devices, exchange(): lax.all_to_all(value, axis, split_axis=0, concat_axis=0, tiled=True, axis...  24.1 us
    pallas_call x14, Pallas kernels, call(): pl.pallas_call(kernel, out_shape=out, **places, scratch_shapes=scratch, c...  15.7 us
    all_to_all x1, blocking collectives, exchange(): lax.all_to_all(value, axis, split_axis=0, concat_axis=0, tiled=True, axis...  14.4 us
    ppermute x3, waiting for transfers between devices, shards(): lax.ppermute(out, plane, across(mask, 1))  13.9 us
    ppermute x3, starting transfers between devices, shards(): others = [lax.ppermute(rows, plane, across(mask, 0)) for mask in MASKS]  11.6 us
    ppermute x3, waiting for transfers between devices, shards(): others = [lax.ppermute(rows, plane, across(mask, 0)) for mask in MASKS]  9.64 us
    ppermute x3, starting transfers between devices, shards(): lax.ppermute(out, plane, across(mask, 1))  9.21 us
  transfers between devices with their start and end apart: 12, of which 7 were waited for; matrix products, arithmetic and copies ran while one was open for 0% of the time, Pallas kernels for 6%

profile of v13, /device:TPU:6, one launch (start us, length us, event | category | flops | bytes accessed | tf_op | source)
XLA Modules:
  0.0 139.3 jit_solution(12885015231790218719)
XLA Ops:
  0.0 0.7 copy-done.3
  0.7 2.0 %shard_map.64 = bf16[896,128]{1,0:T(8,128)(2,1)} custom-call(s32[4,256]{1,0:T(4,128)S(1)} %bitcast.18, bf16[128,3072]{1,0:T(8,128)(2,1)} %tokens_ref.1), custom_call_target="tpu_custom_call" | custom-call | tf_op jit(solution)/shard_map/pallas_call | solution.py:251
  2.7 0.0 copy-start.1
  2.7 0.0 copy-start
  2.7 15.3 %all-to-all-start = ((bf16[16,56,128]{2,1,0:T(8,128)(2,1)}), bf16[16,56,128]{2,1,0:T(8,128)(2,1)S(1)}, u32[]{:S(2)}, u32[]{:S(2)}) async-start(bf16[16,56,128]{2,1,0:T(8,128)(2,1)} %bitcast.1), calls=%async_computation | async-start | bytes 458752 | tf_op jit(solution)/shard_map/all_to_all | solution.py:269
  18.0 1.9 %collective-permute-start.1 = (bf16[168,3072]{1,0:T(8,128)(2,1)}, bf16[168,3072]{1,0:T(8,128)(2,1)}, u32[]{:S(2)}, u32[]{:S(2)}) collective-permute-start(bf16[168,3072]{1,0:T(8,128)(2,1)} %bitcast.10), channel_id=1, source_target_pairs={{0,1},{1,0},{2,3},{3,2},{4,5},{5,4},{6,7},{7,6},{8,9},{9,8},{10,11... | collective-permute-start | bytes 3096584 | tf_op jit(solution)/shard_map/ppermute | solution.py:265
  20.0 15.4 %all-to-all-done = bf16[16,56,128]{2,1,0:T(8,128)(2,1)S(1)} async-done(((bf16[16,56,128]{2,1,0:T(8,128)(2,1)}), bf16[16,56,128]{2,1,0:T(8,128)(2,1)S(1)}, u32[]{:S(2)}, u32[]{:S(2)}) %all-to-all-start) | async-done | bytes 229408 | tf_op jit(solution)/shard_map/all_to_all | solution.py:269
  35.4 1.0 shard_map.65
  36.5 4.3 %all-to-all-start.1 = ((bf16[4,816,128]{2,1,0:T(8,128)(2,1)}), bf16[4,816,128]{2,1,0:T(8,128)(2,1)S(1)}, u32[]{:S(2)}, u32[]{:S(2)}) async-start(bf16[4,816,128]{2,1,0:T(8,128)(2,1)} %shard_map.65), calls=%async_computation.1 | async-start | bytes 1671168 | tf_op jit(solution)/shard_map/all_to_all | solution.py:269
  40.8 0.0 copy-done.1
  40.8 1.9 %collective-permute-start.2 = (bf16[168,3072]{1,0:T(8,128)(2,1)S(1)}, bf16[168,3072]{1,0:T(8,128)(2,1)}, u32[]{:S(2)}, u32[]{:S(2)}) collective-permute-start(bf16[168,3072]{1,0:T(8,128)(2,1)S(1)} %bitcast.12), channel_id=1, source_target_pairs={{0,1},{1,0},{2,3},{3,2},{4,5},{5,4},{6,7},{7,6},{8,9},{9,8},{10,11... | collective-permute-start | bytes 3096584 | tf_op jit(solution)/shard_map/ppermute | solution.py:265
  42.7 2.4 %collective-permute-start.3 = (bf16[168,3072]{1,0:T(8,128)(2,1)}, bf16[168,3072]{1,0:T(8,128)(2,1)}, u32[]{:S(2)}, u32[]{:S(2)}) collective-permute-start(bf16[168,3072]{1,0:T(8,128)(2,1)} %bitcast.14), channel_id=1, source_target_pairs={{0,1},{1,0},{2,3},{3,2},{4,5},{5,4},{6,7},{7,6},{8,9},{9,8},{10,11... | collective-permute-start | bytes 3096584 | tf_op jit(solution)/shard_map/ppermute | solution.py:265
  45.1 3.4 %all-to-all-done.1.x_ref = bf16[4,816,128]{2,1,0:T(8,128)(2,1)S(1)} async-done(((bf16[4,816,128]{2,1,0:T(8,128)(2,1)}), bf16[4,816,128]{2,1,0:T(8,128)(2,1)S(1)}, u32[]{:S(2)}, u32[]{:S(2)}) %all-to-all-start.1) | async-done | bytes 835616 | tf_op jit(solution)/shard_map/all_to_all | solution.py:269
  48.5 4.8 %collective-permute-start.5 = (bf16[4,816,128]{2,1,0:T(8,128)(2,1)S(1)}, bf16[4,816,128]{2,1,0:T(8,128)(2,1)S(1)}, u32[]{:S(2)}, u32[]{:S(2)}) collective-permute-start(bf16[4,816,128]{2,1,0:T(8,128)(2,1)S(1)} %all-to-all-done.1.x_ref), channel_id=1, source_target_pairs={{0,480},{32,448},{64,416},{96,384},{128,352},{160,320},{192,288},{... | collective-permute-start | bytes 2506760 | tf_op jit(solution)/shard_map/ppermute | solution.py:294
  53.2 2.2 %collective-permute-start.4 = (bf16[4,816,128]{2,1,0:T(8,128)(2,1)S(1)}, bf16[4,816,128]{2,1,0:T(8,128)(2,1)S(1)}, u32[]{:S(2)}, u32[]{:S(2)}) collective-permute-start(bf16[4,816,128]{2,1,0:T(8,128)(2,1)S(1)} %all-to-all-done.1.x_ref), channel_id=1, source_target_pairs={{0,384},{32,416},{64,448},{96,480},{128,256},{160,288},{192,320},{... | collective-permute-start | bytes 2506760 | tf_op jit(solution)/shard_map/ppermute | solution.py:294
  55.5 0.0 collective-permute-done.1.gate1
  55.5 4.6 %collective-permute-start = (bf16[4,816,128]{2,1,0:T(8,128)(2,1)S(1)}, bf16[4,816,128]{2,1,0:T(8,128)(2,1)S(1)}, u32[]{:S(2)}, u32[]{:S(2)}) collective-permute-start(bf16[4,816,128]{2,1,0:T(8,128)(2,1)S(1)} %all-to-all-done.1.x_ref), channel_id=1, source_target_pairs={{0,96},{32,64},{64,32},{96,0},{128,224},{160,192},{192,160},{224,1... | collective-permute-start | bytes 2506760 | tf_op jit(solution)/shard_map/ppermute | solution.py:294
  60.1 0.0 collective-permute-done.2.up1
  60.1 0.0 collective-permute-done.3.down1
  60.1 0.0 copy-done
  60.1 0.0 copy-start.2
  60.2 1.2 copy-done.2
  61.4 2.3 %shard_map.66 = (bf16[768,3072]{1,0:T(8,128)(2,1)S(1)}, bf16[384,3072]{1,0:T(8,128)(2,1)S(1)}) custom-call(bf16[168,3072]{1,0:T(8,128)(2,1)S(1)} %bitcast.11, bf16[168,3072]{1,0:T(8,128)(2,1)S(1)} %bitcast.13, bf16[168,3072]{1,0:T(8,128)(2,1)S(1)} %bitcast.15, bf16[168,3072]{1,0:T(8,128)(2,1)} %collective-permute-done.1.gate1, ...), custom_call_target="tpu_custom_call" | custom-call | tf_op jit(solution)/shard_map/pallas_call | solution.py:251
  63.7 0.9 shard_map.67.sofar_ref
  64.6 1.7 %collective-permute-done.5.x_ref = bf16[4,816,128]{2,1,0:T(8,128)(2,1)S(1)} collective-permute-done((bf16[4,816,128]{2,1,0:T(8,128)(2,1)S(1)}, bf16[4,816,128]{2,1,0:T(8,128)(2,1)S(1)}, u32[]{:S(2)}, u32[]{:S(2)}) %collective-permute-start.5) | collective-permute-done | bytes 835616 | tf_op jit(solution)/shard_map/ppermute | solution.py:294
  66.3 0.9 shard_map.68.sofar_ref
  67.2 7.9 %collective-permute-done.4.x_ref = bf16[4,816,128]{2,1,0:T(8,128)(2,1)S(1)} collective-permute-done((bf16[4,816,128]{2,1,0:T(8,128)(2,1)S(1)}, bf16[4,816,128]{2,1,0:T(8,128)(2,1)S(1)}, u32[]{:S(2)}, u32[]{:S(2)}) %collective-permute-start.4) | collective-permute-done | bytes 835616 | tf_op jit(solution)/shard_map/ppermute | solution.py:294
  75.1 0.9 shard_map.69.sofar_ref
  76.0 0.0 collective-permute-done.x_ref
  76.1 3.4 %shard_map.70 = (bf16[544,384]{1,0:T(8,128)(2,1)S(1)}, bf16[4,816,128]{2,1,0:T(8,128)(2,1)S(1)}, bf16[4,816,128]{2,1,0:T(8,128)(2,1)S(1)}, bf16[4,816,128]{2,1,0:T(8,128)(2,1)S(1)}) custom-call(bf16[4,816,128]{2,1,0:T(8,128)(2,1)S(1)} %collective-permute-done.x_ref, bf16[768,3072]{1,0:T(8,128)(2,1)S(1)} %get-tuple-element.11.weights_ref, ...), custom_call_target="tpu_custom_call" | custom-call | tf_op jit(solution)/shard_map/pallas_call | solution.py:251
  79.4 1.9 %collective-permute-start.6 = (bf16[4,816,128]{2,1,0:T(8,128)(2,1)S(1)}, bf16[4,816,128]{2,1,0:T(8,128)(2,1)S(1)}, u32[]{:S(2)}, u32[]{:S(2)}) collective-permute-start(bf16[4,816,128]{2,1,0:T(8,128)(2,1)S(1)} %get-tuple-element.14), channel_id=1, source_target_pairs={{0,160},{32,128},{64,224},{96,192},{128,32},{160,0},{192,96},{224,... | collective-permute-start | bytes 2506760 | tf_op jit(solution)/shard_map/ppermute | solution.py:306
  81.3 2.7 %collective-permute-start.7 = (bf16[4,816,128]{2,1,0:T(8,128)(2,1)S(1)}, bf16[4,816,128]{2,1,0:T(8,128)(2,1)S(1)}, u32[]{:S(2)}, u32[]{:S(2)}) collective-permute-start(bf16[4,816,128]{2,1,0:T(8,128)(2,1)S(1)} %get-tuple-element.15), channel_id=1, source_target_pairs={{0,128},{32,160},{64,192},{96,224},{128,0},{160,32},{192,64},{224,... | collective-permute-start | bytes 2506760 | tf_op jit(solution)/shard_map/ppermute | solution.py:306
  84.1 4.5 %collective-permute-start.8 = (bf16[4,816,128]{2,1,0:T(8,128)(2,1)S(1)}, bf16[4,816,128]{2,1,0:T(8,128)(2,1)S(1)}, u32[]{:S(2)}, u32[]{:S(2)}) collective-permute-start(bf16[4,816,128]{2,1,0:T(8,128)(2,1)S(1)} %get-tuple-element.16), channel_id=1, source_target_pairs={{0,32},{32,0},{64,96},{96,64},{128,160},{160,128},{192,224},{224,1... | collective-permute-start | bytes 2506760 | tf_op jit(solution)/shard_map/ppermute | solution.py:306
  88.6 0.9 shard_map.71.a
  89.6 5.3 %collective-permute-done.6.b = bf16[4,816,128]{2,1,0:T(8,128)(2,1)S(1)} collective-permute-done((bf16[4,816,128]{2,1,0:T(8,128)(2,1)S(1)}, bf16[4,816,128]{2,1,0:T(8,128)(2,1)S(1)}, u32[]{:S(2)}, u32[]{:S(2)}) %collective-permute-start.6) | collective-permute-done | bytes 835616 | tf_op jit(solution)/shard_map/ppermute | solution.py:306
  94.8 0.2 shard_map.72.a
  95.0 8.7 %collective-permute-done.7.b = bf16[4,816,128]{2,1,0:T(8,128)(2,1)S(1)} collective-permute-done((bf16[4,816,128]{2,1,0:T(8,128)(2,1)S(1)}, bf16[4,816,128]{2,1,0:T(8,128)(2,1)S(1)}, u32[]{:S(2)}, u32[]{:S(2)}) %collective-permute-start.7) | collective-permute-done | bytes 835616 | tf_op jit(solution)/shard_map/ppermute | solution.py:306
  103.7 0.2 shard_map.73.a
  103.9 0.0 collective-permute-done.8.b
  103.9 0.2 shard_map.74
  104.1 0.0 copy-start.4
  104.1 0.0 copy-start.5
  104.1 14.4 %all_to_all.20.parts_ref = bf16[4,816,128]{2,1,0:T(8,128)(2,1)S(1)} all-to-all(bf16[4,816,128]{2,1,0:T(8,128)(2,1)S(1)} %shard_map.74), channel_id=1, replica_groups={{480,384,96,0},{416,448,32,64},{224,128,352,256},{160,192,288,320},{1,3..., dimensions={0} | all-to-all | bytes 1671168 | tf_op jit(solution)/shard_map/all_to_all | solution.py:269
  118.5 0.9 shard_map.75
  119.4 4.5 %all-to-all-start.3 = ((bf16[16,56,128]{2,1,0:T(8,128)(2,1)}), bf16[16,56,128]{2,1,0:T(8,128)(2,1)S(1)}, u32[]{:S(2)}, u32[]{:S(2)}) async-start(bf16[16,56,128]{2,1,0:T(8,128)(2,1)} %bitcast.6), calls=%async_computation.3 | async-start | bytes 458752 | tf_op jit(solution)/shard_map/all_to_all | solution.py:269
  124.0 0.8 shard_map.76.gates_ref
  124.7 13.3 %all-to-all-done.3 = bf16[16,56,128]{2,1,0:T(8,128)(2,1)S(1)} async-done(((bf16[16,56,128]{2,1,0:T(8,128)(2,1)}), bf16[16,56,128]{2,1,0:T(8,128)(2,1)S(1)}, u32[]{:S(2)}, u32[]{:S(2)}) %all-to-all-start.3) | async-done | bytes 229408 | tf_op jit(solution)/shard_map/all_to_all | solution.py:269
  138.1 1.2 shard_map.77
  (3 shorter events, 0.0 us)
Async XLA Ops:
  0.0 0.7 copy-start.3
  2.7 38.1 %copy-start.1 = (bf16[1,168,3072]{2,1,0:T(8,128)(2,1)S(1)}, bf16[1,168,3072]{2,1,0:T(8,128)(2,1)}, u32[]{:S(2)}) copy-start(bf16[1,168,3072]{2,1,0:T(8,128)(2,1)} %param.10) | copy-start | bytes 3096580
  2.7 57.4 %copy-start = (bf16[1,168,3072]{2,1,0:T(8,128)(2,1)S(1)}, bf16[1,168,3072]{2,1,0:T(8,128)(2,1)}, u32[]{:S(2)}) copy-start(bf16[1,168,3072]{2,1,0:T(8,128)(2,1)} %param.9) | copy-start | bytes 3096580
  2.7 32.7 %all-to-all-start = ((bf16[16,56,128]{2,1,0:T(8,128)(2,1)}), bf16[16,56,128]{2,1,0:T(8,128)(2,1)S(1)}, u32[]{:S(2)}, u32[]{:S(2)}) async-start(bf16[16,56,128]{2,1,0:T(8,128)(2,1)} %bitcast.1), calls=%async_computation | async-start | bytes 458752 | tf_op jit(solution)/shard_map/all_to_all | solution.py:269
  18.0 37.5 %collective-permute-start.1 = (bf16[168,3072]{1,0:T(8,128)(2,1)}, bf16[168,3072]{1,0:T(8,128)(2,1)}, u32[]{:S(2)}, u32[]{:S(2)}) collective-permute-start(bf16[168,3072]{1,0:T(8,128)(2,1)} %bitcast.10), channel_id=1, source_target_pairs={{0,1},{1,0},{2,3},{3,2},{4,5},{5,4},{6,7},{7,6},{8,9},{9,8},{10,11... | collective-permute-start | bytes 3096584 | tf_op jit(solution)/shard_map/ppermute | solution.py:265
  36.5 12.0 %all-to-all-start.1 = ((bf16[4,816,128]{2,1,0:T(8,128)(2,1)}), bf16[4,816,128]{2,1,0:T(8,128)(2,1)S(1)}, u32[]{:S(2)}, u32[]{:S(2)}) async-start(bf16[4,816,128]{2,1,0:T(8,128)(2,1)} %shard_map.65), calls=%async_computation.1 | async-start | bytes 1671168 | tf_op jit(solution)/shard_map/all_to_all | solution.py:269
  40.8 19.3 %collective-permute-start.2 = (bf16[168,3072]{1,0:T(8,128)(2,1)S(1)}, bf16[168,3072]{1,0:T(8,128)(2,1)}, u32[]{:S(2)}, u32[]{:S(2)}) collective-permute-start(bf16[168,3072]{1,0:T(8,128)(2,1)S(1)} %bitcast.12), channel_id=1, source_target_pairs={{0,1},{1,0},{2,3},{3,2},{4,5},{5,4},{6,7},{7,6},{8,9},{9,8},{10,11... | collective-permute-start | bytes 3096584 | tf_op jit(solution)/shard_map/ppermute | solution.py:265
  42.7 17.4 %collective-permute-start.3 = (bf16[168,3072]{1,0:T(8,128)(2,1)}, bf16[168,3072]{1,0:T(8,128)(2,1)}, u32[]{:S(2)}, u32[]{:S(2)}) collective-permute-start(bf16[168,3072]{1,0:T(8,128)(2,1)} %bitcast.14), channel_id=1, source_target_pairs={{0,1},{1,0},{2,3},{3,2},{4,5},{5,4},{6,7},{7,6},{8,9},{9,8},{10,11... | collective-permute-start | bytes 3096584 | tf_op jit(solution)/shard_map/ppermute | solution.py:265
  48.5 17.8 %collective-permute-start.5 = (bf16[4,816,128]{2,1,0:T(8,128)(2,1)S(1)}, bf16[4,816,128]{2,1,0:T(8,128)(2,1)S(1)}, u32[]{:S(2)}, u32[]{:S(2)}) collective-permute-start(bf16[4,816,128]{2,1,0:T(8,128)(2,1)S(1)} %all-to-all-done.1.x_ref), channel_id=1, source_target_pairs={{0,480},{32,448},{64,416},{96,384},{128,352},{160,320},{192,288},{... | collective-permute-start | bytes 2506760 | tf_op jit(solution)/shard_map/ppermute | solution.py:294
  53.2 21.9 %collective-permute-start.4 = (bf16[4,816,128]{2,1,0:T(8,128)(2,1)S(1)}, bf16[4,816,128]{2,1,0:T(8,128)(2,1)S(1)}, u32[]{:S(2)}, u32[]{:S(2)}) collective-permute-start(bf16[4,816,128]{2,1,0:T(8,128)(2,1)S(1)} %all-to-all-done.1.x_ref), channel_id=1, source_target_pairs={{0,384},{32,416},{64,448},{96,480},{128,256},{160,288},{192,320},{... | collective-permute-start | bytes 2506760 | tf_op jit(solution)/shard_map/ppermute | solution.py:294
  55.5 20.6 %collective-permute-start = (bf16[4,816,128]{2,1,0:T(8,128)(2,1)S(1)}, bf16[4,816,128]{2,1,0:T(8,128)(2,1)S(1)}, u32[]{:S(2)}, u32[]{:S(2)}) collective-permute-start(bf16[4,816,128]{2,1,0:T(8,128)(2,1)S(1)} %all-to-all-done.1.x_ref), channel_id=1, source_target_pairs={{0,96},{32,64},{64,32},{96,0},{128,224},{160,192},{192,160},{224,1... | collective-permute-start | bytes 2506760 | tf_op jit(solution)/shard_map/ppermute | solution.py:294
  60.1 1.2 copy-start.2
  79.4 15.4 %collective-permute-start.6 = (bf16[4,816,128]{2,1,0:T(8,128)(2,1)S(1)}, bf16[4,816,128]{2,1,0:T(8,128)(2,1)S(1)}, u32[]{:S(2)}, u32[]{:S(2)}) collective-permute-start(bf16[4,816,128]{2,1,0:T(8,128)(2,1)S(1)} %get-tuple-element.14), channel_id=1, source_target_pairs={{0,160},{32,128},{64,224},{96,192},{128,32},{160,0},{192,96},{224,... | collective-permute-start | bytes 2506760 | tf_op jit(solution)/shard_map/ppermute | solution.py:306
  81.3 22.3 %collective-permute-start.7 = (bf16[4,816,128]{2,1,0:T(8,128)(2,1)S(1)}, bf16[4,816,128]{2,1,0:T(8,128)(2,1)S(1)}, u32[]{:S(2)}, u32[]{:S(2)}) collective-permute-start(bf16[4,816,128]{2,1,0:T(8,128)(2,1)S(1)} %get-tuple-element.15), channel_id=1, source_target_pairs={{0,128},{32,160},{64,192},{96,224},{128,0},{160,32},{192,64},{224,... | collective-permute-start | bytes 2506760 | tf_op jit(solution)/shard_map/ppermute | solution.py:306
  84.1 19.8 %collective-permute-start.8 = (bf16[4,816,128]{2,1,0:T(8,128)(2,1)S(1)}, bf16[4,816,128]{2,1,0:T(8,128)(2,1)S(1)}, u32[]{:S(2)}, u32[]{:S(2)}) collective-permute-start(bf16[4,816,128]{2,1,0:T(8,128)(2,1)S(1)} %get-tuple-element.16), channel_id=1, source_target_pairs={{0,32},{32,0},{64,96},{96,64},{128,160},{160,128},{192,224},{224,1... | collective-permute-start | bytes 2506760 | tf_op jit(solution)/shard_map/ppermute | solution.py:306
  104.1 19.9 %copy-start.4 = (s32[256,4]{0,1:T(4,128)S(1)}, s32[256,4]{0,1:T(4,128)}, u32[]{:S(2)}) copy-start(s32[256,4]{0,1:T(4,128)} %param.7) | copy-start | bytes 12292
  104.1 19.9 %copy-start.5 = (f32[256,4]{0,1:T(4,128)S(1)}, f32[256,4]{0,1:T(4,128)}, u32[]{:S(2)}) copy-start(f32[256,4]{0,1:T(4,128)} %param.8) | copy-start | bytes 12292
  119.4 18.6 %all-to-all-start.3 = ((bf16[16,56,128]{2,1,0:T(8,128)(2,1)}), bf16[16,56,128]{2,1,0:T(8,128)(2,1)S(1)}, u32[]{:S(2)}, u32[]{:S(2)}) async-start(bf16[16,56,128]{2,1,0:T(8,128)(2,1)} %bitcast.6), calls=%async_computation.3 | async-start | bytes 458752 | tf_op jit(solution)/shard_map/all_to_all | solution.py:269
